TPU v7x, 128 devices: a whole 4x4x4 slice. The times are simulated.
128 devices in a mesh: fsdp: 128 (over x, y, z, core).
Axes of the slice: x: 4, y: 4, z: 4, core: 2. Of those that a mesh axis runs over, the one named last changes fastest.
Arguments:
- hidden_in: bfloat16 [16384, 1024], P('fsdp'), may hold values from -6 to 6
- cotangent: bfloat16 [16384, 1024], P('fsdp'), may hold values from -6 to 6
- seq_lengths: int32 [512], replicated, may hold values from 1 to 125, as said below
- seq_owner: int32 [512], replicated, may hold values from 0 to 127, as said below
- routes: int32 [16384, 8], P('fsdp'), may hold values from 0 to 31, all different within a row; in each aligned block of 128 rows (0 to 127, 128 to 255, ...) at most 36 rows name the same one
- query_key_value_weight: bfloat16 [2, 1024, 2048], P(None, 'fsdp'), may hold values from -0.25 to 0.25
- out_weight: bfloat16 [2, 1024, 1024], P(None, 'fsdp'), may hold values from -0.75 to 0.75
- router_weight: bfloat16 [2, 1024, 32], P(None, 'fsdp'), may hold values from -0.09375 to 0.09375
- gain_attn: bfloat16 [2, 1024], P(None, 'fsdp'), may hold values from 0.5 to 1.5
- gain_mlp: bfloat16 [2, 1024], P(None, 'fsdp'), may hold values from 0.5 to 1.5
- expert_in: bfloat16 [2, 16384, 2048], P(None, 'fsdp'), may hold values from -0.1875 to 0.1875
- expert_out: bfloat16 [2, 16384, 1024], P(None, 'fsdp'), may hold values from -1 to 1
Outputs:
- out_hidden: bfloat16 [16384, 1024], P('fsdp')
- grad_hidden: float32 [16384, 1024], P('fsdp')
- grad_qkv: float32 [2, 1024, 2048], P(None, 'fsdp')
- grad_out_proj: float32 [2, 1024, 1024], P(None, 'fsdp')
- grad_router: float32 [2, 1024, 32], P(None, 'fsdp')
- grad_gain_attn: float32 [2, 1024], P(None, 'fsdp')
- grad_gain_mlp: float32 [2, 1024], P(None, 'fsdp')
- grad_expert_in: float32 [2, 16384, 2048], P(None, 'fsdp')
- grad_expert_out: float32 [2, 16384, 1024], P(None, 'fsdp')
Inputs may be any that keep to these rules, and one draw needn't show every extreme that they name: `routes`: of the rows of one device (128 rows, aligned blocks), no expert is named by more than 36, and in every draw some expert is named by exactly 36 of one device's rows. `seq_lengths`: the 4 sequences of one device sum to at most 128 tokens; some sequence has exactly 125. `seq_owner`: every device owns exactly 4 sequences.
All inputs are finite; a program needn't handle non-finite values.
Results may differ from a plain program's by a relative error of at most 0.035.
Values may be sent and summed in bfloat16 or wider, within the bound.
No kernel may reach another device: no remote copies, remote signals or barrier semaphores. Data moves between devices by JAX's collectives and lax.ppermute only.
A program may use at most 320 MiB of HBM per device.

v0:
```python
import math

import jax
import jax.numpy as jnp
from jax import lax
from jax.sharding import PartitionSpec as P

MODEL_WIDTH = 1024
QUERY_HEADS = 16
KEY_VALUE_HEADS = 8
HEAD_SIZE = 64
E = 32
TOPK = 8
LAYER_COUNT = 2
SEQ_DEV = 4
TOK_DEV = 128
CAP = 36


EPSILON = 1e-06
ROPE_BASE = 10000.0
MASKED = -1e30


def sent_together(arrays, axis, dim, along):
    widths = [math.prod(a.shape[along:]) for a in arrays]
    both = jnp.concatenate(
        [a.reshape(*a.shape[:along], w) for a, w in zip(arrays, widths)], axis=along
    )
    out = lax.all_gather(both, axis, axis=dim, tiled=True)
    pieces = jnp.split(out, [sum(widths[:k]) for k in range(1, len(widths))], axis=along)
    return tuple((b.reshape(*out.shape[:along], *a.shape[along:]) for a, b in zip(arrays, pieces)))


def cut_along(value, dim, devices):
    before, after = (value.shape[:dim], value.shape[dim + 1 :])
    return jnp.moveaxis(value.reshape(*before, devices, -1, *after), dim, 0)


def sum_packed(arrays, axis, dims):
    devices = lax.axis_size(axis)
    pieces = [cut_along(a, dim, devices) for a, dim in zip(arrays, dims)]
    lines = jnp.concatenate([b.reshape(devices, -1) for b in pieces], axis=1)
    extent = max(16, -(-lines.shape[1] // 1024) * 8)
    lines = jnp.pad(lines, ((0, 0), (0, extent * 128 - lines.shape[1]))).reshape(-1, 128)
    flat, at, finished = (lax.psum_scatter(lines, axis, tiled=True).reshape(-1), 0, [])
    for b in pieces:
        part = b[0]
        finished.append(flat[at : at + part.size].reshape(part.shape))
        at += part.size
    return tuple(finished)


def seq_layout(seq_lengths, seq_owner, device):
    owned_seq = seq_owner == device
    ranking = jnp.cumsum(owned_seq.astype(jnp.int32)) - 1
    counter = jnp.arange(SEQ_DEV, dtype=jnp.int32)
    picker = (owned_seq[None, :] & (ranking[None, :] == counter[:, None])).astype(jnp.int32)
    own_lengths = jnp.sum(picker * seq_lengths[None, :], axis=1)
    seq_ends = jnp.cumsum(own_lengths)
    slot_ids = jnp.arange(TOK_DEV, dtype=jnp.int32)
    segment = jnp.sum((slot_ids[:, None] >= seq_ends[None, :]).astype(jnp.int32), axis=1)
    seq_starts = seq_ends - own_lengths
    first_slot = jnp.sum(
        jnp.where(segment[:, None] == counter[None, :], seq_starts[None, :], 0), axis=1
    )
    position = slot_ids - first_slot
    allowed = (segment[:, None] == segment[None, :]) & (slot_ids[:, None] >= slot_ids[None, :])
    return (position, segment < SEQ_DEV, allowed)


def rope_tables(position):
    half_size = HEAD_SIZE // 2
    exponent = jnp.arange(half_size, dtype=jnp.float32) * (2.0 / HEAD_SIZE)
    frequency = jnp.exp(-math.log(ROPE_BASE) * exponent)
    angles = position.astype(jnp.float32)[:, None] * frequency[None, :]
    return (jnp.cos(angles), jnp.sin(angles))


def apply_rotation(values, cosine_table, sine_values):
    half_size = values.shape[-1] // 2
    first_half = values[..., :half_size]
    second_half = values[..., half_size:]
    cos_wide = cosine_table[:, None, :]
    sin_wide = sine_values[:, None, :]
    return jnp.concatenate(
        [
            first_half * cos_wide - second_half * sin_wide,
            second_half * cos_wide + first_half * sin_wide,
        ],
        axis=-1,
    )


def unrotate(grad_rot, cosine_table, sine_values):
    half_size = grad_rot.shape[-1] // 2
    first_half = grad_rot[..., :half_size]
    second_half = grad_rot[..., half_size:]
    cos_wide = cosine_table[:, None, :]
    sin_wide = sine_values[:, None, :]
    return jnp.concatenate(
        [
            first_half * cos_wide + second_half * sin_wide,
            second_half * cos_wide - first_half * sin_wide,
        ],
        axis=-1,
    )


def rounded(values):
    return lax.optimization_barrier(values.astype(jnp.bfloat16)).astype(jnp.float32)


def dispatch_index(route_block, live_row):
    row_count = route_block.shape[0]
    onehot = (
        (route_block[:, :, None] == jnp.arange(E, dtype=jnp.int32)[None, None, :])
        & live_row[:, None, None]
    ).astype(jnp.int32)
    flat_hits = onehot.reshape(row_count * TOPK, E)
    earlier = jnp.cumsum(flat_hits, axis=0) - flat_hits
    slot_number = jnp.sum(earlier * flat_hits, axis=1)
    valid_row = jnp.repeat(live_row, TOPK)
    flat_index = jnp.where(valid_row, route_block.reshape(-1) * CAP + slot_number, E * CAP)
    return (flat_index, valid_row)


def fill_buffer(values_low, flat_index):
    width = values_low.shape[-1]
    return jnp.zeros((E * CAP, width), jnp.bfloat16).at[flat_index].set(values_low, mode="drop")


def pack_rows(values_low, flat_index, devices):
    group_size = devices // E
    width = values_low.shape[-1]
    buffer = fill_buffer(values_low, flat_index)
    return jnp.broadcast_to(buffer.reshape(E, 1, CAP, width), (E, group_size, CAP, width)).reshape(
        devices, CAP, width
    )


def unpack_sum(returned, devices):
    group_size = devices // E
    return jnp.sum(
        returned.astype(jnp.float32).reshape(E, group_size, CAP, MODEL_WIDTH), axis=1
    ).reshape(E * CAP, MODEL_WIDTH)


def norm_back(grad_norm, normed, inverse):
    return inverse * (grad_norm - normed * jnp.mean(grad_norm * normed, axis=-1, keepdims=True))


def probabilities(rotated_query, rotated_key, allowed):
    scores = jnp.einsum(
        "tkgd,ukd->kgtu", rotated_query, rotated_key, preferred_element_type=jnp.float32
    ) * HEAD_SIZE ** (-0.5)
    scores = jnp.where(allowed[None, None], scores, MASKED)
    biggest = jnp.max(scores, axis=-1, keepdims=True)
    exp_scores = jnp.exp(scores - biggest)
    return exp_scores / jnp.sum(exp_scores, axis=-1, keepdims=True)


def attend_forward(hidden, weights, live, allowed, cosine_table, sine_values):
    qkv_full, out_full, router_full, gain_one, gain_two = weights
    token_total = hidden.shape[0]
    query_width = QUERY_HEADS * HEAD_SIZE
    key_value_width = KEY_VALUE_HEADS * HEAD_SIZE
    inverse = lax.rsqrt(jnp.mean(hidden * hidden, axis=-1, keepdims=True) + EPSILON)
    normed = hidden * inverse
    normed_low = (normed * gain_one.astype(jnp.float32)).astype(jnp.bfloat16)
    projected_rows = jnp.dot(normed_low, qkv_full, preferred_element_type=jnp.float32)
    rotated_query = apply_rotation(
        projected_rows[:, :query_width].reshape(token_total, QUERY_HEADS, HEAD_SIZE),
        cosine_table,
        sine_values,
    ).astype(jnp.bfloat16)
    rotated_query = rotated_query.reshape(
        token_total, KEY_VALUE_HEADS, QUERY_HEADS // KEY_VALUE_HEADS, HEAD_SIZE
    )
    rotated_key = apply_rotation(
        projected_rows[:, query_width : query_width + key_value_width].reshape(
            token_total, KEY_VALUE_HEADS, HEAD_SIZE
        ),
        cosine_table,
        sine_values,
    ).astype(jnp.bfloat16)
    reduced_value = (
        projected_rows[:, query_width + key_value_width :]
        .reshape(token_total, KEY_VALUE_HEADS, HEAD_SIZE)
        .astype(jnp.bfloat16)
    )
    softmaxed = probabilities(rotated_query, rotated_key, allowed)
    mixed = jnp.einsum(
        "kgtu,ukd->tkgd",
        softmaxed.astype(jnp.bfloat16),
        reduced_value,
        preferred_element_type=jnp.float32,
    )
    mixed_low = (mixed.reshape(token_total, query_width) * live[:, None]).astype(jnp.bfloat16)
    attn_out = jnp.dot(mixed_low, out_full, preferred_element_type=jnp.float32)
    return (
        hidden + attn_out,
        (inverse, normed, normed_low, rotated_query, rotated_key, reduced_value, mixed_low),
    )


def expert_forward(hidden, weights, expert_in_l, expert_out_l, live, routes, flat_index, devices):
    qkv_full, out_full, router_full, gain_one, gain_two = weights
    token_total = hidden.shape[0]
    inverse_two = lax.rsqrt(jnp.mean(hidden * hidden, axis=-1, keepdims=True) + EPSILON)
    normed_two = hidden * inverse_two
    routed_in = (normed_two * gain_two.astype(jnp.float32)).astype(jnp.bfloat16)
    logits = jnp.dot(routed_in, router_full, preferred_element_type=jnp.float32)
    chosen = jnp.take_along_axis(logits, routes, axis=1)
    top_logit = jnp.max(chosen, axis=-1, keepdims=True)
    exp_chosen = jnp.exp(chosen - top_logit)
    gate_prob = exp_chosen / jnp.sum(exp_chosen, axis=-1, keepdims=True)
    gate_live = gate_prob * live[:, None]
    repeated = jnp.repeat(routed_in, TOPK, axis=0)
    rows_flat = lax.all_to_all(
        pack_rows(repeated, flat_index, devices), "fsdp", split_axis=0, concat_axis=0, tiled=True
    ).reshape(-1, MODEL_WIDTH)
    gate_pre = lax.dot_general(
        rows_flat,
        expert_in_l[:, :MODEL_WIDTH],
        (((1,), (1,)), ((), ())),
        preferred_element_type=jnp.float32,
    )
    up_pre = lax.dot_general(
        rows_flat,
        expert_in_l[:, MODEL_WIDTH:],
        (((1,), (1,)), ((), ())),
        preferred_element_type=jnp.float32,
    )
    units = (jax.nn.silu(gate_pre) * up_pre).astype(jnp.bfloat16)
    partial_value = jnp.dot(units, expert_out_l, preferred_element_type=jnp.float32).astype(
        jnp.bfloat16
    )
    summed = unpack_sum(
        lax.all_to_all(
            partial_value.reshape(devices, CAP, MODEL_WIDTH),
            "fsdp",
            split_axis=0,
            concat_axis=0,
            tiled=True,
        ),
        devices,
    )
    picked = summed[jnp.clip(flat_index, 0, E * CAP - 1)].reshape(token_total, TOPK, MODEL_WIDTH)
    result = hidden + jnp.sum(gate_live[:, :, None] * picked, axis=1)
    return (
        result,
        (
            inverse_two,
            normed_two,
            routed_in,
            gate_prob,
            gate_live,
            picked,
            gate_pre,
            up_pre,
            rows_flat,
        ),
    )


def expert_backward(
    grad_out,
    weights,
    expert_in_l,
    expert_out_l,
    live,
    routes,
    flat_index,
    valid_row,
    expert_stash,
    devices,
):
    qkv_full, out_full, router_full, gain_one, gain_two = weights
    (
        inverse_two,
        normed_two,
        routed_in,
        gate_prob,
        gate_live,
        picked,
        gate_pre,
        up_pre,
        rows_flat,
    ) = expert_stash
    token_total = grad_out.shape[0]
    grad_gate = jnp.sum(picked * grad_out[:, None, :], axis=-1) * live[:, None]
    grad_chosen = gate_prob * (grad_gate - jnp.sum(gate_prob * grad_gate, axis=-1, keepdims=True))
    onehot_routes = (routes[:, :, None] == jnp.arange(E, dtype=jnp.int32)[None, None, :]).astype(
        jnp.float32
    )
    grad_logits = jnp.sum(grad_chosen[:, :, None] * onehot_routes, axis=1).astype(jnp.bfloat16)
    router_grad = lax.dot_general(
        routed_in, grad_logits, (((0,), (0,)), ((), ())), preferred_element_type=jnp.float32
    )
    grad_routed = lax.dot_general(
        grad_logits, router_full, (((1,), (1,)), ((), ())), preferred_element_type=jnp.float32
    )
    slot_grads = (
        (gate_live[:, :, None] * grad_out[:, None, :])
        .reshape(token_total * TOPK, MODEL_WIDTH)
        .astype(jnp.bfloat16)
    )
    grad_rows = lax.all_to_all(
        pack_rows(slot_grads, flat_index, devices), "fsdp", split_axis=0, concat_axis=0, tiled=True
    ).reshape(-1, MODEL_WIDTH)
    sigmoid_pre = jax.nn.sigmoid(gate_pre)
    activated = gate_pre * sigmoid_pre
    units = (activated * up_pre).astype(jnp.bfloat16)
    out_grad = lax.dot_general(
        units, grad_rows, (((0,), (0,)), ((), ())), preferred_element_type=jnp.float32
    )
    grad_units = lax.dot_general(
        grad_rows, expert_out_l, (((1,), (1,)), ((), ())), preferred_element_type=jnp.float32
    )
    grad_gate_pre = (
        grad_units * up_pre * (sigmoid_pre * (1.0 + gate_pre * (1.0 - sigmoid_pre)))
    ).astype(jnp.bfloat16)
    grad_up_pre = (grad_units * activated).astype(jnp.bfloat16)
    gate_w_grad = lax.dot_general(
        grad_gate_pre, rows_flat, (((0,), (0,)), ((), ())), preferred_element_type=jnp.float32
    )
    up_w_grad = lax.dot_general(
        grad_up_pre, rows_flat, (((0,), (0,)), ((), ())), preferred_element_type=jnp.float32
    )
    grad_in_rows = jnp.dot(
        grad_gate_pre, expert_in_l[:, :MODEL_WIDTH], preferred_element_type=jnp.float32
    )
    grad_in_rows = (
        grad_in_rows
        + jnp.dot(grad_up_pre, expert_in_l[:, MODEL_WIDTH:], preferred_element_type=jnp.float32)
    ).astype(jnp.bfloat16)
    grad_slots = unpack_sum(
        lax.all_to_all(
            grad_in_rows.reshape(devices, CAP, MODEL_WIDTH),
            "fsdp",
            split_axis=0,
            concat_axis=0,
            tiled=True,
        ),
        devices,
    )
    gathered = (
        grad_slots[jnp.clip(flat_index, 0, E * CAP - 1)] * valid_row.astype(jnp.float32)[:, None]
    )
    grad_routed = grad_routed + jnp.sum(gathered.reshape(token_total, TOPK, MODEL_WIDTH), axis=1)
    gain_two_grad = jnp.sum(grad_routed * normed_two, axis=0)
    grad_h1 = grad_out + norm_back(
        grad_routed * gain_two.astype(jnp.float32), normed_two, inverse_two
    )
    in_grad = jnp.concatenate([gate_w_grad, up_w_grad], axis=1)
    return (grad_h1, router_grad, gain_two_grad, in_grad, out_grad)


def attend_backward(grad_h1, weights, live, allowed, cosine_table, sine_values, attn_stash):
    qkv_full, out_full, router_full, gain_one, gain_two = weights
    inverse, normed, normed_low, rotated_query, rotated_key, reduced_value, mixed_low = attn_stash
    token_total = grad_h1.shape[0]
    query_width = QUERY_HEADS * HEAD_SIZE
    key_value_width = KEY_VALUE_HEADS * HEAD_SIZE
    grad_low = grad_h1.astype(jnp.bfloat16)
    proj_grad = lax.dot_general(
        mixed_low, grad_low, (((0,), (0,)), ((), ())), preferred_element_type=jnp.float32
    )
    mixed_gradient = lax.dot_general(
        grad_low, out_full, (((1,), (1,)), ((), ())), preferred_element_type=jnp.float32
    ).astype(jnp.bfloat16)
    mixed_gradient = jnp.where(live[:, None] > 0.5, mixed_gradient, jnp.zeros_like(mixed_gradient))
    mixed_gradient = mixed_gradient.reshape(
        token_total, KEY_VALUE_HEADS, QUERY_HEADS // KEY_VALUE_HEADS, HEAD_SIZE
    )
    softmaxed = probabilities(rotated_query, rotated_key, allowed)
    grad_probs = jnp.einsum(
        "tkgd,ukd->kgtu", mixed_gradient, reduced_value, preferred_element_type=jnp.float32
    )
    grad_value = jnp.einsum(
        "kgtu,tkgd->ukd",
        softmaxed.astype(jnp.bfloat16),
        mixed_gradient,
        preferred_element_type=jnp.float32,
    )
    grad_scores = (
        softmaxed * (grad_probs - jnp.sum(softmaxed * grad_probs, axis=-1, keepdims=True))
    ).astype(jnp.bfloat16)
    grad_query = jnp.einsum(
        "kgtu,ukd->tkgd", grad_scores, rotated_key, preferred_element_type=jnp.float32
    ) * HEAD_SIZE ** (-0.5)
    grad_key = jnp.einsum(
        "kgtu,tkgd->ukd", grad_scores, rotated_query, preferred_element_type=jnp.float32
    ) * HEAD_SIZE ** (-0.5)
    grad_query = unrotate(
        rounded(grad_query.reshape(token_total, QUERY_HEADS, HEAD_SIZE)), cosine_table, sine_values
    ).astype(jnp.bfloat16)
    grad_key = unrotate(rounded(grad_key), cosine_table, sine_values).astype(jnp.bfloat16)
    grad_proj = jnp.concatenate(
        [
            grad_query.reshape(token_total, query_width),
            grad_key.reshape(token_total, key_value_width),
            grad_value.astype(jnp.bfloat16).reshape(token_total, key_value_width),
        ],
        axis=1,
    )
    qkv_grad = lax.dot_general(
        normed_low, grad_proj, (((0,), (0,)), ((), ())), preferred_element_type=jnp.float32
    )
    grad_normed = lax.dot_general(
        grad_proj, qkv_full, (((1,), (1,)), ((), ())), preferred_element_type=jnp.float32
    )
    gain_one_grad = jnp.sum(grad_normed * normed, axis=0)
    grad_input = grad_h1 + norm_back(grad_normed * gain_one.astype(jnp.float32), normed, inverse)
    return (grad_input, qkv_grad, proj_grad, gain_one_grad)


def on_device(
    hidden_in,
    cotangent,
    seq_lengths,
    seq_owner,
    routes,
    query_key_value_weight,
    out_weight,
    router_weight,
    gain_attn,
    gain_mlp,
    expert_in,
    expert_out,
):
    devices = lax.axis_size("fsdp")
    device = lax.axis_index("fsdp")
    position, live_row, allowed = seq_layout(seq_lengths, seq_owner, device)
    live = live_row.astype(jnp.float32)
    cosine_table, sine_values = rope_tables(position)
    flat_index, valid_row = dispatch_index(routes, live_row)
    hidden = hidden_in.astype(jnp.float32)
    saved_layers = []
    for layer_index in range(LAYER_COUNT):
        weights = sent_together(
            (
                query_key_value_weight[layer_index],
                out_weight[layer_index],
                router_weight[layer_index],
                gain_attn[layer_index],
                gain_mlp[layer_index],
            ),
            "fsdp",
            0,
            1,
        )
        hidden, attn_stash = attend_forward(
            hidden, weights, live, allowed, cosine_table, sine_values
        )
        hidden, expert_stash = expert_forward(
            hidden,
            weights,
            expert_in[layer_index],
            expert_out[layer_index],
            live,
            routes,
            flat_index,
            devices,
        )
        saved_layers.append((attn_stash, expert_stash))
    output_low = hidden.astype(jnp.bfloat16)
    grad_hidden = cotangent.astype(jnp.float32)
    layer_grads = [None] * LAYER_COUNT
    expert_grads = [None] * LAYER_COUNT
    for layer_index in reversed(range(LAYER_COUNT)):
        weights = sent_together(
            (
                query_key_value_weight[layer_index],
                out_weight[layer_index],
                router_weight[layer_index],
                gain_attn[layer_index],
                gain_mlp[layer_index],
            ),
            "fsdp",
            0,
            1,
        )
        attn_stash, expert_stash = saved_layers[layer_index]
        grad_hidden, router_grad, gain_two_grad, in_grad, out_grad = expert_backward(
            grad_hidden,
            weights,
            expert_in[layer_index],
            expert_out[layer_index],
            live,
            routes,
            flat_index,
            valid_row,
            expert_stash,
            devices,
        )
        grad_hidden, qkv_grad, proj_grad, gain_one_grad = attend_backward(
            grad_hidden, weights, live, allowed, cosine_table, sine_values, attn_stash
        )
        layer_grads[layer_index] = sum_packed(
            (qkv_grad, proj_grad, router_grad, gain_one_grad, gain_two_grad),
            "fsdp",
            (0, 0, 0, 0, 0),
        )
        expert_grads[layer_index] = (in_grad, out_grad)
    stacked = tuple(
        (
            jnp.stack([layer_grads[layer_index][member] for layer_index in range(LAYER_COUNT)])
            for member in range(5)
        )
    )
    grad_in_experts = jnp.stack(
        [expert_grads[layer_index][0] for layer_index in range(LAYER_COUNT)]
    )
    grad_out_experts = jnp.stack(
        [expert_grads[layer_index][1] for layer_index in range(LAYER_COUNT)]
    )
    return (
        output_low,
        grad_hidden,
        stacked[0],
        stacked[1],
        stacked[2],
        stacked[3],
        stacked[4],
        grad_in_experts,
        grad_out_experts,
    )


def solution(mesh):
    placed = (
        P("fsdp", None),
        P("fsdp", None),
        P(),
        P(),
        P("fsdp", None),
        P(None, "fsdp", None),
        P(None, "fsdp", None),
        P(None, "fsdp", None),
        P(None, "fsdp"),
        P(None, "fsdp"),
        P(None, "fsdp", None),
        P(None, "fsdp", None),
    )
    return jax.shard_map(
        on_device,
        mesh=mesh,
        in_specs=placed,
        out_specs=(
            P("fsdp", None),
            P("fsdp", None),
            P(None, "fsdp", None),
            P(None, "fsdp", None),
            P(None, "fsdp", None),
            P(None, "fsdp"),
            P(None, "fsdp"),
            P(None, "fsdp", None),
            P(None, "fsdp", None),
        ),
        check_vma=False,
    )
```

profile of v0, /device:TPU:2, one launch (start us, length us, event | category | flops | bytes accessed | tf_op | source)
XLA Modules:
  0.0 1839.0 jit_solution(17377285830469298411)
XLA Ops:
  18.9 9.0 reduce-window.31
  29.9 53.4 %all-gather.3.cloned.1.call-done = bf16[1024,3106]{1,0:T(8,128)(2,1)} async-done(((bf16[8,3106]{1,0:T(8,128)(2,1)}), bf16[1024,3106]{1,0:T(8,128)(2,1)}) %all-gather.3.cloned.1.call-update) | async-done | bytes 6361104 | tf_op jit(solution)/shard_map/all_gather | solution.py:30
  93.3 7.0 scatter_custom_fusion
  108.1 7.3 all-to-all-start
  116.8 132.2 %all-to-all-done = bf16[128,36,1024]{2,1,0:T(8,128)(2,1)} async-done(((bf16[128,36,1024]{2,1,0:T(8,128)(2,1)}), bf16[128,36,1024]{2,1,0:T(8,128)(2,1)}, u32[]{:S(2)}, u32[]{:S(2)}) %all-to-all-start) | async-done | bytes 9437216 | tf_op jit(solution)/shard_map/all_to_all | solution.py:220
  249.0 13.1 reshape.630
  262.1 6.3 fusion.122
  279.3 13.1 reshape.631
  292.4 11.1 all-to-all-start.1
  304.9 7.0 gather_fusion.4
  314.2 120.7 %all-to-all-done.1 = bf16[128,36,1024]{2,1,0:T(8,128)(2,1)} async-done(((bf16[128,36,1024]{2,1,0:T(8,128)(2,1)}), bf16[128,36,1024]{2,1,0:T(8,128)(2,1)}, u32[]{:S(2)}, u32[]{:S(2)}) %all-to-all-start.1) | async-done | bytes 9437216 | tf_op jit(solution)/shard_map/all_to_all | solution.py:240
  434.9 9.6 convert_reduce_fusion.3
  444.5 5.2 reshape.634
  449.8 8.7 gather_fusion
  471.4 7.3 scatter_custom_fusion.1
  486.4 11.1 all-to-all-start.2
  499.0 7.0 gather_fusion.5
  506.5 7.5 scatter_custom_fusion.2
  516.6 113.7 %all-to-all-done.2 = bf16[128,36,1024]{2,1,0:T(8,128)(2,1)} async-done(((bf16[128,36,1024]{2,1,0:T(8,128)(2,1)}), bf16[128,36,1024]{2,1,0:T(8,128)(2,1)}, u32[]{:S(2)}, u32[]{:S(2)}) %all-to-all-start.2) | async-done | bytes 9437216 | tf_op jit(solution)/shard_map/all_to_all | solution.py:220
  630.3 5.4 broadcast_in_dim.92
  635.7 11.3 all-to-all-start.4
  647.0 13.1 reshape.641
  660.0 7.9 fusion.108
  672.1 106.3 %all-to-all-done.4 = bf16[128,36,1024]{2,1,0:T(8,128)(2,1)} async-done(((bf16[128,36,1024]{2,1,0:T(8,128)(2,1)}), bf16[128,36,1024]{2,1,0:T(8,128)(2,1)}, u32[]{:S(2)}, u32[]{:S(2)}) %all-to-all-start.4) | async-done | bytes 9437216 | tf_op jit(solution)/shard_map/all_to_all | solution.py:309
  778.4 13.1 reshape.648
  791.5 8.3 multiply_convert_fusion.2
  805.9 13.1 reshape.642
  819.0 11.7 all-to-all-start.3
  830.7 7.9 fusion.110
  838.6 10.6 add_convert_fusion.1
  849.2 13.1 reshape.649
  862.2 99.9 %all-to-all-done.3 = bf16[128,36,1024]{2,1,0:T(8,128)(2,1)} async-done(((bf16[128,36,1024]{2,1,0:T(8,128)(2,1)}), bf16[128,36,1024]{2,1,0:T(8,128)(2,1)}, u32[]{:S(2)}, u32[]{:S(2)}) %all-to-all-start.3) | async-done | bytes 9437216 | tf_op jit(solution)/shard_map/all_to_all | solution.py:240
  962.1 11.1 all-to-all-start.5
  973.4 9.7 convert_reduce_fusion.2
  983.0 5.3 reshape.645
  988.3 8.8 gather_fusion.1
  1001.0 104.9 %all-to-all-done.5 = bf16[128,36,1024]{2,1,0:T(8,128)(2,1)} async-done(((bf16[128,36,1024]{2,1,0:T(8,128)(2,1)}), bf16[128,36,1024]{2,1,0:T(8,128)(2,1)}, u32[]{:S(2)}, u32[]{:S(2)}) %all-to-all-start.5) | async-done | bytes 9437216 | tf_op jit(solution)/shard_map/all_to_all | solution.py:339
  1105.9 9.7 convert_reduce_fusion.1
  1115.6 5.3 reshape.652
  1120.9 8.8 gather_fusion.2
  1146.4 7.5 scatter_custom_fusion.3
  1156.5 5.3 broadcast_in_dim.95
  1161.8 130.9 %all_to_all.40 = bf16[128,36,1024]{2,1,0:T(8,128)(2,1)} all-to-all(bf16[128,36,1024]{2,1,0:T(8,128)(2,1)} %bitcast.366), channel_id=1, replica_groups=mesh['fsdp'=128] {'fsdp'}, dimensions={0} | all-to-all | bytes 18874368 | tf_op jit(solution)/shard_map/all_to_all | solution.py:309
  1292.7 13.1 reshape.656
  1305.8 8.0 multiply_convert_fusion
  1313.9 7.9 fusion.120
  1321.8 10.7 add_convert_fusion
  1332.5 13.1 reshape.657
  1345.6 8.7 all-to-all-start.7
  1366.1 5.3 reshape_reshape.22
  1376.0 9.4 reshape_reshape.21
  1385.5 15.3 concatenate.85
  1400.7 10.8 pad.8
  1411.5 12.2 reshape.668
  1423.7 63.2 %all-to-all-done.7 = bf16[128,36,1024]{2,1,0:T(8,128)(2,1)} async-done(((bf16[128,36,1024]{2,1,0:T(8,128)(2,1)}), bf16[128,36,1024]{2,1,0:T(8,128)(2,1)}, u32[]{:S(2)}, u32[]{:S(2)}) %all-to-all-start.7) | async-done | bytes 9437216 | tf_op jit(solution)/shard_map/all_to_all | solution.py:339
  1486.9 9.6 convert_reduce_fusion
  1501.7 9.2 gather_fusion.3
  1542.2 9.3 reshape_reshape.18
  1551.5 15.3 concatenate.84
  1566.8 10.7 pad.7
  1577.5 12.3 reshape.665
  1591.1 5.2 fusion.187
  1596.4 5.4 fusion.186
  1614.1 211.3 %all-reduce.7.cloned.1.call-done = (f32[25600,128]{1,0:T(8,128)}, f32[25600,128]{1,0:T(8,128)}) async-done(((f32[25600,128]{1,0:T(8,128)}, f32[25600,128]{1,0:T(8,128)}), (f32[25600,128]{1,0:T(8,128)}, f32[25600,128]{1,0:T(8,128)})) %all-reduce.7.cloned.1.call-update) | async-done | bytes 26214416
  (454 shorter events, 177.5 us)
Async XLA Ops:
  7.2 76.1 %all-gather.3.cloned.1.call-start = ((), (), s32[]{:S(2)}) async-start(), calls=%async_computation.8 | async-start | bytes 6604800 | tf_op jit(solution)/shard_map/all_gather | solution.py:30
  29.6 58.4 %copy-start.98 = (f32[128]{0:T(128)}, f32[128]{0:T(128)S(1)}, u32[]{:S(2)}) copy-start(f32[128]{0:T(128)S(1)} %add_rsqrt_fusion.3) | copy-start | bytes 1540
  29.7 437.9 %copy-start.88 = (pred[128,128]{0,1:T(8,128)(4,1)}, pred[128,128]{0,1:T(8,128)(4,1)S(1)}, u32[]{:S(2)}) copy-start(pred[128,128]{0,1:T(8,128)(4,1)S(1)} %fusion.147) | copy-start | bytes 49156
  29.7 63.6 %copy-start.106 = (s32[1024,1]{0,1:T(1,128)}, s32[1024,1]{0,1:T(1,128)S(1)}, u32[]{:S(2)}) copy-start(s32[1024,1]{0,1:T(1,128)S(1)} %get-tuple-element.66) | copy-start | bytes 12292
  29.9 436.1 %copy-start.36 = (f32[128,32]{0,1:T(8,128)}, f32[128,32]{0,1:T(8,128)S(1)}, u32[]{:S(2)}) copy-start(f32[128,32]{0,1:T(8,128)S(1)} %get-tuple-element.69) | copy-start | bytes 49156
  29.9 436.1 %copy-start.38 = (f32[128,32]{0,1:T(8,128)}, f32[128,32]{0,1:T(8,128)S(1)}, u32[]{:S(2)}) copy-start(f32[128,32]{0,1:T(8,128)S(1)} %get-tuple-element.70) | copy-start | bytes 49156
  84.8 8.4 copy-start.84
  93.1 368.9 %copy-start.2 = (f32[128,1024]{1,0:T(8,128)}, f32[128,1024]{1,0:T(8,128)S(1)}, u32[]{:S(2)}) copy-start(f32[128,1024]{1,0:T(8,128)S(1)} %get-tuple-element.81) | copy-start | bytes 1572868
  93.2 9.7 copy-start.104
  93.3 210.4 %copy-start.26 = (bf16[128,1024]{1,0:T(8,128)(2,1)}, bf16[128,1024]{1,0:T(8,128)(2,1)S(1)}, u32[]{:S(2)}) copy-start(bf16[128,1024]{1,0:T(8,128)(2,1)S(1)} %multiply_convert_fusion.10) | copy-start | bytes 786436
  108.1 7.6 copy-start.108
  108.1 7.7 copy-start.107
  108.1 7.8 copy-start.97
  108.1 8.6 copy-start.44
  108.1 140.9 %all-to-all-start = ((bf16[128,36,1024]{2,1,0:T(8,128)(2,1)}), bf16[128,36,1024]{2,1,0:T(8,128)(2,1)}, u32[]{:S(2)}, u32[]{:S(2)}) async-start(bf16[128,36,1024]{2,1,0:T(8,128)(2,1)} %bitcast.363), calls=%async_computation | async-start | bytes 20971520 | tf_op jit(solution)/shard_map/all_to_all | solution.py:220
  115.4 197.3 %all-gather.5.cloned.1.call-start = ((), (), s32[]{:S(2)}) async-start(), calls=%async_computation.9 | async-start | bytes 6604800 | tf_op jit(solution)/shard_map/all_gather | solution.py:30
  116.8 151.6 %copy-start.31 = (bf16[128,2048]{1,0:T(8,128)(2,1)}, bf16[128,2048]{1,0:T(8,128)(2,1)S(1)}, u32[]{:S(2)}) copy-start(bf16[128,2048]{1,0:T(8,128)(2,1)S(1)} %get-tuple-element.38) | copy-start | bytes 1572868
  262.1 7.0 copy-start.1
  292.4 11.1 copy-start.68
  292.4 142.5 %all-to-all-start.1 = ((bf16[128,36,1024]{2,1,0:T(8,128)(2,1)}), bf16[128,36,1024]{2,1,0:T(8,128)(2,1)}, u32[]{:S(2)}, u32[]{:S(2)}) async-start(bf16[128,36,1024]{2,1,0:T(8,128)(2,1)} %reshape.631), calls=%async_computation.1 | async-start | bytes 20971520 | tf_op jit(solution)/shard_map/all_to_all | solution.py:240
  312.0 132.5 %copy-start.66 = (f32[128,8]{0,1:T(8,128)}, f32[128,8]{0,1:T(8,128)S(1)}, u32[]{:S(2)}) copy-start(f32[128,8]{0,1:T(8,128)S(1)} %copy.218) | copy-start | bytes 12292
  312.1 132.4 %copy-start.95 = (f32[128]{0:T(128)}, f32[128]{0:T(128)S(1)}, u32[]{:S(2)}) copy-start(f32[128]{0:T(128)S(1)} %fusion.158) | copy-start | bytes 1540
  314.2 148.0 %copy-start.64 = (f32[1024]{0:T(1024)}, f32[1024]{0:T(1024)S(1)}, u32[]{:S(2)}) copy-start(f32[1024]{0:T(1024)S(1)} %get-tuple-element.11) | copy-start | bytes 12292
  314.2 156.5 %copy-start.86 = (f32[1024]{0:T(1024)}, f32[1024]{0:T(1024)S(1)}, u32[]{:S(2)}) copy-start(f32[1024]{0:T(1024)S(1)} %get-tuple-element.10) | copy-start | bytes 12292
  462.1 6.2 copy-start.8
  470.6 10.6 copy-start.100
  471.4 26.3 %copy-start.28 = (bf16[128,1024]{1,0:T(8,128)(2,1)}, bf16[128,1024]{1,0:T(8,128)(2,1)S(1)}, u32[]{:S(2)}) copy-start(bf16[128,1024]{1,0:T(8,128)(2,1)S(1)} %multiply_convert_fusion.8) | copy-start | bytes 786436
  486.4 11.1 copy-start.40
  486.4 143.8 %all-to-all-start.2 = ((bf16[128,36,1024]{2,1,0:T(8,128)(2,1)}), bf16[128,36,1024]{2,1,0:T(8,128)(2,1)}, u32[]{:S(2)}, u32[]{:S(2)}) async-start(bf16[128,36,1024]{2,1,0:T(8,128)(2,1)} %bitcast.364), calls=%async_computation.2 | async-start | bytes 20971520 | tf_op jit(solution)/shard_map/all_to_all | solution.py:220
  497.7 8.8 copy-start.24
  635.7 142.7 %all-to-all-start.4 = ((bf16[128,36,1024]{2,1,0:T(8,128)(2,1)}), bf16[128,36,1024]{2,1,0:T(8,128)(2,1)}, u32[]{:S(2)}, u32[]{:S(2)}) async-start(bf16[128,36,1024]{2,1,0:T(8,128)(2,1)} %bitcast.365), calls=%async_computation.4 | async-start | bytes 20971520 | tf_op jit(solution)/shard_map/all_to_all | solution.py:309
  660.0 7.9 copy-start
  791.5 9.3 copy-start.48
  799.9 30.8 %copy-start.10 = (bf16[4608,128]{1,0:T(8,128)(2,1)}, bf16[4608,128]{1,0:T(8,128)(2,1)S(1)}, u32[]{:S(2)}) copy-start(bf16[4608,128]{1,0:T(8,128)(2,1)S(1)} %get-tuple-element.35) | copy-start | bytes 3538948
  799.9 38.7 %copy-start.14 = (bf16[4608,128]{1,0:T(8,128)(2,1)}, bf16[4608,128]{1,0:T(8,128)(2,1)S(1)}, u32[]{:S(2)}) copy-start(bf16[4608,128]{1,0:T(8,128)(2,1)S(1)} %get-tuple-element.34) | copy-start | bytes 3538948
  819.0 143.1 %all-to-all-start.3 = ((bf16[128,36,1024]{2,1,0:T(8,128)(2,1)}), bf16[128,36,1024]{2,1,0:T(8,128)(2,1)}, u32[]{:S(2)}, u32[]{:S(2)}) async-start(bf16[128,36,1024]{2,1,0:T(8,128)(2,1)} %reshape.642), calls=%async_computation.3 | async-start | bytes 20971520 | tf_op jit(solution)/shard_map/all_to_all | solution.py:240
  962.1 143.8 %all-to-all-start.5 = ((bf16[128,36,1024]{2,1,0:T(8,128)(2,1)}), bf16[128,36,1024]{2,1,0:T(8,128)(2,1)}, u32[]{:S(2)}, u32[]{:S(2)}) async-start(bf16[128,36,1024]{2,1,0:T(8,128)(2,1)} %reshape.649), calls=%async_computation.5 | async-start | bytes 20971520 | tf_op jit(solution)/shard_map/all_to_all | solution.py:339
  988.3 8.8 copy-start.25
  1129.8 6.0 copy-start.109
  1135.7 9.7 copy-start.22
  1292.7 13.2 copy-start.49
  1305.8 8.1 copy-start.32
  1313.9 7.9 copy-start.12
  1345.6 8.8 copy-start.29
  1345.6 11.2 copy-start.19
  1345.6 141.3 %all-to-all-start.7 = ((bf16[128,36,1024]{2,1,0:T(8,128)(2,1)}), bf16[128,36,1024]{2,1,0:T(8,128)(2,1)}, u32[]{:S(2)}, u32[]{:S(2)}) async-start(bf16[128,36,1024]{2,1,0:T(8,128)(2,1)} %reshape.657), calls=%async_computation.7 | async-start | bytes 20971520 | tf_op jit(solution)/shard_map/all_to_all | solution.py:339
  1354.2 5.9 copy-start.67
  1354.2 5.9 copy-start.90
  1354.3 5.9 copy-start.96
  1354.3 6.0 copy-start.27
  1354.3 8.2 copy-start.23
  1354.3 471.2 %all-reduce.7.cloned.1.call-start = ((), (), s32[]{:S(2)}) async-start(), calls=%async_computation.10 | async-start | bytes 52428800
  1376.0 9.4 copy-start.53
  1514.5 6.0 copy-start.55
  1514.5 6.0 copy-start.57
  1514.5 6.0 copy-start.74
  1514.5 6.0 copy-start.92
  1516.1 6.6 copy-start.45
  1591.1 10.8 slice-start.3
  1591.1 10.8 slice-start.4
  1596.4 7.2 slice-start.6
  1596.4 8.4 slice-start.7
  1602.0 5.7 slice-start
  1602.0 5.9 slice-start.1
  (65 other events, 206.4 us)
Sparse Core Ops, SparseCore 0:
  13.5 69.6 all-gather.2
  119.8 164.9 all-gather.4
  1590.0 235.3 all-reduce.6
where the time goes:
time: 1850 us; the launch traced here: 1840 us
  waiting for transfers between devices  1010 us (55%)
  local copies, waits for them, and re-layouts  355 us (19%)
  matrix products  161 us (9%)
  blocking collectives  131 us (7%)
  other arithmetic  97.4 us (5%)
  starting transfers between devices  72.7 us (4%)
    all_to_all x2, waiting for transfers between devices, expert_forward(): lax.all_to_all(pack_rows(repeated, flat_index, devices), 'fsdp', split_ax...  246 us
    all_to_all x2, waiting for transfers between devices, expert_forward(): lax.all_to_all(partial_value.reshape(devices, CAP, MODEL_WIDTH), 'fsdp',...  221 us
    unnamed x4, waiting for transfers between devices  211 us
    all_to_all x2, waiting for transfers between devices, expert_backward(): lax.all_to_all(grad_in_rows.reshape(devices, CAP, MODEL_WIDTH), 'fsdp', s...  168 us
    all_to_all x1, blocking collectives, expert_backward(): lax.all_to_all(pack_rows(slot_grads, flat_index, devices), 'fsdp', split_...  131 us
    all_to_all x1, waiting for transfers between devices, expert_backward(): lax.all_to_all(pack_rows(slot_grads, flat_index, devices), 'fsdp', split_...  106 us
    all_gather x2, waiting for transfers between devices, sent_together(): out = lax.all_gather(both, axis, axis=dim, tiled=True)  53.4 us
    reduce_sum x4, other arithmetic, unpack_sum(): jnp.sum(returned.astype(jnp.float32).reshape(E, group_size, CAP, MODEL_WI...  38.6 us
  transfers between devices with their start and end apart: 10, of which 9 were waited for; matrix products, arithmetic and copies ran while one was open for 14% of the time, Pallas kernels for 0%

commit v1 on v0

v1 whole, which is shorter than its diff:
```python
import math

import jax
import jax.numpy as jnp
from jax import lax
from jax.sharding import Mesh, PartitionSpec as P

MODEL_WIDTH = 1024
QUERY_HEADS = 16
KEY_VALUE_HEADS = 8
HEAD_SIZE = 64
E = 32
TOPK = 8
LAYER_COUNT = 2
SEQ_DEV = 4
TOK_DEV = 128
CAP = 36


EPSILON = 1e-06
ROPE_BASE = 10000.0
MASKED = -1e30

ROOM = 40
ROWS = E * ROOM
AXES = ("x", "y", "zh", "zl", "c")
EXPERT_AXES = ("x", "y", "zh")
CHIP_AXES = ("x", "y", "zh", "zl")
SWAP = [(0, 1), (1, 0)]


def sent_together(arrays, axis, dim, along):
    widths = [math.prod(a.shape[along:]) for a in arrays]
    both = jnp.concatenate(
        [a.reshape(*a.shape[:along], w) for a, w in zip(arrays, widths)], axis=along
    )
    out = lax.all_gather(both, axis, axis=dim, tiled=True)
    pieces = jnp.split(out, [sum(widths[:k]) for k in range(1, len(widths))], axis=along)
    return tuple((b.reshape(*out.shape[:along], *a.shape[along:]) for a, b in zip(arrays, pieces)))


def seq_layout(seq_lengths, seq_owner, device):
    owned_seq = seq_owner == device
    ranking = jnp.cumsum(owned_seq.astype(jnp.int32)) - 1
    counter = jnp.arange(SEQ_DEV, dtype=jnp.int32)
    picker = (owned_seq[None, :] & (ranking[None, :] == counter[:, None])).astype(jnp.int32)
    own_lengths = jnp.sum(picker * seq_lengths[None, :], axis=1)
    seq_ends = jnp.cumsum(own_lengths)
    slot_ids = jnp.arange(TOK_DEV, dtype=jnp.int32)
    segment = jnp.sum((slot_ids[:, None] >= seq_ends[None, :]).astype(jnp.int32), axis=1)
    seq_starts = seq_ends - own_lengths
    first_slot = jnp.sum(
        jnp.where(segment[:, None] == counter[None, :], seq_starts[None, :], 0), axis=1
    )
    position = slot_ids - first_slot
    allowed = (segment[:, None] == segment[None, :]) & (slot_ids[:, None] >= slot_ids[None, :])
    return (position, segment < SEQ_DEV, allowed)


def rope_tables(position):
    half_size = HEAD_SIZE // 2
    exponent = jnp.arange(half_size, dtype=jnp.float32) * (2.0 / HEAD_SIZE)
    frequency = jnp.exp(-math.log(ROPE_BASE) * exponent)
    angles = position.astype(jnp.float32)[:, None] * frequency[None, :]
    return (jnp.cos(angles), jnp.sin(angles))


def apply_rotation(values, cosine_table, sine_values):
    half_size = values.shape[-1] // 2
    first_half = values[..., :half_size]
    second_half = values[..., half_size:]
    cos_wide = cosine_table[:, None, :]
    sin_wide = sine_values[:, None, :]
    return jnp.concatenate(
        [
            first_half * cos_wide - second_half * sin_wide,
            second_half * cos_wide + first_half * sin_wide,
        ],
        axis=-1,
    )


def unrotate(grad_rot, cosine_table, sine_values):
    half_size = grad_rot.shape[-1] // 2
    first_half = grad_rot[..., :half_size]
    second_half = grad_rot[..., half_size:]
    cos_wide = cosine_table[:, None, :]
    sin_wide = sine_values[:, None, :]
    return jnp.concatenate(
        [
            first_half * cos_wide + second_half * sin_wide,
            second_half * cos_wide - first_half * sin_wide,
        ],
        axis=-1,
    )


def rounded(values):
    return lax.optimization_barrier(values.astype(jnp.bfloat16)).astype(jnp.float32)


def dispatch_table(route_block, live_row):
    experts = jnp.arange(E, dtype=jnp.int32)
    routed = jnp.any(route_block[:, :, None] == experts[None, None, :], axis=1)
    hits = (routed & live_row[:, None]).astype(jnp.bfloat16)
    slot_ids = jnp.arange(TOK_DEV, dtype=jnp.int32)
    before = (slot_ids[None, :] < slot_ids[:, None]).astype(jnp.bfloat16)
    rank = jnp.dot(before, hits, preferred_element_type=jnp.float32)
    code = jnp.where(hits > 0, rank, -1.0).astype(jnp.bfloat16)
    spread = spread_table()
    wide = jnp.dot(code, spread, preferred_element_type=jnp.float32)
    place = (jnp.arange(ROWS, dtype=jnp.int32) % ROOM).astype(jnp.float32)
    chosen = (wide == place[None, :]).astype(jnp.bfloat16)
    return routed, chosen


def spread_table():
    rows = jnp.arange(ROWS, dtype=jnp.int32) // ROOM
    return (jnp.arange(E, dtype=jnp.int32)[:, None] == rows[None, :]).astype(jnp.bfloat16)


def trade_rows(rows):
    return lax.all_to_all(
        rows.reshape(E, ROOM, MODEL_WIDTH), EXPERT_AXES, split_axis=0, concat_axis=0, tiled=True
    ).reshape(ROWS, MODEL_WIDTH)


def gather_expert(own):
    pair = jnp.concatenate([own, lax.ppermute(own, "zl", SWAP)], axis=0)
    return jnp.concatenate([pair, lax.ppermute(pair, "c", SWAP)], axis=0)


def scatter_expert(grad):
    half = grad.shape[0] // 2
    quarter = half // 2
    kept, given = grad[:half], grad[half:].astype(jnp.bfloat16)
    kept = kept + lax.ppermute(given, "c", SWAP).astype(jnp.float32)
    own, other = kept[:quarter], kept[quarter:].astype(jnp.bfloat16)
    return own + lax.ppermute(other, "zl", SWAP).astype(jnp.float32)


def scatter_dense(grad):
    width = grad.shape[1]
    core = lax.axis_index("c")
    blocks = grad.reshape(64, 2, MODEL_WIDTH // 128, width)
    given = lax.dynamic_slice_in_dim(blocks, 1 - core, 1, axis=1).astype(jnp.bfloat16)
    kept = lax.dynamic_slice_in_dim(blocks, core, 1, axis=1)
    kept = kept + lax.ppermute(given, "c", SWAP).astype(jnp.float32)
    kept = kept.reshape(64, MODEL_WIDTH // 128, width).astype(jnp.bfloat16)
    parts = lax.all_to_all(kept, CHIP_AXES, split_axis=0, concat_axis=0, tiled=True)
    return jnp.sum(parts.astype(jnp.float32), axis=0)


def norm_back(grad_norm, normed, inverse):
    return inverse * (grad_norm - normed * jnp.mean(grad_norm * normed, axis=-1, keepdims=True))


def probabilities(rotated_query, rotated_key, allowed):
    scores = jnp.einsum(
        "tkgd,ukd->kgtu", rotated_query, rotated_key, preferred_element_type=jnp.float32
    ) * HEAD_SIZE ** (-0.5)
    scores = jnp.where(allowed[None, None], scores, MASKED)
    biggest = jnp.max(scores, axis=-1, keepdims=True)
    exp_scores = jnp.exp(scores - biggest)
    return exp_scores / jnp.sum(exp_scores, axis=-1, keepdims=True)


def attend_forward(hidden, weights, live, allowed, cosine_table, sine_values):
    qkv_full, out_full, router_full, gain_one, gain_two = weights
    token_total = hidden.shape[0]
    query_width = QUERY_HEADS * HEAD_SIZE
    key_value_width = KEY_VALUE_HEADS * HEAD_SIZE
    inverse = lax.rsqrt(jnp.mean(hidden * hidden, axis=-1, keepdims=True) + EPSILON)
    normed = hidden * inverse
    normed_low = (normed * gain_one.astype(jnp.float32)).astype(jnp.bfloat16)
    projected_rows = jnp.dot(normed_low, qkv_full, preferred_element_type=jnp.float32)
    rotated_query = apply_rotation(
        projected_rows[:, :query_width].reshape(token_total, QUERY_HEADS, HEAD_SIZE),
        cosine_table,
        sine_values,
    ).astype(jnp.bfloat16)
    rotated_query = rotated_query.reshape(
        token_total, KEY_VALUE_HEADS, QUERY_HEADS // KEY_VALUE_HEADS, HEAD_SIZE
    )
    rotated_key = apply_rotation(
        projected_rows[:, query_width : query_width + key_value_width].reshape(
            token_total, KEY_VALUE_HEADS, HEAD_SIZE
        ),
        cosine_table,
        sine_values,
    ).astype(jnp.bfloat16)
    reduced_value = (
        projected_rows[:, query_width + key_value_width :]
        .reshape(token_total, KEY_VALUE_HEADS, HEAD_SIZE)
        .astype(jnp.bfloat16)
    )
    softmaxed = probabilities(rotated_query, rotated_key, allowed)
    mixed = jnp.einsum(
        "kgtu,ukd->tkgd",
        softmaxed.astype(jnp.bfloat16),
        reduced_value,
        preferred_element_type=jnp.float32,
    )
    mixed_low = (mixed.reshape(token_total, query_width) * live[:, None]).astype(jnp.bfloat16)
    attn_out = jnp.dot(mixed_low, out_full, preferred_element_type=jnp.float32)
    return (
        hidden + attn_out,
        (inverse, normed, normed_low, rotated_query, rotated_key, reduced_value, mixed_low),
    )


def expert_forward(hidden, weights, expert_in_l, expert_out_l, live, routed, chosen):
    qkv_full, out_full, router_full, gain_one, gain_two = weights
    inverse_two = lax.rsqrt(jnp.mean(hidden * hidden, axis=-1, keepdims=True) + EPSILON)
    normed_two = hidden * inverse_two
    routed_in = (normed_two * gain_two.astype(jnp.float32)).astype(jnp.bfloat16)
    rows = lax.dot_general(
        chosen, routed_in, (((0,), (0,)), ((), ())), preferred_element_type=jnp.float32
    ).astype(jnp.bfloat16)
    rows_here = trade_rows(rows)
    logits = jnp.dot(routed_in, router_full, preferred_element_type=jnp.float32)
    masked = jnp.where(routed, logits, MASKED)
    exp_chosen = jnp.where(routed, jnp.exp(masked - jnp.max(masked, axis=-1, keepdims=True)), 0.0)
    gate_prob = exp_chosen / jnp.sum(exp_chosen, axis=-1, keepdims=True)
    gate_wide = jnp.dot(
        gate_prob.astype(jnp.bfloat16), spread_table(), preferred_element_type=jnp.float32
    ).astype(jnp.bfloat16)
    mixing = gate_wide * chosen
    gate_pre = lax.dot_general(
        rows_here,
        expert_in_l[:, :MODEL_WIDTH],
        (((1,), (1,)), ((), ())),
        preferred_element_type=jnp.float32,
    )
    up_pre = lax.dot_general(
        rows_here,
        expert_in_l[:, MODEL_WIDTH:],
        (((1,), (1,)), ((), ())),
        preferred_element_type=jnp.float32,
    )
    units = (jax.nn.silu(gate_pre) * up_pre).astype(jnp.bfloat16)
    results = jnp.dot(units, expert_out_l, preferred_element_type=jnp.float32).astype(jnp.bfloat16)
    returned = trade_rows(results)
    result = hidden + jnp.dot(mixing, returned, preferred_element_type=jnp.float32)
    stash = (inverse_two, normed_two, routed_in, gate_prob, mixing, returned)
    return result, stash + (gate_pre, up_pre, rows_here)


def expert_backward(grad_out, weights, expert_in_l, expert_out_l, chosen, expert_stash):
    qkv_full, out_full, router_full, gain_one, gain_two = weights
    (
        inverse_two,
        normed_two,
        routed_in,
        gate_prob,
        mixing,
        returned,
        gate_pre,
        up_pre,
        rows_here,
    ) = expert_stash
    grad_out_low = grad_out.astype(jnp.bfloat16)
    slot_grads = lax.dot_general(
        mixing, grad_out_low, (((0,), (0,)), ((), ())), preferred_element_type=jnp.float32
    ).astype(jnp.bfloat16)
    grad_rows = trade_rows(slot_grads)
    products = lax.dot_general(
        grad_out_low, returned, (((1,), (1,)), ((), ())), preferred_element_type=jnp.float32
    )
    grad_gate = lax.dot_general(
        products * chosen.astype(jnp.float32),
        spread_table().astype(jnp.float32),
        (((1,), (1,)), ((), ())),
        precision=lax.Precision.HIGHEST,
        preferred_element_type=jnp.float32,
    )
    grad_chosen = gate_prob * (grad_gate - jnp.sum(gate_prob * grad_gate, axis=-1, keepdims=True))
    grad_logits = grad_chosen.astype(jnp.bfloat16)
    router_grad = lax.dot_general(
        routed_in, grad_logits, (((0,), (0,)), ((), ())), preferred_element_type=jnp.float32
    )
    grad_routed = lax.dot_general(
        grad_logits, router_full, (((1,), (1,)), ((), ())), preferred_element_type=jnp.float32
    )
    sigmoid_pre = jax.nn.sigmoid(gate_pre)
    activated = gate_pre * sigmoid_pre
    units = (activated * up_pre).astype(jnp.bfloat16)
    grad_units = lax.dot_general(
        grad_rows, expert_out_l, (((1,), (1,)), ((), ())), preferred_element_type=jnp.float32
    )
    grad_gate_pre = (
        grad_units * up_pre * (sigmoid_pre * (1.0 + gate_pre * (1.0 - sigmoid_pre)))
    ).astype(jnp.bfloat16)
    grad_up_pre = (grad_units * activated).astype(jnp.bfloat16)
    grad_in_rows = jnp.dot(
        grad_gate_pre, expert_in_l[:, :MODEL_WIDTH], preferred_element_type=jnp.float32
    )
    grad_in_rows = (
        grad_in_rows
        + jnp.dot(grad_up_pre, expert_in_l[:, MODEL_WIDTH:], preferred_element_type=jnp.float32)
    ).astype(jnp.bfloat16)
    grad_slots = trade_rows(grad_in_rows)
    out_grad = lax.dot_general(
        units, grad_rows, (((0,), (0,)), ((), ())), preferred_element_type=jnp.float32
    )
    gate_w_grad = lax.dot_general(
        grad_gate_pre, rows_here, (((0,), (0,)), ((), ())), preferred_element_type=jnp.float32
    )
    up_w_grad = lax.dot_general(
        grad_up_pre, rows_here, (((0,), (0,)), ((), ())), preferred_element_type=jnp.float32
    )
    in_grad = jnp.concatenate([scatter_expert(gate_w_grad), scatter_expert(up_w_grad)], axis=1)
    out_grad = scatter_expert(out_grad)
    grad_routed = grad_routed + jnp.dot(chosen, grad_slots, preferred_element_type=jnp.float32)
    gain_two_grad = jnp.sum(grad_routed * normed_two, axis=0)
    grad_h1 = grad_out + norm_back(
        grad_routed * gain_two.astype(jnp.float32), normed_two, inverse_two
    )
    return (grad_h1, router_grad, gain_two_grad, in_grad, out_grad)


def attend_backward(grad_h1, weights, live, allowed, cosine_table, sine_values, attn_stash):
    qkv_full, out_full, router_full, gain_one, gain_two = weights
    inverse, normed, normed_low, rotated_query, rotated_key, reduced_value, mixed_low = attn_stash
    token_total = grad_h1.shape[0]
    query_width = QUERY_HEADS * HEAD_SIZE
    key_value_width = KEY_VALUE_HEADS * HEAD_SIZE
    grad_low = grad_h1.astype(jnp.bfloat16)
    proj_grad = lax.dot_general(
        mixed_low, grad_low, (((0,), (0,)), ((), ())), preferred_element_type=jnp.float32
    )
    mixed_gradient = lax.dot_general(
        grad_low, out_full, (((1,), (1,)), ((), ())), preferred_element_type=jnp.float32
    ).astype(jnp.bfloat16)
    mixed_gradient = jnp.where(live[:, None] > 0.5, mixed_gradient, jnp.zeros_like(mixed_gradient))
    mixed_gradient = mixed_gradient.reshape(
        token_total, KEY_VALUE_HEADS, QUERY_HEADS // KEY_VALUE_HEADS, HEAD_SIZE
    )
    softmaxed = probabilities(rotated_query, rotated_key, allowed)
    grad_probs = jnp.einsum(
        "tkgd,ukd->kgtu", mixed_gradient, reduced_value, preferred_element_type=jnp.float32
    )
    grad_value = jnp.einsum(
        "kgtu,tkgd->ukd",
        softmaxed.astype(jnp.bfloat16),
        mixed_gradient,
        preferred_element_type=jnp.float32,
    )
    grad_scores = (
        softmaxed * (grad_probs - jnp.sum(softmaxed * grad_probs, axis=-1, keepdims=True))
    ).astype(jnp.bfloat16)
    grad_query = jnp.einsum(
        "kgtu,ukd->tkgd", grad_scores, rotated_key, preferred_element_type=jnp.float32
    ) * HEAD_SIZE ** (-0.5)
    grad_key = jnp.einsum(
        "kgtu,tkgd->ukd", grad_scores, rotated_query, preferred_element_type=jnp.float32
    ) * HEAD_SIZE ** (-0.5)
    grad_query = unrotate(
        rounded(grad_query.reshape(token_total, QUERY_HEADS, HEAD_SIZE)), cosine_table, sine_values
    ).astype(jnp.bfloat16)
    grad_key = unrotate(rounded(grad_key), cosine_table, sine_values).astype(jnp.bfloat16)
    grad_proj = jnp.concatenate(
        [
            grad_query.reshape(token_total, query_width),
            grad_key.reshape(token_total, key_value_width),
            grad_value.astype(jnp.bfloat16).reshape(token_total, key_value_width),
        ],
        axis=1,
    )
    qkv_grad = lax.dot_general(
        normed_low, grad_proj, (((0,), (0,)), ((), ())), preferred_element_type=jnp.float32
    )
    grad_normed = lax.dot_general(
        grad_proj, qkv_full, (((1,), (1,)), ((), ())), preferred_element_type=jnp.float32
    )
    gain_one_grad = jnp.sum(grad_normed * normed, axis=0)
    grad_input = grad_h1 + norm_back(grad_normed * gain_one.astype(jnp.float32), normed, inverse)
    return (grad_input, qkv_grad, proj_grad, gain_one_grad)


def on_device(
    hidden_in,
    cotangent,
    seq_lengths,
    seq_owner,
    routes,
    query_key_value_weight,
    out_weight,
    router_weight,
    gain_attn,
    gain_mlp,
    expert_in,
    expert_out,
):
    layers = range(LAYER_COUNT)
    device = lax.axis_index(AXES)
    dense = [
        sent_together(
            (
                query_key_value_weight[layer],
                out_weight[layer],
                router_weight[layer],
                gain_attn[layer],
                gain_mlp[layer],
            ),
            AXES,
            0,
            1,
        )
        for layer in layers
    ]
    experts_in = [gather_expert(expert_in[layer]) for layer in layers]
    experts_out = [gather_expert(expert_out[layer]) for layer in layers]
    position, live_row, allowed = seq_layout(seq_lengths, seq_owner, device)
    live = live_row.astype(jnp.float32)
    cosine_table, sine_values = rope_tables(position)
    routed, chosen = dispatch_table(routes, live_row)
    hidden = hidden_in.astype(jnp.float32)
    saved_layers = []
    for layer in layers:
        hidden, attn_stash = attend_forward(
            hidden, dense[layer], live, allowed, cosine_table, sine_values
        )
        hidden, expert_stash = expert_forward(
            hidden, dense[layer], experts_in[layer], experts_out[layer], live, routed, chosen
        )
        saved_layers.append((attn_stash, expert_stash))
    output_low = hidden.astype(jnp.bfloat16)
    grad_hidden = cotangent.astype(jnp.float32)
    layer_grads = [None] * LAYER_COUNT
    for layer in reversed(layers):
        attn_stash, expert_stash = saved_layers[layer]
        grad_hidden, router_grad, gain_two_grad, in_grad, out_grad = expert_backward(
            grad_hidden, dense[layer], experts_in[layer], experts_out[layer], chosen, expert_stash
        )
        grad_hidden, qkv_grad, proj_grad, gain_one_grad = attend_backward(
            grad_hidden, dense[layer], live, allowed, cosine_table, sine_values, attn_stash
        )
        small = jnp.concatenate(
            [
                router_grad,
                gain_one_grad[:, None],
                gain_two_grad[:, None],
                jnp.zeros((MODEL_WIDTH, 128 - E - 2), jnp.float32),
            ],
            axis=1,
        )
        small = scatter_dense(small)
        layer_grads[layer] = (
            scatter_dense(qkv_grad),
            scatter_dense(proj_grad),
            small[:, :E],
            small[:, E],
            small[:, E + 1],
            in_grad,
            out_grad,
        )
    stacked = tuple(
        jnp.stack([layer_grads[layer][member] for layer in layers]) for member in range(7)
    )
    return (output_low, grad_hidden) + stacked


def solution(mesh):
    grid = Mesh(mesh.devices.reshape(4, 4, 2, 2, 2), AXES)
    placed = (
        P(AXES, None),
        P(AXES, None),
        P(),
        P(),
        P(AXES, None),
        P(None, AXES, None),
        P(None, AXES, None),
        P(None, AXES, None),
        P(None, AXES),
        P(None, AXES),
        P(None, AXES, None),
        P(None, AXES, None),
    )
    return jax.shard_map(
        on_device,
        mesh=grid,
        in_specs=placed,
        out_specs=(
            P(AXES, None),
            P(AXES, None),
            P(None, AXES, None),
            P(None, AXES, None),
            P(None, AXES, None),
            P(None, AXES),
            P(None, AXES),
            P(None, AXES, None),
            P(None, AXES, None),
        ),
        check_vma=False,
    )
```

time: 1850 us -> 759 us (0.41)
  waiting for transfers between devices: 1010 us -> 371 us
  local copies, waits for them, and re-layouts: 355 us -> 44.2 us
  blocking collectives: 131 us -> 0 us
  starting transfers between devices: 72.7 us -> 124 us
  other arithmetic: 97.4 us -> 56.8 us
  matrix products: 161 us -> 134 us
    all_to_all x7 -> x14, waiting for transfers between devices: 741 us -> 145 us  [the longest x8 93.3 us: trade_rows(): lax.all_to_all(rows.reshape(E, ROOM, MODEL_WIDTH), EXPERT_AXES, split_axi...]
    unnamed x4 -> x2, waiting for transfers between devices: 211 us -> 0.03 us
    ppermute x0 -> x26, waiting for transfers between devices: none -> 162 us  [the longest x4 95.3 us: gather_expert(): pair = jnp.concatenate([own, lax.ppermute(own, 'zl', SWAP)], axis=0)]
    reshape x20 -> x0, local copies, waits for them, and re-layouts: 152 us -> none  [the longest x2 26.3 us: expert_backward(): grad_rows = lax.all_to_all(pack_rows(slot_grads, flat_index, devices), 'f...]
    all_to_all x1 -> x0, blocking collectives: 131 us -> none  [expert_backward(): lax.all_to_all(pack_rows(slot_grads, flat_index, devices), 'fsdp', split_...]
    reduce_sum x14 -> x6, other arithmetic: 55.6 us -> 5.25 us  [scatter_dense(): return jnp.sum(parts.astype(jnp.float32), axis=0)]
    gather x12 -> x0, local copies, waits for them, and re-layouts: 50 us -> none  [the longest x2 18 us: expert_backward(): grad_slots[jnp.clip(flat_index, 0, E * CAP - 1)]]
    all_to_all x7 -> x14, starting transfers between devices: 72.2 us -> 111 us  [the longest x8 63.2 us: trade_rows(): lax.all_to_all(rows.reshape(E, ROOM, MODEL_WIDTH), EXPERT_AXES, split_axi...]
  transfers between devices with their start and end apart: 10 -> 42, of which waited for: 9 -> 21; matrix products, arithmetic and copies ran while one was open for 14% -> 22% of each run, Pallas kernels for 0% -> 0%
where the time goes in v1:
time: 759 us; the launch traced here: 746 us
  waiting for transfers between devices  371 us (49%)
  matrix products  134 us (18%)
  starting transfers between devices  124 us (16%)
  other arithmetic  56.8 us (7%)
  local copies, waits for them, and re-layouts  44.2 us (6%)
  between operations  16.7 us (2%)
    ppermute x4, waiting for transfers between devices, gather_expert(): pair = jnp.concatenate([own, lax.ppermute(own, 'zl', SWAP)], axis=0)  95.3 us
    all_to_all x8, waiting for transfers between devices, trade_rows(): lax.all_to_all(rows.reshape(E, ROOM, MODEL_WIDTH), EXPERT_AXES, split_axi...  93.3 us
    ppermute x6, waiting for transfers between devices, scatter_expert(): return own + lax.ppermute(other, 'zl', SWAP).astype(jnp.float32)  66.7 us
    all_gather x2, waiting for transfers between devices, sent_together(): out = lax.all_gather(both, axis, axis=dim, tiled=True)  63.4 us
    all_to_all x8, starting transfers between devices, trade_rows(): lax.all_to_all(rows.reshape(E, ROOM, MODEL_WIDTH), EXPERT_AXES, split_axi...  63.2 us
    all_to_all x6, waiting for transfers between devices, scatter_dense(): lax.all_to_all(kept, CHIP_AXES, split_axis=0, concat_axis=0, tiled=True)  52 us
    all_to_all x6, starting transfers between devices, scatter_dense(): lax.all_to_all(kept, CHIP_AXES, split_axis=0, concat_axis=0, tiled=True)  48.1 us
    convert_element_type x6, other arithmetic, scatter_dense(): kept = kept.reshape(64, MODEL_WIDTH // 128, width).astype(jnp.bfloat16)  18 us
  transfers between devices with their start and end apart: 42, of which 21 were waited for; matrix products, arithmetic and copies ran while one was open for 22% of the time, Pallas kernels for 0%

profile of v1, /device:TPU:2, one launch (start us, length us, event | category | flops | bytes accessed | tf_op | source)
XLA Modules:
  0.0 746.2 jit_solution(13328471740409655616)
XLA Ops:
  18.3 63.4 %all-gather.3.cloned.1.call-done = bf16[1024,3106]{1,0:T(8,128)(2,1)} async-done(((bf16[8,3106]{1,0:T(8,128)(2,1)}), bf16[1024,3106]{1,0:T(8,128)(2,1)}) %all-gather.3.cloned.1.call-update) | async-done | bytes 6361104 | tf_op jit(solution)/shard_map/all_gather | solution.py:37
  83.2 3.0 fusion.8
  94.6 7.4 all-to-all-start
  104.8 40.2 %collective-permute-done = bf16[128,2048]{1,0:T(8,128)(2,1)S(1)} collective-permute-done((bf16[128,2048]{1,0:T(8,128)(2,1)S(1)}, bf16[128,2048]{1,0:T(8,128)(2,1)S(1)}, u32[]{:S(2)}, u32[]{:S(2)}) %collective-permute-start) | collective-permute-done | bytes 524320 | tf_op jit(solution)/shard_map/ppermute | solution.py:129
  147.4 7.2 collective-permute-done.2
  157.1 3.8 fusion.77
  160.9 3.4 multiply_convert_fusion.5
  164.4 4.5 convolution_convert_fusion.4
  168.9 10.6 %all-to-all-start.1 = ((bf16[32,40,1024]{2,1,0:T(8,128)(2,1)}), bf16[32,40,1024]{2,1,0:T(8,128)(2,1)S(1)}, u32[]{:S(2)}, u32[]{:S(2)}) async-start(bf16[32,40,1024]{2,1,0:T(8,128)(2,1)} %bitcast.358), calls=%async_computation.1 | async-start | bytes 5242880 | tf_op jit(solution)/shard_map/all_to_all | solution.py:123
  183.3 31.3 %all-to-all-done.1 = bf16[32,40,1024]{2,1,0:T(8,128)(2,1)S(1)} async-done(((bf16[32,40,1024]{2,1,0:T(8,128)(2,1)}), bf16[32,40,1024]{2,1,0:T(8,128)(2,1)S(1)}, u32[]{:S(2)}, u32[]{:S(2)}) %all-to-all-start.1) | async-done | bytes 2621472 | tf_op jit(solution)/shard_map/all_to_all | solution.py:123
  216.9 3.0 fusion.4
  229.5 7.9 %all-to-all-start.2 = ((bf16[32,40,1024]{2,1,0:T(8,128)(2,1)}), bf16[32,40,1024]{2,1,0:T(8,128)(2,1)S(1)}, u32[]{:S(2)}, u32[]{:S(2)}) async-start(bf16[32,40,1024]{2,1,0:T(8,128)(2,1)} %bitcast.356), calls=%async_computation.2 | async-start | bytes 5242880 | tf_op jit(solution)/shard_map/all_to_all | solution.py:123
  239.8 3.3 convolution_convert_fusion.1
  243.1 28.7 %all-to-all-done.2 = bf16[32,40,1024]{2,1,0:T(8,128)(2,1)S(1)} async-done(((bf16[32,40,1024]{2,1,0:T(8,128)(2,1)}), bf16[32,40,1024]{2,1,0:T(8,128)(2,1)S(1)}, u32[]{:S(2)}, u32[]{:S(2)}) %all-to-all-start.2) | async-done | bytes 2621472 | tf_op jit(solution)/shard_map/all_to_all | solution.py:123
  271.8 6.3 all-to-all-start.4
  278.2 39.9 %collective-permute-done.4 = bf16[128,2048]{1,0:T(8,128)(2,1)S(1)} collective-permute-done((bf16[128,2048]{1,0:T(8,128)(2,1)}, bf16[128,2048]{1,0:T(8,128)(2,1)S(1)}, u32[]{:S(2)}, u32[]{:S(2)}) %collective-permute-start.4) | collective-permute-done | bytes 524320 | tf_op jit(solution)/shard_map/ppermute | solution.py:129
  320.4 7.9 %collective-permute-done.6 = bf16[128,1024]{1,0:T(8,128)(2,1)S(1)} collective-permute-done((bf16[128,1024]{1,0:T(8,128)(2,1)}, bf16[128,1024]{1,0:T(8,128)(2,1)S(1)}, u32[]{:S(2)}, u32[]{:S(2)}) %collective-permute-start.6) | collective-permute-done | bytes 262176 | tf_op jit(solution)/shard_map/ppermute | solution.py:129
  330.0 3.1 fusion.67
  333.2 3.7 fusion.94
  336.9 3.9 multiply_convert_fusion.3
  340.8 4.4 convolution_convert_fusion.2
  345.2 9.4 %all-to-all-start.3 = ((bf16[32,40,1024]{2,1,0:T(8,128)(2,1)}), bf16[32,40,1024]{2,1,0:T(8,128)(2,1)S(1)}, u32[]{:S(2)}, u32[]{:S(2)}) async-start(bf16[32,40,1024]{2,1,0:T(8,128)(2,1)} %bitcast.357), calls=%async_computation.3 | async-start | bytes 5242880 | tf_op jit(solution)/shard_map/all_to_all | solution.py:123
  355.3 3.8 fusion.195
  366.0 3.0 add_convert_fusion.1
  369.0 20.6 %all-to-all-done.3 = bf16[32,40,1024]{2,1,0:T(8,128)(2,1)S(1)} async-done(((bf16[32,40,1024]{2,1,0:T(8,128)(2,1)}), bf16[32,40,1024]{2,1,0:T(8,128)(2,1)S(1)}, u32[]{:S(2)}, u32[]{:S(2)}) %all-to-all-start.3) | async-done | bytes 2621472 | tf_op jit(solution)/shard_map/all_to_all | solution.py:123
  389.6 8.6 %all-to-all-start.5 = ((bf16[32,40,1024]{2,1,0:T(8,128)(2,1)}), bf16[32,40,1024]{2,1,0:T(8,128)(2,1)}, u32[]{:S(2)}, u32[]{:S(2)}) async-start(bf16[32,40,1024]{2,1,0:T(8,128)(2,1)} %bitcast.351), calls=%async_computation.5 | async-start | bytes 5242880 | tf_op jit(solution)/shard_map/all_to_all | solution.py:123
  398.2 3.8 fusion.193
  408.1 25.4 %collective-permute-done.25 = bf16[128,1024]{1,0:T(8,128)(2,1)S(1)} collective-permute-done((bf16[128,1024]{1,0:T(8,128)(2,1)S(1)}, bf16[128,1024]{1,0:T(8,128)(2,1)S(1)}, u32[]{:S(2)}, u32[]{:S(2)}) %collective-permute-start.25) | collective-permute-done | bytes 262176 | tf_op jit(solution)/shard_map/ppermute | solution.py:139
  434.4 4.8 collective-permute-done.19
  440.0 4.4 collective-permute-done.21
  451.5 3.1 fusion.48
  466.7 2.5 fusion.111
  469.3 4.2 copy-done.1
  475.6 2.6 fusion.64
  478.2 10.3 %all-to-all-start.11 = ((bf16[64,8,1024]{2,1,0:T(8,128)(2,1)}), bf16[64,8,1024]{2,1,0:T(8,128)(2,1)}, u32[]{:S(2)}, u32[]{:S(2)}) async-start(bf16[64,8,1024]{2,1,0:T(8,128)(2,1)} %fusion.64), calls=%async_computation.11 | async-start | bytes 2097152 | tf_op jit(solution)/shard_map/all_to_all | solution.py:150
  488.5 4.2 multiply_reduce_fusion.3
  496.0 9.7 %all-to-all-done.11 = bf16[64,8,1024]{2,1,0:T(8,128)(2,1)} async-done(((bf16[64,8,1024]{2,1,0:T(8,128)(2,1)}), bf16[64,8,1024]{2,1,0:T(8,128)(2,1)}, u32[]{:S(2)}, u32[]{:S(2)}) %all-to-all-start.11) | async-done | bytes 1048608 | tf_op jit(solution)/shard_map/all_to_all | solution.py:150
  505.8 6.0 all-to-all-start.6
  517.7 3.0 convolution_multiply_fusion
  526.6 4.9 fusion.16
  531.5 12.7 %all-to-all-done.6 = bf16[32,40,1024]{2,1,0:T(8,128)(2,1)} async-done(((bf16[32,40,1024]{2,1,0:T(8,128)(2,1)}), bf16[32,40,1024]{2,1,0:T(8,128)(2,1)}, u32[]{:S(2)}, u32[]{:S(2)}) %all-to-all-start.6) | async-done | bytes 2621472 | tf_op jit(solution)/shard_map/all_to_all | solution.py:123
  544.2 6.2 multiply_convert_fusion.1
  552.0 3.0 add_convert_fusion
  555.0 6.9 all-to-all-start.7
  561.9 3.8 fusion.194
  574.0 23.4 %collective-permute-done.23 = bf16[128,1024]{1,0:T(8,128)(2,1)S(1)} collective-permute-done((bf16[128,1024]{1,0:T(8,128)(2,1)S(1)}, bf16[128,1024]{1,0:T(8,128)(2,1)S(1)}, u32[]{:S(2)}, u32[]{:S(2)}) %collective-permute-start.23) | collective-permute-done | bytes 262176 | tf_op jit(solution)/shard_map/ppermute | solution.py:139
  598.3 4.7 collective-permute-done.15
  603.9 4.0 collective-permute-done.17
  608.8 9.7 %all-to-all-start.9 = ((bf16[64,8,2048]{2,1,0:T(8,128)(2,1)}), bf16[64,8,2048]{2,1,0:T(8,128)(2,1)}, u32[]{:S(2)}, u32[]{:S(2)}) async-start(bf16[64,8,2048]{2,1,0:T(8,128)(2,1)} %fusion.16), calls=%async_computation.9 | async-start | bytes 4194304 | tf_op jit(solution)/shard_map/all_to_all | solution.py:150
  620.8 2.6 fusion.51
  630.6 6.0 fusion.88
  636.6 2.8 fusion.98
  641.3 2.7 dynamic-slice_convert_fusion.3
  647.6 10.3 %all-to-all-start.13 = ((bf16[64,8,128]{2,1,0:T(8,128)(2,1)}), bf16[64,8,128]{2,1,0:T(8,128)(2,1)S(1)}, u32[]{:S(2)}, u32[]{:S(2)}) async-start(bf16[64,8,128]{2,1,0:T(8,128)(2,1)} %fusion.115), calls=%async_computation.13 | async-start | bytes 262144 | tf_op jit(solution)/shard_map/all_to_all | solution.py:150
  659.6 7.2 all-to-all-done.13
  666.8 6.0 all-to-all-start.12
  672.8 3.4 fusion.63
  676.2 5.5 all-to-all-done.12
  682.3 6.0 all-to-all-start.10
  689.9 4.8 fusion.15
  694.8 8.9 %all-to-all-done.10 = bf16[64,8,1024]{2,1,0:T(8,128)(2,1)S(1)} async-done(((bf16[64,8,1024]{2,1,0:T(8,128)(2,1)}), bf16[64,8,1024]{2,1,0:T(8,128)(2,1)S(1)}, u32[]{:S(2)}, u32[]{:S(2)}) %all-to-all-start.10) | async-done | bytes 1048608 | tf_op jit(solution)/shard_map/all_to_all | solution.py:150
  704.7 5.8 all-to-all-start.8
  710.6 2.6 convert_reduce_fusion
  717.4 20.6 %all-to-all-done.8 = bf16[64,8,2048]{2,1,0:T(8,128)(2,1)S(1)} async-done(((bf16[64,8,2048]{2,1,0:T(8,128)(2,1)}), bf16[64,8,2048]{2,1,0:T(8,128)(2,1)S(1)}, u32[]{:S(2)}, u32[]{:S(2)}) %all-to-all-start.8) | async-done | bytes 2097184 | tf_op jit(solution)/shard_map/all_to_all | solution.py:150
  (483 shorter events, 138.6 us)
Async XLA Ops:
  7.2 76.0 %copy-start.24 = (bf16[128,1024]{1,0:T(8,128)(2,1)S(1)}, bf16[128,1024]{1,0:T(8,128)(2,1)}, u32[]{:S(2)}) copy-start(bf16[128,1024]{1,0:T(8,128)(2,1)} %param.12) | copy-start | bytes 786436
  7.2 74.6 %all-gather.3.cloned.1.call-start = ((), (), s32[]{:S(2)}) async-start(), calls=%async_computation.14 | async-start | bytes 6604800 | tf_op jit(solution)/shard_map/all_gather | solution.py:37
  11.8 169.0 %all-gather.5.cloned.1.call-start = ((), (), s32[]{:S(2)}) async-start(), calls=%async_computation.15 | async-start | bytes 6604800 | tf_op jit(solution)/shard_map/all_gather | solution.py:37
  17.1 69.1 %copy-start.109 = (f32[128]{0:T(128)}, f32[128]{0:T(128)S(1)}, u32[]{:S(2)}) copy-start(f32[128]{0:T(128)S(1)} %add_rsqrt_fusion.3) | copy-start | bytes 1540
  17.7 204.4 %copy-start.104 = (pred[128,128]{0,1:T(8,128)(4,1)}, pred[128,128]{0,1:T(8,128)(4,1)S(1)}, u32[]{:S(2)}) copy-start(pred[128,128]{0,1:T(8,128)(4,1)S(1)} %fusion.130) | copy-start | bytes 49156
  94.6 62.5 %all-to-all-start = ((bf16[32,40,1024]{2,1,0:T(8,128)(2,1)}), bf16[32,40,1024]{2,1,0:T(8,128)(2,1)S(1)}, u32[]{:S(2)}, u32[]{:S(2)}) async-start(bf16[32,40,1024]{2,1,0:T(8,128)(2,1)} %bitcast.355), calls=%async_computation | async-start | bytes 5242880 | tf_op jit(solution)/shard_map/all_to_all | solution.py:123
  102.1 43.1 %copy-start.74 = (bf16[2,128,1024]{2,1,0:T(8,128)(2,1)S(1)}, bf16[2,128,1024]{2,1,0:T(8,128)(2,1)}, u32[]{:S(2)}) copy-start(bf16[2,128,1024]{2,1,0:T(8,128)(2,1)} %param.23) | copy-start | bytes 1572868
  104.3 40.7 %collective-permute-start = (bf16[128,2048]{1,0:T(8,128)(2,1)S(1)}, bf16[128,2048]{1,0:T(8,128)(2,1)S(1)}, u32[]{:S(2)}, u32[]{:S(2)}) collective-permute-start(bf16[128,2048]{1,0:T(8,128)(2,1)S(1)} %get-tuple-element.33), channel_id=1, source_target_pairs={{0,2},{2,0},{1,3},{3,1},{4,6},{6,4},{5,7},{7,5},{8,10},{10,8},{9,1... | collective-permute-start | bytes 1572872 | tf_op jit(solution)/shard_map/ppermute | solution.py:129
  145.0 10.5 %collective-permute-start.1 = (bf16[256,2048]{1,0:T(8,128)(2,1)S(1)}, bf16[256,2048]{1,0:T(8,128)(2,1)S(1)}, u32[]{:S(2)}, u32[]{:S(2)}) collective-permute-start(bf16[256,2048]{1,0:T(8,128)(2,1)S(1)} %pad_maximum_fusion.3), channel_id=1, source_target_pairs={{0,1},{1,0},{2,3},{3,2},{4,5},{5,4},{6,7},{7,6},{8,9},{9,8},{10,11... | collective-permute-start | bytes 3145736 | tf_op jit(solution)/shard_map/ppermute | solution.py:130
  145.9 9.6 %copy-start.69 = (bf16[128,1024]{1,0:T(8,128)(2,1)}, bf16[128,1024]{1,0:T(8,128)(2,1)S(1)}, u32[]{:S(2)}) copy-start(bf16[128,1024]{1,0:T(8,128)(2,1)S(1)} %get-tuple-element.43) | copy-start | bytes 786436
  145.9 8.7 %collective-permute-start.2 = (bf16[128,1024]{1,0:T(8,128)(2,1)S(1)}, bf16[128,1024]{1,0:T(8,128)(2,1)S(1)}, u32[]{:S(2)}, u32[]{:S(2)}) collective-permute-start(bf16[128,1024]{1,0:T(8,128)(2,1)S(1)} %get-tuple-element.43), channel_id=1, source_target_pairs={{0,2},{2,0},{1,3},{3,1},{4,6},{6,4},{5,7},{7,5},{8,10},{10,8},{9,1... | collective-permute-start | bytes 786440 | tf_op jit(solution)/shard_map/ppermute | solution.py:129
  155.5 8.8 %collective-permute-start.3 = (bf16[256,1024]{1,0:T(8,128)(2,1)}, bf16[256,1024]{1,0:T(8,128)(2,1)}, u32[]{:S(2)}, u32[]{:S(2)}) collective-permute-start(bf16[256,1024]{1,0:T(8,128)(2,1)} %pad_maximum_fusion.8), channel_id=1, source_target_pairs={{0,1},{1,0},{2,3},{3,2},{4,5},{5,4},{6,7},{7,6},{8,9},{9,8},{10,11... | collective-permute-start | bytes 1572872 | tf_op jit(solution)/shard_map/ppermute | solution.py:130
  168.9 45.7 %all-to-all-start.1 = ((bf16[32,40,1024]{2,1,0:T(8,128)(2,1)}), bf16[32,40,1024]{2,1,0:T(8,128)(2,1)S(1)}, u32[]{:S(2)}, u32[]{:S(2)}) async-start(bf16[32,40,1024]{2,1,0:T(8,128)(2,1)} %bitcast.358), calls=%async_computation.1 | async-start | bytes 5242880 | tf_op jit(solution)/shard_map/all_to_all | solution.py:123
  180.8 39.1 %copy-start.107 = (f32[128]{0:T(128)}, f32[128]{0:T(128)S(1)}, u32[]{:S(2)}) copy-start(f32[128]{0:T(128)S(1)} %fusion.141) | copy-start | bytes 1540
  220.7 238.2 %copy-start.81 = (bf16[128,8,32]{0,2,1:T(8,128)(2,1)}, bf16[128,8,32]{0,2,1:T(8,128)(2,1)S(1)}, u32[]{:S(2)}) copy-start(bf16[128,8,32]{0,2,1:T(8,128)(2,1)S(1)} %get-tuple-element.48) | copy-start | bytes 196612
  222.2 236.1 %copy-start.105 = (f32[8,2,128]{2,1,0:T(2,128)}, f32[8,2,128]{2,1,0:T(2,128)S(1)}, u32[]{:S(2)}) copy-start(f32[8,2,128]{2,1,0:T(2,128)S(1)} %get-tuple-element.79) | copy-start | bytes 24580
  229.5 42.2 %all-to-all-start.2 = ((bf16[32,40,1024]{2,1,0:T(8,128)(2,1)}), bf16[32,40,1024]{2,1,0:T(8,128)(2,1)S(1)}, u32[]{:S(2)}, u32[]{:S(2)}) async-start(bf16[32,40,1024]{2,1,0:T(8,128)(2,1)} %bitcast.356), calls=%async_computation.2 | async-start | bytes 5242880 | tf_op jit(solution)/shard_map/all_to_all | solution.py:123
  271.8 65.1 %copy-start.4 = (bf16[32,40,1024]{2,1,0:T(8,128)(2,1)}, bf16[32,40,1024]{2,1,0:T(8,128)(2,1)S(1)}, u32[]{:S(2)}) copy-start(bf16[32,40,1024]{2,1,0:T(8,128)(2,1)S(1)} %all-to-all-done.2) | copy-start | bytes 7864324
  271.8 61.4 %all-to-all-start.4 = ((bf16[32,40,1024]{2,1,0:T(8,128)(2,1)}), bf16[32,40,1024]{2,1,0:T(8,128)(2,1)}, u32[]{:S(2)}, u32[]{:S(2)}) async-start(bf16[32,40,1024]{2,1,0:T(8,128)(2,1)} %bitcast.354), calls=%async_computation.4 | async-start | bytes 5242880 | tf_op jit(solution)/shard_map/all_to_all | solution.py:123
  278.0 51.7 %copy-start.36 = (bf16[128,2048]{1,0:T(8,128)(2,1)S(1)}, bf16[128,2048]{1,0:T(8,128)(2,1)}, u32[]{:S(2)}) copy-start(bf16[128,2048]{1,0:T(8,128)(2,1)} %get-tuple-element.32) | copy-start | bytes 1572868
  278.0 40.1 %collective-permute-start.4 = (bf16[128,2048]{1,0:T(8,128)(2,1)}, bf16[128,2048]{1,0:T(8,128)(2,1)S(1)}, u32[]{:S(2)}, u32[]{:S(2)}) collective-permute-start(bf16[128,2048]{1,0:T(8,128)(2,1)} %get-tuple-element.32), channel_id=1, source_target_pairs={{0,2},{2,0},{1,3},{3,1},{4,6},{6,4},{5,7},{7,5},{8,10},{10,8},{9,1... | collective-permute-start | bytes 1572872 | tf_op jit(solution)/shard_map/ppermute | solution.py:129
  319.3 10.4 %collective-permute-start.5 = (bf16[256,2048]{1,0:T(8,128)(2,1)S(1)}, bf16[256,2048]{1,0:T(8,128)(2,1)S(1)}, u32[]{:S(2)}, u32[]{:S(2)}) collective-permute-start(bf16[256,2048]{1,0:T(8,128)(2,1)S(1)} %pad_maximum_fusion.5), channel_id=1, source_target_pairs={{0,1},{1,0},{2,3},{3,2},{4,5},{5,4},{6,7},{7,6},{8,9},{9,8},{10,11... | collective-permute-start | bytes 3145736 | tf_op jit(solution)/shard_map/ppermute | solution.py:130
  319.4 8.9 %collective-permute-start.6 = (bf16[128,1024]{1,0:T(8,128)(2,1)}, bf16[128,1024]{1,0:T(8,128)(2,1)S(1)}, u32[]{:S(2)}, u32[]{:S(2)}) collective-permute-start(bf16[128,1024]{1,0:T(8,128)(2,1)} %get-tuple-element.42), channel_id=1, source_target_pairs={{0,2},{2,0},{1,3},{3,1},{4,6},{6,4},{5,7},{7,5},{8,10},{10,8},{9,1... | collective-permute-start | bytes 786440 | tf_op jit(solution)/shard_map/ppermute | solution.py:129
  329.4 3.7 collective-permute-start.7
  345.2 44.4 %all-to-all-start.3 = ((bf16[32,40,1024]{2,1,0:T(8,128)(2,1)}), bf16[32,40,1024]{2,1,0:T(8,128)(2,1)S(1)}, u32[]{:S(2)}, u32[]{:S(2)}) async-start(bf16[32,40,1024]{2,1,0:T(8,128)(2,1)} %bitcast.357), calls=%async_computation.3 | async-start | bytes 5242880 | tf_op jit(solution)/shard_map/all_to_all | solution.py:123
  360.1 42.1 %collective-permute-start.24 = (bf16[256,1024]{1,0:T(8,128)(2,1)}, bf16[256,1024]{1,0:T(8,128)(2,1)}, u32[]{:S(2)}, u32[]{:S(2)}) collective-permute-start(bf16[256,1024]{1,0:T(8,128)(2,1)} %slice.456), channel_id=1, source_target_pairs={{0,1},{1,0},{2,3},{3,2},{4,5},{5,4},{6,7},{7,6},{8,9},{9,8},{10,11... | collective-permute-start | bytes 1572872 | tf_op jit(solution)/shard_map/ppermute | solution.py:137
  364.4 40.0 %collective-permute-start.18 = (bf16[256,1024]{1,0:T(8,128)(2,1)}, bf16[256,1024]{1,0:T(8,128)(2,1)}, u32[]{:S(2)}, u32[]{:S(2)}) collective-permute-start(bf16[256,1024]{1,0:T(8,128)(2,1)} %slice.459), channel_id=1, source_target_pairs={{0,1},{1,0},{2,3},{3,2},{4,5},{5,4},{6,7},{7,6},{8,9},{9,8},{10,11... | collective-permute-start | bytes 1572872 | tf_op jit(solution)/shard_map/ppermute | solution.py:137
  389.6 57.1 %all-to-all-start.5 = ((bf16[32,40,1024]{2,1,0:T(8,128)(2,1)}), bf16[32,40,1024]{2,1,0:T(8,128)(2,1)}, u32[]{:S(2)}, u32[]{:S(2)}) async-start(bf16[32,40,1024]{2,1,0:T(8,128)(2,1)} %bitcast.351), calls=%async_computation.5 | async-start | bytes 5242880 | tf_op jit(solution)/shard_map/all_to_all | solution.py:123
  402.2 5.0 collective-permute-start.20
  403.6 29.8 %collective-permute-start.25 = (bf16[128,1024]{1,0:T(8,128)(2,1)S(1)}, bf16[128,1024]{1,0:T(8,128)(2,1)S(1)}, u32[]{:S(2)}, u32[]{:S(2)}) collective-permute-start(bf16[128,1024]{1,0:T(8,128)(2,1)S(1)} %slice.462), channel_id=1, source_target_pairs={{0,2},{2,0},{1,3},{3,1},{4,6},{6,4},{5,7},{7,5},{8,10},{10,8},{9,1... | collective-permute-start | bytes 786440 | tf_op jit(solution)/shard_map/ppermute | solution.py:139
  405.7 33.5 %collective-permute-start.19 = (bf16[128,1024]{1,0:T(8,128)(2,1)S(1)}, bf16[128,1024]{1,0:T(8,128)(2,1)S(1)}, u32[]{:S(2)}, u32[]{:S(2)}) collective-permute-start(bf16[128,1024]{1,0:T(8,128)(2,1)S(1)} %slice.465), channel_id=1, source_target_pairs={{0,2},{2,0},{1,3},{3,1},{4,6},{6,4},{5,7},{7,5},{8,10},{10,8},{9,1... | collective-permute-start | bytes 786440 | tf_op jit(solution)/shard_map/ppermute | solution.py:139
  407.3 38.0 %copy-start.47 = (bf16[128,1024]{1,0:T(8,128)(2,1)S(1)}, bf16[128,1024]{1,0:T(8,128)(2,1)}, u32[]{:S(2)}) copy-start(bf16[128,1024]{1,0:T(8,128)(2,1)} %param.13) | copy-start | bytes 786436
  407.4 37.0 %collective-permute-start.21 = (bf16[128,1024]{1,0:T(8,128)(2,1)S(1)}, bf16[128,1024]{1,0:T(8,128)(2,1)S(1)}, u32[]{:S(2)}, u32[]{:S(2)}) collective-permute-start(bf16[128,1024]{1,0:T(8,128)(2,1)S(1)} %slice.464), channel_id=1, source_target_pairs={{0,2},{2,0},{1,3},{3,1},{4,6},{6,4},{5,7},{7,5},{8,10},{10,8},{9,1... | collective-permute-start | bytes 786440 | tf_op jit(solution)/shard_map/ppermute | solution.py:139
  463.5 12.1 %collective-permute-start.11 = (bf16[64,1,8,1024]{3,2,1,0:T(8,128)(2,1)}, bf16[64,1,8,1024]{3,2,1,0:T(8,128)(2,1)}, u32[]{:S(2)}, u32[]{:S(2)}) collective-permute-start(bf16[64,1,8,1024]{3,2,1,0:T(8,128)(2,1)} %dynamic-slice_convert_fusion.2), channel_id=1, source_target_pairs={{0,1},{1,0},{2,3},{3,2},{4,5},{5,4},{6,7},{7,6},{8,9},{9,8},{10,11... | collective-permute-start | bytes 3145736 | tf_op jit(solution)/shard_map/ppermute | solution.py:148
  475.1 51.5 %collective-permute-start.9 = (bf16[64,1,8,2048]{3,2,1,0:T(8,128)(2,1)}, bf16[64,1,8,2048]{3,2,1,0:T(8,128)(2,1)}, u32[]{:S(2)}, u32[]{:S(2)}) collective-permute-start(bf16[64,1,8,2048]{3,2,1,0:T(8,128)(2,1)} %dynamic-slice_convert_fusion), channel_id=1, source_target_pairs={{0,1},{1,0},{2,3},{3,2},{4,5},{5,4},{6,7},{7,6},{8,9},{9,8},{10,11... | collective-permute-start | bytes 6291464 | tf_op jit(solution)/shard_map/ppermute | solution.py:148
  478.2 27.6 %all-to-all-start.11 = ((bf16[64,8,1024]{2,1,0:T(8,128)(2,1)}), bf16[64,8,1024]{2,1,0:T(8,128)(2,1)}, u32[]{:S(2)}, u32[]{:S(2)}) async-start(bf16[64,8,1024]{2,1,0:T(8,128)(2,1)} %fusion.64), calls=%async_computation.11 | async-start | bytes 2097152 | tf_op jit(solution)/shard_map/all_to_all | solution.py:150
  505.8 38.4 %all-to-all-start.6 = ((bf16[32,40,1024]{2,1,0:T(8,128)(2,1)}), bf16[32,40,1024]{2,1,0:T(8,128)(2,1)}, u32[]{:S(2)}, u32[]{:S(2)}) async-start(bf16[32,40,1024]{2,1,0:T(8,128)(2,1)} %bitcast.353), calls=%async_computation.6 | async-start | bytes 5242880 | tf_op jit(solution)/shard_map/all_to_all | solution.py:123
  514.3 6.4 copy-start.108
  526.6 17.6 %copy-start.71 = (bf16[128,1024]{1,0:T(8,128)(2,1)S(1)}, bf16[128,1024]{1,0:T(8,128)(2,1)}, u32[]{:S(2)}) copy-start(bf16[128,1024]{1,0:T(8,128)(2,1)} %copy-done.69) | copy-start | bytes 786436
  526.6 17.6 %copy-start.87 = (bf16[128,1024]{1,0:T(8,128)(2,1)S(1)}, bf16[128,1024]{1,0:T(8,128)(2,1)}, u32[]{:S(2)}) copy-start(bf16[128,1024]{1,0:T(8,128)(2,1)} %copy-done.85) | copy-start | bytes 786436
  555.0 53.8 %all-to-all-start.7 = ((bf16[32,40,1024]{2,1,0:T(8,128)(2,1)}), bf16[32,40,1024]{2,1,0:T(8,128)(2,1)S(1)}, u32[]{:S(2)}, u32[]{:S(2)}) async-start(bf16[32,40,1024]{2,1,0:T(8,128)(2,1)} %bitcast.73), calls=%async_computation.7 | async-start | bytes 5242880 | tf_op jit(solution)/shard_map/all_to_all | solution.py:123
  565.8 4.0 collective-permute-start.22
  567.5 3.9 collective-permute-start.14
  569.7 2.7 collective-permute-start.16
  570.0 27.4 %collective-permute-start.23 = (bf16[128,1024]{1,0:T(8,128)(2,1)S(1)}, bf16[128,1024]{1,0:T(8,128)(2,1)S(1)}, u32[]{:S(2)}, u32[]{:S(2)}) collective-permute-start(bf16[128,1024]{1,0:T(8,128)(2,1)S(1)} %slice.463), channel_id=1, source_target_pairs={{0,2},{2,0},{1,3},{3,1},{4,6},{6,4},{5,7},{7,5},{8,10},{10,8},{9,1... | collective-permute-start | bytes 786440 | tf_op jit(solution)/shard_map/ppermute | solution.py:139
  571.6 31.4 %collective-permute-start.15 = (bf16[128,1024]{1,0:T(8,128)(2,1)S(1)}, bf16[128,1024]{1,0:T(8,128)(2,1)S(1)}, u32[]{:S(2)}, u32[]{:S(2)}) collective-permute-start(bf16[128,1024]{1,0:T(8,128)(2,1)S(1)} %slice.467), channel_id=1, source_target_pairs={{0,2},{2,0},{1,3},{3,1},{4,6},{6,4},{5,7},{7,5},{8,10},{10,8},{9,1... | collective-permute-start | bytes 786440 | tf_op jit(solution)/shard_map/ppermute | solution.py:139
  572.6 35.3 %collective-permute-start.17 = (bf16[128,1024]{1,0:T(8,128)(2,1)S(1)}, bf16[128,1024]{1,0:T(8,128)(2,1)S(1)}, u32[]{:S(2)}, u32[]{:S(2)}) collective-permute-start(bf16[128,1024]{1,0:T(8,128)(2,1)S(1)} %slice.466), channel_id=1, source_target_pairs={{0,2},{2,0},{1,3},{3,1},{4,6},{6,4},{5,7},{7,5},{8,10},{10,8},{9,1... | collective-permute-start | bytes 786440 | tf_op jit(solution)/shard_map/ppermute | solution.py:139
  608.8 38.8 %all-to-all-start.9 = ((bf16[64,8,2048]{2,1,0:T(8,128)(2,1)}), bf16[64,8,2048]{2,1,0:T(8,128)(2,1)}, u32[]{:S(2)}, u32[]{:S(2)}) async-start(bf16[64,8,2048]{2,1,0:T(8,128)(2,1)} %fusion.16), calls=%async_computation.9 | async-start | bytes 4194304 | tf_op jit(solution)/shard_map/all_to_all | solution.py:150
  620.8 15.8 %copy-start.31 = (f32[128,1024]{1,0:T(8,128)}, f32[128,1024]{1,0:T(8,128)S(1)}, u32[]{:S(2)}) copy-start(f32[128,1024]{1,0:T(8,128)S(1)} %multiply_add_fusion) | copy-start | bytes 1572868
  628.5 8.2 %copy-start = (f32[1024,2048]{1,0:T(8,128)}, f32[1024,2048]{1,0:T(8,128)S(1)}, u32[]{:S(2)}) copy-start(f32[1024,2048]{1,0:T(8,128)S(1)} %fusion.110) | copy-start | bytes 25165828
  630.4 59.6 %collective-permute-start.8 = (bf16[64,1,8,2048]{3,2,1,0:T(8,128)(2,1)}, bf16[64,1,8,2048]{3,2,1,0:T(8,128)(2,1)}, u32[]{:S(2)}, u32[]{:S(2)}) collective-permute-start(bf16[64,1,8,2048]{3,2,1,0:T(8,128)(2,1)} %dynamic-slice_convert_fusion.1), channel_id=1, source_target_pairs={{0,1},{1,0},{2,3},{3,2},{4,5},{5,4},{6,7},{7,6},{8,9},{9,8},{10,11... | collective-permute-start | bytes 6291464 | tf_op jit(solution)/shard_map/ppermute | solution.py:148
  644.1 28.8 %collective-permute-start.10 = (bf16[64,1,8,1024]{3,2,1,0:T(8,128)(2,1)}, bf16[64,1,8,1024]{3,2,1,0:T(8,128)(2,1)}, u32[]{:S(2)}, u32[]{:S(2)}) collective-permute-start(bf16[64,1,8,1024]{3,2,1,0:T(8,128)(2,1)} %dynamic-slice_convert_fusion.3), channel_id=1, source_target_pairs={{0,1},{1,0},{2,3},{3,2},{4,5},{5,4},{6,7},{7,6},{8,9},{9,8},{10,11... | collective-permute-start | bytes 3145736 | tf_op jit(solution)/shard_map/ppermute | solution.py:148
  644.8 2.1 collective-permute-start.13
  646.4 11.6 %collective-permute-start.12 = (bf16[64,1,8,128]{3,2,0,1:T(8,128)(2,1)S(1)}, bf16[64,1,8,128]{3,2,0,1:T(8,128)(2,1)S(1)}, u32[]{:S(2)}, u32[]{:S(2)}) collective-permute-start(bf16[64,1,8,128]{3,2,0,1:T(8,128)(2,1)S(1)} %dynamic-slice_convert_fusion.5), channel_id=1, source_target_pairs={{0,1},{1,0},{2,3},{3,2},{4,5},{5,4},{6,7},{7,6},{8,9},{9,8},{10,11... | collective-permute-start | bytes 393224 | tf_op jit(solution)/shard_map/ppermute | solution.py:148
  647.6 19.2 %all-to-all-start.13 = ((bf16[64,8,128]{2,1,0:T(8,128)(2,1)}), bf16[64,8,128]{2,1,0:T(8,128)(2,1)S(1)}, u32[]{:S(2)}, u32[]{:S(2)}) async-start(bf16[64,8,128]{2,1,0:T(8,128)(2,1)} %fusion.115), calls=%async_computation.13 | async-start | bytes 262144 | tf_op jit(solution)/shard_map/all_to_all | solution.py:150
  666.8 14.8 %all-to-all-start.12 = ((bf16[64,8,128]{2,1,0:T(8,128)(2,1)}), bf16[64,8,128]{2,1,0:T(8,128)(2,1)S(1)}, u32[]{:S(2)}, u32[]{:S(2)}) async-start(bf16[64,8,128]{2,1,0:T(8,128)(2,1)} %fusion.114), calls=%async_computation.12 | async-start | bytes 262144 | tf_op jit(solution)/shard_map/all_to_all | solution.py:150
  672.8 15.5 %copy-start.58 = (f32[128,1024]{1,0:T(8,128)S(1)}, f32[128,1024]{1,0:T(8,128)}, u32[]{:S(2)}) copy-start(f32[128,1024]{1,0:T(8,128)} %slice_add_fusion.11) | copy-start | bytes 1572868
  672.8 15.5 %copy-start.59 = (f32[128,1024]{1,0:T(8,128)S(1)}, f32[128,1024]{1,0:T(8,128)}, u32[]{:S(2)}) copy-start(f32[128,1024]{1,0:T(8,128)} %slice_add_fusion.10) | copy-start | bytes 1572868
  676.2 12.2 %copy-start.43 = (f32[1,128,2048]{2,1,0:T(8,128)S(1)}, f32[1,128,2048]{2,1,0:T(8,128)}, u32[]{:S(2)}) copy-start(f32[1,128,2048]{2,1,0:T(8,128)} %maximum_bitcast_fusion.1) | copy-start | bytes 3145732
  682.3 21.4 %all-to-all-start.10 = ((bf16[64,8,1024]{2,1,0:T(8,128)(2,1)}), bf16[64,8,1024]{2,1,0:T(8,128)(2,1)S(1)}, u32[]{:S(2)}, u32[]{:S(2)}) async-start(bf16[64,8,1024]{2,1,0:T(8,128)(2,1)} %fusion.63), calls=%async_computation.10 | async-start | bytes 2097152 | tf_op jit(solution)/shard_map/all_to_all | solution.py:150
  694.8 18.4 %copy-start.32 = (f32[128,1024]{1,0:T(8,128)S(1)}, f32[128,1024]{1,0:T(8,128)}, u32[]{:S(2)}) copy-start(f32[128,1024]{1,0:T(8,128)} %copy-done.31) | copy-start | bytes 1572868
  694.8 18.4 %copy-start.73 = (f32[128,1024]{1,0:T(8,128)S(1)}, f32[128,1024]{1,0:T(8,128)}, u32[]{:S(2)}) copy-start(f32[128,1024]{1,0:T(8,128)} %get-tuple-element.96) | copy-start | bytes 1572868
  704.7 33.3 %all-to-all-start.8 = ((bf16[64,8,2048]{2,1,0:T(8,128)(2,1)}), bf16[64,8,2048]{2,1,0:T(8,128)(2,1)S(1)}, u32[]{:S(2)}, u32[]{:S(2)}) async-start(bf16[64,8,2048]{2,1,0:T(8,128)(2,1)} %fusion.15), calls=%async_computation.8 | async-start | bytes 4194304 | tf_op jit(solution)/shard_map/all_to_all | solution.py:150
  714.2 24.1 %copy-start.84 = (f32[8,2048]{1,0:T(8,128)S(1)}, f32[8,2048]{1,0:T(8,128)}, u32[]{:S(2)}) copy-start(f32[8,2048]{1,0:T(8,128)} %convert_reduce_fusion) | copy-start | bytes 196612
  (98 other events, 286.5 us)
Sparse Core Ops, SparseCore 0:
  12.0 69.7 all-gather.2
  85.3 86.5 all-gather.4

commit v2 on v1

--- a/solution.py
+++ b/solution.py
@@ -209,7 +209,7 @@
     )
 
 
-def expert_forward(hidden, weights, expert_in_l, expert_out_l, live, routed, chosen):
+def route_rows(hidden, weights, routed, chosen):
     qkv_full, out_full, router_full, gain_one, gain_two = weights
     inverse_two = lax.rsqrt(jnp.mean(hidden * hidden, axis=-1, keepdims=True) + EPSILON)
     normed_two = hidden * inverse_two
@@ -217,7 +217,6 @@
     rows = lax.dot_general(
         chosen, routed_in, (((0,), (0,)), ((), ())), preferred_element_type=jnp.float32
     ).astype(jnp.bfloat16)
-    rows_here = trade_rows(rows)
     logits = jnp.dot(routed_in, router_full, preferred_element_type=jnp.float32)
     masked = jnp.where(routed, logits, MASKED)
     exp_chosen = jnp.where(routed, jnp.exp(masked - jnp.max(masked, axis=-1, keepdims=True)), 0.0)
@@ -225,7 +224,19 @@
     gate_wide = jnp.dot(
         gate_prob.astype(jnp.bfloat16), spread_table(), preferred_element_type=jnp.float32
     ).astype(jnp.bfloat16)
-    mixing = gate_wide * chosen
+    return rows, (inverse_two, normed_two, routed_in, gate_prob, gate_wide * chosen)
+
+
+def slot_gradients(grad_out, mixing):
+    return lax.dot_general(
+        mixing,
+        grad_out.astype(jnp.bfloat16),
+        (((0,), (0,)), ((), ())),
+        preferred_element_type=jnp.float32,
+    ).astype(jnp.bfloat16)
+
+
+def feed_forward(rows_here, expert_in_l, expert_out_l):
     gate_pre = lax.dot_general(
         rows_here,
         expert_in_l[:, :MODEL_WIDTH],
@@ -240,32 +251,48 @@
     )
     units = (jax.nn.silu(gate_pre) * up_pre).astype(jnp.bfloat16)
     results = jnp.dot(units, expert_out_l, preferred_element_type=jnp.float32).astype(jnp.bfloat16)
-    returned = trade_rows(results)
-    result = hidden + jnp.dot(mixing, returned, preferred_element_type=jnp.float32)
-    stash = (inverse_two, normed_two, routed_in, gate_prob, mixing, returned)
-    return result, stash + (gate_pre, up_pre, rows_here)
-
-
-def expert_backward(grad_out, weights, expert_in_l, expert_out_l, chosen, expert_stash):
+    return results, (gate_pre, up_pre)
+
+
+def feed_backward(grad_rows, rows_here, pre, expert_in_l, expert_out_l):
+    gate_pre, up_pre = pre
+    sigmoid_pre = jax.nn.sigmoid(gate_pre)
+    activated = gate_pre * sigmoid_pre
+    units = (activated * up_pre).astype(jnp.bfloat16)
+    grad_units = lax.dot_general(
+        grad_rows, expert_out_l, (((1,), (1,)), ((), ())), preferred_element_type=jnp.float32
+    )
+    grad_gate_pre = (
+        grad_units * up_pre * (sigmoid_pre * (1.0 + gate_pre * (1.0 - sigmoid_pre)))
+    ).astype(jnp.bfloat16)
+    grad_up_pre = (grad_units * activated).astype(jnp.bfloat16)
+    grad_in_rows = jnp.dot(
+        grad_gate_pre, expert_in_l[:, :MODEL_WIDTH], preferred_element_type=jnp.float32
+    )
+    grad_in_rows = (
+        grad_in_rows
+        + jnp.dot(grad_up_pre, expert_in_l[:, MODEL_WIDTH:], preferred_element_type=jnp.float32)
+    ).astype(jnp.bfloat16)
+    out_grad = lax.dot_general(
+        units, grad_rows, (((0,), (0,)), ((), ())), preferred_element_type=jnp.float32
+    )
+    gate_w_grad = lax.dot_general(
+        grad_gate_pre, rows_here, (((0,), (0,)), ((), ())), preferred_element_type=jnp.float32
+    )
+    up_w_grad = lax.dot_general(
+        grad_up_pre, rows_here, (((0,), (0,)), ((), ())), preferred_element_type=jnp.float32
+    )
+    return grad_in_rows, (gate_w_grad, up_w_grad, out_grad)
+
+
+def route_backward(grad_out, weights, chosen, returned, stash):
     qkv_full, out_full, router_full, gain_one, gain_two = weights
-    (
-        inverse_two,
-        normed_two,
-        routed_in,
-        gate_prob,
-        mixing,
+    inverse_two, normed_two, routed_in, gate_prob, mixing = stash
+    products = lax.dot_general(
+        grad_out.astype(jnp.bfloat16),
         returned,
-        gate_pre,
-        up_pre,
-        rows_here,
-    ) = expert_stash
-    grad_out_low = grad_out.astype(jnp.bfloat16)
-    slot_grads = lax.dot_general(
-        mixing, grad_out_low, (((0,), (0,)), ((), ())), preferred_element_type=jnp.float32
-    ).astype(jnp.bfloat16)
-    grad_rows = trade_rows(slot_grads)
-    products = lax.dot_general(
-        grad_out_low, returned, (((1,), (1,)), ((), ())), preferred_element_type=jnp.float32
+        (((1,), (1,)), ((), ())),
+        preferred_element_type=jnp.float32,
     )
     grad_gate = lax.dot_general(
         products * chosen.astype(jnp.float32),
@@ -282,41 +309,18 @@
     grad_routed = lax.dot_general(
         grad_logits, router_full, (((1,), (1,)), ((), ())), preferred_element_type=jnp.float32
     )
-    sigmoid_pre = jax.nn.sigmoid(gate_pre)
-    activated = gate_pre * sigmoid_pre
-    units = (activated * up_pre).astype(jnp.bfloat16)
-    grad_units = lax.dot_general(
-        grad_rows, expert_out_l, (((1,), (1,)), ((), ())), preferred_element_type=jnp.float32
-    )
-    grad_gate_pre = (
-        grad_units * up_pre * (sigmoid_pre * (1.0 + gate_pre * (1.0 - sigmoid_pre)))
-    ).astype(jnp.bfloat16)
-    grad_up_pre = (grad_units * activated).astype(jnp.bfloat16)
-    grad_in_rows = jnp.dot(
-        grad_gate_pre, expert_in_l[:, :MODEL_WIDTH], preferred_element_type=jnp.float32
-    )
-    grad_in_rows = (
-        grad_in_rows
-        + jnp.dot(grad_up_pre, expert_in_l[:, MODEL_WIDTH:], preferred_element_type=jnp.float32)
-    ).astype(jnp.bfloat16)
-    grad_slots = trade_rows(grad_in_rows)
-    out_grad = lax.dot_general(
-        units, grad_rows, (((0,), (0,)), ((), ())), preferred_element_type=jnp.float32
-    )
-    gate_w_grad = lax.dot_general(
-        grad_gate_pre, rows_here, (((0,), (0,)), ((), ())), preferred_element_type=jnp.float32
-    )
-    up_w_grad = lax.dot_general(
-        grad_up_pre, rows_here, (((0,), (0,)), ((), ())), preferred_element_type=jnp.float32
-    )
-    in_grad = jnp.concatenate([scatter_expert(gate_w_grad), scatter_expert(up_w_grad)], axis=1)
-    out_grad = scatter_expert(out_grad)
+    return router_grad, grad_routed
+
+
+def rows_backward(grad_out, weights, chosen, grad_slots, grad_routed, stash):
+    qkv_full, out_full, router_full, gain_one, gain_two = weights
+    inverse_two, normed_two, routed_in, gate_prob, mixing = stash
     grad_routed = grad_routed + jnp.dot(chosen, grad_slots, preferred_element_type=jnp.float32)
     gain_two_grad = jnp.sum(grad_routed * normed_two, axis=0)
     grad_h1 = grad_out + norm_back(
         grad_routed * gain_two.astype(jnp.float32), normed_two, inverse_two
     )
-    return (grad_h1, router_grad, gain_two_grad, in_grad, out_grad)
+    return grad_h1, gain_two_grad
 
 
 def attend_backward(grad_h1, weights, live, allowed, cosine_table, sine_values, attn_stash):
@@ -393,66 +397,85 @@
     expert_out,
 ):
     layers = range(LAYER_COUNT)
+    last = LAYER_COUNT - 1
     device = lax.axis_index(AXES)
-    dense = [
-        sent_together(
-            (
-                query_key_value_weight[layer],
-                out_weight[layer],
-                router_weight[layer],
-                gain_attn[layer],
-                gain_mlp[layer],
-            ),
-            AXES,
-            0,
-            1,
+    own_dense = [
+        (
+            query_key_value_weight[layer],
+            out_weight[layer],
+            router_weight[layer],
+            gain_attn[layer],
+            gain_mlp[layer],
         )
         for layer in layers
     ]
-    experts_in = [gather_expert(expert_in[layer]) for layer in layers]
-    experts_out = [gather_expert(expert_out[layer]) for layer in layers]
+    experts = [
+        (gather_expert(expert_in[layer]), gather_expert(expert_out[layer])) for layer in layers
+    ]
+    dense = []
+    for layer in layers:
+        dense.append(sent_together(own_dense[layer], AXES, 0, 1))
+        if layer == 0:
+            dense[0], experts, own_dense = lax.optimization_barrier((dense[0], experts, own_dense))
     position, live_row, allowed = seq_layout(seq_lengths, seq_owner, device)
     live = live_row.astype(jnp.float32)
     cosine_table, sine_values = rope_tables(position)
     routed, chosen = dispatch_table(routes, live_row)
     hidden = hidden_in.astype(jnp.float32)
-    saved_layers = []
+    grad_hidden = cotangent.astype(jnp.float32)
+    saved = []
     for layer in layers:
         hidden, attn_stash = attend_forward(
             hidden, dense[layer], live, allowed, cosine_table, sine_values
         )
-        hidden, expert_stash = expert_forward(
-            hidden, dense[layer], experts_in[layer], experts_out[layer], live, routed, chosen
-        )
-        saved_layers.append((attn_stash, expert_stash))
+        rows, route_stash = route_rows(hidden, dense[layer], routed, chosen)
+        rows_here = trade_rows(rows)
+        grad_rows = None
+        if layer == last:
+            slots = slot_gradients(grad_hidden, route_stash[-1])
+            slots, rows_here = lax.optimization_barrier((slots, rows_here))
+            grad_rows = trade_rows(slots)
+        results, pre = feed_forward(rows_here, *experts[layer])
+        returned = trade_rows(results)
+        hidden = hidden + jnp.dot(route_stash[-1], returned, preferred_element_type=jnp.float32)
+        saved.append((attn_stash, route_stash, rows_here, pre, returned, grad_rows))
     output_low = hidden.astype(jnp.bfloat16)
-    grad_hidden = cotangent.astype(jnp.float32)
     layer_grads = [None] * LAYER_COUNT
     for layer in reversed(layers):
-        attn_stash, expert_stash = saved_layers[layer]
-        grad_hidden, router_grad, gain_two_grad, in_grad, out_grad = expert_backward(
-            grad_hidden, dense[layer], experts_in[layer], experts_out[layer], chosen, expert_stash
+        attn_stash, route_stash, rows_here, pre, returned, grad_rows = saved[layer]
+        if grad_rows is None:
+            grad_rows = trade_rows(slot_gradients(grad_hidden, route_stash[-1]))
+        grad_in_rows, expert_grads = feed_backward(grad_rows, rows_here, pre, *experts[layer])
+        grad_slots = trade_rows(grad_in_rows)
+        router_grad, grad_routed = route_backward(
+            grad_hidden, dense[layer], chosen, returned, route_stash
+        )
+        grad_slots, expert_grads = lax.optimization_barrier((grad_slots, expert_grads))
+        gate_w_grad, up_w_grad, out_grad = [scatter_expert(g) for g in expert_grads]
+        grad_h1, gain_two_grad = rows_backward(
+            grad_hidden, dense[layer], chosen, grad_slots, grad_routed, route_stash
         )
         grad_hidden, qkv_grad, proj_grad, gain_one_grad = attend_backward(
-            grad_hidden, dense[layer], live, allowed, cosine_table, sine_values, attn_stash
+            grad_h1, dense[layer], live, allowed, cosine_table, sine_values, attn_stash
         )
-        small = jnp.concatenate(
-            [
-                router_grad,
-                gain_one_grad[:, None],
-                gain_two_grad[:, None],
-                jnp.zeros((MODEL_WIDTH, 128 - E - 2), jnp.float32),
-            ],
-            axis=1,
-        )
-        small = scatter_dense(small)
+        query_width = qkv_grad.shape[1]
+        fill = jnp.zeros((MODEL_WIDTH, 128 - E - 2), jnp.float32)
+        small = [router_grad, gain_one_grad[:, None], gain_two_grad[:, None], fill]
+        if layer == last:
+            done = scatter_dense(jnp.concatenate([qkv_grad, proj_grad] + small, axis=1))
+            qkv_done, proj_done = done[:, :query_width], done[:, query_width:-128]
+            small_done = done[:, -128:]
+        else:
+            proj_done = scatter_dense(proj_grad)
+            done = scatter_dense(jnp.concatenate([qkv_grad] + small, axis=1))
+            qkv_done, small_done = done[:, :query_width], done[:, -128:]
         layer_grads[layer] = (
-            scatter_dense(qkv_grad),
-            scatter_dense(proj_grad),
-            small[:, :E],
-            small[:, E],
-            small[:, E + 1],
-            in_grad,
+            qkv_done,
+            proj_done,
+            small_done[:, :E],
+            small_done[:, E],
+            small_done[:, E + 1],
+            jnp.concatenate([gate_w_grad, up_w_grad], axis=1),
             out_grad,
         )
     stacked = tuple(

time: 759 us -> 695 us (0.916)
  waiting for transfers between devices: 371 us -> 245 us
  blocking collectives: 0 us -> 43.7 us
  local copies, waits for them, and re-layouts: 44.2 us -> 84.7 us
  starting transfers between devices: 124 us -> 89 us
  matrix products: 134 us -> 143 us
    ppermute x4, waiting for transfers between devices: 95.3 us -> 29.9 us  [gather_expert(): pair = jnp.concatenate([own, lax.ppermute(own, 'zl', SWAP)], axis=0)]
    all_to_all x8 -> x7, waiting for transfers between devices: 93.3 us -> 143 us  [trade_rows(): lax.all_to_all(rows.reshape(E, ROOM, MODEL_WIDTH), EXPERT_AXES, split_axi...]
    ppermute x6, waiting for transfers between devices: 66.7 us -> 21.5 us  [scatter_expert(): return own + lax.ppermute(other, 'zl', SWAP).astype(jnp.float32)]
    all_to_all x0 -> x1, blocking collectives: none -> 43.7 us  [trade_rows(): lax.all_to_all(rows.reshape(E, ROOM, MODEL_WIDTH), EXPERT_AXES, split_axi...]
    all_gather x2, waiting for transfers between devices: 63.4 us -> 20.9 us  [sent_together(): out = lax.all_gather(both, axis, axis=dim, tiled=True)]
    concatenate x10 -> x7, local copies, waits for them, and re-layouts: 6.09 us -> 30.7 us  [the longest x3 17.2 us: on_device(): done = scatter_dense(jnp.concatenate([qkv_grad, proj_grad] + small, axis=1))]
    all_to_all x6 -> x3, starting transfers between devices: 48.1 us -> 24.3 us  [scatter_dense(): lax.all_to_all(kept, CHIP_AXES, split_axis=0, concat_axis=0, tiled=True)]
    all_to_all x6 -> x3, waiting for transfers between devices: 52 us -> 28.9 us  [scatter_dense(): lax.all_to_all(kept, CHIP_AXES, split_axis=0, concat_axis=0, tiled=True)]
  transfers between devices with their start and end apart: 42 -> 35, of which waited for: 21 -> 18; matrix products, arithmetic and copies ran while one was open for 22% -> 30% of each run, Pallas kernels for 0% -> 0%
where the time goes in v2:
time: 695 us; the launch traced here: 683 us
  waiting for transfers between devices  245 us (35%)
  matrix products  143 us (21%)
  starting transfers between devices  89 us (13%)
  local copies, waits for them, and re-layouts  84.7 us (12%)
  other arithmetic  61.7 us (9%)
  blocking collectives  43.7 us (6%)
  between operations  16.4 us (2%)
    all_to_all x7, waiting for transfers between devices, trade_rows(): lax.all_to_all(rows.reshape(E, ROOM, MODEL_WIDTH), EXPERT_AXES, split_axi...  143 us
    all_to_all x7, starting transfers between devices, trade_rows(): lax.all_to_all(rows.reshape(E, ROOM, MODEL_WIDTH), EXPERT_AXES, split_axi...  52 us
    all_to_all x1, blocking collectives, trade_rows(): lax.all_to_all(rows.reshape(E, ROOM, MODEL_WIDTH), EXPERT_AXES, split_axi...  43.7 us
    ppermute x4, waiting for transfers between devices, gather_expert(): pair = jnp.concatenate([own, lax.ppermute(own, 'zl', SWAP)], axis=0)  29.9 us
    all_to_all x3, waiting for transfers between devices, scatter_dense(): lax.all_to_all(kept, CHIP_AXES, split_axis=0, concat_axis=0, tiled=True)  28.9 us
    all_to_all x3, starting transfers between devices, scatter_dense(): lax.all_to_all(kept, CHIP_AXES, split_axis=0, concat_axis=0, tiled=True)  24.3 us
    ppermute x6, waiting for transfers between devices, scatter_expert(): return own + lax.ppermute(other, 'zl', SWAP).astype(jnp.float32)  21.5 us
    all_gather x2, waiting for transfers between devices, sent_together(): out = lax.all_gather(both, axis, axis=dim, tiled=True)  20.9 us
  transfers between devices with their start and end apart: 35, of which 18 were waited for; matrix products, arithmetic and copies ran while one was open for 30% of the time, Pallas kernels for 0%

profile of v2, /device:TPU:2, one launch (start us, length us, event | category | flops | bytes accessed | tf_op | source)
XLA Modules:
  0.0 683.0 jit_solution(9217894532319459508)
XLA Ops:
  16.7 10.6 %collective-permute-done.4 = bf16[128,2048]{1,0:T(8,128)(2,1)S(1)} collective-permute-done((bf16[128,2048]{1,0:T(8,128)(2,1)S(1)}, bf16[128,2048]{1,0:T(8,128)(2,1)S(1)}, u32[]{:S(2)}, u32[]{:S(2)}) %collective-permute-start.4) | collective-permute-done | bytes 524320 | tf_op jit(solution)/shard_map/ppermute | solution.py:129
  28.4 16.3 %collective-permute-done.6 = bf16[128,1024]{1,0:T(8,128)(2,1)S(1)} collective-permute-done((bf16[128,1024]{1,0:T(8,128)(2,1)S(1)}, bf16[128,1024]{1,0:T(8,128)(2,1)S(1)}, u32[]{:S(2)}, u32[]{:S(2)}) %collective-permute-start.6) | collective-permute-done | bytes 262176 | tf_op jit(solution)/shard_map/ppermute | solution.py:129
  47.1 3.0 collective-permute-done.2
  55.3 2.7 pad_maximum_fusion.1
  58.1 2.7 pad_maximum_fusion
  60.8 20.9 %all-gather.3.cloned.1.call-done = bf16[1024,3106]{1,0:T(8,128)(2,1)} async-done(((bf16[8,3106]{1,0:T(8,128)(2,1)}), bf16[1024,3106]{1,0:T(8,128)(2,1)}) %all-gather.3.cloned.1.call-update) | async-done | bytes 6361104 | tf_op jit(solution)/shard_map/all_gather | solution.py:37
  86.8 5.6 split.40
  96.4 3.0 fusion.107
  110.0 43.7 %all_to_all.55 = bf16[32,40,1024]{2,1,0:T(8,128)(2,1)S(1)} all-to-all(bf16[32,40,1024]{2,1,0:T(8,128)(2,1)S(1)} %bitcast.363), channel_id=1, replica_groups=mesh['x'=4,'y'=4,'zh'=2,'zl'=2,'c'=2] {'x','y','zh'}, dimensions={0} | all-to-all | bytes 5242880 | tf_op jit(solution)/shard_map/all_to_all | solution.py:123
  155.3 3.4 multiply_convert_fusion.5
  158.7 3.0 convolution_convert_fusion.4
  161.7 6.4 all-to-all-start.1
  170.5 32.9 %all-to-all-done.1 = bf16[32,40,1024]{2,1,0:T(8,128)(2,1)S(1)} async-done(((bf16[32,40,1024]{2,1,0:T(8,128)(2,1)}), bf16[32,40,1024]{2,1,0:T(8,128)(2,1)S(1)}, u32[]{:S(2)}, u32[]{:S(2)}) %all-to-all-start.1) | async-done | bytes 2621472 | tf_op jit(solution)/shard_map/all_to_all | solution.py:123
  203.3 2.5 multiply_reduce_fusion.9
  207.5 3.1 fusion.4
  217.0 2.4 convolution_convert_fusion.2
  219.4 8.4 %all-to-all-start.2 = ((bf16[32,40,1024]{2,1,0:T(8,128)(2,1)}), bf16[32,40,1024]{2,1,0:T(8,128)(2,1)S(1)}, u32[]{:S(2)}, u32[]{:S(2)}) async-start(bf16[32,40,1024]{2,1,0:T(8,128)(2,1)} %bitcast.361), calls=%async_computation.2 | async-start | bytes 5242880 | tf_op jit(solution)/shard_map/all_to_all | solution.py:123
  230.1 3.3 convolution_convert_fusion.3
  233.4 27.4 %all-to-all-done.2 = bf16[32,40,1024]{2,1,0:T(8,128)(2,1)S(1)} async-done(((bf16[32,40,1024]{2,1,0:T(8,128)(2,1)}), bf16[32,40,1024]{2,1,0:T(8,128)(2,1)S(1)}, u32[]{:S(2)}, u32[]{:S(2)}) %all-to-all-start.2) | async-done | bytes 2621472 | tf_op jit(solution)/shard_map/all_to_all | solution.py:123
  260.8 6.8 %all-to-all-start.4 = ((bf16[32,40,1024]{2,1,0:T(8,128)(2,1)}), bf16[32,40,1024]{2,1,0:T(8,128)(2,1)}, u32[]{:S(2)}, u32[]{:S(2)}) async-start(bf16[32,40,1024]{2,1,0:T(8,128)(2,1)} %bitcast.362), calls=%async_computation.4 | async-start | bytes 5242880 | tf_op jit(solution)/shard_map/all_to_all | solution.py:123
  267.7 4.4 fusion.49
  272.1 3.1 fusion.53
  275.1 25.3 %all-to-all-done.4 = bf16[32,40,1024]{2,1,0:T(8,128)(2,1)} async-done(((bf16[32,40,1024]{2,1,0:T(8,128)(2,1)}), bf16[32,40,1024]{2,1,0:T(8,128)(2,1)}, u32[]{:S(2)}, u32[]{:S(2)}) %all-to-all-start.4) | async-done | bytes 2621472 | tf_op jit(solution)/shard_map/all_to_all | solution.py:123
  300.4 7.8 %multiply_convert_fusion.2 = (bf16[1280,512]{1,0:T(8,128)(2,1)}, bf16[1280,512]{1,0:T(8,128)(2,1)}, bf16[1280,512]{1,0:T(8,128)(2,1)S(1)}) fusion(f32[1280,512]{1,0:T(8,128)} %fusion.53, f32[1280,512]{1,0:T(8,128)} %fusion.49, bf16[1280,1024]{1,0:T(8,128)(2,1)} %bitcast.54, bf16[512,1024]{1,0:T(8,128)(2,1)} %pad_maximum_fusion.6), kind=kOutput, calls=%fused_computation.23 | convolution fusion | flops 1352007680 | bytes 12845056 | tf_op jit(solution)/shard_map/dot_general | solution.py:262
  308.2 3.0 convolution_convert_fusion.1
  311.2 7.0 %all-to-all-start.3 = ((bf16[32,40,1024]{2,1,0:T(8,128)(2,1)}), bf16[32,40,1024]{2,1,0:T(8,128)(2,1)S(1)}, u32[]{:S(2)}, u32[]{:S(2)}) async-start(bf16[32,40,1024]{2,1,0:T(8,128)(2,1)} %bitcast.365), calls=%async_computation.3 | async-start | bytes 5242880 | tf_op jit(solution)/shard_map/all_to_all | solution.py:123
  318.2 3.3 fusion.51
  321.6 3.0 add_convert_fusion.2
  324.5 25.5 %all-to-all-done.3 = bf16[32,40,1024]{2,1,0:T(8,128)(2,1)S(1)} async-done(((bf16[32,40,1024]{2,1,0:T(8,128)(2,1)}), bf16[32,40,1024]{2,1,0:T(8,128)(2,1)S(1)}, u32[]{:S(2)}, u32[]{:S(2)}) %all-to-all-start.3) | async-done | bytes 2621472 | tf_op jit(solution)/shard_map/all_to_all | solution.py:123
  350.0 7.7 %all-to-all-start.5 = ((bf16[32,40,1024]{2,1,0:T(8,128)(2,1)}), bf16[32,40,1024]{2,1,0:T(8,128)(2,1)}, u32[]{:S(2)}, u32[]{:S(2)}) async-start(bf16[32,40,1024]{2,1,0:T(8,128)(2,1)} %bitcast.358), calls=%async_computation.5 | async-start | bytes 5242880 | tf_op jit(solution)/shard_map/all_to_all | solution.py:123
  357.8 5.2 fusion.163
  362.9 2.8 fusion.162
  365.8 2.9 fusion.161
  371.9 17.1 %all-to-all-done.5 = bf16[32,40,1024]{2,1,0:T(8,128)(2,1)} async-done(((bf16[32,40,1024]{2,1,0:T(8,128)(2,1)}), bf16[32,40,1024]{2,1,0:T(8,128)(2,1)}, u32[]{:S(2)}, u32[]{:S(2)}) %all-to-all-start.5) | async-done | bytes 2621472 | tf_op jit(solution)/shard_map/all_to_all | solution.py:123
  393.7 3.1 fusion.35
  404.2 4.0 multiply_reduce_fusion.3
  410.3 2.4 convolution_convert_fusion
  412.6 4.6 fusion.91
  426.5 6.7 all-to-all-start.6
  433.2 3.9 fusion.79
  437.9 14.9 %concatenate.148 = f32[64,2,8,3200]{3,2,1,0:T(8,128)} concatenate(f32[64,2,8,2048]{3,2,1,0:T(8,128)} %bitcast.344, f32[64,2,8,1024]{3,2,1,0:T(8,128)} %fusion.79, f32[64,2,8,32]{3,2,1,0:T(8,128)} %bitcast.369, f32[64,2,8,1]{3,2,1,0:T(8,128)} %concatenate.153, f32[64,2,8,1]{3,2,1,0:T(8,128)} %concatenate.154, f32[64,2,8,94]{3,2,1,0:T(8,128)} %concatenate.142), dimensions={3} | concatenate | bytes 26214400 | tf_op jit(solution)/shard_map/concatenate | solution.py:465
  452.9 4.9 dynamic-slice_convert_fusion
  467.0 5.0 collective-permute-done.22
  472.9 4.8 collective-permute-done.18
  477.7 5.5 collective-permute-done.16
  484.1 5.9 multiply_convert_fusion
  491.6 3.0 add_convert_fusion.1
  494.6 9.1 %all-to-all-start.7 = ((bf16[32,40,1024]{2,1,0:T(8,128)(2,1)}), bf16[32,40,1024]{2,1,0:T(8,128)(2,1)S(1)}, u32[]{:S(2)}, u32[]{:S(2)}) async-start(bf16[32,40,1024]{2,1,0:T(8,128)(2,1)} %bitcast.75), calls=%async_computation.7 | async-start | bytes 5242880 | tf_op jit(solution)/shard_map/all_to_all | solution.py:123
  505.9 4.8 fusion.167
  510.7 2.9 fusion.166
  513.6 2.8 fusion.165
  516.4 6.1 fusion.6
  522.5 15.3 %all-to-all-done.7 = bf16[32,40,1024]{2,1,0:T(8,128)(2,1)S(1)} async-done(((bf16[32,40,1024]{2,1,0:T(8,128)(2,1)}), bf16[32,40,1024]{2,1,0:T(8,128)(2,1)S(1)}, u32[]{:S(2)}, u32[]{:S(2)}) %all-to-all-start.7) | async-done | bytes 2621472 | tf_op jit(solution)/shard_map/all_to_all | solution.py:123
  539.2 7.1 %all-to-all-start.9 = ((bf16[64,8,3200]{2,1,0:T(8,128)(2,1)}), bf16[64,8,3200]{2,1,0:T(8,128)(2,1)S(1)}, u32[]{:S(2)}, u32[]{:S(2)}) async-start(bf16[64,8,3200]{2,1,0:T(8,128)(2,1)} %fusion.6), calls=%async_computation.9 | async-start | bytes 6553600 | tf_op jit(solution)/shard_map/all_to_all | solution.py:150
  552.4 2.5 fusion.43
  558.0 4.7 fusion.89
  574.5 10.4 %concatenate.143 = f32[64,2,8,2176]{3,2,1,0:T(8,128)} concatenate(f32[64,2,8,2048]{3,2,1,0:T(8,128)} %bitcast.345, f32[64,2,8,32]{3,2,1,0:T(8,128)} %bitcast.368, f32[64,2,8,1]{3,2,1,0:T(8,128)} %concatenate.151, f32[64,2,8,1]{3,2,1,0:T(8,128)} %concatenate.152, f32[64,2,8,94]{3,2,1,0:T(8,128)} %concatenate.142), dimensions={3} | concatenate | bytes 17825792 | tf_op jit(solution)/shard_map/concatenate | solution.py:470
  584.9 4.0 dynamic-slice_convert_fusion.1
  603.6 4.7 collective-permute-done.14
  610.6 10.5 %all-to-all-start.10 = ((bf16[64,8,1024]{2,1,0:T(8,128)(2,1)}), bf16[64,8,1024]{2,1,0:T(8,128)(2,1)}, u32[]{:S(2)}, u32[]{:S(2)}) async-start(bf16[64,8,1024]{2,1,0:T(8,128)(2,1)} %fusion.47), calls=%async_computation.10 | async-start | bytes 2097152 | tf_op jit(solution)/shard_map/all_to_all | solution.py:150
  623.0 4.7 fusion.12
  627.7 8.8 %all-to-all-done.10 = bf16[64,8,1024]{2,1,0:T(8,128)(2,1)} async-done(((bf16[64,8,1024]{2,1,0:T(8,128)(2,1)}), bf16[64,8,1024]{2,1,0:T(8,128)(2,1)}, u32[]{:S(2)}, u32[]{:S(2)}) %all-to-all-start.10) | async-done | bytes 1048608 | tf_op jit(solution)/shard_map/all_to_all | solution.py:150
  636.6 6.6 all-to-all-start.8
  651.1 20.1 %all-to-all-done.8 = bf16[64,8,2176]{2,1,0:T(8,128)(2,1)} async-done(((bf16[64,8,2176]{2,1,0:T(8,128)(2,1)}), bf16[64,8,2176]{2,1,0:T(8,128)(2,1)}, u32[]{:S(2)}, u32[]{:S(2)}) %all-to-all-start.8) | async-done | bytes 2228256 | tf_op jit(solution)/shard_map/all_to_all | solution.py:150
  (456 shorter events, 146.7 us)
Async XLA Ops:
  7.2 7.4 %copy-start.66 = (bf16[2,128,1024]{2,1,0:T(8,128)(2,1)S(1)}, bf16[2,128,1024]{2,1,0:T(8,128)(2,1)}, u32[]{:S(2)}) copy-start(bf16[2,128,1024]{2,1,0:T(8,128)(2,1)} %param.23) | copy-start | bytes 1572868
  7.2 74.5 %all-gather.3.cloned.1.call-start = ((), (), s32[]{:S(2)}) async-start(), calls=%async_computation.11 | async-start | bytes 6604800 | tf_op jit(solution)/shard_map/all_gather | solution.py:37
  11.1 194.7 %all-gather.5.cloned.1.call-start = ((), (), s32[]{:S(2)}) async-start(), calls=%async_computation.12 | async-start | bytes 6604800 | tf_op jit(solution)/shard_map/all_gather | solution.py:37
  12.5 14.9 %collective-permute-start.4 = (bf16[128,2048]{1,0:T(8,128)(2,1)S(1)}, bf16[128,2048]{1,0:T(8,128)(2,1)S(1)}, u32[]{:S(2)}, u32[]{:S(2)}) collective-permute-start(bf16[128,2048]{1,0:T(8,128)(2,1)S(1)} %get-tuple-element.80), channel_id=1, source_target_pairs={{0,2},{2,0},{1,3},{3,1},{4,6},{6,4},{5,7},{7,5},{8,10},{10,8},{9,1... | collective-permute-start | bytes 1572872 | tf_op jit(solution)/shard_map/ppermute | solution.py:129
  14.5 31.1 %collective-permute-start = (bf16[128,2048]{1,0:T(8,128)(2,1)S(1)}, bf16[128,2048]{1,0:T(8,128)(2,1)S(1)}, u32[]{:S(2)}, u32[]{:S(2)}) collective-permute-start(bf16[128,2048]{1,0:T(8,128)(2,1)S(1)} %get-tuple-element.81), channel_id=1, source_target_pairs={{0,2},{2,0},{1,3},{3,1},{4,6},{6,4},{5,7},{7,5},{8,10},{10,8},{9,1... | collective-permute-start | bytes 1572872 | tf_op jit(solution)/shard_map/ppermute | solution.py:129
  14.6 30.1 %collective-permute-start.6 = (bf16[128,1024]{1,0:T(8,128)(2,1)S(1)}, bf16[128,1024]{1,0:T(8,128)(2,1)S(1)}, u32[]{:S(2)}, u32[]{:S(2)}) collective-permute-start(bf16[128,1024]{1,0:T(8,128)(2,1)S(1)} %get-tuple-element.90), channel_id=1, source_target_pairs={{0,2},{2,0},{1,3},{3,1},{4,6},{6,4},{5,7},{7,5},{8,10},{10,8},{9,1... | collective-permute-start | bytes 786440 | tf_op jit(solution)/shard_map/ppermute | solution.py:129
  16.6 33.5 %collective-permute-start.2 = (bf16[128,1024]{1,0:T(8,128)(2,1)S(1)}, bf16[128,1024]{1,0:T(8,128)(2,1)S(1)}, u32[]{:S(2)}, u32[]{:S(2)}) collective-permute-start(bf16[128,1024]{1,0:T(8,128)(2,1)S(1)} %get-tuple-element.91), channel_id=1, source_target_pairs={{0,2},{2,0},{1,3},{3,1},{4,6},{6,4},{5,7},{7,5},{8,10},{10,8},{9,1... | collective-permute-start | bytes 786440 | tf_op jit(solution)/shard_map/ppermute | solution.py:129
  28.4 27.0 %collective-permute-start.5 = (bf16[256,2048]{1,0:T(8,128)(2,1)}, bf16[256,2048]{1,0:T(8,128)(2,1)}, u32[]{:S(2)}, u32[]{:S(2)}) collective-permute-start(bf16[256,2048]{1,0:T(8,128)(2,1)} %pad_maximum_fusion.5), channel_id=1, source_target_pairs={{0,1},{1,0},{2,3},{3,2},{4,5},{5,4},{6,7},{7,6},{8,9},{9,8},{10,11... | collective-permute-start | bytes 3145736 | tf_op jit(solution)/shard_map/ppermute | solution.py:130
  45.6 5.4 collective-permute-start.7
  46.6 11.4 %collective-permute-start.1 = (bf16[256,2048]{1,0:T(8,128)(2,1)}, bf16[256,2048]{1,0:T(8,128)(2,1)}, u32[]{:S(2)}, u32[]{:S(2)}) collective-permute-start(bf16[256,2048]{1,0:T(8,128)(2,1)} %pad_maximum_fusion.3), channel_id=1, source_target_pairs={{0,1},{1,0},{2,3},{3,2},{4,5},{5,4},{6,7},{7,6},{8,9},{9,8},{10,11... | collective-permute-start | bytes 3145736 | tf_op jit(solution)/shard_map/ppermute | solution.py:130
  50.9 2.3 collective-permute-start.3
  86.7 21.6 %copy-start.6 = (bf16[1024,1024]{1,0:T(8,128)(2,1)}, bf16[1024,1024]{1,0:T(8,128)(2,1)S(1)}, u32[]{:S(2)}) copy-start(bf16[1024,1024]{1,0:T(8,128)(2,1)S(1)} %split.41) | copy-start | bytes 6291460
  86.7 6.5 copy-start.112
  86.7 7.2 %copy-start.113 = (s32[512]{0:T(512)S(1)}, s32[512]{0:T(512)}, u32[]{:S(2)}) copy-start(s32[512]{0:T(512)} %param.14) | copy-start | bytes 6148
  86.7 7.7 %copy-start.109 = (s32[128,8]{0,1:T(8,128)S(1)}, s32[128,8]{0,1:T(8,128)}, u32[]{:S(2)}) copy-start(s32[128,8]{0,1:T(8,128)} %param.16) | copy-start | bytes 12292
  86.8 7.7 %copy-start.18 = (bf16[128,1024]{1,0:T(8,128)(2,1)S(1)}, bf16[128,1024]{1,0:T(8,128)(2,1)}, u32[]{:S(2)}) copy-start(bf16[128,1024]{1,0:T(8,128)(2,1)} %param.12) | copy-start | bytes 786436
  95.9 307.9 %copy-start.52 = (f32[128,32]{0,1:T(8,128)}, f32[128,32]{0,1:T(8,128)S(1)}, u32[]{:S(2)}) copy-start(f32[128,32]{0,1:T(8,128)S(1)} %get-tuple-element.107) | copy-start | bytes 49156
  100.3 8.6 %copy-start.86 = (f32[1024]{0:T(1024)}, f32[1024]{0:T(1024)S(1)}, u32[]{:S(2)}) copy-start(f32[1024]{0:T(1024)S(1)} %convert_element_type.394) | copy-start | bytes 12292
  108.9 94.4 %copy-start.9 = (f32[128,1024]{1,0:T(8,128)}, f32[128,1024]{1,0:T(8,128)S(1)}, u32[]{:S(2)}) copy-start(f32[128,1024]{1,0:T(8,128)S(1)} %get-tuple-element.118) | copy-start | bytes 1572868
  108.9 44.8 %copy-start.107 = (f32[128]{0:T(128)}, f32[128]{0:T(128)S(1)}, u32[]{:S(2)}) copy-start(f32[128]{0:T(128)S(1)} %add_rsqrt_fusion.2) | copy-start | bytes 1540
  109.1 44.6 %copy-start.36 = (bf16[128,1024]{1,0:T(8,128)(2,1)}, bf16[128,1024]{1,0:T(8,128)(2,1)S(1)}, u32[]{:S(2)}) copy-start(bf16[128,1024]{1,0:T(8,128)(2,1)S(1)} %multiply_convert_fusion.10) | copy-start | bytes 786436
  110.0 43.7 %copy-start.30 = (bf16[512,2048]{1,0:T(8,128)(2,1)S(1)}, bf16[512,2048]{1,0:T(8,128)(2,1)}, u32[]{:S(2)}) copy-start(bf16[512,2048]{1,0:T(8,128)(2,1)} %pad_maximum_fusion) | copy-start | bytes 6291460
  161.7 41.7 %all-to-all-start.1 = ((bf16[32,40,1024]{2,1,0:T(8,128)(2,1)}), bf16[32,40,1024]{2,1,0:T(8,128)(2,1)S(1)}, u32[]{:S(2)}, u32[]{:S(2)}) async-start(bf16[32,40,1024]{2,1,0:T(8,128)(2,1)} %bitcast.364), calls=%async_computation.1 | async-start | bytes 5242880 | tf_op jit(solution)/shard_map/all_to_all | solution.py:123
  169.4 36.4 %copy-start.98 = (f32[128]{0:T(128)}, f32[128]{0:T(128)S(1)}, u32[]{:S(2)}) copy-start(f32[128]{0:T(128)S(1)} %fusion.120) | copy-start | bytes 1540
  203.3 7.3 %copy-start.4 = (bf16[32,40,1024]{2,1,0:T(8,128)(2,1)}, bf16[32,40,1024]{2,1,0:T(8,128)(2,1)S(1)}, u32[]{:S(2)}) copy-start(bf16[32,40,1024]{2,1,0:T(8,128)(2,1)S(1)} %all-to-all-done.1) | copy-start | bytes 7864324
  213.9 5.5 copy-start.49
  219.4 41.4 %all-to-all-start.2 = ((bf16[32,40,1024]{2,1,0:T(8,128)(2,1)}), bf16[32,40,1024]{2,1,0:T(8,128)(2,1)S(1)}, u32[]{:S(2)}, u32[]{:S(2)}) async-start(bf16[32,40,1024]{2,1,0:T(8,128)(2,1)} %bitcast.361), calls=%async_computation.2 | async-start | bytes 5242880 | tf_op jit(solution)/shard_map/all_to_all | solution.py:123
  229.1 140.6 %copy-start.90 = (f32[128]{0:T(128)}, f32[128]{0:T(128)S(1)}, u32[]{:S(2)}) copy-start(f32[128]{0:T(128)S(1)} %get-tuple-element.129) | copy-start | bytes 1540
  229.1 140.6 %copy-start.100 = (f32[128]{0:T(128)}, f32[128]{0:T(128)S(1)}, u32[]{:S(2)}) copy-start(f32[128]{0:T(128)S(1)} %fusion.122) | copy-start | bytes 1540
  260.8 11.3 %copy-start.2 = (bf16[32,40,1024]{2,1,0:T(8,128)(2,1)}, bf16[32,40,1024]{2,1,0:T(8,128)(2,1)S(1)}, u32[]{:S(2)}) copy-start(bf16[32,40,1024]{2,1,0:T(8,128)(2,1)S(1)} %all-to-all-done.2) | copy-start | bytes 7864324
  260.8 39.6 %all-to-all-start.4 = ((bf16[32,40,1024]{2,1,0:T(8,128)(2,1)}), bf16[32,40,1024]{2,1,0:T(8,128)(2,1)}, u32[]{:S(2)}, u32[]{:S(2)}) async-start(bf16[32,40,1024]{2,1,0:T(8,128)(2,1)} %bitcast.362), calls=%async_computation.4 | async-start | bytes 5242880 | tf_op jit(solution)/shard_map/all_to_all | solution.py:123
  300.4 7.8 %copy-start.63 = (bf16[512,1024]{1,0:T(8,128)(2,1)S(1)}, bf16[512,1024]{1,0:T(8,128)(2,1)}, u32[]{:S(2)}) copy-start(bf16[512,1024]{1,0:T(8,128)(2,1)} %pad_maximum_fusion.6) | copy-start | bytes 3145732
  311.2 38.8 %all-to-all-start.3 = ((bf16[32,40,1024]{2,1,0:T(8,128)(2,1)}), bf16[32,40,1024]{2,1,0:T(8,128)(2,1)S(1)}, u32[]{:S(2)}, u32[]{:S(2)}) async-start(bf16[32,40,1024]{2,1,0:T(8,128)(2,1)} %bitcast.365), calls=%async_computation.3 | async-start | bytes 5242880 | tf_op jit(solution)/shard_map/all_to_all | solution.py:123
  350.0 39.0 %all-to-all-start.5 = ((bf16[32,40,1024]{2,1,0:T(8,128)(2,1)}), bf16[32,40,1024]{2,1,0:T(8,128)(2,1)}, u32[]{:S(2)}, u32[]{:S(2)}) async-start(bf16[32,40,1024]{2,1,0:T(8,128)(2,1)} %bitcast.358), calls=%async_computation.5 | async-start | bytes 5242880 | tf_op jit(solution)/shard_map/all_to_all | solution.py:123
  357.7 5.2 copy-start.3
  357.8 5.2 copy-start.27
  371.9 20.8 %copy-start.102 = (f32[128]{0:T(128)S(1)}, f32[128]{0:T(128)}, u32[]{:S(2)}) copy-start(f32[128]{0:T(128)} %copy-done.101) | copy-start | bytes 1540
  392.7 5.9 copy-start.94
  424.9 35.8 %collective-permute-start.21 = (bf16[256,1024]{1,0:T(8,128)(2,1)}, bf16[256,1024]{1,0:T(8,128)(2,1)}, u32[]{:S(2)}, u32[]{:S(2)}) collective-permute-start(bf16[256,1024]{1,0:T(8,128)(2,1)} %slice.478), channel_id=1, source_target_pairs={{0,1},{1,0},{2,3},{3,2},{4,5},{5,4},{6,7},{7,6},{8,9},{9,8},{10,11... | collective-permute-start | bytes 1572872 | tf_op jit(solution)/shard_map/ppermute | solution.py:137
  424.9 37.4 %collective-permute-start.17 = (bf16[256,1024]{1,0:T(8,128)(2,1)}, bf16[256,1024]{1,0:T(8,128)(2,1)}, u32[]{:S(2)}, u32[]{:S(2)}) collective-permute-start(bf16[256,1024]{1,0:T(8,128)(2,1)} %slice.480), channel_id=1, source_target_pairs={{0,1},{1,0},{2,3},{3,2},{4,5},{5,4},{6,7},{7,6},{8,9},{9,8},{10,11... | collective-permute-start | bytes 1572872 | tf_op jit(solution)/shard_map/ppermute | solution.py:137
  425.4 40.2 %collective-permute-start.15 = (bf16[256,1024]{1,0:T(8,128)(2,1)}, bf16[256,1024]{1,0:T(8,128)(2,1)}, u32[]{:S(2)}, u32[]{:S(2)}) collective-permute-start(bf16[256,1024]{1,0:T(8,128)(2,1)} %slice.481), channel_id=1, source_target_pairs={{0,1},{1,0},{2,3},{3,2},{4,5},{5,4},{6,7},{7,6},{8,9},{9,8},{10,11... | collective-permute-start | bytes 1572872 | tf_op jit(solution)/shard_map/ppermute | solution.py:137
  426.5 57.6 %all-to-all-start.6 = ((bf16[32,40,1024]{2,1,0:T(8,128)(2,1)}), bf16[32,40,1024]{2,1,0:T(8,128)(2,1)}, u32[]{:S(2)}, u32[]{:S(2)}) async-start(bf16[32,40,1024]{2,1,0:T(8,128)(2,1)} %bitcast.359), calls=%async_computation.6 | async-start | bytes 5242880 | tf_op jit(solution)/shard_map/all_to_all | solution.py:123
  452.9 4.9 copy-start.45
  452.9 4.9 copy-start.99
  452.9 5.6 copy-start.43
  458.3 58.1 %collective-permute-start.9 = (bf16[64,1,8,3200]{3,2,1,0:T(8,128)(2,1)}, bf16[64,1,8,3200]{3,2,1,0:T(8,128)(2,1)}, u32[]{:S(2)}, u32[]{:S(2)}) collective-permute-start(bf16[64,1,8,3200]{3,2,1,0:T(8,128)(2,1)} %dynamic-slice_convert_fusion), channel_id=1, source_target_pairs={{0,1},{1,0},{2,3},{3,2},{4,5},{5,4},{6,7},{7,6},{8,9},{9,8},{10,11... | collective-permute-start | bytes 9830408 | tf_op jit(solution)/shard_map/ppermute | solution.py:148
  462.2 9.9 %collective-permute-start.22 = (bf16[128,1024]{1,0:T(8,128)(2,1)S(1)}, bf16[128,1024]{1,0:T(8,128)(2,1)S(1)}, u32[]{:S(2)}, u32[]{:S(2)}) collective-permute-start(bf16[128,1024]{1,0:T(8,128)(2,1)S(1)} %slice.484), channel_id=1, source_target_pairs={{0,2},{2,0},{1,3},{3,1},{4,6},{6,4},{5,7},{7,5},{8,10},{10,8},{9,1... | collective-permute-start | bytes 786440 | tf_op jit(solution)/shard_map/ppermute | solution.py:139
  463.5 14.1 %collective-permute-start.18 = (bf16[128,1024]{1,0:T(8,128)(2,1)S(1)}, bf16[128,1024]{1,0:T(8,128)(2,1)S(1)}, u32[]{:S(2)}, u32[]{:S(2)}) collective-permute-start(bf16[128,1024]{1,0:T(8,128)(2,1)S(1)} %slice.486), channel_id=1, source_target_pairs={{0,2},{2,0},{1,3},{3,1},{4,6},{6,4},{5,7},{7,5},{8,10},{10,8},{9,1... | collective-permute-start | bytes 786440 | tf_op jit(solution)/shard_map/ppermute | solution.py:139
  466.9 17.3 %copy-start.61 = (bf16[512,1024]{1,0:T(8,128)(2,1)S(1)}, bf16[512,1024]{1,0:T(8,128)(2,1)}, u32[]{:S(2)}) copy-start(bf16[512,1024]{1,0:T(8,128)(2,1)} %pad_maximum_fusion.4) | copy-start | bytes 3145732
  466.9 16.3 %collective-permute-start.16 = (bf16[128,1024]{1,0:T(8,128)(2,1)S(1)}, bf16[128,1024]{1,0:T(8,128)(2,1)S(1)}, u32[]{:S(2)}, u32[]{:S(2)}) collective-permute-start(bf16[128,1024]{1,0:T(8,128)(2,1)S(1)} %slice.487), channel_id=1, source_target_pairs={{0,2},{2,0},{1,3},{3,1},{4,6},{6,4},{5,7},{7,5},{8,10},{10,8},{9,1... | collective-permute-start | bytes 786440 | tf_op jit(solution)/shard_map/ppermute | solution.py:139
  484.1 5.9 copy-start.31
  494.6 43.2 %all-to-all-start.7 = ((bf16[32,40,1024]{2,1,0:T(8,128)(2,1)}), bf16[32,40,1024]{2,1,0:T(8,128)(2,1)S(1)}, u32[]{:S(2)}, u32[]{:S(2)}) async-start(bf16[32,40,1024]{2,1,0:T(8,128)(2,1)} %bitcast.75), calls=%async_computation.7 | async-start | bytes 5242880 | tf_op jit(solution)/shard_map/all_to_all | solution.py:123
  539.2 71.3 %all-to-all-start.9 = ((bf16[64,8,3200]{2,1,0:T(8,128)(2,1)}), bf16[64,8,3200]{2,1,0:T(8,128)(2,1)S(1)}, u32[]{:S(2)}, u32[]{:S(2)}) async-start(bf16[64,8,3200]{2,1,0:T(8,128)(2,1)} %fusion.6), calls=%async_computation.9 | async-start | bytes 6553600 | tf_op jit(solution)/shard_map/all_to_all | solution.py:150
  572.6 18.8 %collective-permute-start.19 = (bf16[256,1024]{1,0:T(8,128)(2,1)}, bf16[256,1024]{1,0:T(8,128)(2,1)}, u32[]{:S(2)}, u32[]{:S(2)}) collective-permute-start(bf16[256,1024]{1,0:T(8,128)(2,1)} %slice.479), channel_id=1, source_target_pairs={{0,1},{1,0},{2,3},{3,2},{4,5},{5,4},{6,7},{7,6},{8,9},{9,8},{10,11... | collective-permute-start | bytes 1572872 | tf_op jit(solution)/shard_map/ppermute | solution.py:137
  572.6 22.4 %collective-permute-start.13 = (bf16[256,1024]{1,0:T(8,128)(2,1)}, bf16[256,1024]{1,0:T(8,128)(2,1)}, u32[]{:S(2)}, u32[]{:S(2)}) collective-permute-start(bf16[256,1024]{1,0:T(8,128)(2,1)} %slice.482), channel_id=1, source_target_pairs={{0,1},{1,0},{2,3},{3,2},{4,5},{5,4},{6,7},{7,6},{8,9},{9,8},{10,11... | collective-permute-start | bytes 1572872 | tf_op jit(solution)/shard_map/ppermute | solution.py:137
  573.1 23.7 %collective-permute-start.11 = (bf16[256,1024]{1,0:T(8,128)(2,1)}, bf16[256,1024]{1,0:T(8,128)(2,1)}, u32[]{:S(2)}, u32[]{:S(2)}) collective-permute-start(bf16[256,1024]{1,0:T(8,128)(2,1)} %slice.483), channel_id=1, source_target_pairs={{0,1},{1,0},{2,3},{3,2},{4,5},{5,4},{6,7},{7,6},{8,9},{9,8},{10,11... | collective-permute-start | bytes 1572872 | tf_op jit(solution)/shard_map/ppermute | solution.py:137
  588.9 34.2 %collective-permute-start.8 = (bf16[64,1,8,2176]{3,2,1,0:T(8,128)(2,1)}, bf16[64,1,8,2176]{3,2,1,0:T(8,128)(2,1)}, u32[]{:S(2)}, u32[]{:S(2)}) collective-permute-start(bf16[64,1,8,2176]{3,2,1,0:T(8,128)(2,1)} %dynamic-slice_convert_fusion.1), channel_id=1, source_target_pairs={{0,1},{1,0},{2,3},{3,2},{4,5},{5,4},{6,7},{7,6},{8,9},{9,8},{10,11... | collective-permute-start | bytes 6684680 | tf_op jit(solution)/shard_map/ppermute | solution.py:148
  590.3 18.9 %collective-permute-start.10 = (bf16[64,1,8,1024]{3,2,1,0:T(8,128)(2,1)S(1)}, bf16[64,1,8,1024]{3,2,1,0:T(8,128)(2,1)S(1)}, u32[]{:S(2)}, u32[]{:S(2)}) collective-permute-start(bf16[64,1,8,1024]{3,2,1,0:T(8,128)(2,1)S(1)} %dynamic-slice_convert_fusion.2), channel_id=1, source_target_pairs={{0,1},{1,0},{2,3},{3,2},{4,5},{5,4},{6,7},{7,6},{8,9},{9,8},{10,11... | collective-permute-start | bytes 3145736 | tf_op jit(solution)/shard_map/ppermute | solution.py:148
  591.4 5.4 copy-start.23
  593.4 9.3 %collective-permute-start.20 = (bf16[128,1024]{1,0:T(8,128)(2,1)S(1)}, bf16[128,1024]{1,0:T(8,128)(2,1)S(1)}, u32[]{:S(2)}, u32[]{:S(2)}) collective-permute-start(bf16[128,1024]{1,0:T(8,128)(2,1)S(1)} %slice.485), channel_id=1, source_target_pairs={{0,2},{2,0},{1,3},{3,1},{4,6},{6,4},{5,7},{7,5},{8,10},{10,8},{9,1... | collective-permute-start | bytes 786440 | tf_op jit(solution)/shard_map/ppermute | solution.py:139
  596.2 12.1 %collective-permute-start.14 = (bf16[128,1024]{1,0:T(8,128)(2,1)S(1)}, bf16[128,1024]{1,0:T(8,128)(2,1)S(1)}, u32[]{:S(2)}, u32[]{:S(2)}) collective-permute-start(bf16[128,1024]{1,0:T(8,128)(2,1)S(1)} %slice.488), channel_id=1, source_target_pairs={{0,2},{2,0},{1,3},{3,1},{4,6},{6,4},{5,7},{7,5},{8,10},{10,8},{9,1... | collective-permute-start | bytes 786440 | tf_op jit(solution)/shard_map/ppermute | solution.py:139
  599.8 21.3 %collective-permute-start.12 = (bf16[128,1024]{1,0:T(8,128)(2,1)}, bf16[128,1024]{1,0:T(8,128)(2,1)S(1)}, u32[]{:S(2)}, u32[]{:S(2)}) collective-permute-start(bf16[128,1024]{1,0:T(8,128)(2,1)} %slice.489), channel_id=1, source_target_pairs={{0,2},{2,0},{1,3},{3,1},{4,6},{6,4},{5,7},{7,5},{8,10},{10,8},{9,1... | collective-permute-start | bytes 786440 | tf_op jit(solution)/shard_map/ppermute | solution.py:139
  610.6 26.0 %all-to-all-start.10 = ((bf16[64,8,1024]{2,1,0:T(8,128)(2,1)}), bf16[64,8,1024]{2,1,0:T(8,128)(2,1)}, u32[]{:S(2)}, u32[]{:S(2)}) async-start(bf16[64,8,1024]{2,1,0:T(8,128)(2,1)} %fusion.47), calls=%async_computation.10 | async-start | bytes 2097152 | tf_op jit(solution)/shard_map/all_to_all | solution.py:150
  636.6 34.6 %all-to-all-start.8 = ((bf16[64,8,2176]{2,1,0:T(8,128)(2,1)}), bf16[64,8,2176]{2,1,0:T(8,128)(2,1)}, u32[]{:S(2)}, u32[]{:S(2)}) async-start(bf16[64,8,2176]{2,1,0:T(8,128)(2,1)} %fusion.12), calls=%async_computation.8 | async-start | bytes 4456448 | tf_op jit(solution)/shard_map/all_to_all | solution.py:150
  (86 other events, 200.0 us)
Sparse Core Ops, SparseCore 0:
  11.6 70.0 all-gather.2
  93.4 92.2 all-gather.4

commit v3 on v2

--- a/solution.py
+++ b/solution.py
@@ -26,17 +26,33 @@
 AXES = ("x", "y", "zh", "zl", "c")
 EXPERT_AXES = ("x", "y", "zh")
 CHIP_AXES = ("x", "y", "zh", "zl")
+Z_AXES = ("zh", "zl")
+PLANE_AXES = ("x", "y")
+DENSE_WIDTHS = (2048, 1024, E, 1, 1)
+HALF = MODEL_WIDTH // 2
 SWAP = [(0, 1), (1, 0)]
 
 
-def sent_together(arrays, axis, dim, along):
-    widths = [math.prod(a.shape[along:]) for a in arrays]
-    both = jnp.concatenate(
-        [a.reshape(*a.shape[:along], w) for a, w in zip(arrays, widths)], axis=along
-    )
-    out = lax.all_gather(both, axis, axis=dim, tiled=True)
-    pieces = jnp.split(out, [sum(widths[:k]) for k in range(1, len(widths))], axis=along)
-    return tuple((b.reshape(*out.shape[:along], *a.shape[along:]) for a, b in zip(arrays, pieces)))
+def sent_together(arrays, axis):
+    both = jnp.concatenate([a.reshape(a.shape[0], -1) for a in arrays], axis=1)
+    return lax.all_gather(both, axis, axis=0, tiled=True)
+
+
+def sent_by_chips(own):
+    core = lax.axis_index("c")
+    copies = jnp.broadcast_to(own[None], (64,) + own.shape)
+    mine = lax.all_to_all(copies, CHIP_AXES, split_axis=0, concat_axis=0, tiled=True)
+    other = lax.ppermute(mine, "c", SWAP)
+    pair = [jnp.where(core == 0, mine, other), jnp.where(core == 0, other, mine)]
+    return jnp.stack(pair, axis=1).reshape(MODEL_WIDTH, -1)
+
+
+def cut_weights(gathered, widths):
+    at, pieces = 0, []
+    for width in widths:
+        pieces.append(gathered[:, at : at + width])
+        at += width
+    return tuple(pieces[:-2]) + (pieces[-2][:, 0], pieces[-1][:, 0])
 
 
 def seq_layout(seq_lengths, seq_owner, device):
@@ -139,16 +155,50 @@
     return own + lax.ppermute(other, "zl", SWAP).astype(jnp.float32)
 
 
-def scatter_dense(grad):
-    width = grad.shape[1]
-    core = lax.axis_index("c")
-    blocks = grad.reshape(64, 2, MODEL_WIDTH // 128, width)
-    given = lax.dynamic_slice_in_dim(blocks, 1 - core, 1, axis=1).astype(jnp.bfloat16)
-    kept = lax.dynamic_slice_in_dim(blocks, core, 1, axis=1)
-    kept = kept + lax.ppermute(given, "c", SWAP).astype(jnp.float32)
-    kept = kept.reshape(64, MODEL_WIDTH // 128, width).astype(jnp.bfloat16)
-    parts = lax.all_to_all(kept, CHIP_AXES, split_axis=0, concat_axis=0, tiled=True)
+def order_table():
+    at = jnp.arange(MODEL_WIDTH, dtype=jnp.int32)
+    core = (at // HALF + lax.axis_index("c")) % 2
+    depth, plane, row = at // 128 % 4, at // 8 % 16, at % 8
+    source = (plane * 4 + depth) * 16 + core * 8 + row
+    return (at[:, None] == source[None, :]).astype(jnp.bfloat16)
+
+
+def reorder(values, order):
+    return jnp.dot(values, order, preferred_element_type=jnp.float32).astype(jnp.bfloat16)
+
+
+def weight_halves(left, right):
+    pair = (((0,), (0,)), ((), ()))
+    kept = lax.dot_general(left[:, :HALF], right, pair, preferred_element_type=jnp.float32)
+    given = lax.dot_general(left[:, HALF:], right, pair, preferred_element_type=jnp.float32)
+    return kept, given.astype(jnp.bfloat16)
+
+
+def small_halves(router_grad, gain_one_grad, gain_two_grad, order):
+    fill = jnp.zeros((MODEL_WIDTH, 128 - E - 2), jnp.float32)
+    small = jnp.concatenate(
+        [router_grad, gain_one_grad[:, None], gain_two_grad[:, None], fill], axis=1
+    ).astype(jnp.bfloat16)
+    moved = lax.dot_general(
+        order, small, (((0,), (0,)), ((), ())), preferred_element_type=jnp.float32
+    )
+    return moved[:HALF], moved[HALF:].astype(jnp.bfloat16)
+
+
+def core_sum(halves):
+    kept, given = halves
+    return (kept + lax.ppermute(given, "c", SWAP).astype(jnp.float32)).astype(jnp.bfloat16)
+
+
+def chip_sum(parts):
+    parts = parts.reshape(64, 8, -1)
+    parts = lax.all_to_all(parts, Z_AXES + PLANE_AXES, split_axis=0, concat_axis=0, tiled=True)
     return jnp.sum(parts.astype(jnp.float32), axis=0)
+
+
+def chip_sum_aside(parts):
+    parts = lax.psum_scatter(parts, Z_AXES, scatter_dimension=0, tiled=True)
+    return lax.psum_scatter(parts, PLANE_AXES, scatter_dimension=0, tiled=True).astype(jnp.float32)
 
 
 def norm_back(grad_norm, normed, inverse):
@@ -165,8 +215,7 @@
     return exp_scores / jnp.sum(exp_scores, axis=-1, keepdims=True)
 
 
-def attend_forward(hidden, weights, live, allowed, cosine_table, sine_values):
-    qkv_full, out_full, router_full, gain_one, gain_two = weights
+def attend_forward(hidden, qkv_full, gain_one, live, allowed, cosine_table, sine_values):
     token_total = hidden.shape[0]
     query_width = QUERY_HEADS * HEAD_SIZE
     key_value_width = KEY_VALUE_HEADS * HEAD_SIZE
@@ -202,11 +251,7 @@
         preferred_element_type=jnp.float32,
     )
     mixed_low = (mixed.reshape(token_total, query_width) * live[:, None]).astype(jnp.bfloat16)
-    attn_out = jnp.dot(mixed_low, out_full, preferred_element_type=jnp.float32)
-    return (
-        hidden + attn_out,
-        (inverse, normed, normed_low, rotated_query, rotated_key, reduced_value, mixed_low),
-    )
+    return inverse, normed, normed_low, rotated_query, rotated_key, reduced_value, mixed_low
 
 
 def route_rows(hidden, weights, routed, chosen):
@@ -323,16 +368,16 @@
     return grad_h1, gain_two_grad
 
 
-def attend_backward(grad_h1, weights, live, allowed, cosine_table, sine_values, attn_stash):
+def attend_backward(
+    grad_h1, weights, live, allowed, cosine_table, sine_values, attn_stash, attn_moved, mixed_moved
+):
     qkv_full, out_full, router_full, gain_one, gain_two = weights
     inverse, normed, normed_low, rotated_query, rotated_key, reduced_value, mixed_low = attn_stash
     token_total = grad_h1.shape[0]
     query_width = QUERY_HEADS * HEAD_SIZE
     key_value_width = KEY_VALUE_HEADS * HEAD_SIZE
     grad_low = grad_h1.astype(jnp.bfloat16)
-    proj_grad = lax.dot_general(
-        mixed_low, grad_low, (((0,), (0,)), ((), ())), preferred_element_type=jnp.float32
-    )
+    proj_halves = weight_halves(mixed_moved, grad_low)
     mixed_gradient = lax.dot_general(
         grad_low, out_full, (((1,), (1,)), ((), ())), preferred_element_type=jnp.float32
     ).astype(jnp.bfloat16)
@@ -371,15 +416,13 @@
         ],
         axis=1,
     )
-    qkv_grad = lax.dot_general(
-        normed_low, grad_proj, (((0,), (0,)), ((), ())), preferred_element_type=jnp.float32
-    )
+    qkv_halves = weight_halves(attn_moved, grad_proj)
     grad_normed = lax.dot_general(
         grad_proj, qkv_full, (((1,), (1,)), ((), ())), preferred_element_type=jnp.float32
     )
     gain_one_grad = jnp.sum(grad_normed * normed, axis=0)
     grad_input = grad_h1 + norm_back(grad_normed * gain_one.astype(jnp.float32), normed, inverse)
-    return (grad_input, qkv_grad, proj_grad, gain_one_grad)
+    return (grad_input, qkv_halves, proj_halves, gain_one_grad)
 
 
 def on_device(
@@ -399,6 +442,7 @@
     layers = range(LAYER_COUNT)
     last = LAYER_COUNT - 1
     device = lax.axis_index(AXES)
+    order = order_table()
     own_dense = [
         (
             query_key_value_weight[layer],
@@ -409,14 +453,18 @@
         )
         for layer in layers
     ]
+    lead = [own_dense[0][member].reshape(8, -1) for member in (0, 2, 3, 4)]
+    fill = jnp.zeros((8, 128 - E - 2), jnp.bfloat16)
+    lead_first = sent_by_chips(jnp.concatenate(lead + [fill], axis=1))
+    lead_first, out_own, expert_in, expert_out = lax.optimization_barrier(
+        (lead_first, own_dense[0][1], expert_in, expert_out)
+    )
+    lead_first = cut_weights(lead_first, (2048, E, 1, 1))
+    out_first = sent_by_chips(out_own)
+    dense = [(lead_first[0], out_first) + lead_first[1:], None]
     experts = [
         (gather_expert(expert_in[layer]), gather_expert(expert_out[layer])) for layer in layers
     ]
-    dense = []
-    for layer in layers:
-        dense.append(sent_together(own_dense[layer], AXES, 0, 1))
-        if layer == 0:
-            dense[0], experts, own_dense = lax.optimization_barrier((dense[0], experts, own_dense))
     position, live_row, allowed = seq_layout(seq_lengths, seq_owner, device)
     live = live_row.astype(jnp.float32)
     cosine_table, sine_values = rope_tables(position)
@@ -425,63 +473,78 @@
     grad_hidden = cotangent.astype(jnp.float32)
     saved = []
     for layer in layers:
-        hidden, attn_stash = attend_forward(
-            hidden, dense[layer], live, allowed, cosine_table, sine_values
+        attn_stash = attend_forward(
+            hidden, dense[layer][0], dense[layer][3], live, allowed, cosine_table, sine_values
         )
+        mixed_low = attn_stash[-1]
+        hidden = hidden + jnp.dot(mixed_low, dense[layer][1], preferred_element_type=jnp.float32)
         rows, route_stash = route_rows(hidden, dense[layer], routed, chosen)
+        if layer == 0:
+            rows, experts, own_dense = lax.optimization_barrier((rows, experts, own_dense))
+            dense[1] = cut_weights(sent_together(own_dense[1], AXES), DENSE_WIDTHS)
         rows_here = trade_rows(rows)
+        moved = reorder(attn_stash[2], order), reorder(mixed_low, order)
         grad_rows = None
         if layer == last:
             slots = slot_gradients(grad_hidden, route_stash[-1])
             slots, rows_here = lax.optimization_barrier((slots, rows_here))
             grad_rows = trade_rows(slots)
         results, pre = feed_forward(rows_here, *experts[layer])
+        if layer == last:
+            results, grad_rows = lax.optimization_barrier((results, grad_rows))
         returned = trade_rows(results)
         hidden = hidden + jnp.dot(route_stash[-1], returned, preferred_element_type=jnp.float32)
-        saved.append((attn_stash, route_stash, rows_here, pre, returned, grad_rows))
+        saved.append((attn_stash, moved, route_stash, rows_here, pre, returned, grad_rows))
     output_low = hidden.astype(jnp.bfloat16)
     layer_grads = [None] * LAYER_COUNT
+    after = ()
     for layer in reversed(layers):
-        attn_stash, route_stash, rows_here, pre, returned, grad_rows = saved[layer]
+        attn_stash, moved, route_stash, rows_here, pre, returned, grad_rows = saved[layer]
         if grad_rows is None:
-            grad_rows = trade_rows(slot_gradients(grad_hidden, route_stash[-1]))
+            slots = slot_gradients(grad_hidden, route_stash[-1])
+            slots, after = lax.optimization_barrier((slots, after))
+            grad_rows = trade_rows(slots)
         grad_in_rows, expert_grads = feed_backward(grad_rows, rows_here, pre, *experts[layer])
         grad_slots = trade_rows(grad_in_rows)
         router_grad, grad_routed = route_backward(
             grad_hidden, dense[layer], chosen, returned, route_stash
         )
         grad_slots, expert_grads = lax.optimization_barrier((grad_slots, expert_grads))
-        gate_w_grad, up_w_grad, out_grad = [scatter_expert(g) for g in expert_grads]
+        expert_grads = [scatter_expert(g) for g in expert_grads]
         grad_h1, gain_two_grad = rows_backward(
             grad_hidden, dense[layer], chosen, grad_slots, grad_routed, route_stash
         )
-        grad_hidden, qkv_grad, proj_grad, gain_one_grad = attend_backward(
-            grad_h1, dense[layer], live, allowed, cosine_table, sine_values, attn_stash
+        grad_hidden, qkv_halves, proj_halves, gain_one_grad = attend_backward(
+            grad_h1, dense[layer], live, allowed, cosine_table, sine_values, attn_stash, *moved
         )
-        query_width = qkv_grad.shape[1]
-        fill = jnp.zeros((MODEL_WIDTH, 128 - E - 2), jnp.float32)
-        small = [router_grad, gain_one_grad[:, None], gain_two_grad[:, None], fill]
+        small = small_halves(router_grad, gain_one_grad, gain_two_grad, order)
         if layer == last:
-            done = scatter_dense(jnp.concatenate([qkv_grad, proj_grad] + small, axis=1))
-            qkv_done, proj_done = done[:, :query_width], done[:, query_width:-128]
-            small_done = done[:, -128:]
+            after = expert_grads
+            sums = [core_sum(halves) for halves in (qkv_halves, proj_halves, small)]
+            done = chip_sum_aside(jnp.concatenate(sums, axis=1))
+            proj_done, done = done[:, 2048:3072], jnp.concatenate(
+                [done[:, :2048], done[:, 3072:]], axis=1
+            )
         else:
-            proj_done = scatter_dense(proj_grad)
-            done = scatter_dense(jnp.concatenate([qkv_grad] + small, axis=1))
-            qkv_done, small_done = done[:, :query_width], done[:, -128:]
+            proj_done = chip_sum(core_sum(proj_halves))
+            sums = [core_sum(halves) for halves in (qkv_halves, small)]
+            done = chip_sum(jnp.concatenate(sums, axis=1))
+        qkv_done, small_done = done[:, :2048], done[:, 2048:]
         layer_grads[layer] = (
             qkv_done,
             proj_done,
             small_done[:, :E],
             small_done[:, E],
             small_done[:, E + 1],
-            jnp.concatenate([gate_w_grad, up_w_grad], axis=1),
-            out_grad,
+            expert_grads,
         )
-    stacked = tuple(
-        jnp.stack([layer_grads[layer][member] for layer in layers]) for member in range(7)
-    )
-    return (output_low, grad_hidden) + stacked
+    stacked = [
+        jnp.stack([layer_grads[layer][member] for layer in layers]) for member in range(5)
+    ]
+    grads = [layer_grads[0][5], after]
+    stacked.append(jnp.stack([jnp.concatenate(g[:2], axis=1) for g in grads]))
+    stacked.append(jnp.stack([g[2] for g in grads]))
+    return (output_low, grad_hidden) + tuple(stacked)
 
 
 def solution(mesh):

time: 695 us -> 725 us (1.043)
  waiting for transfers between devices: 245 us -> 307 us
  local copies, waits for them, and re-layouts: 84.7 us -> 39.7 us
  matrix products: 143 us -> 152 us
  starting transfers between devices: 89 us -> 96.3 us
    unnamed x2 -> x4, waiting for transfers between devices: 0.03 us -> 81.5 us
    concatenate x9 -> x3, local copies, waits for them, and re-layouts: 32.1 us -> 1.39 us  [the longest x1 0.71 us: sent_together(): both = jnp.concatenate([a.reshape(a.shape[0], -1) for a in arrays], axis=1)]
    all_gather x2 -> x1, waiting for transfers between devices: 20.9 us -> 5.68 us  [sent_together(): return lax.all_gather(both, axis, axis=0, tiled=True)]
    dot_general x6 -> x16, matrix products: 16.7 us -> 30.3 us  [the longest x4 9.58 us: reorder(): jnp.dot(values, order, preferred_element_type=jnp.float32)]
    another operation x12 -> x21, other arithmetic: 1.97 us -> 14.8 us  [the longest x4 4.02 us: sent_by_chips(): return jnp.stack(pair, axis=1).reshape(MODEL_WIDTH, -1)]
    ppermute x4, waiting for transfers between devices: 29.9 us -> 18.3 us  [gather_expert(): pair = jnp.concatenate([own, lax.ppermute(own, 'zl', SWAP)], axis=0)]
    split x4 -> x0, local copies, waits for them, and re-layouts: 10.6 us -> none  [sent_together(): jnp.split(out, [sum(widths[:k]) for k in range(1, len(widths))], axis=along)]
    convert_element_type x4 -> x3, other arithmetic: 12.2 us -> 2.18 us  [the longest x2 1.37 us: core_sum(): (kept + lax.ppermute(given, 'c', SWAP).astype(jnp.float32)).astype(jnp.bf...]
  transfers between devices with their start and end apart: 35 -> 42, of which waited for: 18 -> 18; matrix products, arithmetic and copies ran while one was open for 30% -> 28% of each run, Pallas kernels for 0% -> 0%
where the time goes in v3:
time: 725 us; the launch traced here: 714 us
  waiting for transfers between devices  307 us (42%)
  matrix products  152 us (21%)
  starting transfers between devices  96.3 us (13%)
  other arithmetic  59.3 us (8%)
  blocking collectives  43.1 us (6%)
  local copies, waits for them, and re-layouts  39.7 us (5%)
  between operations  16.7 us (2%)
    all_to_all x7, waiting for transfers between devices, trade_rows(): lax.all_to_all(rows.reshape(E, ROOM, MODEL_WIDTH), EXPERT_AXES, split_axi...  144 us
    unnamed x4, waiting for transfers between devices  81.5 us
    all_to_all x7, starting transfers between devices, trade_rows(): lax.all_to_all(rows.reshape(E, ROOM, MODEL_WIDTH), EXPERT_AXES, split_axi...  50.5 us
    all_to_all x1, blocking collectives, trade_rows(): lax.all_to_all(rows.reshape(E, ROOM, MODEL_WIDTH), EXPERT_AXES, split_axi...  43.1 us
    all_to_all x2, waiting for transfers between devices, sent_by_chips(): lax.all_to_all(copies, CHIP_AXES, split_axis=0, concat_axis=0, tiled=True)  28.5 us
    ppermute x6, waiting for transfers between devices, scatter_expert(): return own + lax.ppermute(other, 'zl', SWAP).astype(jnp.float32)  18.5 us
    all_to_all x2, starting transfers between devices, sent_by_chips(): lax.all_to_all(copies, CHIP_AXES, split_axis=0, concat_axis=0, tiled=True)  18.5 us
    ppermute x4, waiting for transfers between devices, gather_expert(): pair = jnp.concatenate([own, lax.ppermute(own, 'zl', SWAP)], axis=0)  18.3 us
  transfers between devices with their start and end apart: 42, of which 18 were waited for; matrix products, arithmetic and copies ran while one was open for 28% of the time, Pallas kernels for 0%

profile of v3, /device:TPU:2, one launch (start us, length us, event | category | flops | bytes accessed | tf_op | source)
XLA Modules:
  0.0 714.1 jit_solution(13856230768582940120)
XLA Ops:
  11.7 11.6 %all-to-all-start = ((bf16[64,8,2176]{2,1,0:T(8,128)(2,1)}), bf16[64,8,2176]{2,1,0:T(8,128)(2,1)S(1)}, u32[]{:S(2)}, u32[]{:S(2)}) async-start(bf16[64,8,2176]{2,1,0:T(8,128)(2,1)} %broadcast_in_dim.75), calls=%async_computation | async-start | bytes 4456448 | tf_op jit(solution)/shard_map/all_to_all | solution.py:44
  24.5 28.5 %all-to-all-done = bf16[64,8,2176]{2,1,0:T(8,128)(2,1)S(1)} async-done(((bf16[64,8,2176]{2,1,0:T(8,128)(2,1)}), bf16[64,8,2176]{2,1,0:T(8,128)(2,1)S(1)}, u32[]{:S(2)}, u32[]{:S(2)}) %all-to-all-start) | async-done | bytes 2228256 | tf_op jit(solution)/shard_map/all_to_all | solution.py:44
  65.7 6.9 all-to-all-start.1
  85.9 11.8 %collective-permute-done.6 = bf16[128,2048]{1,0:T(8,128)(2,1)} collective-permute-done((bf16[128,2048]{1,0:T(8,128)(2,1)S(1)}, bf16[128,2048]{1,0:T(8,128)(2,1)}, u32[]{:S(2)}, u32[]{:S(2)}) %collective-permute-start.6) | collective-permute-done | bytes 524320 | tf_op jit(solution)/shard_map/ppermute | solution.py:145
  102.1 6.5 collective-permute-done.2
  113.0 2.5 fusion.94
  119.8 2.9 pad_maximum_fusion.4
  122.7 2.9 pad_maximum_fusion.3
  130.6 43.1 %all_to_all.60 = bf16[32,40,1024]{2,1,0:T(8,128)(2,1)S(1)} all-to-all(bf16[32,40,1024]{2,1,0:T(8,128)(2,1)S(1)} %bitcast.356), channel_id=1, replica_groups=mesh['x'=4,'y'=4,'zh'=2,'zl'=2,'c'=2] {'x','y','zh'}, dimensions={0} | all-to-all | bytes 5242880 | tf_op jit(solution)/shard_map/all_to_all | solution.py:139
  175.3 3.4 multiply_convert_fusion.5
  178.7 3.0 convolution_convert_fusion.4
  181.7 6.8 all-to-all-start.3
  190.9 34.0 %all-to-all-done.3 = bf16[32,40,1024]{2,1,0:T(8,128)(2,1)S(1)} async-done(((bf16[32,40,1024]{2,1,0:T(8,128)(2,1)}), bf16[32,40,1024]{2,1,0:T(8,128)(2,1)S(1)}, u32[]{:S(2)}, u32[]{:S(2)}) %all-to-all-start.3) | async-done | bytes 2621472 | tf_op jit(solution)/shard_map/all_to_all | solution.py:139
  224.9 2.5 multiply_reduce_fusion.9
  227.4 5.7 all-gather.2.cloned.1.call-done
  234.5 3.1 fusion.10
  244.8 2.4 convolution_convert_fusion.2
  247.3 8.1 %all-to-all-start.4 = ((bf16[32,40,1024]{2,1,0:T(8,128)(2,1)}), bf16[32,40,1024]{2,1,0:T(8,128)(2,1)S(1)}, u32[]{:S(2)}, u32[]{:S(2)}) async-start(bf16[32,40,1024]{2,1,0:T(8,128)(2,1)} %bitcast.358), calls=%async_computation.4 | async-start | bytes 5242880 | tf_op jit(solution)/shard_map/all_to_all | solution.py:139
  257.7 3.4 convolution_convert_fusion.3
  261.1 28.4 %all-to-all-done.4 = bf16[32,40,1024]{2,1,0:T(8,128)(2,1)S(1)} async-done(((bf16[32,40,1024]{2,1,0:T(8,128)(2,1)}), bf16[32,40,1024]{2,1,0:T(8,128)(2,1)S(1)}, u32[]{:S(2)}, u32[]{:S(2)}) %all-to-all-start.4) | async-done | bytes 2621472 | tf_op jit(solution)/shard_map/all_to_all | solution.py:139
  289.5 7.8 %all-to-all-start.5 = ((bf16[32,40,1024]{2,1,0:T(8,128)(2,1)}), bf16[32,40,1024]{2,1,0:T(8,128)(2,1)}, u32[]{:S(2)}, u32[]{:S(2)}) async-start(bf16[32,40,1024]{2,1,0:T(8,128)(2,1)} %bitcast.357), calls=%async_computation.5 | async-start | bytes 5242880 | tf_op jit(solution)/shard_map/all_to_all | solution.py:139
  297.3 3.0 fusion.71
  300.3 3.5 multiply_convert_fusion.4
  304.9 3.0 convolution_convert_fusion.1
  307.9 22.8 %all-to-all-done.5 = bf16[32,40,1024]{2,1,0:T(8,128)(2,1)} async-done(((bf16[32,40,1024]{2,1,0:T(8,128)(2,1)}), bf16[32,40,1024]{2,1,0:T(8,128)(2,1)}, u32[]{:S(2)}, u32[]{:S(2)}) %all-to-all-start.5) | async-done | bytes 2621472 | tf_op jit(solution)/shard_map/all_to_all | solution.py:139
  330.7 7.0 all-to-all-start.6
  339.6 2.6 fusion.48
  342.2 6.2 multiply_convert_fusion.2
  350.0 3.1 add_convert_fusion.1
  353.1 16.3 %all-to-all-done.6 = bf16[32,40,1024]{2,1,0:T(8,128)(2,1)S(1)} async-done(((bf16[32,40,1024]{2,1,0:T(8,128)(2,1)}), bf16[32,40,1024]{2,1,0:T(8,128)(2,1)S(1)}, u32[]{:S(2)}, u32[]{:S(2)}) %all-to-all-start.6) | async-done | bytes 2621472 | tf_op jit(solution)/shard_map/all_to_all | solution.py:139
  369.4 6.8 all-to-all-start.7
  376.2 2.7 fusion.50
  378.9 2.6 fusion.51
  383.2 4.8 fusion.232
  388.0 2.9 fusion.231
  390.9 2.9 fusion.230
  395.3 12.7 %all-to-all-done.7 = bf16[32,40,1024]{2,1,0:T(8,128)(2,1)} async-done(((bf16[32,40,1024]{2,1,0:T(8,128)(2,1)}), bf16[32,40,1024]{2,1,0:T(8,128)(2,1)}, u32[]{:S(2)}, u32[]{:S(2)}) %all-to-all-start.7) | async-done | bytes 2621472 | tf_op jit(solution)/shard_map/all_to_all | solution.py:139
  408.0 2.3 fusion.233
  412.7 3.1 fusion.53
  417.7 2.4 fusion.60
  426.3 4.4 multiply_reduce_fusion.3
  431.0 2.3 convolution_convert_fusion
  436.9 5.8 collective-permute-done.15
  443.6 4.7 collective-permute-done.13
  449.2 4.3 collective-permute-done.11
  454.3 7.3 %all-to-all-start.8 = ((bf16[32,40,1024]{2,1,0:T(8,128)(2,1)}), bf16[32,40,1024]{2,1,0:T(8,128)(2,1)}, u32[]{:S(2)}, u32[]{:S(2)}) async-start(bf16[32,40,1024]{2,1,0:T(8,128)(2,1)} %bitcast.355), calls=%async_computation.8 | async-start | bytes 5242880 | tf_op jit(solution)/shard_map/all_to_all | solution.py:139
  466.0 2.9 convolution_multiply_fusion
  471.4 2.5 fusion.3
  480.2 15.8 %all-to-all-done.8 = bf16[32,40,1024]{2,1,0:T(8,128)(2,1)} async-done(((bf16[32,40,1024]{2,1,0:T(8,128)(2,1)}), bf16[32,40,1024]{2,1,0:T(8,128)(2,1)}, u32[]{:S(2)}, u32[]{:S(2)}) %all-to-all-start.8) | async-done | bytes 2621472 | tf_op jit(solution)/shard_map/all_to_all | solution.py:139
  496.0 6.2 multiply_convert_fusion
  503.7 3.0 add_convert_fusion
  506.7 6.8 all-to-all-start.9
  516.6 2.4 add_convert_fusion.2
  522.1 4.8 fusion.236
  526.9 2.9 fusion.235
  529.9 2.9 fusion.234
  532.7 14.3 %all-to-all-done.9 = bf16[32,40,1024]{2,1,0:T(8,128)(2,1)} async-done(((bf16[32,40,1024]{2,1,0:T(8,128)(2,1)}), bf16[32,40,1024]{2,1,0:T(8,128)(2,1)}, u32[]{:S(2)}, u32[]{:S(2)}) %all-to-all-start.9) | async-done | bytes 2621472 | tf_op jit(solution)/shard_map/all_to_all | solution.py:139
  562.9 3.9 fusion.89
  580.7 3.7 collective-permute-done.27
  586.7 7.0 all-to-all-start.11
  597.4 2.4 add_convert_fusion.3
  601.5 8.5 %all-to-all-done.11 = bf16[64,8,1024]{2,1,0:T(8,128)(2,1)S(1)} async-done(((bf16[64,8,1024]{2,1,0:T(8,128)(2,1)}), bf16[64,8,1024]{2,1,0:T(8,128)(2,1)S(1)}, u32[]{:S(2)}, u32[]{:S(2)}) %all-to-all-start.11) | async-done | bytes 1048608 | tf_op jit(solution)/shard_map/all_to_all | solution.py:195
  610.1 5.8 all-to-all-start.10
  621.2 81.5 %all-reduce.3.cloned.1.call-done = bf16[128,3200]{1,0:T(8,128)(2,1)} async-done(((bf16[128,3200]{1,0:T(8,128)(2,1)}), bf16[128,3200]{1,0:T(8,128)(2,1)}) %all-reduce.3.cloned.1.call-update) | async-done | bytes 819216
  (515 shorter events, 155.1 us)
Async XLA Ops:
  11.7 11.7 %copy-start.116 = (s32[512]{0:T(512)S(1)}, s32[512]{0:T(512)}, u32[]{:S(2)}) copy-start(s32[512]{0:T(512)} %param.15) | copy-start | bytes 6148
  11.7 12.3 %copy-start.117 = (s32[512]{0:T(512)S(1)}, s32[512]{0:T(512)}, u32[]{:S(2)}) copy-start(s32[512]{0:T(512)} %param.14) | copy-start | bytes 6148
  11.7 41.4 %copy-start.112 = (s32[128,8]{0,1:T(8,128)S(1)}, s32[128,8]{0,1:T(8,128)}, u32[]{:S(2)}) copy-start(s32[128,8]{0,1:T(8,128)} %param.16) | copy-start | bytes 12292
  11.7 41.4 %copy-start.43 = (bf16[128,1024]{1,0:T(8,128)(2,1)S(1)}, bf16[128,1024]{1,0:T(8,128)(2,1)}, u32[]{:S(2)}) copy-start(bf16[128,1024]{1,0:T(8,128)(2,1)} %param.12) | copy-start | bytes 786436
  11.7 42.9 %copy-start.101 = (bf16[2,8,1024]{2,1,0:T(8,128)(2,1)S(1)}, bf16[2,8,1024]{2,1,0:T(8,128)(2,1)}, u32[]{:S(2)}) copy-start(bf16[2,8,1024]{2,1,0:T(8,128)(2,1)} %param.18) | copy-start | bytes 98308
  11.7 41.2 %all-to-all-start = ((bf16[64,8,2176]{2,1,0:T(8,128)(2,1)}), bf16[64,8,2176]{2,1,0:T(8,128)(2,1)S(1)}, u32[]{:S(2)}, u32[]{:S(2)}) async-start(bf16[64,8,2176]{2,1,0:T(8,128)(2,1)} %broadcast_in_dim.75), calls=%async_computation | async-start | bytes 4456448 | tf_op jit(solution)/shard_map/all_to_all | solution.py:44
  53.0 4.5 collective-permute-start
  60.6 23.5 %collective-permute-start.8 = (bf16[128,1024]{1,0:T(8,128)(2,1)S(1)}, bf16[128,1024]{1,0:T(8,128)(2,1)}, u32[]{:S(2)}, u32[]{:S(2)}) collective-permute-start(bf16[128,1024]{1,0:T(8,128)(2,1)S(1)} %get-tuple-element.105), channel_id=1, source_target_pairs={{0,2},{2,0},{1,3},{3,1},{4,6},{6,4},{5,7},{7,5},{8,10},{10,8},{9,1... | collective-permute-start | bytes 786440 | tf_op jit(solution)/shard_map/ppermute | solution.py:145
  61.4 38.4 %collective-permute-start.4 = (bf16[128,1024]{1,0:T(8,128)(2,1)S(1)}, bf16[128,1024]{1,0:T(8,128)(2,1)}, u32[]{:S(2)}, u32[]{:S(2)}) collective-permute-start(bf16[128,1024]{1,0:T(8,128)(2,1)S(1)} %get-tuple-element.106), channel_id=1, source_target_pairs={{0,2},{2,0},{1,3},{3,1},{4,6},{6,4},{5,7},{7,5},{8,10},{10,8},{9,1... | collective-permute-start | bytes 786440 | tf_op jit(solution)/shard_map/ppermute | solution.py:145
  65.7 46.5 %all-to-all-start.1 = ((bf16[64,8,1024]{2,1,0:T(8,128)(2,1)}), bf16[64,8,1024]{2,1,0:T(8,128)(2,1)S(1)}, u32[]{:S(2)}, u32[]{:S(2)}) async-start(bf16[64,8,1024]{2,1,0:T(8,128)(2,1)} %broadcast_in_dim.80), calls=%async_computation.1 | async-start | bytes 2097152 | tf_op jit(solution)/shard_map/all_to_all | solution.py:44
  72.6 160.5 %all-gather.2.cloned.1.call-start = ((), (), s32[]{:S(2)}) async-start(), calls=%async_computation.13 | async-start | bytes 6604800 | tf_op jit(solution)/shard_map/all_gather | solution.py:38
  73.9 23.8 %collective-permute-start.6 = (bf16[128,2048]{1,0:T(8,128)(2,1)S(1)}, bf16[128,2048]{1,0:T(8,128)(2,1)}, u32[]{:S(2)}, u32[]{:S(2)}) collective-permute-start(bf16[128,2048]{1,0:T(8,128)(2,1)S(1)} %get-tuple-element.95), channel_id=1, source_target_pairs={{0,2},{2,0},{1,3},{3,1},{4,6},{6,4},{5,7},{7,5},{8,10},{10,8},{9,1... | collective-permute-start | bytes 1572872 | tf_op jit(solution)/shard_map/ppermute | solution.py:145
  75.4 33.2 %collective-permute-start.2 = (bf16[128,2048]{1,0:T(8,128)(2,1)S(1)}, bf16[128,2048]{1,0:T(8,128)(2,1)}, u32[]{:S(2)}, u32[]{:S(2)}) collective-permute-start(bf16[128,2048]{1,0:T(8,128)(2,1)S(1)} %get-tuple-element.96), channel_id=1, source_target_pairs={{0,2},{2,0},{1,3},{3,1},{4,6},{6,4},{5,7},{7,5},{8,10},{10,8},{9,1... | collective-permute-start | bytes 1572872 | tf_op jit(solution)/shard_map/ppermute | solution.py:145
  77.8 35.2 %copy-start.90 = (bf16[128,16,32]{0,2,1:T(8,128)(2,1)}, bf16[128,16,32]{0,2,1:T(8,128)(2,1)S(1)}, u32[]{:S(2)}) copy-start(bf16[128,16,32]{0,2,1:T(8,128)(2,1)S(1)} %get-tuple-element.103) | copy-start | bytes 393220
  82.3 30.7 %copy-start.75 = (bf16[128,8,32]{0,2,1:T(8,128)(2,1)}, bf16[128,8,32]{0,2,1:T(8,128)(2,1)S(1)}, u32[]{:S(2)}) copy-start(bf16[128,8,32]{0,2,1:T(8,128)(2,1)S(1)} %get-tuple-element.113) | copy-start | bytes 196612
  82.3 30.7 %copy-start.77 = (bf16[128,8,32]{0,2,1:T(8,128)(2,1)}, bf16[128,8,32]{0,2,1:T(8,128)(2,1)S(1)}, u32[]{:S(2)}) copy-start(bf16[128,8,32]{0,2,1:T(8,128)(2,1)S(1)} %get-tuple-element.114) | copy-start | bytes 196612
  85.9 24.9 %copy-start.92 = (bf16[128,16,32]{0,2,1:T(8,128)(2,1)S(1)}, bf16[128,16,32]{0,2,1:T(8,128)(2,1)}, u32[]{:S(2)}) copy-start(bf16[128,16,32]{0,2,1:T(8,128)(2,1)} %get-tuple-element.104) | copy-start | bytes 393220
  85.9 24.9 %copy-start.102 = (pred[128,128]{0,1:T(8,128)(4,1)S(1)}, pred[128,128]{0,1:T(8,128)(4,1)}, u32[]{:S(2)}) copy-start(pred[128,128]{0,1:T(8,128)(4,1)} %fusion.153) | copy-start | bytes 49156
  85.9 29.6 %collective-permute-start.9 = (bf16[256,1024]{1,0:T(8,128)(2,1)}, bf16[256,1024]{1,0:T(8,128)(2,1)}, u32[]{:S(2)}, u32[]{:S(2)}) collective-permute-start(bf16[256,1024]{1,0:T(8,128)(2,1)} %pad_maximum_fusion.12), channel_id=1, source_target_pairs={{0,1},{1,0},{2,3},{3,2},{4,5},{5,4},{6,7},{7,6},{8,9},{9,8},{10,11... | collective-permute-start | bytes 1572872 | tf_op jit(solution)/shard_map/ppermute | solution.py:146
  99.8 20.0 %collective-permute-start.7 = (bf16[256,2048]{1,0:T(8,128)(2,1)}, bf16[256,2048]{1,0:T(8,128)(2,1)}, u32[]{:S(2)}, u32[]{:S(2)}) collective-permute-start(bf16[256,2048]{1,0:T(8,128)(2,1)} %pad_maximum_fusion.8), channel_id=1, source_target_pairs={{0,1},{1,0},{2,3},{3,2},{4,5},{5,4},{6,7},{7,6},{8,9},{9,8},{10,11... | collective-permute-start | bytes 3145736 | tf_op jit(solution)/shard_map/ppermute | solution.py:146
  101.6 16.0 %collective-permute-start.5 = (bf16[256,1024]{1,0:T(8,128)(2,1)}, bf16[256,1024]{1,0:T(8,128)(2,1)}, u32[]{:S(2)}, u32[]{:S(2)}) collective-permute-start(bf16[256,1024]{1,0:T(8,128)(2,1)} %pad_maximum_fusion.11), channel_id=1, source_target_pairs={{0,1},{1,0},{2,3},{3,2},{4,5},{5,4},{6,7},{7,6},{8,9},{9,8},{10,11... | collective-permute-start | bytes 1572872 | tf_op jit(solution)/shard_map/ppermute | solution.py:146
  110.7 12.0 %collective-permute-start.3 = (bf16[256,2048]{1,0:T(8,128)(2,1)}, bf16[256,2048]{1,0:T(8,128)(2,1)}, u32[]{:S(2)}, u32[]{:S(2)}) collective-permute-start(bf16[256,2048]{1,0:T(8,128)(2,1)} %pad_maximum_fusion.6), channel_id=1, source_target_pairs={{0,1},{1,0},{2,3},{3,2},{4,5},{5,4},{6,7},{7,6},{8,9},{9,8},{10,11... | collective-permute-start | bytes 3145736 | tf_op jit(solution)/shard_map/ppermute | solution.py:146
  112.2 13.4 %collective-permute-start.1 = (bf16[64,8,1024]{2,1,0:T(8,128)(2,1)S(1)}, bf16[64,8,1024]{2,1,0:T(8,128)(2,1)}, u32[]{:S(2)}, u32[]{:S(2)}) collective-permute-start(bf16[64,8,1024]{2,1,0:T(8,128)(2,1)S(1)} %all-to-all-done.1), channel_id=1, source_target_pairs={{0,1},{1,0},{2,3},{3,2},{4,5},{5,4},{6,7},{7,6},{8,9},{9,8},{10,11... | collective-permute-start | bytes 3145736 | tf_op jit(solution)/shard_map/ppermute | solution.py:45
  128.5 96.3 %copy-start.7 = (f32[128,1024]{1,0:T(8,128)}, f32[128,1024]{1,0:T(8,128)S(1)}, u32[]{:S(2)}) copy-start(f32[128,1024]{1,0:T(8,128)S(1)} %get-tuple-element.137) | copy-start | bytes 1572868
  130.6 43.1 %copy-start.24 = (bf16[512,2048]{1,0:T(8,128)(2,1)S(1)}, bf16[512,2048]{1,0:T(8,128)(2,1)}, u32[]{:S(2)}) copy-start(bf16[512,2048]{1,0:T(8,128)(2,1)} %pad_maximum_fusion.3) | copy-start | bytes 6291460
  181.7 43.2 %all-to-all-start.3 = ((bf16[32,40,1024]{2,1,0:T(8,128)(2,1)}), bf16[32,40,1024]{2,1,0:T(8,128)(2,1)S(1)}, u32[]{:S(2)}, u32[]{:S(2)}) async-start(bf16[32,40,1024]{2,1,0:T(8,128)(2,1)} %bitcast.365), calls=%async_computation.3 | async-start | bytes 5242880 | tf_op jit(solution)/shard_map/all_to_all | solution.py:139
  189.8 47.8 %copy-start.106 = (f32[128]{0:T(128)}, f32[128]{0:T(128)S(1)}, u32[]{:S(2)}) copy-start(f32[128]{0:T(128)S(1)} %fusion.164) | copy-start | bytes 1540
  224.9 12.8 %copy-start.4 = (bf16[32,40,1024]{2,1,0:T(8,128)(2,1)}, bf16[32,40,1024]{2,1,0:T(8,128)(2,1)S(1)}, u32[]{:S(2)}) copy-start(bf16[32,40,1024]{2,1,0:T(8,128)(2,1)S(1)} %all-to-all-done.3) | copy-start | bytes 7864324
  227.4 10.3 %copy-start.123 = (f32[128]{0:T(128)}, f32[128]{0:T(128)S(1)}, u32[]{:S(2)}) copy-start(f32[128]{0:T(128)S(1)} %add_rsqrt_fusion.1) | copy-start | bytes 1540
  247.3 42.2 %all-to-all-start.4 = ((bf16[32,40,1024]{2,1,0:T(8,128)(2,1)}), bf16[32,40,1024]{2,1,0:T(8,128)(2,1)S(1)}, u32[]{:S(2)}, u32[]{:S(2)}) async-start(bf16[32,40,1024]{2,1,0:T(8,128)(2,1)} %bitcast.358), calls=%async_computation.4 | async-start | bytes 5242880 | tf_op jit(solution)/shard_map/all_to_all | solution.py:139
  289.5 10.8 %copy-start.2 = (bf16[32,40,1024]{2,1,0:T(8,128)(2,1)}, bf16[32,40,1024]{2,1,0:T(8,128)(2,1)S(1)}, u32[]{:S(2)}) copy-start(bf16[32,40,1024]{2,1,0:T(8,128)(2,1)S(1)} %all-to-all-done.4) | copy-start | bytes 7864324
  289.5 41.2 %all-to-all-start.5 = ((bf16[32,40,1024]{2,1,0:T(8,128)(2,1)}), bf16[32,40,1024]{2,1,0:T(8,128)(2,1)}, u32[]{:S(2)}, u32[]{:S(2)}) async-start(bf16[32,40,1024]{2,1,0:T(8,128)(2,1)} %bitcast.357), calls=%async_computation.5 | async-start | bytes 5242880 | tf_op jit(solution)/shard_map/all_to_all | solution.py:139
  330.7 38.8 %all-to-all-start.6 = ((bf16[32,40,1024]{2,1,0:T(8,128)(2,1)}), bf16[32,40,1024]{2,1,0:T(8,128)(2,1)S(1)}, u32[]{:S(2)}, u32[]{:S(2)}) async-start(bf16[32,40,1024]{2,1,0:T(8,128)(2,1)} %bitcast.364), calls=%async_computation.6 | async-start | bytes 5242880 | tf_op jit(solution)/shard_map/all_to_all | solution.py:139
  339.6 42.0 %copy-start.110 = (s32[1024]{0:T(1024)}, s32[1024]{0:T(1024)S(1)}, u32[]{:S(2)}) copy-start(s32[1024]{0:T(1024)S(1)} %fusion.188) | copy-start | bytes 12292
  369.4 38.6 %all-to-all-start.7 = ((bf16[32,40,1024]{2,1,0:T(8,128)(2,1)}), bf16[32,40,1024]{2,1,0:T(8,128)(2,1)}, u32[]{:S(2)}, u32[]{:S(2)}) async-start(bf16[32,40,1024]{2,1,0:T(8,128)(2,1)} %bitcast.354), calls=%async_computation.7 | async-start | bytes 5242880 | tf_op jit(solution)/shard_map/all_to_all | solution.py:139
  424.9 8.4 %collective-permute-start.14 = (bf16[256,1024]{1,0:T(8,128)(2,1)S(1)}, bf16[256,1024]{1,0:T(8,128)(2,1)S(1)}, u32[]{:S(2)}, u32[]{:S(2)}) collective-permute-start(bf16[256,1024]{1,0:T(8,128)(2,1)S(1)} %slice.644), channel_id=1, source_target_pairs={{0,1},{1,0},{2,3},{3,2},{4,5},{5,4},{6,7},{7,6},{8,9},{9,8},{10,11... | collective-permute-start | bytes 1572872 | tf_op jit(solution)/shard_map/ppermute | solution.py:153
  425.0 9.3 %collective-permute-start.12 = (bf16[256,1024]{1,0:T(8,128)(2,1)S(1)}, bf16[256,1024]{1,0:T(8,128)(2,1)S(1)}, u32[]{:S(2)}, u32[]{:S(2)}) collective-permute-start(bf16[256,1024]{1,0:T(8,128)(2,1)S(1)} %slice.645), channel_id=1, source_target_pairs={{0,1},{1,0},{2,3},{3,2},{4,5},{5,4},{6,7},{7,6},{8,9},{9,8},{10,11... | collective-permute-start | bytes 1572872 | tf_op jit(solution)/shard_map/ppermute | solution.py:153
  425.5 10.4 %collective-permute-start.10 = (bf16[256,1024]{1,0:T(8,128)(2,1)S(1)}, bf16[256,1024]{1,0:T(8,128)(2,1)S(1)}, u32[]{:S(2)}, u32[]{:S(2)}) collective-permute-start(bf16[256,1024]{1,0:T(8,128)(2,1)S(1)} %slice.646), channel_id=1, source_target_pairs={{0,1},{1,0},{2,3},{3,2},{4,5},{5,4},{6,7},{7,6},{8,9},{9,8},{10,11... | collective-permute-start | bytes 1572872 | tf_op jit(solution)/shard_map/ppermute | solution.py:153
  433.5 9.2 %collective-permute-start.15 = (bf16[128,1024]{1,0:T(8,128)(2,1)S(1)}, bf16[128,1024]{1,0:T(8,128)(2,1)S(1)}, u32[]{:S(2)}, u32[]{:S(2)}) collective-permute-start(bf16[128,1024]{1,0:T(8,128)(2,1)S(1)} %slice.650), channel_id=1, source_target_pairs={{0,2},{2,0},{1,3},{3,1},{4,6},{6,4},{5,7},{7,5},{8,10},{10,8},{9,1... | collective-permute-start | bytes 786440 | tf_op jit(solution)/shard_map/ppermute | solution.py:155
  434.5 13.8 %collective-permute-start.13 = (bf16[128,1024]{1,0:T(8,128)(2,1)S(1)}, bf16[128,1024]{1,0:T(8,128)(2,1)S(1)}, u32[]{:S(2)}, u32[]{:S(2)}) collective-permute-start(bf16[128,1024]{1,0:T(8,128)(2,1)S(1)} %slice.651), channel_id=1, source_target_pairs={{0,2},{2,0},{1,3},{3,1},{4,6},{6,4},{5,7},{7,5},{8,10},{10,8},{9,1... | collective-permute-start | bytes 786440 | tf_op jit(solution)/shard_map/ppermute | solution.py:155
  436.0 17.4 %collective-permute-start.11 = (bf16[128,1024]{1,0:T(8,128)(2,1)S(1)}, bf16[128,1024]{1,0:T(8,128)(2,1)S(1)}, u32[]{:S(2)}, u32[]{:S(2)}) collective-permute-start(bf16[128,1024]{1,0:T(8,128)(2,1)S(1)} %slice.652), channel_id=1, source_target_pairs={{0,2},{2,0},{1,3},{3,1},{4,6},{6,4},{5,7},{7,5},{8,10},{10,8},{9,1... | collective-permute-start | bytes 786440 | tf_op jit(solution)/shard_map/ppermute | solution.py:155
  454.3 41.6 %all-to-all-start.8 = ((bf16[32,40,1024]{2,1,0:T(8,128)(2,1)}), bf16[32,40,1024]{2,1,0:T(8,128)(2,1)}, u32[]{:S(2)}, u32[]{:S(2)}) async-start(bf16[32,40,1024]{2,1,0:T(8,128)(2,1)} %bitcast.355), calls=%async_computation.8 | async-start | bytes 5242880 | tf_op jit(solution)/shard_map/all_to_all | solution.py:139
  474.0 5.5 collective-permute-start.20
  475.5 39.2 %collective-permute-start.19 = (bf16[512,1024]{1,0:T(8,128)(2,1)}, bf16[512,1024]{1,0:T(8,128)(2,1)}, u32[]{:S(2)}, u32[]{:S(2)}) collective-permute-start(bf16[512,1024]{1,0:T(8,128)(2,1)} %convolution_convert_fusion.11), channel_id=1, source_target_pairs={{0,1},{1,0},{2,3},{3,2},{4,5},{5,4},{6,7},{7,6},{8,9},{9,8},{10,11... | collective-permute-start | bytes 3145736 | tf_op jit(solution)/shard_map/ppermute | solution.py:190
  479.3 37.2 %collective-permute-start.18 = (bf16[512,2048]{1,0:T(8,128)(2,1)}, bf16[512,2048]{1,0:T(8,128)(2,1)}, u32[]{:S(2)}, u32[]{:S(2)}) collective-permute-start(bf16[512,2048]{1,0:T(8,128)(2,1)} %convolution_convert_fusion.6), channel_id=1, source_target_pairs={{0,1},{1,0},{2,3},{3,2},{4,5},{5,4},{6,7},{7,6},{8,9},{9,8},{10,11... | collective-permute-start | bytes 6291464 | tf_op jit(solution)/shard_map/ppermute | solution.py:190
  506.7 40.4 %all-to-all-start.9 = ((bf16[32,40,1024]{2,1,0:T(8,128)(2,1)}), bf16[32,40,1024]{2,1,0:T(8,128)(2,1)}, u32[]{:S(2)}, u32[]{:S(2)}) async-start(bf16[32,40,1024]{2,1,0:T(8,128)(2,1)} %bitcast.83), calls=%async_computation.9 | async-start | bytes 5242880 | tf_op jit(solution)/shard_map/all_to_all | solution.py:139
  513.5 88.0 %reduce-scatter.2.cloned.1.call-start = ((), (), s32[]{:S(2)}) async-start(), calls=%async_computation.14 | async-start | bytes 4096000 | tf_op jit(solution)/shard_map/reduce_scatter | solution.py:200
  532.7 16.6 %copy-start.8 = (f32[128,1024]{1,0:T(8,128)S(1)}, f32[128,1024]{1,0:T(8,128)}, u32[]{:S(2)}) copy-start(f32[128,1024]{1,0:T(8,128)} %copy-done.7) | copy-start | bytes 1572868
  532.7 16.6 %copy-start.109 = (f32[128]{0:T(128)S(1)}, f32[128]{0:T(128)}, u32[]{:S(2)}) copy-start(f32[128]{0:T(128)} %copy-done.108) | copy-start | bytes 1540
  532.7 18.1 %copy-start.14 = (f32[128,1024]{1,0:T(8,128)S(1)}, f32[128,1024]{1,0:T(8,128)}, u32[]{:S(2)}) copy-start(f32[128,1024]{1,0:T(8,128)} %copy-done.13) | copy-start | bytes 1572868
  558.2 15.7 %collective-permute-start.26 = (bf16[256,1024]{1,0:T(8,128)(2,1)}, bf16[256,1024]{1,0:T(8,128)(2,1)}, u32[]{:S(2)}, u32[]{:S(2)}) collective-permute-start(bf16[256,1024]{1,0:T(8,128)(2,1)} %slice.641), channel_id=1, source_target_pairs={{0,1},{1,0},{2,3},{3,2},{4,5},{5,4},{6,7},{7,6},{8,9},{9,8},{10,11... | collective-permute-start | bytes 1572872 | tf_op jit(solution)/shard_map/ppermute | solution.py:153
  558.4 16.9 %collective-permute-start.24 = (bf16[256,1024]{1,0:T(8,128)(2,1)}, bf16[256,1024]{1,0:T(8,128)(2,1)}, u32[]{:S(2)}, u32[]{:S(2)}) collective-permute-start(bf16[256,1024]{1,0:T(8,128)(2,1)} %slice.642), channel_id=1, source_target_pairs={{0,1},{1,0},{2,3},{3,2},{4,5},{5,4},{6,7},{7,6},{8,9},{9,8},{10,11... | collective-permute-start | bytes 1572872 | tf_op jit(solution)/shard_map/ppermute | solution.py:153
  558.9 20.4 %collective-permute-start.22 = (bf16[256,1024]{1,0:T(8,128)(2,1)}, bf16[256,1024]{1,0:T(8,128)(2,1)}, u32[]{:S(2)}, u32[]{:S(2)}) collective-permute-start(bf16[256,1024]{1,0:T(8,128)(2,1)} %slice.643), channel_id=1, source_target_pairs={{0,1},{1,0},{2,3},{3,2},{4,5},{5,4},{6,7},{7,6},{8,9},{9,8},{10,11... | collective-permute-start | bytes 1572872 | tf_op jit(solution)/shard_map/ppermute | solution.py:153
  568.5 4.2 collective-permute-start.17
  571.1 26.3 %collective-permute-start.16 = (bf16[512,2048]{1,0:T(8,128)(2,1)}, bf16[512,2048]{1,0:T(8,128)(2,1)}, u32[]{:S(2)}, u32[]{:S(2)}) collective-permute-start(bf16[512,2048]{1,0:T(8,128)(2,1)} %convolution_convert_fusion.7), channel_id=1, source_target_pairs={{0,1},{1,0},{2,3},{3,2},{4,5},{5,4},{6,7},{7,6},{8,9},{9,8},{10,11... | collective-permute-start | bytes 6291464 | tf_op jit(solution)/shard_map/ppermute | solution.py:190
  572.7 12.6 %collective-permute-start.21 = (bf16[512,1024]{1,0:T(8,128)(2,1)S(1)}, bf16[512,1024]{1,0:T(8,128)(2,1)S(1)}, u32[]{:S(2)}, u32[]{:S(2)}) collective-permute-start(bf16[512,1024]{1,0:T(8,128)(2,1)S(1)} %convolution_convert_fusion.10), channel_id=1, source_target_pairs={{0,1},{1,0},{2,3},{3,2},{4,5},{5,4},{6,7},{7,6},{8,9},{9,8},{10,11... | collective-permute-start | bytes 3145736 | tf_op jit(solution)/shard_map/ppermute | solution.py:190
  575.2 9.2 %collective-permute-start.27 = (bf16[128,1024]{1,0:T(8,128)(2,1)S(1)}, bf16[128,1024]{1,0:T(8,128)(2,1)S(1)}, u32[]{:S(2)}, u32[]{:S(2)}) collective-permute-start(bf16[128,1024]{1,0:T(8,128)(2,1)S(1)} %slice.647), channel_id=1, source_target_pairs={{0,2},{2,0},{1,3},{3,1},{4,6},{6,4},{5,7},{7,5},{8,10},{10,8},{9,1... | collective-permute-start | bytes 786440 | tf_op jit(solution)/shard_map/ppermute | solution.py:155
  577.3 16.4 %collective-permute-start.25 = (bf16[128,1024]{1,0:T(8,128)(2,1)}, bf16[128,1024]{1,0:T(8,128)(2,1)}, u32[]{:S(2)}, u32[]{:S(2)}) collective-permute-start(bf16[128,1024]{1,0:T(8,128)(2,1)} %slice.648), channel_id=1, source_target_pairs={{0,2},{2,0},{1,3},{3,1},{4,6},{6,4},{5,7},{7,5},{8,10},{10,8},{9,1... | collective-permute-start | bytes 786440 | tf_op jit(solution)/shard_map/ppermute | solution.py:155
  580.6 14.9 %collective-permute-start.23 = (bf16[128,1024]{1,0:T(8,128)(2,1)S(1)}, bf16[128,1024]{1,0:T(8,128)(2,1)S(1)}, u32[]{:S(2)}, u32[]{:S(2)}) collective-permute-start(bf16[128,1024]{1,0:T(8,128)(2,1)S(1)} %slice.649), channel_id=1, source_target_pairs={{0,2},{2,0},{1,3},{3,1},{4,6},{6,4},{5,7},{7,5},{8,10},{10,8},{9,1... | collective-permute-start | bytes 786440 | tf_op jit(solution)/shard_map/ppermute | solution.py:155
  586.7 10.7 %copy-start.49 = (bf16[128,16,64]{0,2,1:T(8,128)(2,1)S(1)}, bf16[128,16,64]{0,2,1:T(8,128)(2,1)}, u32[]{:S(2)}) copy-start(bf16[128,16,64]{0,2,1:T(8,128)(2,1)} %copy-done.48) | copy-start | bytes 786436
  586.7 10.8 %copy-start.74 = (bf16[8,64,128]{2,1,0:T(8,128)(2,1)S(1)}, bf16[8,64,128]{2,1,0:T(8,128)(2,1)}, u32[]{:S(2)}) copy-start(bf16[8,64,128]{2,1,0:T(8,128)(2,1)} %copy-done.73) | copy-start | bytes 393220
  586.7 23.4 %all-to-all-start.11 = ((bf16[64,8,1024]{2,1,0:T(8,128)(2,1)}), bf16[64,8,1024]{2,1,0:T(8,128)(2,1)S(1)}, u32[]{:S(2)}, u32[]{:S(2)}) async-start(bf16[64,8,1024]{2,1,0:T(8,128)(2,1)} %fusion.65), calls=%async_computation.12 | async-start | bytes 2097152 | tf_op jit(solution)/shard_map/all_to_all | solution.py:195
  593.7 109.0 %all-reduce.3.cloned.1.call-start = ((), (), s32[]{:S(2)}) async-start(), calls=%async_computation.15 | async-start | bytes 1638400
  610.1 94.3 %all-to-all-start.10 = ((bf16[64,8,2176]{2,1,0:T(8,128)(2,1)}), bf16[64,8,2176]{2,1,0:T(8,128)(2,1)S(1)}, u32[]{:S(2)}, u32[]{:S(2)}) async-start(bf16[64,8,2176]{2,1,0:T(8,128)(2,1)} %maximum_bitcast_fusion), calls=%async_computation.10 | async-start | bytes 4456448 | tf_op jit(solution)/shard_map/all_to_all | solution.py:195
  (108 other events, 363.5 us)
Sparse Core Ops, SparseCore 0:
  130.7 102.3 all-gather.1
  520.9 52.1 reduce-scatter.1
  601.6 100.9 all-reduce.2

commit v4 on v3

--- a/solution.py
+++ b/solution.py
@@ -27,7 +27,7 @@
 EXPERT_AXES = ("x", "y", "zh")
 CHIP_AXES = ("x", "y", "zh", "zl")
 Z_AXES = ("zh", "zl")
-PLANE_AXES = ("x", "y")
+GROUP_AXES = ("zl", "c")
 DENSE_WIDTHS = (2048, 1024, E, 1, 1)
 HALF = MODEL_WIDTH // 2
 SWAP = [(0, 1), (1, 0)]
@@ -141,18 +141,14 @@
     ).reshape(ROWS, MODEL_WIDTH)
 
 
-def gather_expert(own):
-    pair = jnp.concatenate([own, lax.ppermute(own, "zl", SWAP)], axis=0)
-    return jnp.concatenate([pair, lax.ppermute(pair, "c", SWAP)], axis=0)
-
-
-def scatter_expert(grad):
-    half = grad.shape[0] // 2
-    quarter = half // 2
-    kept, given = grad[:half], grad[half:].astype(jnp.bfloat16)
-    kept = kept + lax.ppermute(given, "c", SWAP).astype(jnp.float32)
-    own, other = kept[:quarter], kept[quarter:].astype(jnp.bfloat16)
-    return own + lax.ppermute(other, "zl", SWAP).astype(jnp.float32)
+def gather_expert(own_in, own_out):
+    both = jnp.concatenate([own_in, own_out], axis=1)
+    return lax.all_gather(both, GROUP_AXES, axis=0, tiled=True)
+
+
+def scatter_expert(grads):
+    both = jnp.concatenate(grads, axis=1).astype(jnp.bfloat16)
+    return lax.psum_scatter(both, GROUP_AXES, scatter_dimension=0, tiled=True)
 
 
 def order_table():
@@ -192,13 +188,14 @@
 
 def chip_sum(parts):
     parts = parts.reshape(64, 8, -1)
-    parts = lax.all_to_all(parts, Z_AXES + PLANE_AXES, split_axis=0, concat_axis=0, tiled=True)
+    parts = lax.all_to_all(parts, Z_AXES + ("x", "y"), split_axis=0, concat_axis=0, tiled=True)
     return jnp.sum(parts.astype(jnp.float32), axis=0)
 
 
 def chip_sum_aside(parts):
     parts = lax.psum_scatter(parts, Z_AXES, scatter_dimension=0, tiled=True)
-    return lax.psum_scatter(parts, PLANE_AXES, scatter_dimension=0, tiled=True).astype(jnp.float32)
+    parts = lax.psum_scatter(parts, "x", scatter_dimension=0, tiled=True)
+    return lax.psum_scatter(parts, "y", scatter_dimension=0, tiled=True).astype(jnp.float32)
 
 
 def norm_back(grad_norm, normed, inverse):
@@ -281,7 +278,8 @@
     ).astype(jnp.bfloat16)
 
 
-def feed_forward(rows_here, expert_in_l, expert_out_l):
+def feed_forward(rows_here, expert):
+    expert_in_l, expert_out_l = expert[:, : 2 * MODEL_WIDTH], expert[:, 2 * MODEL_WIDTH :]
     gate_pre = lax.dot_general(
         rows_here,
         expert_in_l[:, :MODEL_WIDTH],
@@ -299,7 +297,8 @@
     return results, (gate_pre, up_pre)
 
 
-def feed_backward(grad_rows, rows_here, pre, expert_in_l, expert_out_l):
+def feed_backward(grad_rows, rows_here, pre, expert):
+    expert_in_l, expert_out_l = expert[:, : 2 * MODEL_WIDTH], expert[:, 2 * MODEL_WIDTH :]
     gate_pre, up_pre = pre
     sigmoid_pre = jax.nn.sigmoid(gate_pre)
     activated = gate_pre * sigmoid_pre
@@ -377,10 +376,11 @@
     query_width = QUERY_HEADS * HEAD_SIZE
     key_value_width = KEY_VALUE_HEADS * HEAD_SIZE
     grad_low = grad_h1.astype(jnp.bfloat16)
-    proj_halves = weight_halves(mixed_moved, grad_low)
+    proj_sum = core_sum(weight_halves(mixed_moved, grad_low))
     mixed_gradient = lax.dot_general(
         grad_low, out_full, (((1,), (1,)), ((), ())), preferred_element_type=jnp.float32
     ).astype(jnp.bfloat16)
+    mixed_gradient, proj_sum = lax.optimization_barrier((mixed_gradient, proj_sum))
     mixed_gradient = jnp.where(live[:, None] > 0.5, mixed_gradient, jnp.zeros_like(mixed_gradient))
     mixed_gradient = mixed_gradient.reshape(
         token_total, KEY_VALUE_HEADS, QUERY_HEADS // KEY_VALUE_HEADS, HEAD_SIZE
@@ -422,7 +422,7 @@
     )
     gain_one_grad = jnp.sum(grad_normed * normed, axis=0)
     grad_input = grad_h1 + norm_back(grad_normed * gain_one.astype(jnp.float32), normed, inverse)
-    return (grad_input, qkv_halves, proj_halves, gain_one_grad)
+    return (grad_input, qkv_halves, proj_sum, gain_one_grad)
 
 
 def on_device(
@@ -462,9 +462,7 @@
     lead_first = cut_weights(lead_first, (2048, E, 1, 1))
     out_first = sent_by_chips(out_own)
     dense = [(lead_first[0], out_first) + lead_first[1:], None]
-    experts = [
-        (gather_expert(expert_in[layer]), gather_expert(expert_out[layer])) for layer in layers
-    ]
+    experts = [gather_expert(expert_in[0], expert_out[0]), None]
     position, live_row, allowed = seq_layout(seq_lengths, seq_owner, device)
     live = live_row.astype(jnp.float32)
     cosine_table, sine_values = rope_tables(position)
@@ -480,8 +478,13 @@
         hidden = hidden + jnp.dot(mixed_low, dense[layer][1], preferred_element_type=jnp.float32)
         rows, route_stash = route_rows(hidden, dense[layer], routed, chosen)
         if layer == 0:
-            rows, experts, own_dense = lax.optimization_barrier((rows, experts, own_dense))
-            dense[1] = cut_weights(sent_together(own_dense[1], AXES), DENSE_WIDTHS)
+            rows, own_dense = lax.optimization_barrier((rows, own_dense))
+            gathered = sent_together(own_dense[1], AXES)
+            gathered, expert_in, expert_out = lax.optimization_barrier(
+                (gathered, expert_in, expert_out)
+            )
+            dense[1] = cut_weights(gathered, DENSE_WIDTHS)
+            experts[1] = gather_expert(expert_in[1], expert_out[1])
         rows_here = trade_rows(rows)
         moved = reorder(attn_stash[2], order), reorder(mixed_low, order)
         grad_rows = None
@@ -489,62 +492,57 @@
             slots = slot_gradients(grad_hidden, route_stash[-1])
             slots, rows_here = lax.optimization_barrier((slots, rows_here))
             grad_rows = trade_rows(slots)
-        results, pre = feed_forward(rows_here, *experts[layer])
+        results, pre = feed_forward(rows_here, experts[layer])
         if layer == last:
             results, grad_rows = lax.optimization_barrier((results, grad_rows))
         returned = trade_rows(results)
         hidden = hidden + jnp.dot(route_stash[-1], returned, preferred_element_type=jnp.float32)
         saved.append((attn_stash, moved, route_stash, rows_here, pre, returned, grad_rows))
     output_low = hidden.astype(jnp.bfloat16)
-    layer_grads = [None] * LAYER_COUNT
-    after = ()
+    expert_sums = [None] * LAYER_COUNT
     for layer in reversed(layers):
         attn_stash, moved, route_stash, rows_here, pre, returned, grad_rows = saved[layer]
         if grad_rows is None:
             slots = slot_gradients(grad_hidden, route_stash[-1])
-            slots, after = lax.optimization_barrier((slots, after))
-            grad_rows = trade_rows(slots)
-        grad_in_rows, expert_grads = feed_backward(grad_rows, rows_here, pre, *experts[layer])
+            grad_rows, sums = lax.optimization_barrier((trade_rows(slots), sums))
+            sums.append(jnp.zeros_like(sums[-1]))
+            done_last = chip_sum_aside(jnp.concatenate(sums, axis=1))[:, :-128]
+        grad_in_rows, expert_grads = feed_backward(grad_rows, rows_here, pre, experts[layer])
         grad_slots = trade_rows(grad_in_rows)
         router_grad, grad_routed = route_backward(
             grad_hidden, dense[layer], chosen, returned, route_stash
         )
         grad_slots, expert_grads = lax.optimization_barrier((grad_slots, expert_grads))
-        expert_grads = [scatter_expert(g) for g in expert_grads]
+        expert_grads = scatter_expert(expert_grads)
         grad_h1, gain_two_grad = rows_backward(
             grad_hidden, dense[layer], chosen, grad_slots, grad_routed, route_stash
         )
-        grad_hidden, qkv_halves, proj_halves, gain_one_grad = attend_backward(
+        grad_hidden, qkv_halves, proj_sum, gain_one_grad = attend_backward(
             grad_h1, dense[layer], live, allowed, cosine_table, sine_values, attn_stash, *moved
         )
         small = small_halves(router_grad, gain_one_grad, gain_two_grad, order)
         if layer == last:
-            after = expert_grads
-            sums = [core_sum(halves) for halves in (qkv_halves, proj_halves, small)]
-            done = chip_sum_aside(jnp.concatenate(sums, axis=1))
-            proj_done, done = done[:, 2048:3072], jnp.concatenate(
-                [done[:, :2048], done[:, 3072:]], axis=1
-            )
+            sums = [core_sum(qkv_halves), proj_sum, core_sum(small)]
         else:
-            proj_done = chip_sum(core_sum(proj_halves))
+            proj_done = chip_sum(proj_sum)
             sums = [core_sum(halves) for halves in (qkv_halves, small)]
             done = chip_sum(jnp.concatenate(sums, axis=1))
-        qkv_done, small_done = done[:, :2048], done[:, 2048:]
-        layer_grads[layer] = (
-            qkv_done,
-            proj_done,
-            small_done[:, :E],
-            small_done[:, E],
-            small_done[:, E + 1],
-            expert_grads,
-        )
-    stacked = [
-        jnp.stack([layer_grads[layer][member] for layer in layers]) for member in range(5)
-    ]
-    grads = [layer_grads[0][5], after]
-    stacked.append(jnp.stack([jnp.concatenate(g[:2], axis=1) for g in grads]))
-    stacked.append(jnp.stack([g[2] for g in grads]))
-    return (output_low, grad_hidden) + tuple(stacked)
+        expert_sums[layer] = expert_grads
+    first = [done[:, :2048], proj_done, done[:, 2048:]]
+    second = [done_last[:, :2048], done_last[:, 2048:3072], done_last[:, 3072:]]
+    qkv, proj, small = [jnp.stack(pair) for pair in zip(first, second)]
+    both = jnp.stack(expert_sums).astype(jnp.float32)
+    return (
+        output_low,
+        grad_hidden,
+        qkv,
+        proj,
+        small[:, :, :E],
+        small[:, :, E],
+        small[:, :, E + 1],
+        both[:, :, : 2 * MODEL_WIDTH],
+        both[:, :, 2 * MODEL_WIDTH :],
+    )
 
 
 def solution(mesh):

time: 725 us -> 726 us (level)
  blocking collectives: 43.1 us -> 82.2 us
  local copies, waits for them, and re-layouts: 39.7 us -> 23.4 us
  other arithmetic: 59.3 us -> 43.2 us
  starting transfers between devices: 96.3 us -> 83.7 us
  matrix products: 152 us -> 163 us
  waiting for transfers between devices: 307 us -> 299 us
    unnamed x4 -> x8, waiting for transfers between devices: 81.5 us -> 0.13 us
    all_to_all x0 -> x1, blocking collectives: none -> 42.1 us  [sent_by_chips(): lax.all_to_all(copies, CHIP_AXES, split_axis=0, concat_axis=0, tiled=True)]
    reduce_scatter x1, waiting for transfers between devices: 0.01 us -> 40 us  [chip_sum_aside(): parts = lax.psum_scatter(parts, Z_AXES, scatter_dimension=0, tiled=True)]
    ppermute x20 -> x0, waiting for transfers between devices: 36.9 us -> none  [the longest x6 18.5 us: scatter_expert(): return own + lax.ppermute(other, 'zl', SWAP).astype(jnp.float32)]
    all_to_all x2, waiting for transfers between devices: 8.54 us -> 38.4 us  [chip_sum(): lax.all_to_all(parts, Z_AXES + ('x', 'y'), split_axis=0, concat_axis=0, t...]
    all_to_all x7, waiting for transfers between devices: 144 us -> 163 us  [trade_rows(): lax.all_to_all(rows.reshape(E, ROOM, MODEL_WIDTH), EXPERT_AXES, split_axi...]
    all_gather x1, waiting for transfers between devices: 5.68 us -> 23.9 us  [sent_together(): return lax.all_gather(both, axis, axis=0, tiled=True)]
    reduce_scatter x0 -> x4, waiting for transfers between devices: none -> 14 us  [the longest x1 14 us: chip_sum_aside(): lax.psum_scatter(parts, 'y', scatter_dimension=0, tiled=True)]
  transfers between devices with their start and end apart: 42 -> 26, of which waited for: 18 -> 15; matrix products, arithmetic and copies ran while one was open for 28% -> 25% of each run, Pallas kernels for 0% -> 0%
where the time goes in v4:
time: 726 us; the launch traced here: 712 us
  waiting for transfers between devices  299 us (41%)
  matrix products  163 us (22%)
  starting transfers between devices  83.7 us (12%)
  blocking collectives  82.2 us (11%)
  other arithmetic  43.2 us (6%)
  local copies, waits for them, and re-layouts  23.4 us (3%)
  between operations  16.3 us (2%)
    all_to_all x7, waiting for transfers between devices, trade_rows(): lax.all_to_all(rows.reshape(E, ROOM, MODEL_WIDTH), EXPERT_AXES, split_axi...  163 us
    all_to_all x7, starting transfers between devices, trade_rows(): lax.all_to_all(rows.reshape(E, ROOM, MODEL_WIDTH), EXPERT_AXES, split_axi...  61.5 us
    all_to_all x1, blocking collectives, sent_by_chips(): lax.all_to_all(copies, CHIP_AXES, split_axis=0, concat_axis=0, tiled=True)  42.1 us
    all_to_all x1, blocking collectives, trade_rows(): lax.all_to_all(rows.reshape(E, ROOM, MODEL_WIDTH), EXPERT_AXES, split_axi...  40.1 us
    reduce_scatter x1, waiting for transfers between devices, chip_sum_aside(): parts = lax.psum_scatter(parts, Z_AXES, scatter_dimension=0, tiled=True)  40 us
    all_to_all x2, waiting for transfers between devices, chip_sum(): lax.all_to_all(parts, Z_AXES + ('x', 'y'), split_axis=0, concat_axis=0, t...  38.4 us
    all_gather x1, waiting for transfers between devices, sent_together(): return lax.all_gather(both, axis, axis=0, tiled=True)  23.9 us
    all_to_all x1, waiting for transfers between devices, sent_by_chips(): lax.all_to_all(copies, CHIP_AXES, split_axis=0, concat_axis=0, tiled=True)  15.6 us
  transfers between devices with their start and end apart: 26, of which 15 were waited for; matrix products, arithmetic and copies ran while one was open for 25% of the time, Pallas kernels for 0%

profile of v4, /device:TPU:2, one launch (start us, length us, event | category | flops | bytes accessed | tf_op | source)
XLA Modules:
  0.0 711.5 jit_solution(8628846626307559679)
XLA Ops:
  9.9 42.1 %all_to_all.60 = bf16[64,8,2176]{2,1,0:T(8,128)(2,1)S(1)} all-to-all(bf16[64,8,2176]{2,1,0:T(8,128)(2,1)S(1)} %broadcast_in_dim.77), channel_id=1, replica_groups=mesh['x'=4,'y'=4,'zh'=2,'zl'=2,'c'=2] {'x','y','zh','zl'}, dimensions={0} | all-to-all | bytes 4456448 | tf_op jit(solution)/shard_map/all_to_all | solution.py:44
  53.1 3.4 collective-permute-done
  58.5 2.5 pad_maximum_fusion
  63.9 6.4 all-to-all-start.1
  72.5 15.6 %all-to-all-done.1 = bf16[64,8,1024]{2,1,0:T(8,128)(2,1)S(1)} async-done(((bf16[64,8,1024]{2,1,0:T(8,128)(2,1)}), bf16[64,8,1024]{2,1,0:T(8,128)(2,1)S(1)}, u32[]{:S(2)}, u32[]{:S(2)}) %all-to-all-start.1) | async-done | bytes 1048608 | tf_op jit(solution)/shard_map/all_to_all | solution.py:44
  88.1 3.0 fusion.14
  97.1 2.4 convolution_convert_fusion.5
  100.4 40.1 %all_to_all.61 = bf16[32,40,1024]{2,1,0:T(8,128)(2,1)S(1)} all-to-all(bf16[32,40,1024]{2,1,0:T(8,128)(2,1)} %bitcast.342), channel_id=1, replica_groups=mesh['x'=4,'y'=4,'zh'=2,'zl'=2,'c'=2] {'x','y','zh'}, dimensions={0} | all-to-all | bytes 5242880 | tf_op jit(solution)/shard_map/all_to_all | solution.py:139
  140.5 3.8 fusion.79
  144.3 3.4 multiply_convert_fusion.5
  147.8 3.1 convolution_convert_fusion.4
  150.9 6.5 all-to-all-start.3
  159.8 32.4 %all-to-all-done.3 = bf16[32,40,1024]{2,1,0:T(8,128)(2,1)S(1)} async-done(((bf16[32,40,1024]{2,1,0:T(8,128)(2,1)}), bf16[32,40,1024]{2,1,0:T(8,128)(2,1)S(1)}, u32[]{:S(2)}, u32[]{:S(2)}) %all-to-all-start.3) | async-done | bytes 2621472 | tf_op jit(solution)/shard_map/all_to_all | solution.py:139
  192.2 2.5 multiply_reduce_fusion.9
  194.8 23.9 %all-gather.6.cloned.1.call-done = bf16[1024,3106]{1,0:T(8,128)(2,1)} async-done(((bf16[8,3106]{1,0:T(8,128)(2,1)}), bf16[1024,3106]{1,0:T(8,128)(2,1)}) %all-gather.6.cloned.1.call-update) | async-done | bytes 6361104 | tf_op jit(solution)/shard_map/all_gather | solution.py:38
  220.1 3.2 fusion.10
  232.9 2.5 convolution_convert_fusion.2
  235.3 7.4 %all-to-all-start.4 = ((bf16[32,40,1024]{2,1,0:T(8,128)(2,1)}), bf16[32,40,1024]{2,1,0:T(8,128)(2,1)S(1)}, u32[]{:S(2)}, u32[]{:S(2)}) async-start(bf16[32,40,1024]{2,1,0:T(8,128)(2,1)} %bitcast.344), calls=%async_computation.4 | async-start | bytes 5242880 | tf_op jit(solution)/shard_map/all_to_all | solution.py:139
  245.1 3.3 convolution_convert_fusion.3
  248.4 28.5 %all-to-all-done.4 = bf16[32,40,1024]{2,1,0:T(8,128)(2,1)S(1)} async-done(((bf16[32,40,1024]{2,1,0:T(8,128)(2,1)}), bf16[32,40,1024]{2,1,0:T(8,128)(2,1)S(1)}, u32[]{:S(2)}, u32[]{:S(2)}) %all-to-all-start.4) | async-done | bytes 2621472 | tf_op jit(solution)/shard_map/all_to_all | solution.py:139
  276.9 19.5 %all-to-all-start.5 = ((bf16[32,40,1024]{2,1,0:T(8,128)(2,1)}), bf16[32,40,1024]{2,1,0:T(8,128)(2,1)}, u32[]{:S(2)}, u32[]{:S(2)}) async-start(bf16[32,40,1024]{2,1,0:T(8,128)(2,1)} %bitcast.343), calls=%async_computation.5 | async-start | bytes 5242880 | tf_op jit(solution)/shard_map/all_to_all | solution.py:139
  296.5 3.0 fusion.69
  299.5 3.4 multiply_convert_fusion.4
  303.9 3.0 convolution_convert_fusion.1
  306.9 23.2 %all-to-all-done.5 = bf16[32,40,1024]{2,1,0:T(8,128)(2,1)} async-done(((bf16[32,40,1024]{2,1,0:T(8,128)(2,1)}), bf16[32,40,1024]{2,1,0:T(8,128)(2,1)}, u32[]{:S(2)}, u32[]{:S(2)}) %all-to-all-start.5) | async-done | bytes 2621472 | tf_op jit(solution)/shard_map/all_to_all | solution.py:139
  330.1 6.0 all-to-all-start.6
  336.1 6.2 multiply_convert_fusion.2
  343.9 3.0 add_convert_fusion.1
  346.9 21.3 %all-to-all-done.6 = bf16[32,40,1024]{2,1,0:T(8,128)(2,1)S(1)} async-done(((bf16[32,40,1024]{2,1,0:T(8,128)(2,1)}), bf16[32,40,1024]{2,1,0:T(8,128)(2,1)S(1)}, u32[]{:S(2)}, u32[]{:S(2)}) %all-to-all-start.6) | async-done | bytes 2621472 | tf_op jit(solution)/shard_map/all_to_all | solution.py:139
  368.2 6.8 all-to-all-start.7
  375.1 2.6 fusion.48
  377.7 4.8 fusion.236
  382.5 2.5 fusion.235
  385.0 2.5 fusion.234
  389.1 18.5 %all-to-all-done.7 = bf16[32,40,1024]{2,1,0:T(8,128)(2,1)} async-done(((bf16[32,40,1024]{2,1,0:T(8,128)(2,1)}), bf16[32,40,1024]{2,1,0:T(8,128)(2,1)}, u32[]{:S(2)}, u32[]{:S(2)}) %all-to-all-start.7) | async-done | bytes 2621472 | tf_op jit(solution)/shard_map/all_to_all | solution.py:139
  414.8 2.4 fusion.45
  425.3 2.4 fusion.56
  430.0 3.9 multiply_reduce_fusion.5
  437.3 6.9 all-to-all-start.8
  444.2 3.3 convolution_convert_fusion.7
  450.5 2.4 fusion.5
  455.2 3.7 add_convert_fusion.3
  459.0 20.2 %all-to-all-done.8 = bf16[32,40,1024]{2,1,0:T(8,128)(2,1)} async-done(((bf16[32,40,1024]{2,1,0:T(8,128)(2,1)}), bf16[32,40,1024]{2,1,0:T(8,128)(2,1)}, u32[]{:S(2)}, u32[]{:S(2)}) %all-to-all-start.8) | async-done | bytes 2621472 | tf_op jit(solution)/shard_map/all_to_all | solution.py:139
  479.2 3.4 maximum_maximum_fusion
  482.7 40.0 %reduce-scatter.6.cloned.1.call-done = bf16[128,3328]{1,0:T(8,128)(2,1)} async-done(((bf16[512,3328]{1,0:T(8,128)(2,1)}), bf16[128,3328]{1,0:T(8,128)(2,1)}) %reduce-scatter.6.cloned.1.call-update) | async-done | bytes 851984 | tf_op jit(solution)/shard_map/reduce_scatter | solution.py:196
  523.0 3.1 pad_maximum_fusion.2
  526.1 6.2 multiply_convert_fusion
  533.9 3.0 add_convert_fusion
  536.9 8.3 %all-to-all-start.9 = ((bf16[32,40,1024]{2,1,0:T(8,128)(2,1)}), bf16[32,40,1024]{2,1,0:T(8,128)(2,1)}, u32[]{:S(2)}, u32[]{:S(2)}) async-start(bf16[32,40,1024]{2,1,0:T(8,128)(2,1)} %bitcast.339), calls=%async_computation.9 | async-start | bytes 5242880 | tf_op jit(solution)/shard_map/all_to_all | solution.py:139
  545.3 2.6 fusion.50
  547.9 3.0 convolution_multiply_fusion
  551.4 4.5 fusion.240
  555.9 2.5 fusion.239
  558.4 2.5 fusion.238
  561.0 18.9 %all-to-all-done.9 = bf16[32,40,1024]{2,1,0:T(8,128)(2,1)} async-done(((bf16[32,40,1024]{2,1,0:T(8,128)(2,1)}), bf16[32,40,1024]{2,1,0:T(8,128)(2,1)}, u32[]{:S(2)}, u32[]{:S(2)}) %all-to-all-start.9) | async-done | bytes 2621472 | tf_op jit(solution)/shard_map/all_to_all | solution.py:139
  590.0 2.7 convolution_convert_fusion.12
  592.7 2.7 add_convert_fusion.4
  610.4 4.7 fusion.90
  618.2 7.2 %all-to-all-start.11 = ((bf16[64,8,1024]{2,1,0:T(8,128)(2,1)}), bf16[64,8,1024]{2,1,0:T(8,128)(2,1)}, u32[]{:S(2)}, u32[]{:S(2)}) async-start(bf16[64,8,1024]{2,1,0:T(8,128)(2,1)} %bitcast.350), calls=%async_computation.14 | async-start | bytes 2097152 | tf_op jit(solution)/shard_map/all_to_all | solution.py:191
  626.4 2.5 add_convert_fusion.2
  630.6 13.5 %all-to-all-done.11 = bf16[64,8,1024]{2,1,0:T(8,128)(2,1)} async-done(((bf16[64,8,1024]{2,1,0:T(8,128)(2,1)}), bf16[64,8,1024]{2,1,0:T(8,128)(2,1)}, u32[]{:S(2)}, u32[]{:S(2)}) %all-to-all-start.11) | async-done | bytes 1048608 | tf_op jit(solution)/shard_map/all_to_all | solution.py:191
  644.0 6.4 all-to-all-start.10
  655.2 25.0 %all-to-all-done.10 = bf16[64,8,2176]{2,1,0:T(8,128)(2,1)} async-done(((bf16[64,8,2176]{2,1,0:T(8,128)(2,1)}), bf16[64,8,2176]{2,1,0:T(8,128)(2,1)}, u32[]{:S(2)}, u32[]{:S(2)}) %all-to-all-start.10) | async-done | bytes 2228256 | tf_op jit(solution)/shard_map/all_to_all | solution.py:191
  687.0 14.0 %reduce-scatter.10.cloned.1.call-done = bf16[8,3328]{1,0:T(8,128)(2,1)} async-done(((bf16[32,3328]{1,0:T(8,128)(2,1)}), bf16[8,3328]{1,0:T(8,128)(2,1)}) %reduce-scatter.10.cloned.1.call-update) | async-done | bytes 53264 | tf_op jit(solution)/shard_map/reduce_scatter | solution.py:198
  (426 shorter events, 111.3 us)
Async XLA Ops:
  7.2 133.4 %all-gather.4.cloned.1.call-start = ((), (), s32[]{:S(2)}) async-start(), calls=%async_computation.17 | async-start | bytes 3932160 | tf_op jit(solution)/shard_map/all_gather | solution.py:146
  9.9 42.1 %copy-start.101 = (s32[512]{0:T(512)S(1)}, s32[512]{0:T(512)}, u32[]{:S(2)}) copy-start(s32[512]{0:T(512)} %param.15) | copy-start | bytes 6148
  9.9 42.7 %copy-start.102 = (s32[512]{0:T(512)S(1)}, s32[512]{0:T(512)}, u32[]{:S(2)}) copy-start(s32[512]{0:T(512)} %param.14) | copy-start | bytes 6148
  9.9 43.2 %copy-start.88 = (bf16[2,8,1024]{2,1,0:T(8,128)(2,1)S(1)}, bf16[2,8,1024]{2,1,0:T(8,128)(2,1)}, u32[]{:S(2)}) copy-start(bf16[2,8,1024]{2,1,0:T(8,128)(2,1)} %param.18) | copy-start | bytes 98308
  52.0 4.5 collective-permute-start
  63.9 24.2 %all-to-all-start.1 = ((bf16[64,8,1024]{2,1,0:T(8,128)(2,1)}), bf16[64,8,1024]{2,1,0:T(8,128)(2,1)S(1)}, u32[]{:S(2)}, u32[]{:S(2)}) async-start(bf16[64,8,1024]{2,1,0:T(8,128)(2,1)} %broadcast_in_dim.82), calls=%async_computation.1 | async-start | bytes 2097152 | tf_op jit(solution)/shard_map/all_to_all | solution.py:44
  70.3 148.4 %all-gather.6.cloned.1.call-start = ((), (), s32[]{:S(2)}) async-start(), calls=%async_computation.18 | async-start | bytes 6604800 | tf_op jit(solution)/shard_map/all_gather | solution.py:38
  70.4 20.7 %copy-start.103 = (f32[128]{0:T(128)}, f32[128]{0:T(128)S(1)}, u32[]{:S(2)}) copy-start(f32[128]{0:T(128)S(1)} %add_rsqrt_fusion.3) | copy-start | bytes 1540
  70.5 354.9 %copy-start.89 = (pred[128,128]{0,1:T(8,128)(4,1)}, pred[128,128]{0,1:T(8,128)(4,1)S(1)}, u32[]{:S(2)}) copy-start(pred[128,128]{0,1:T(8,128)(4,1)S(1)} %fusion.153) | copy-start | bytes 49156
  88.1 6.7 collective-permute-start.1
  97.0 95.3 %copy-start.6 = (f32[128,1024]{1,0:T(8,128)}, f32[128,1024]{1,0:T(8,128)S(1)}, u32[]{:S(2)}) copy-start(f32[128,1024]{1,0:T(8,128)S(1)} %get-tuple-element.137) | copy-start | bytes 1572868
  150.9 41.4 %all-to-all-start.3 = ((bf16[32,40,1024]{2,1,0:T(8,128)(2,1)}), bf16[32,40,1024]{2,1,0:T(8,128)(2,1)S(1)}, u32[]{:S(2)}, u32[]{:S(2)}) async-start(bf16[32,40,1024]{2,1,0:T(8,128)(2,1)} %bitcast.356), calls=%async_computation.3 | async-start | bytes 5242880 | tf_op jit(solution)/shard_map/all_to_all | solution.py:139
  157.4 139.1 %all-gather.8.cloned.1.call-start = ((), (), s32[]{:S(2)}) async-start(), calls=%async_computation.19 | async-start | bytes 3932160 | tf_op jit(solution)/shard_map/all_gather | solution.py:146
  192.2 31.1 %copy-start.4 = (bf16[32,40,1024]{2,1,0:T(8,128)(2,1)}, bf16[32,40,1024]{2,1,0:T(8,128)(2,1)S(1)}, u32[]{:S(2)}) copy-start(bf16[32,40,1024]{2,1,0:T(8,128)(2,1)S(1)} %all-to-all-done.3) | copy-start | bytes 7864324
  194.8 218.4 %copy-start.105 = (f32[128]{0:T(128)}, f32[128]{0:T(128)S(1)}, u32[]{:S(2)}) copy-start(f32[128]{0:T(128)S(1)} %add_rsqrt_fusion.1) | copy-start | bytes 1540
  220.1 4.3 copy-start.50
  229.8 5.6 copy-start.53
  235.3 41.6 %all-to-all-start.4 = ((bf16[32,40,1024]{2,1,0:T(8,128)(2,1)}), bf16[32,40,1024]{2,1,0:T(8,128)(2,1)S(1)}, u32[]{:S(2)}, u32[]{:S(2)}) async-start(bf16[32,40,1024]{2,1,0:T(8,128)(2,1)} %bitcast.344), calls=%async_computation.4 | async-start | bytes 5242880 | tf_op jit(solution)/shard_map/all_to_all | solution.py:139
  276.9 22.5 %copy-start.2 = (bf16[32,40,1024]{2,1,0:T(8,128)(2,1)}, bf16[32,40,1024]{2,1,0:T(8,128)(2,1)S(1)}, u32[]{:S(2)}) copy-start(bf16[32,40,1024]{2,1,0:T(8,128)(2,1)S(1)} %all-to-all-done.4) | copy-start | bytes 7864324
  276.9 53.2 %all-to-all-start.5 = ((bf16[32,40,1024]{2,1,0:T(8,128)(2,1)}), bf16[32,40,1024]{2,1,0:T(8,128)(2,1)}, u32[]{:S(2)}, u32[]{:S(2)}) async-start(bf16[32,40,1024]{2,1,0:T(8,128)(2,1)} %bitcast.343), calls=%async_computation.5 | async-start | bytes 5242880 | tf_op jit(solution)/shard_map/all_to_all | solution.py:139
  330.1 38.1 %all-to-all-start.6 = ((bf16[32,40,1024]{2,1,0:T(8,128)(2,1)}), bf16[32,40,1024]{2,1,0:T(8,128)(2,1)S(1)}, u32[]{:S(2)}, u32[]{:S(2)}) async-start(bf16[32,40,1024]{2,1,0:T(8,128)(2,1)} %bitcast.355), calls=%async_computation.6 | async-start | bytes 5242880 | tf_op jit(solution)/shard_map/all_to_all | solution.py:139
  336.1 6.2 copy-start.63
  368.2 39.4 %all-to-all-start.7 = ((bf16[32,40,1024]{2,1,0:T(8,128)(2,1)}), bf16[32,40,1024]{2,1,0:T(8,128)(2,1)}, u32[]{:S(2)}, u32[]{:S(2)}) async-start(bf16[32,40,1024]{2,1,0:T(8,128)(2,1)} %bitcast.340), calls=%async_computation.7 | async-start | bytes 5242880 | tf_op jit(solution)/shard_map/all_to_all | solution.py:139
  375.1 38.1 %copy-start.97 = (s32[1024]{0:T(1024)}, s32[1024]{0:T(1024)S(1)}, u32[]{:S(2)}) copy-start(s32[1024]{0:T(1024)S(1)} %fusion.192) | copy-start | bytes 12292
  377.7 4.8 copy-start.3
  377.7 4.8 copy-start.18
  407.6 4.4 copy-start.34
  412.2 5.1 copy-start.11
  412.6 4.7 collective-permute-start.2
  430.0 4.9 copy-start.32
  437.3 42.0 %all-to-all-start.8 = ((bf16[32,40,1024]{2,1,0:T(8,128)(2,1)}), bf16[32,40,1024]{2,1,0:T(8,128)(2,1)}, u32[]{:S(2)}, u32[]{:S(2)}) async-start(bf16[32,40,1024]{2,1,0:T(8,128)(2,1)} %bitcast.341), calls=%async_computation.8 | async-start | bytes 5242880 | tf_op jit(solution)/shard_map/all_to_all | solution.py:139
  444.2 5.9 copy-start.92
  444.2 6.3 copy-start.98
  444.2 78.5 %reduce-scatter.6.cloned.1.call-start = ((), (), s32[]{:S(2)}) async-start(), calls=%async_computation.20 | async-start | bytes 4259840 | tf_op jit(solution)/shard_map/reduce_scatter | solution.py:196
  447.5 7.7 %collective-permute-start.3 = (bf16[512,2048]{1,0:T(8,128)(2,1)}, bf16[512,2048]{1,0:T(8,128)(2,1)}, u32[]{:S(2)}, u32[]{:S(2)}) collective-permute-start(bf16[512,2048]{1,0:T(8,128)(2,1)} %convolution_convert_fusion.7), channel_id=1, source_target_pairs={{0,1},{1,0},{2,3},{3,2},{4,5},{5,4},{6,7},{7,6},{8,9},{9,8},{10,11... | collective-permute-start | bytes 6291464 | tf_op jit(solution)/shard_map/ppermute | solution.py:186
  447.6 11.4 %copy-start.107 = (bf16[128]{0:T(256)(128)(2,1)}, bf16[128]{0:T(256)(128)(2,1)S(1)}, u32[]{:S(2)}) copy-start(bf16[128]{0:T(256)(128)(2,1)S(1)} %pad.34.clone) | copy-start | bytes 772
  450.1 5.1 copy-start.39
  450.1 5.1 copy-start.59
  450.1 5.1 copy-start.72
  453.0 1.6 collective-permute-start.4
  482.7 199.5 %reduce-scatter.8.cloned.1.call-start = ((), (), s32[]{:S(2)}) async-start(), calls=%async_computation.21 | async-start | bytes 1064960 | tf_op jit(solution)/shard_map/reduce_scatter | solution.py:197
  522.7 159.5 %reduce-scatter.14.cloned.1.call-start = ((), (), s32[]{:S(2)}) async-start(), calls=%async_computation.24 | async-start | bytes 3932160 | tf_op jit(solution)/shard_map/reduce_scatter | solution.py:151
  526.1 6.2 copy-start.61
  536.9 43.0 %all-to-all-start.9 = ((bf16[32,40,1024]{2,1,0:T(8,128)(2,1)}), bf16[32,40,1024]{2,1,0:T(8,128)(2,1)}, u32[]{:S(2)}, u32[]{:S(2)}) async-start(bf16[32,40,1024]{2,1,0:T(8,128)(2,1)} %bitcast.339), calls=%async_computation.9 | async-start | bytes 5242880 | tf_op jit(solution)/shard_map/all_to_all | solution.py:139
  545.2 137.0 %reduce-scatter.12.cloned.1.call-start = ((), (), s32[]{:S(2)}) async-start(), calls=%async_computation.23 | async-start | bytes 3932160 | tf_op jit(solution)/shard_map/reduce_scatter | solution.py:151
  551.4 4.5 copy-start.1
  551.4 4.5 copy-start.16
  561.0 21.3 %copy-start.96 = (f32[128]{0:T(128)S(1)}, f32[128]{0:T(128)}, u32[]{:S(2)}) copy-start(f32[128]{0:T(128)} %copy-done.95) | copy-start | bytes 1540
  583.7 4.4 copy-start.26
  583.7 4.4 copy-start.27
  583.7 4.4 copy-start.28
  586.2 6.5 collective-permute-start.5
  590.0 5.4 copy-start.94
  592.6 5.4 copy-start.86
  592.7 5.4 copy-start.91
  604.7 4.4 copy-start.23
  608.6 17.8 %collective-permute-start.6 = (bf16[512,2048]{1,0:T(8,128)(2,1)}, bf16[512,2048]{1,0:T(8,128)(2,1)}, u32[]{:S(2)}, u32[]{:S(2)}) collective-permute-start(bf16[512,2048]{1,0:T(8,128)(2,1)} %convolution_convert_fusion.6), channel_id=1, source_target_pairs={{0,1},{1,0},{2,3},{3,2},{4,5},{5,4},{6,7},{7,6},{8,9},{9,8},{10,11... | collective-permute-start | bytes 6291464 | tf_op jit(solution)/shard_map/ppermute | solution.py:186
  610.3 4.9 copy-start.71
  610.3 4.9 copy-start.99
  610.3 4.9 copy-start.108
  618.2 7.2 %collective-permute-start.7 = (bf16[512,128]{1,0:T(8,128)(2,1)}, bf16[512,128]{1,0:T(8,128)(2,1)}, u32[]{:S(2)}, u32[]{:S(2)}) collective-permute-start(bf16[512,128]{1,0:T(8,128)(2,1)} %slice.525), channel_id=1, source_target_pairs={{0,1},{1,0},{2,3},{3,2},{4,5},{5,4},{6,7},{7,6},{8,9},{9,8},{10,11... | collective-permute-start | bytes 393224 | tf_op jit(solution)/shard_map/ppermute | solution.py:186
  618.2 25.8 %all-to-all-start.11 = ((bf16[64,8,1024]{2,1,0:T(8,128)(2,1)}), bf16[64,8,1024]{2,1,0:T(8,128)(2,1)}, u32[]{:S(2)}, u32[]{:S(2)}) async-start(bf16[64,8,1024]{2,1,0:T(8,128)(2,1)} %bitcast.350), calls=%async_computation.14 | async-start | bytes 2097152 | tf_op jit(solution)/shard_map/all_to_all | solution.py:191
  644.0 36.1 %all-to-all-start.10 = ((bf16[64,8,2176]{2,1,0:T(8,128)(2,1)}), bf16[64,8,2176]{2,1,0:T(8,128)(2,1)}, u32[]{:S(2)}, u32[]{:S(2)}) async-start(bf16[64,8,2176]{2,1,0:T(8,128)(2,1)} %maximum_bitcast_fusion), calls=%async_computation.10 | async-start | bytes 4456448 | tf_op jit(solution)/shard_map/all_to_all | solution.py:191
  650.4 50.6 %reduce-scatter.10.cloned.1.call-start = ((), (), s32[]{:S(2)}) async-start(), calls=%async_computation.22 | async-start | bytes 266240 | tf_op jit(solution)/shard_map/reduce_scatter | solution.py:198
  (75 other events, 170.8 us)
Sparse Core Ops, SparseCore 0:
  62.2 46.1 all-gather.3
  112.0 106.6 all-gather.5
  225.9 64.3 all-gather.7
  482.8 39.8 reduce-scatter.5
  525.0 19.9 reduce-scatter.7
  547.4 53.5 reduce-scatter.13
  603.5 48.9 reduce-scatter.11
  682.3 18.6 reduce-scatter.9

commit v5 on v4

--- a/solution.py
+++ b/solution.py
@@ -192,12 +192,6 @@
     return jnp.sum(parts.astype(jnp.float32), axis=0)
 
 
-def chip_sum_aside(parts):
-    parts = lax.psum_scatter(parts, Z_AXES, scatter_dimension=0, tiled=True)
-    parts = lax.psum_scatter(parts, "x", scatter_dimension=0, tiled=True)
-    return lax.psum_scatter(parts, "y", scatter_dimension=0, tiled=True).astype(jnp.float32)
-
-
 def norm_back(grad_norm, normed, inverse):
     return inverse * (grad_norm - normed * jnp.mean(grad_norm * normed, axis=-1, keepdims=True))
 
@@ -380,7 +374,6 @@
     mixed_gradient = lax.dot_general(
         grad_low, out_full, (((1,), (1,)), ((), ())), preferred_element_type=jnp.float32
     ).astype(jnp.bfloat16)
-    mixed_gradient, proj_sum = lax.optimization_barrier((mixed_gradient, proj_sum))
     mixed_gradient = jnp.where(live[:, None] > 0.5, mixed_gradient, jnp.zeros_like(mixed_gradient))
     mixed_gradient = mixed_gradient.reshape(
         token_total, KEY_VALUE_HEADS, QUERY_HEADS // KEY_VALUE_HEADS, HEAD_SIZE
@@ -453,16 +446,16 @@
         )
         for layer in layers
     ]
-    lead = [own_dense[0][member].reshape(8, -1) for member in (0, 2, 3, 4)]
+    lead = [part.reshape(8, -1) for part in own_dense[0]]
     fill = jnp.zeros((8, 128 - E - 2), jnp.bfloat16)
-    lead_first = sent_by_chips(jnp.concatenate(lead + [fill], axis=1))
-    lead_first, out_own, expert_in, expert_out = lax.optimization_barrier(
-        (lead_first, own_dense[0][1], expert_in, expert_out)
-    )
-    lead_first = cut_weights(lead_first, (2048, E, 1, 1))
-    out_first = sent_by_chips(out_own)
-    dense = [(lead_first[0], out_first) + lead_first[1:], None]
+    lead = sent_by_chips(jnp.concatenate(lead + [fill], axis=1))
+    dense = [cut_weights(lead, DENSE_WIDTHS), None]
     experts = [gather_expert(expert_in[0], expert_out[0]), None]
+    experts[0], own_dense = lax.optimization_barrier((experts[0], own_dense))
+    gathered = sent_together(own_dense[1], AXES)
+    gathered, expert_in, expert_out = lax.optimization_barrier((gathered, expert_in, expert_out))
+    dense[1] = cut_weights(gathered, DENSE_WIDTHS)
+    experts[1] = gather_expert(expert_in[1], expert_out[1])
     position, live_row, allowed = seq_layout(seq_lengths, seq_owner, device)
     live = live_row.astype(jnp.float32)
     cosine_table, sine_values = rope_tables(position)
@@ -477,14 +470,6 @@
         mixed_low = attn_stash[-1]
         hidden = hidden + jnp.dot(mixed_low, dense[layer][1], preferred_element_type=jnp.float32)
         rows, route_stash = route_rows(hidden, dense[layer], routed, chosen)
-        if layer == 0:
-            rows, own_dense = lax.optimization_barrier((rows, own_dense))
-            gathered = sent_together(own_dense[1], AXES)
-            gathered, expert_in, expert_out = lax.optimization_barrier(
-                (gathered, expert_in, expert_out)
-            )
-            dense[1] = cut_weights(gathered, DENSE_WIDTHS)
-            experts[1] = gather_expert(expert_in[1], expert_out[1])
         rows_here = trade_rows(rows)
         moved = reorder(attn_stash[2], order), reorder(mixed_low, order)
         grad_rows = None
@@ -505,15 +490,16 @@
         if grad_rows is None:
             slots = slot_gradients(grad_hidden, route_stash[-1])
             grad_rows, sums = lax.optimization_barrier((trade_rows(slots), sums))
-            sums.append(jnp.zeros_like(sums[-1]))
-            done_last = chip_sum_aside(jnp.concatenate(sums, axis=1))[:, :-128]
+            joined = jnp.concatenate(sums, axis=1)
         grad_in_rows, expert_grads = feed_backward(grad_rows, rows_here, pre, experts[layer])
         grad_slots = trade_rows(grad_in_rows)
         router_grad, grad_routed = route_backward(
             grad_hidden, dense[layer], chosen, returned, route_stash
         )
-        grad_slots, expert_grads = lax.optimization_barrier((grad_slots, expert_grads))
-        expert_grads = scatter_expert(expert_grads)
+        expert_sums[layer] = scatter_expert(expert_grads)
+        if layer != last:
+            grad_slots, joined = lax.optimization_barrier((grad_slots, joined))
+            done_last = chip_sum(joined)
         grad_h1, gain_two_grad = rows_backward(
             grad_hidden, dense[layer], chosen, grad_slots, grad_routed, route_stash
         )
@@ -521,14 +507,9 @@
             grad_h1, dense[layer], live, allowed, cosine_table, sine_values, attn_stash, *moved
         )
         small = small_halves(router_grad, gain_one_grad, gain_two_grad, order)
-        if layer == last:
-            sums = [core_sum(qkv_halves), proj_sum, core_sum(small)]
-        else:
-            proj_done = chip_sum(proj_sum)
-            sums = [core_sum(halves) for halves in (qkv_halves, small)]
-            done = chip_sum(jnp.concatenate(sums, axis=1))
-        expert_sums[layer] = expert_grads
-    first = [done[:, :2048], proj_done, done[:, 2048:]]
+        sums = [core_sum(qkv_halves), proj_sum, core_sum(small)]
+    done = chip_sum(jnp.concatenate(sums, axis=1))
+    first = [done[:, :2048], done[:, 2048:3072], done[:, 3072:]]
     second = [done_last[:, :2048], done_last[:, 2048:3072], done_last[:, 3072:]]
     qkv, proj, small = [jnp.stack(pair) for pair in zip(first, second)]
     both = jnp.stack(expert_sums).astype(jnp.float32)

time: 726 us -> 657 us (0.905)
  blocking collectives: 82.2 us -> 46.9 us
  waiting for transfers between devices: 299 us -> 270 us
  local copies, waits for them, and re-layouts: 23.4 us -> 33.4 us
    reduce_scatter x3 -> x0, waiting for transfers between devices: 54 us -> none  [the longest x1 40 us: chip_sum_aside(): parts = lax.psum_scatter(parts, Z_AXES, scatter_dimension=0, tiled=True)]
    all_gather x2, waiting for transfers between devices: 0.02 us -> 49.2 us  [gather_expert(): return lax.all_gather(both, GROUP_AXES, axis=0, tiled=True)]
    all_to_all x1 -> x0, blocking collectives: 42.1 us -> none  [sent_by_chips(): lax.all_to_all(copies, CHIP_AXES, split_axis=0, concat_axis=0, tiled=True)]
    all_to_all x7, waiting for transfers between devices: 163 us -> 134 us  [trade_rows(): lax.all_to_all(rows.reshape(E, ROOM, MODEL_WIDTH), EXPERT_AXES, split_axi...]
    all_gather x1, waiting for transfers between devices: 23.9 us -> 0.01 us  [sent_together(): return lax.all_gather(both, axis, axis=0, tiled=True)]
    all_to_all x1, waiting for transfers between devices: 15.6 us -> 38 us  [sent_by_chips(): lax.all_to_all(copies, CHIP_AXES, split_axis=0, concat_axis=0, tiled=True)]
    all_to_all x2, waiting for transfers between devices: 38.4 us -> 47.4 us  [chip_sum(): lax.all_to_all(parts, Z_AXES + ('x', 'y'), split_axis=0, concat_axis=0, t...]
  transfers between devices with their start and end apart: 26 -> 22, of which waited for: 15 -> 12; matrix products, arithmetic and copies ran while one was open for 25% -> 28% of each run, Pallas kernels for 0% -> 0%
where the time goes in v5:
time: 657 us; the launch traced here: 648 us
  waiting for transfers between devices  270 us (41%)
  matrix products  158 us (24%)
  starting transfers between devices  83 us (13%)
  blocking collectives  46.9 us (7%)
  other arithmetic  40.8 us (6%)
  local copies, waits for them, and re-layouts  33.4 us (5%)
  between operations  16.3 us (2%)
    all_to_all x7, waiting for transfers between devices, trade_rows(): lax.all_to_all(rows.reshape(E, ROOM, MODEL_WIDTH), EXPERT_AXES, split_axi...  134 us
    all_to_all x7, starting transfers between devices, trade_rows(): lax.all_to_all(rows.reshape(E, ROOM, MODEL_WIDTH), EXPERT_AXES, split_axi...  55.9 us
    all_gather x2, waiting for transfers between devices, gather_expert(): return lax.all_gather(both, GROUP_AXES, axis=0, tiled=True)  49.2 us
    all_to_all x2, waiting for transfers between devices, chip_sum(): lax.all_to_all(parts, Z_AXES + ('x', 'y'), split_axis=0, concat_axis=0, t...  47.4 us
    all_to_all x1, blocking collectives, trade_rows(): lax.all_to_all(rows.reshape(E, ROOM, MODEL_WIDTH), EXPERT_AXES, split_axi...  46.9 us
    all_to_all x1, waiting for transfers between devices, sent_by_chips(): lax.all_to_all(copies, CHIP_AXES, split_axis=0, concat_axis=0, tiled=True)  38 us
    all_to_all x2, starting transfers between devices, chip_sum(): lax.all_to_all(parts, Z_AXES + ('x', 'y'), split_axis=0, concat_axis=0, t...  13.7 us
  transfers between devices with their start and end apart: 22, of which 12 were waited for; matrix products, arithmetic and copies ran while one was open for 28% of the time, Pallas kernels for 0%

profile of v5, /device:TPU:2, one launch (start us, length us, event | category | flops | bytes accessed | tf_op | source)
XLA Modules:
  0.0 648.4 jit_solution(5263591260726467635)
XLA Ops:
  14.0 11.5 %all-to-all-start = ((bf16[64,8,3200]{2,1,0:T(8,128)(2,1)}), bf16[64,8,3200]{2,1,0:T(8,128)(2,1)S(1)}, u32[]{:S(2)}, u32[]{:S(2)}) async-start(bf16[64,8,3200]{2,1,0:T(8,128)(2,1)} %broadcast_in_dim.73), calls=%async_computation | async-start | bytes 6553600 | tf_op jit(solution)/shard_map/all_to_all | solution.py:44
  28.7 38.0 %all-to-all-done = bf16[64,8,3200]{2,1,0:T(8,128)(2,1)S(1)} async-done(((bf16[64,8,3200]{2,1,0:T(8,128)(2,1)}), bf16[64,8,3200]{2,1,0:T(8,128)(2,1)S(1)}, u32[]{:S(2)}, u32[]{:S(2)}) %all-to-all-start) | async-done | bytes 3276832 | tf_op jit(solution)/shard_map/all_to_all | solution.py:44
  74.6 13.2 %all-gather.4.cloned.1.call-done = bf16[512,3072]{1,0:T(8,128)(2,1)} async-done(((bf16[128,3072]{1,0:T(8,128)(2,1)}), bf16[512,3072]{1,0:T(8,128)(2,1)}) %all-gather.4.cloned.1.call-update) | async-done | bytes 3145744 | tf_op jit(solution)/shard_map/all_gather | solution.py:146
  93.4 2.5 select_bitcast_fusion.1
  102.3 2.2 multiply_reduce_fusion.10
  105.6 46.9 %all_to_all.55 = bf16[32,40,1024]{2,1,0:T(8,128)(2,1)S(1)} all-to-all(bf16[32,40,1024]{2,1,0:T(8,128)(2,1)S(1)} %bitcast.334), channel_id=1, replica_groups=mesh['x'=4,'y'=4,'zh'=2,'zl'=2,'c'=2] {'x','y','zh'}, dimensions={0} | all-to-all | bytes 5242880 | tf_op jit(solution)/shard_map/all_to_all | solution.py:139
  154.0 3.5 multiply_convert_fusion.5
  157.5 3.0 convolution_convert_fusion.4
  160.5 6.4 all-to-all-start.2
  169.4 33.7 %all-to-all-done.2 = bf16[32,40,1024]{2,1,0:T(8,128)(2,1)S(1)} async-done(((bf16[32,40,1024]{2,1,0:T(8,128)(2,1)}), bf16[32,40,1024]{2,1,0:T(8,128)(2,1)S(1)}, u32[]{:S(2)}, u32[]{:S(2)}) %all-to-all-start.2) | async-done | bytes 2621472 | tf_op jit(solution)/shard_map/all_to_all | solution.py:139
  203.0 2.5 multiply_reduce_fusion.9
  207.1 3.2 fusion.14
  216.1 2.2 multiply_reduce_fusion.8
  219.2 2.3 convolution_convert_fusion.2
  221.6 8.3 %all-to-all-start.3 = ((bf16[32,40,1024]{2,1,0:T(8,128)(2,1)}), bf16[32,40,1024]{2,1,0:T(8,128)(2,1)S(1)}, u32[]{:S(2)}, u32[]{:S(2)}) async-start(bf16[32,40,1024]{2,1,0:T(8,128)(2,1)} %bitcast.333), calls=%async_computation.3 | async-start | bytes 5242880 | tf_op jit(solution)/shard_map/all_to_all | solution.py:139
  232.3 3.3 convolution_convert_fusion.3
  235.6 27.8 %all-to-all-done.3 = bf16[32,40,1024]{2,1,0:T(8,128)(2,1)S(1)} async-done(((bf16[32,40,1024]{2,1,0:T(8,128)(2,1)}), bf16[32,40,1024]{2,1,0:T(8,128)(2,1)S(1)}, u32[]{:S(2)}, u32[]{:S(2)}) %all-to-all-start.3) | async-done | bytes 2621472 | tf_op jit(solution)/shard_map/all_to_all | solution.py:139
  263.4 7.0 %all-to-all-start.4 = ((bf16[32,40,1024]{2,1,0:T(8,128)(2,1)}), bf16[32,40,1024]{2,1,0:T(8,128)(2,1)}, u32[]{:S(2)}, u32[]{:S(2)}) async-start(bf16[32,40,1024]{2,1,0:T(8,128)(2,1)} %bitcast.332), calls=%async_computation.4 | async-start | bytes 5242880 | tf_op jit(solution)/shard_map/all_to_all | solution.py:139
  270.4 36.0 %all-gather.8.cloned.1.call-done = bf16[512,3072]{1,0:T(8,128)(2,1)} async-done(((bf16[128,3072]{1,0:T(8,128)(2,1)}), bf16[512,3072]{1,0:T(8,128)(2,1)}) %all-gather.8.cloned.1.call-update) | async-done | bytes 3145744 | tf_op jit(solution)/shard_map/all_gather | solution.py:146
  306.4 3.0 fusion.85
  309.4 3.4 multiply_convert_fusion.4
  313.9 3.1 convolution_convert_fusion.1
  317.0 9.7 %all-to-all-start.5 = ((bf16[32,40,1024]{2,1,0:T(8,128)(2,1)}), bf16[32,40,1024]{2,1,0:T(8,128)(2,1)S(1)}, u32[]{:S(2)}, u32[]{:S(2)}) async-start(bf16[32,40,1024]{2,1,0:T(8,128)(2,1)} %bitcast.339), calls=%async_computation.5 | async-start | bytes 5242880 | tf_op jit(solution)/shard_map/all_to_all | solution.py:139
  326.7 6.2 multiply_convert_fusion.2
  334.5 3.0 add_convert_fusion.1
  337.5 24.8 %all-to-all-done.5 = bf16[32,40,1024]{2,1,0:T(8,128)(2,1)S(1)} async-done(((bf16[32,40,1024]{2,1,0:T(8,128)(2,1)}), bf16[32,40,1024]{2,1,0:T(8,128)(2,1)S(1)}, u32[]{:S(2)}, u32[]{:S(2)}) %all-to-all-start.5) | async-done | bytes 2621472 | tf_op jit(solution)/shard_map/all_to_all | solution.py:139
  362.3 9.6 %all-to-all-start.6 = ((bf16[32,40,1024]{2,1,0:T(8,128)(2,1)}), bf16[32,40,1024]{2,1,0:T(8,128)(2,1)}, u32[]{:S(2)}, u32[]{:S(2)}) async-start(bf16[32,40,1024]{2,1,0:T(8,128)(2,1)} %bitcast.330), calls=%async_computation.6 | async-start | bytes 5242880 | tf_op jit(solution)/shard_map/all_to_all | solution.py:139
  372.6 2.7 fusion.58
  375.3 4.8 convolution_convert_fusion.12
  380.2 2.5 convolution_convert_fusion.13
  382.7 2.5 convolution_convert_fusion.14
  387.3 18.9 %all-to-all-done.6 = bf16[32,40,1024]{2,1,0:T(8,128)(2,1)} async-done(((bf16[32,40,1024]{2,1,0:T(8,128)(2,1)}), bf16[32,40,1024]{2,1,0:T(8,128)(2,1)}, u32[]{:S(2)}, u32[]{:S(2)}) %all-to-all-start.6) | async-done | bytes 2621472 | tf_op jit(solution)/shard_map/all_to_all | solution.py:139
  406.2 2.3 fusion.249
  410.9 3.1 fusion.65
  415.9 2.4 fusion.72
  421.4 3.9 multiply_reduce_fusion.5
  425.3 2.1 convolution_convert_fusion.7
  428.4 2.4 convolution_convert_fusion
  430.8 6.6 %all-to-all-start.7 = ((bf16[32,40,1024]{2,1,0:T(8,128)(2,1)}), bf16[32,40,1024]{2,1,0:T(8,128)(2,1)}, u32[]{:S(2)}, u32[]{:S(2)}) async-start(bf16[32,40,1024]{2,1,0:T(8,128)(2,1)} %bitcast.331), calls=%async_computation.7 | async-start | bytes 5242880 | tf_op jit(solution)/shard_map/all_to_all | solution.py:139
  437.6 3.1 pad_maximum_fusion.3
  441.4 1.9 fusion.59
  443.4 2.6 convolution_convert_fusion.11
  450.6 3.0 fusion.5
  456.7 2.7 add_convert_fusion.5
  459.4 3.7 add_convert_fusion.3
  463.0 9.6 %all-to-all-done.7 = bf16[32,40,1024]{2,1,0:T(8,128)(2,1)} async-done(((bf16[32,40,1024]{2,1,0:T(8,128)(2,1)}), bf16[32,40,1024]{2,1,0:T(8,128)(2,1)}, u32[]{:S(2)}, u32[]{:S(2)}) %all-to-all-start.7) | async-done | bytes 2621472 | tf_op jit(solution)/shard_map/all_to_all | solution.py:139
  472.6 6.3 multiply_convert_fusion
  480.4 3.1 add_convert_fusion
  483.5 8.2 %all-to-all-start.8 = ((bf16[32,40,1024]{2,1,0:T(8,128)(2,1)}), bf16[32,40,1024]{2,1,0:T(8,128)(2,1)}, u32[]{:S(2)}, u32[]{:S(2)}) async-start(bf16[32,40,1024]{2,1,0:T(8,128)(2,1)} %bitcast.329), calls=%async_computation.8 | async-start | bytes 5242880 | tf_op jit(solution)/shard_map/all_to_all | solution.py:139
  493.6 3.8 convolution_convert_fusion.15
  503.2 3.3 pad_maximum_fusion.1
  506.5 19.7 %all-to-all-done.8 = bf16[32,40,1024]{2,1,0:T(8,128)(2,1)} async-done(((bf16[32,40,1024]{2,1,0:T(8,128)(2,1)}), bf16[32,40,1024]{2,1,0:T(8,128)(2,1)}, u32[]{:S(2)}, u32[]{:S(2)}) %all-to-all-start.8) | async-done | bytes 2621472 | tf_op jit(solution)/shard_map/all_to_all | solution.py:139
  526.2 2.4 fusion.250
  531.5 3.1 fusion.62
  539.1 6.8 %all-to-all-start.10 = ((bf16[64,8,3200]{2,1,0:T(8,128)(2,1)}), bf16[64,8,3200]{2,1,0:T(8,128)(2,1)}, u32[]{:S(2)}, u32[]{:S(2)}) async-start(bf16[64,8,3200]{2,1,0:T(8,128)(2,1)} %bitcast.328), calls=%async_computation.10 | async-start | bytes 6553600 | tf_op jit(solution)/shard_map/all_to_all | solution.py:191
  547.0 2.5 fusion.73
  549.6 3.1 convolution_convert_fusion.6
  558.6 4.7 fusion.106
  568.3 2.3 add_convert_fusion.2
  572.4 15.4 %all-to-all-done.10 = bf16[64,8,3200]{2,1,0:T(8,128)(2,1)} async-done(((bf16[64,8,3200]{2,1,0:T(8,128)(2,1)}), bf16[64,8,3200]{2,1,0:T(8,128)(2,1)}, u32[]{:S(2)}, u32[]{:S(2)}) %all-to-all-start.10) | async-done | bytes 3276832 | tf_op jit(solution)/shard_map/all_to_all | solution.py:191
  587.8 7.0 %all-to-all-start.9 = ((bf16[64,8,3200]{2,1,0:T(8,128)(2,1)}), bf16[64,8,3200]{2,1,0:T(8,128)(2,1)}, u32[]{:S(2)}, u32[]{:S(2)}) async-start(bf16[64,8,3200]{2,1,0:T(8,128)(2,1)} %maximum_bitcast_fusion), calls=%async_computation.9 | async-start | bytes 6553600 | tf_op jit(solution)/shard_map/all_to_all | solution.py:191
  597.1 2.4 convert_reduce_fusion
  604.4 32.0 %all-to-all-done.9 = bf16[64,8,3200]{2,1,0:T(8,128)(2,1)} async-done(((bf16[64,8,3200]{2,1,0:T(8,128)(2,1)}), bf16[64,8,3200]{2,1,0:T(8,128)(2,1)}, u32[]{:S(2)}, u32[]{:S(2)}) %all-to-all-start.9) | async-done | bytes 3276832 | tf_op jit(solution)/shard_map/all_to_all | solution.py:191
  636.4 2.4 convert_reduce_fusion.1
  (452 shorter events, 106.6 us)
Async XLA Ops:
  14.0 52.6 %all-to-all-start = ((bf16[64,8,3200]{2,1,0:T(8,128)(2,1)}), bf16[64,8,3200]{2,1,0:T(8,128)(2,1)S(1)}, u32[]{:S(2)}, u32[]{:S(2)}) async-start(bf16[64,8,3200]{2,1,0:T(8,128)(2,1)} %broadcast_in_dim.73), calls=%async_computation | async-start | bytes 6553600 | tf_op jit(solution)/shard_map/all_to_all | solution.py:44
  25.6 41.1 %copy-start.120 = (s32[512]{0:T(512)S(1)}, s32[512]{0:T(512)}, u32[]{:S(2)}) copy-start(s32[512]{0:T(512)} %param.15) | copy-start | bytes 6148
  25.6 47.6 %copy-start.36 = (bf16[128,1024]{1,0:T(8,128)(2,1)S(1)}, bf16[128,1024]{1,0:T(8,128)(2,1)}, u32[]{:S(2)}) copy-start(bf16[128,1024]{1,0:T(8,128)(2,1)} %param.12) | copy-start | bytes 786436
  25.6 62.2 %all-gather.4.cloned.1.call-start = ((), (), s32[]{:S(2)}) async-start(), calls=%async_computation.13 | async-start | bytes 3932160 | tf_op jit(solution)/shard_map/all_gather | solution.py:146
  28.7 176.9 %all-gather.6.cloned.1.call-start = ((), (), s32[]{:S(2)}) async-start(), calls=%async_computation.14 | async-start | bytes 6604800 | tf_op jit(solution)/shard_map/all_gather | solution.py:38
  66.7 26.7 %collective-permute-start = (bf16[64,8,3200]{2,1,0:T(8,128)(2,1)S(1)}, bf16[64,8,3200]{2,1,0:T(8,128)(2,1)}, u32[]{:S(2)}, u32[]{:S(2)}) collective-permute-start(bf16[64,8,3200]{2,1,0:T(8,128)(2,1)S(1)} %all-to-all-done), channel_id=1, source_target_pairs={{0,1},{1,0},{2,3},{3,2},{4,5},{5,4},{6,7},{7,6},{8,9},{9,8},{10,11... | collective-permute-start | bytes 9830408 | tf_op jit(solution)/shard_map/ppermute | solution.py:45
  73.3 23.7 %copy-start.121 = (f32[128]{0:T(128)}, f32[128]{0:T(128)S(1)}, u32[]{:S(2)}) copy-start(f32[128]{0:T(128)S(1)} %add_rsqrt_fusion.3) | copy-start | bytes 1540
  104.5 98.6 %copy-start.7 = (f32[128,1024]{1,0:T(8,128)}, f32[128,1024]{1,0:T(8,128)S(1)}, u32[]{:S(2)}) copy-start(f32[128,1024]{1,0:T(8,128)S(1)} %get-tuple-element.103) | copy-start | bytes 1572868
  104.5 47.9 %copy-start.113 = (f32[128]{0:T(128)}, f32[128]{0:T(128)S(1)}, u32[]{:S(2)}) copy-start(f32[128]{0:T(128)S(1)} %add_rsqrt_fusion.2) | copy-start | bytes 1540
  104.6 47.8 %copy-start.25 = (bf16[128,1024]{1,0:T(8,128)(2,1)}, bf16[128,1024]{1,0:T(8,128)(2,1)S(1)}, u32[]{:S(2)}) copy-start(bf16[128,1024]{1,0:T(8,128)(2,1)S(1)} %multiply_convert_fusion.10) | copy-start | bytes 786436
  105.6 46.9 %copy-start.64 = (bf16[512,3072]{1,0:T(8,128)(2,1)S(1)}, bf16[512,3072]{1,0:T(8,128)(2,1)}, u32[]{:S(2)}) copy-start(bf16[512,3072]{1,0:T(8,128)(2,1)} %all-gather.4.cloned.1.call-done) | copy-start | bytes 9437188
  160.5 42.5 %all-to-all-start.2 = ((bf16[32,40,1024]{2,1,0:T(8,128)(2,1)}), bf16[32,40,1024]{2,1,0:T(8,128)(2,1)S(1)}, u32[]{:S(2)}, u32[]{:S(2)}) async-start(bf16[32,40,1024]{2,1,0:T(8,128)(2,1)} %bitcast.340), calls=%async_computation.2 | async-start | bytes 5242880 | tf_op jit(solution)/shard_map/all_to_all | solution.py:139
  167.0 139.4 %all-gather.8.cloned.1.call-start = ((), (), s32[]{:S(2)}) async-start(), calls=%async_computation.15 | async-start | bytes 3932160 | tf_op jit(solution)/shard_map/all_gather | solution.py:146
  168.3 41.9 %copy-start.96 = (f32[128]{0:T(128)}, f32[128]{0:T(128)S(1)}, u32[]{:S(2)}) copy-start(f32[128]{0:T(128)S(1)} %get-tuple-element.104) | copy-start | bytes 1540
  168.4 41.9 %copy-start.104 = (f32[128]{0:T(128)}, f32[128]{0:T(128)S(1)}, u32[]{:S(2)}) copy-start(f32[128]{0:T(128)S(1)} %fusion.179) | copy-start | bytes 1540
  203.0 7.2 %copy-start.4 = (bf16[32,40,1024]{2,1,0:T(8,128)(2,1)}, bf16[32,40,1024]{2,1,0:T(8,128)(2,1)S(1)}, u32[]{:S(2)}) copy-start(bf16[32,40,1024]{2,1,0:T(8,128)(2,1)S(1)} %all-to-all-done.2) | copy-start | bytes 7864324
  205.6 4.7 copy-start.126
  216.1 5.4 copy-start.55
  221.6 41.8 %all-to-all-start.3 = ((bf16[32,40,1024]{2,1,0:T(8,128)(2,1)}), bf16[32,40,1024]{2,1,0:T(8,128)(2,1)S(1)}, u32[]{:S(2)}, u32[]{:S(2)}) async-start(bf16[32,40,1024]{2,1,0:T(8,128)(2,1)} %bitcast.333), calls=%async_computation.3 | async-start | bytes 5242880 | tf_op jit(solution)/shard_map/all_to_all | solution.py:139
  231.2 155.0 %copy-start.98 = (f32[128]{0:T(128)}, f32[128]{0:T(128)S(1)}, u32[]{:S(2)}) copy-start(f32[128]{0:T(128)S(1)} %get-tuple-element.114) | copy-start | bytes 1540
  231.2 155.0 %copy-start.106 = (f32[128]{0:T(128)}, f32[128]{0:T(128)S(1)}, u32[]{:S(2)}) copy-start(f32[128]{0:T(128)S(1)} %fusion.181) | copy-start | bytes 1540
  263.4 46.0 %copy-start.2 = (bf16[32,40,1024]{2,1,0:T(8,128)(2,1)}, bf16[32,40,1024]{2,1,0:T(8,128)(2,1)S(1)}, u32[]{:S(2)}) copy-start(bf16[32,40,1024]{2,1,0:T(8,128)(2,1)S(1)} %all-to-all-done.3) | copy-start | bytes 7864324
  263.4 53.6 %all-to-all-start.4 = ((bf16[32,40,1024]{2,1,0:T(8,128)(2,1)}), bf16[32,40,1024]{2,1,0:T(8,128)(2,1)}, u32[]{:S(2)}, u32[]{:S(2)}) async-start(bf16[32,40,1024]{2,1,0:T(8,128)(2,1)} %bitcast.332), calls=%async_computation.4 | async-start | bytes 5242880 | tf_op jit(solution)/shard_map/all_to_all | solution.py:139
  317.0 45.3 %all-to-all-start.5 = ((bf16[32,40,1024]{2,1,0:T(8,128)(2,1)}), bf16[32,40,1024]{2,1,0:T(8,128)(2,1)S(1)}, u32[]{:S(2)}, u32[]{:S(2)}) async-start(bf16[32,40,1024]{2,1,0:T(8,128)(2,1)} %bitcast.339), calls=%async_computation.5 | async-start | bytes 5242880 | tf_op jit(solution)/shard_map/all_to_all | solution.py:139
  326.7 6.2 copy-start.67
  362.3 10.3 %copy-start.127 = (f32[128]{0:T(128)S(1)}, f32[128]{0:T(128)}, u32[]{:S(2)}) copy-start(f32[128]{0:T(128)} %copy-done.126) | copy-start | bytes 1540
  362.3 43.8 %all-to-all-start.6 = ((bf16[32,40,1024]{2,1,0:T(8,128)(2,1)}), bf16[32,40,1024]{2,1,0:T(8,128)(2,1)}, u32[]{:S(2)}, u32[]{:S(2)}) async-start(bf16[32,40,1024]{2,1,0:T(8,128)(2,1)} %bitcast.330), calls=%async_computation.6 | async-start | bytes 5242880 | tf_op jit(solution)/shard_map/all_to_all | solution.py:139
  372.6 7.6 %copy-start.115 = (s32[1024]{0:T(1024)}, s32[1024]{0:T(1024)S(1)}, u32[]{:S(2)}) copy-start(s32[1024]{0:T(1024)S(1)} %fusion.207) | copy-start | bytes 12292
  375.3 4.8 copy-start.3
  375.3 4.8 copy-start.22
  409.9 6.0 copy-start.103
  427.4 32.0 %collective-permute-start.1 = (bf16[512,2048]{1,0:T(8,128)(2,1)}, bf16[512,2048]{1,0:T(8,128)(2,1)}, u32[]{:S(2)}, u32[]{:S(2)}) collective-permute-start(bf16[512,2048]{1,0:T(8,128)(2,1)} %convolution_convert_fusion.7), channel_id=1, source_target_pairs={{0,1},{1,0},{2,3},{3,2},{4,5},{5,4},{6,7},{7,6},{8,9},{9,8},{10,11... | collective-permute-start | bytes 6291464 | tf_op jit(solution)/shard_map/ppermute | solution.py:186
  430.8 41.8 %all-to-all-start.7 = ((bf16[32,40,1024]{2,1,0:T(8,128)(2,1)}), bf16[32,40,1024]{2,1,0:T(8,128)(2,1)}, u32[]{:S(2)}, u32[]{:S(2)}) async-start(bf16[32,40,1024]{2,1,0:T(8,128)(2,1)} %bitcast.331), calls=%async_computation.7 | async-start | bytes 5242880 | tf_op jit(solution)/shard_map/all_to_all | solution.py:139
  437.4 162.2 %reduce-scatter.5.cloned.1.call-start = ((), (), s32[]{:S(2)}) async-start(), calls=%async_computation.17 | async-start | bytes 3932160 | tf_op jit(solution)/shard_map/reduce_scatter | solution.py:151
  440.7 5.2 copy-start.92
  440.7 5.2 copy-start.122
  441.4 4.6 copy-start.38
  441.4 6.3 copy-start.28
  443.3 7.2 %copy-start.129 = (bf16[128]{0:T(256)(128)(2,1)S(1)}, bf16[128]{0:T(256)(128)(2,1)}, u32[]{:S(2)}) copy-start(bf16[128]{0:T(256)(128)(2,1)} %pad.34.clone) | copy-start | bytes 772
  446.0 10.7 %collective-permute-start.2 = (bf16[512,1024]{1,0:T(8,128)(2,1)}, bf16[512,1024]{1,0:T(8,128)(2,1)}, u32[]{:S(2)}, u32[]{:S(2)}) collective-permute-start(bf16[512,1024]{1,0:T(8,128)(2,1)} %convolution_convert_fusion.11), channel_id=1, source_target_pairs={{0,1},{1,0},{2,3},{3,2},{4,5},{5,4},{6,7},{7,6},{8,9},{9,8},{10,11... | collective-permute-start | bytes 3145736 | tf_op jit(solution)/shard_map/ppermute | solution.py:186
  453.6 2.4 collective-permute-start.3
  472.6 6.3 copy-start.65
  483.5 8.4 %copy-start.97 = (f32[128]{0:T(128)S(1)}, f32[128]{0:T(128)}, u32[]{:S(2)}) copy-start(f32[128]{0:T(128)} %copy-done.96) | copy-start | bytes 1540
  483.5 8.4 %copy-start.105 = (f32[128]{0:T(128)S(1)}, f32[128]{0:T(128)}, u32[]{:S(2)}) copy-start(f32[128]{0:T(128)} %copy-done.104) | copy-start | bytes 1540
  483.5 42.7 %all-to-all-start.8 = ((bf16[32,40,1024]{2,1,0:T(8,128)(2,1)}), bf16[32,40,1024]{2,1,0:T(8,128)(2,1)}, u32[]{:S(2)}, u32[]{:S(2)}) async-start(bf16[32,40,1024]{2,1,0:T(8,128)(2,1)} %bitcast.329), calls=%async_computation.8 | async-start | bytes 5242880 | tf_op jit(solution)/shard_map/all_to_all | solution.py:139
  491.7 107.9 %reduce-scatter.3.cloned.1.call-start = ((), (), s32[]{:S(2)}) async-start(), calls=%async_computation.16 | async-start | bytes 3932160 | tf_op jit(solution)/shard_map/reduce_scatter | solution.py:151
  506.5 22.1 %copy-start.114 = (f32[128]{0:T(128)S(1)}, f32[128]{0:T(128)}, u32[]{:S(2)}) copy-start(f32[128]{0:T(128)} %copy-done.113) | copy-start | bytes 1540
  530.5 5.3 copy-start.101
  539.1 48.7 %all-to-all-start.10 = ((bf16[64,8,3200]{2,1,0:T(8,128)(2,1)}), bf16[64,8,3200]{2,1,0:T(8,128)(2,1)}, u32[]{:S(2)}, u32[]{:S(2)}) async-start(bf16[64,8,3200]{2,1,0:T(8,128)(2,1)} %bitcast.328), calls=%async_computation.10 | async-start | bytes 6553600 | tf_op jit(solution)/shard_map/all_to_all | solution.py:191
  549.6 6.3 copy-start.26
  552.7 5.6 copy-start.108
  552.7 5.8 copy-start.39
  552.7 5.8 copy-start.93
  552.7 15.5 %collective-permute-start.4 = (bf16[512,2048]{1,0:T(8,128)(2,1)}, bf16[512,2048]{1,0:T(8,128)(2,1)}, u32[]{:S(2)}, u32[]{:S(2)}) collective-permute-start(bf16[512,2048]{1,0:T(8,128)(2,1)} %convolution_convert_fusion.6), channel_id=1, source_target_pairs={{0,1},{1,0},{2,3},{3,2},{4,5},{5,4},{6,7},{7,6},{8,9},{9,8},{10,11... | collective-permute-start | bytes 6291464 | tf_op jit(solution)/shard_map/ppermute | solution.py:186
  555.1 11.4 %collective-permute-start.5 = (bf16[512,1024]{1,0:T(8,128)(2,1)}, bf16[512,1024]{1,0:T(8,128)(2,1)}, u32[]{:S(2)}, u32[]{:S(2)}) collective-permute-start(bf16[512,1024]{1,0:T(8,128)(2,1)} %convolution_convert_fusion.10), channel_id=1, source_target_pairs={{0,1},{1,0},{2,3},{3,2},{4,5},{5,4},{6,7},{7,6},{8,9},{9,8},{10,11... | collective-permute-start | bytes 3145736 | tf_op jit(solution)/shard_map/ppermute | solution.py:186
  558.5 4.9 copy-start.72
  558.6 4.9 copy-start.118
  558.6 4.9 copy-start.130
  563.5 4.7 copy-start.44
  563.5 4.7 copy-start.63
  563.5 4.7 copy-start.74
  565.0 1.4 collective-permute-start.6
  572.4 22.4 %copy-start.32 = (bf16[128,1280]{1,0:T(8,128)(2,1)S(1)}, bf16[128,1280]{1,0:T(8,128)(2,1)}, u32[]{:S(2)}) copy-start(bf16[128,1280]{1,0:T(8,128)(2,1)} %copy-done.31) | copy-start | bytes 983044
  587.8 48.5 %all-to-all-start.9 = ((bf16[64,8,3200]{2,1,0:T(8,128)(2,1)}), bf16[64,8,3200]{2,1,0:T(8,128)(2,1)}, u32[]{:S(2)}, u32[]{:S(2)}) async-start(bf16[64,8,3200]{2,1,0:T(8,128)(2,1)} %maximum_bitcast_fusion), calls=%async_computation.9 | async-start | bytes 6553600 | tf_op jit(solution)/shard_map/all_to_all | solution.py:191
  (93 other events, 205.4 us)
Sparse Core Ops, SparseCore 0:
  28.8 58.9 all-gather.3
  91.3 95.0 all-gather.5
  213.1 93.2 all-gather.7
  440.9 52.8 reduce-scatter.4
  502.4 78.3 reduce-scatter.2

commit v6 on v5

--- a/solution.py
+++ b/solution.py
@@ -27,7 +27,6 @@
 EXPERT_AXES = ("x", "y", "zh")
 CHIP_AXES = ("x", "y", "zh", "zl")
 Z_AXES = ("zh", "zl")
-GROUP_AXES = ("zl", "c")
 DENSE_WIDTHS = (2048, 1024, E, 1, 1)
 HALF = MODEL_WIDTH // 2
 SWAP = [(0, 1), (1, 0)]
@@ -38,13 +37,14 @@
     return lax.all_gather(both, axis, axis=0, tiled=True)
 
 
-def sent_by_chips(own):
+def sent_by_chips(own, beside):
     core = lax.axis_index("c")
     copies = jnp.broadcast_to(own[None], (64,) + own.shape)
     mine = lax.all_to_all(copies, CHIP_AXES, split_axis=0, concat_axis=0, tiled=True)
+    mine, beside = lax.optimization_barrier((mine, beside))
     other = lax.ppermute(mine, "c", SWAP)
     pair = [jnp.where(core == 0, mine, other), jnp.where(core == 0, other, mine)]
-    return jnp.stack(pair, axis=1).reshape(MODEL_WIDTH, -1)
+    return jnp.stack(pair, axis=1).reshape(MODEL_WIDTH, -1), beside
 
 
 def cut_weights(gathered, widths):
@@ -143,12 +143,14 @@
 
 def gather_expert(own_in, own_out):
     both = jnp.concatenate([own_in, own_out], axis=1)
-    return lax.all_gather(both, GROUP_AXES, axis=0, tiled=True)
+    both = lax.all_gather(both, "zl", axis=0, tiled=True)
+    return lax.all_gather(both, "c", axis=0, tiled=True)
 
 
 def scatter_expert(grads):
     both = jnp.concatenate(grads, axis=1).astype(jnp.bfloat16)
-    return lax.psum_scatter(both, GROUP_AXES, scatter_dimension=0, tiled=True)
+    both = lax.psum_scatter(both, "c", scatter_dimension=0, tiled=True)
+    return lax.psum_scatter(both, "zl", scatter_dimension=0, tiled=True)
 
 
 def order_table():
@@ -186,9 +188,9 @@
     return (kept + lax.ppermute(given, "c", SWAP).astype(jnp.float32)).astype(jnp.bfloat16)
 
 
-def chip_sum(parts):
-    parts = parts.reshape(64, 8, -1)
-    parts = lax.all_to_all(parts, Z_AXES + ("x", "y"), split_axis=0, concat_axis=0, tiled=True)
+def chip_sum(parts, axes):
+    parts = parts.reshape(-1, 8, parts.shape[1])
+    parts = lax.all_to_all(parts, axes, split_axis=0, concat_axis=0, tiled=True)
     return jnp.sum(parts.astype(jnp.float32), axis=0)
 
 
@@ -448,7 +450,13 @@
     ]
     lead = [part.reshape(8, -1) for part in own_dense[0]]
     fill = jnp.zeros((8, 128 - E - 2), jnp.bfloat16)
-    lead = sent_by_chips(jnp.concatenate(lead + [fill], axis=1))
+    position, live_row, allowed = seq_layout(seq_lengths, seq_owner, device)
+    live = live_row.astype(jnp.float32)
+    cosine_table, sine_values = rope_tables(position)
+    routed, chosen = dispatch_table(routes, live_row)
+    beside = order, live, allowed, cosine_table, sine_values, routed, chosen
+    lead, beside = sent_by_chips(jnp.concatenate(lead + [fill], axis=1), beside)
+    order, live, allowed, cosine_table, sine_values, routed, chosen = beside
     dense = [cut_weights(lead, DENSE_WIDTHS), None]
     experts = [gather_expert(expert_in[0], expert_out[0]), None]
     experts[0], own_dense = lax.optimization_barrier((experts[0], own_dense))
@@ -456,10 +464,6 @@
     gathered, expert_in, expert_out = lax.optimization_barrier((gathered, expert_in, expert_out))
     dense[1] = cut_weights(gathered, DENSE_WIDTHS)
     experts[1] = gather_expert(expert_in[1], expert_out[1])
-    position, live_row, allowed = seq_layout(seq_lengths, seq_owner, device)
-    live = live_row.astype(jnp.float32)
-    cosine_table, sine_values = rope_tables(position)
-    routed, chosen = dispatch_table(routes, live_row)
     hidden = hidden_in.astype(jnp.float32)
     grad_hidden = cotangent.astype(jnp.float32)
     saved = []
@@ -491,6 +495,7 @@
             slots = slot_gradients(grad_hidden, route_stash[-1])
             grad_rows, sums = lax.optimization_barrier((trade_rows(slots), sums))
             joined = jnp.concatenate(sums, axis=1)
+            joined = lax.psum_scatter(joined, Z_AXES, scatter_dimension=0, tiled=True)
         grad_in_rows, expert_grads = feed_backward(grad_rows, rows_here, pre, experts[layer])
         grad_slots = trade_rows(grad_in_rows)
         router_grad, grad_routed = route_backward(
@@ -499,7 +504,7 @@
         expert_sums[layer] = scatter_expert(expert_grads)
         if layer != last:
             grad_slots, joined = lax.optimization_barrier((grad_slots, joined))
-            done_last = chip_sum(joined)
+            done_last = chip_sum(joined, ("x", "y"))
         grad_h1, gain_two_grad = rows_backward(
             grad_hidden, dense[layer], chosen, grad_slots, grad_routed, route_stash
         )
@@ -508,8 +513,9 @@
         )
         small = small_halves(router_grad, gain_one_grad, gain_two_grad, order)
         sums = [core_sum(qkv_halves), proj_sum, core_sum(small)]
-    done = chip_sum(jnp.concatenate(sums, axis=1))
-    first = [done[:, :2048], done[:, 2048:3072], done[:, 3072:]]
+    proj_done = chip_sum(sums.pop(1), Z_AXES + ("x", "y"))
+    done = chip_sum(jnp.concatenate(sums, axis=1), Z_AXES + ("x", "y"))
+    first = [done[:, :2048], proj_done, done[:, 2048:]]
     second = [done_last[:, :2048], done_last[:, 2048:3072], done_last[:, 3072:]]
     qkv, proj, small = [jnp.stack(pair) for pair in zip(first, second)]
     both = jnp.stack(expert_sums).astype(jnp.float32)

time: 657 us -> 680 us (1.035)
  matrix products: 158 us -> 165 us
    all_gather x2 -> x4, waiting for transfers between devices: 49.2 us -> 107 us  [the longest x2 89.8 us: gather_expert(): both = lax.all_gather(both, 'zl', axis=0, tiled=True)]
    all_to_all x1, waiting for transfers between devices: 38 us -> 0.01 us  [sent_by_chips(): lax.all_to_all(copies, CHIP_AXES, split_axis=0, concat_axis=0, tiled=True)]
    all_to_all x2 -> x3, waiting for transfers between devices: 47.4 us -> 12.5 us  [chip_sum(): parts = lax.all_to_all(parts, axes, split_axis=0, concat_axis=0, tiled=True)]
    reduce_scatter x2 -> x5, waiting for transfers between devices: 0.04 us -> 31.4 us  [the longest x2 27.7 us: scatter_expert(): return lax.psum_scatter(both, 'zl', scatter_dimension=0, tiled=True)]
    all_to_all x7, waiting for transfers between devices: 134 us -> 123 us  [trade_rows(): lax.all_to_all(rows.reshape(E, ROOM, MODEL_WIDTH), EXPERT_AXES, split_axi...]
    all_to_all x2 -> x3, starting transfers between devices: 13.7 us -> 21 us  [chip_sum(): parts = lax.all_to_all(parts, axes, split_axis=0, concat_axis=0, tiled=True)]
  transfers between devices with their start and end apart: 22 -> 28, of which waited for: 12 -> 15; matrix products, arithmetic and copies ran while one was open for 28% -> 31% of each run, Pallas kernels for 0% -> 0%
where the time goes in v6:
time: 680 us; the launch traced here: 669 us
  waiting for transfers between devices  276 us (41%)
  matrix products  165 us (24%)
  starting transfers between devices  87.6 us (13%)
  blocking collectives  46.6 us (7%)
  other arithmetic  40.3 us (6%)
  local copies, waits for them, and re-layouts  37.3 us (5%)
  between operations  16.4 us (2%)
    all_to_all x7, waiting for transfers between devices, trade_rows(): lax.all_to_all(rows.reshape(E, ROOM, MODEL_WIDTH), EXPERT_AXES, split_axi...  123 us
    all_gather x2, waiting for transfers between devices, gather_expert(): both = lax.all_gather(both, 'zl', axis=0, tiled=True)  89.8 us
    all_to_all x7, starting transfers between devices, trade_rows(): lax.all_to_all(rows.reshape(E, ROOM, MODEL_WIDTH), EXPERT_AXES, split_axi...  52.3 us
    all_to_all x1, blocking collectives, trade_rows(): lax.all_to_all(rows.reshape(E, ROOM, MODEL_WIDTH), EXPERT_AXES, split_axi...  46.6 us
    reduce_scatter x2, waiting for transfers between devices, scatter_expert(): return lax.psum_scatter(both, 'zl', scatter_dimension=0, tiled=True)  27.7 us
    all_to_all x3, starting transfers between devices, chip_sum(): parts = lax.all_to_all(parts, axes, split_axis=0, concat_axis=0, tiled=True)  21 us
    all_gather x2, waiting for transfers between devices, gather_expert(): return lax.all_gather(both, 'c', axis=0, tiled=True)  17.4 us
  transfers between devices with their start and end apart: 28, of which 15 were waited for; matrix products, arithmetic and copies ran while one was open for 31% of the time, Pallas kernels for 0%

profile of v6, /device:TPU:2, one launch (start us, length us, event | category | flops | bytes accessed | tf_op | source)
XLA Modules:
  0.0 668.9 jit_solution(18419286602771902616)
XLA Ops:
  12.4 11.8 %all-to-all-start = ((bf16[64,8,3200]{2,1,0:T(8,128)(2,1)}), bf16[64,8,3200]{2,1,0:T(8,128)(2,1)}, u32[]{:S(2)}, u32[]{:S(2)}) async-start(bf16[64,8,3200]{2,1,0:T(8,128)(2,1)} %broadcast_in_dim.73), calls=%async_computation | async-start | bytes 6553600 | tf_op jit(solution)/shard_map/all_to_all | solution.py:43
  27.9 50.2 %all-gather.6.cloned.1.call-done = bf16[256,3072]{1,0:T(8,128)(2,1)} async-done(((bf16[128,3072]{1,0:T(8,128)(2,1)}), bf16[256,3072]{1,0:T(8,128)(2,1)}) %all-gather.6.cloned.1.call-update) | async-done | bytes 1572880 | tf_op jit(solution)/shard_map/all_gather | solution.py:146
  79.7 17.1 %all-gather.8.cloned.1.call-done = bf16[512,3072]{1,0:T(8,128)(2,1)} async-done(((bf16[256,3072]{1,0:T(8,128)(2,1)}), bf16[512,3072]{1,0:T(8,128)(2,1)}) %all-gather.8.cloned.1.call-update) | async-done | bytes 3145744 | tf_op jit(solution)/shard_map/all_gather | solution.py:147
  97.9 3.5 select_bitcast_fusion.1
  110.3 2.4 fusion.235
  117.7 46.6 %all_to_all.60 = bf16[32,40,1024]{2,1,0:T(8,128)(2,1)S(1)} all-to-all(bf16[32,40,1024]{2,1,0:T(8,128)(2,1)S(1)} %bitcast.338), channel_id=1, replica_groups=mesh['x'=4,'y'=4,'zh'=2,'zl'=2,'c'=2] {'x','y','zh'}, dimensions={0} | all-to-all | bytes 5242880 | tf_op jit(solution)/shard_map/all_to_all | solution.py:139
  165.9 3.5 multiply_convert_fusion.5
  169.4 3.0 convolution_convert_fusion.4
  172.4 7.1 %all-to-all-start.2 = ((bf16[32,40,1024]{2,1,0:T(8,128)(2,1)}), bf16[32,40,1024]{2,1,0:T(8,128)(2,1)}, u32[]{:S(2)}, u32[]{:S(2)}) async-start(bf16[32,40,1024]{2,1,0:T(8,128)(2,1)} %bitcast.344), calls=%async_computation.2 | async-start | bytes 5242880 | tf_op jit(solution)/shard_map/all_to_all | solution.py:139
  181.9 32.4 %all-to-all-done.2 = bf16[32,40,1024]{2,1,0:T(8,128)(2,1)} async-done(((bf16[32,40,1024]{2,1,0:T(8,128)(2,1)}), bf16[32,40,1024]{2,1,0:T(8,128)(2,1)}, u32[]{:S(2)}, u32[]{:S(2)}) %all-to-all-start.2) | async-done | bytes 2621472 | tf_op jit(solution)/shard_map/all_to_all | solution.py:139
  214.3 2.5 multiply_reduce_fusion.9
  218.4 2.9 fusion.9
  235.6 2.3 multiply_reduce_fusion.8
  238.8 2.3 convolution_convert_fusion.2
  241.2 8.6 %all-to-all-start.3 = ((bf16[32,40,1024]{2,1,0:T(8,128)(2,1)}), bf16[32,40,1024]{2,1,0:T(8,128)(2,1)}, u32[]{:S(2)}, u32[]{:S(2)}) async-start(bf16[32,40,1024]{2,1,0:T(8,128)(2,1)} %bitcast.336), calls=%async_computation.3 | async-start | bytes 5242880 | tf_op jit(solution)/shard_map/all_to_all | solution.py:139
  249.8 39.6 %all-gather.12.cloned.1.call-done = bf16[256,3072]{1,0:T(8,128)(2,1)} async-done(((bf16[128,3072]{1,0:T(8,128)(2,1)}), bf16[256,3072]{1,0:T(8,128)(2,1)}) %all-gather.12.cloned.1.call-update) | async-done | bytes 1572880 | tf_op jit(solution)/shard_map/all_gather | solution.py:146
  292.7 3.3 convolution_convert_fusion.3
  296.1 10.5 %all-to-all-start.4 = ((bf16[32,40,1024]{2,1,0:T(8,128)(2,1)}), bf16[32,40,1024]{2,1,0:T(8,128)(2,1)}, u32[]{:S(2)}, u32[]{:S(2)}) async-start(bf16[32,40,1024]{2,1,0:T(8,128)(2,1)} %bitcast.337), calls=%async_computation.4 | async-start | bytes 5242880 | tf_op jit(solution)/shard_map/all_to_all | solution.py:139
  306.8 3.8 fusion.72
  310.5 6.0 multiply_convert_fusion.4
  317.6 3.0 convolution_convert_fusion.1
  320.7 20.2 %all-to-all-done.4 = bf16[32,40,1024]{2,1,0:T(8,128)(2,1)} async-done(((bf16[32,40,1024]{2,1,0:T(8,128)(2,1)}), bf16[32,40,1024]{2,1,0:T(8,128)(2,1)}, u32[]{:S(2)}, u32[]{:S(2)}) %all-to-all-start.4) | async-done | bytes 2621472 | tf_op jit(solution)/shard_map/all_to_all | solution.py:139
  340.9 6.7 %all-to-all-start.5 = ((bf16[32,40,1024]{2,1,0:T(8,128)(2,1)}), bf16[32,40,1024]{2,1,0:T(8,128)(2,1)}, u32[]{:S(2)}, u32[]{:S(2)}) async-start(bf16[32,40,1024]{2,1,0:T(8,128)(2,1)} %bitcast.343), calls=%async_computation.5 | async-start | bytes 5242880 | tf_op jit(solution)/shard_map/all_to_all | solution.py:139
  351.2 5.4 multiply_convert_fusion.2
  358.2 3.0 add_convert_fusion.1
  361.2 20.0 %all-to-all-done.5 = bf16[32,40,1024]{2,1,0:T(8,128)(2,1)} async-done(((bf16[32,40,1024]{2,1,0:T(8,128)(2,1)}), bf16[32,40,1024]{2,1,0:T(8,128)(2,1)}, u32[]{:S(2)}, u32[]{:S(2)}) %all-to-all-start.5) | async-done | bytes 2621472 | tf_op jit(solution)/shard_map/all_to_all | solution.py:139
  381.1 6.4 all-to-all-start.6
  387.7 3.8 convolution_convert_fusion.12
  391.5 3.4 convolution_convert_fusion.13
  395.0 3.3 convolution_convert_fusion.14
  400.1 2.7 fusion.13
  406.0 13.5 %all-to-all-done.6 = bf16[32,40,1024]{2,1,0:T(8,128)(2,1)} async-done(((bf16[32,40,1024]{2,1,0:T(8,128)(2,1)}), bf16[32,40,1024]{2,1,0:T(8,128)(2,1)}, u32[]{:S(2)}, u32[]{:S(2)}) %all-to-all-start.6) | async-done | bytes 2621472 | tf_op jit(solution)/shard_map/all_to_all | solution.py:139
  419.5 2.6 multiply_reduce_fusion.4
  423.8 3.1 fusion.51
  433.2 2.4 fusion.58
  435.7 4.2 multiply_reduce_fusion.5
  440.9 2.4 convolution_convert_fusion
  443.4 6.7 all-to-all-start.7
  450.1 3.3 convolution_convert_fusion.7
  465.2 2.7 add_convert_fusion.5
  467.9 3.6 add_convert_fusion.3
  471.6 10.5 %all-to-all-done.7 = bf16[32,40,1024]{2,1,0:T(8,128)(2,1)} async-done(((bf16[32,40,1024]{2,1,0:T(8,128)(2,1)}), bf16[32,40,1024]{2,1,0:T(8,128)(2,1)}, u32[]{:S(2)}, u32[]{:S(2)}) %all-to-all-start.7) | async-done | bytes 2621472 | tf_op jit(solution)/shard_map/all_to_all | solution.py:139
  482.1 3.3 pad_maximum_fusion.1
  485.5 3.8 convolution_convert_fusion.15
  489.3 5.7 multiply_convert_fusion
  500.1 3.3 fusion.80
  503.4 4.3 add_convert_fusion
  507.7 6.5 all-to-all-start.8
  516.9 2.7 convolution_multiply_fusion
  520.3 26.9 %all-to-all-done.8 = bf16[32,40,1024]{2,1,0:T(8,128)(2,1)} async-done(((bf16[32,40,1024]{2,1,0:T(8,128)(2,1)}), bf16[32,40,1024]{2,1,0:T(8,128)(2,1)}, u32[]{:S(2)}, u32[]{:S(2)}) %all-to-all-start.8) | async-done | bytes 2621472 | tf_op jit(solution)/shard_map/all_to_all | solution.py:139
  547.2 3.6 reduce-scatter.6.cloned.1.call-done
  550.8 2.3 fusion.239
  555.5 2.4 fusion.48
  563.8 3.2 convolution_convert_fusion.6
  571.2 7.3 %all-to-all-start.10 = ((bf16[16,8,3200]{2,1,0:T(8,128)(2,1)}), bf16[16,8,3200]{2,1,0:T(8,128)(2,1)}, u32[]{:S(2)}, u32[]{:S(2)}) async-start(bf16[16,8,3200]{2,1,0:T(8,128)(2,1)} %bitcast.363), calls=%async_computation.11 | async-start | bytes 1638400 | tf_op jit(solution)/shard_map/all_to_all | solution.py:193
  578.7 4.9 fusion.93
  585.7 2.7 fusion.63
  588.4 2.7 all-to-all-done.10
  591.1 7.9 %all-to-all-start.11 = ((bf16[64,8,1024]{2,1,0:T(8,128)(2,1)}), bf16[64,8,1024]{2,1,0:T(8,128)(2,1)}, u32[]{:S(2)}, u32[]{:S(2)}) async-start(bf16[64,8,1024]{2,1,0:T(8,128)(2,1)} %fusion.63), calls=%async_computation.12 | async-start | bytes 2097152 | tf_op jit(solution)/shard_map/all_to_all | solution.py:193
  599.0 3.0 fusion.41
  602.1 2.3 add_convert_fusion.2
  606.0 9.7 %all-to-all-done.11 = bf16[64,8,1024]{2,1,0:T(8,128)(2,1)} async-done(((bf16[64,8,1024]{2,1,0:T(8,128)(2,1)}), bf16[64,8,1024]{2,1,0:T(8,128)(2,1)}, u32[]{:S(2)}, u32[]{:S(2)}) %all-to-all-start.11) | async-done | bytes 1048608 | tf_op jit(solution)/shard_map/all_to_all | solution.py:193
  615.7 5.8 all-to-all-start.9
  627.0 27.7 %reduce-scatter.10.cloned.1.call-done = bf16[128,3072]{1,0:T(8,128)(2,1)} async-done(((bf16[256,3072]{1,0:T(8,128)(2,1)}), bf16[128,3072]{1,0:T(8,128)(2,1)}) %reduce-scatter.10.cloned.1.call-update) | async-done | bytes 786448 | tf_op jit(solution)/shard_map/reduce_scatter | solution.py:153
  (439 shorter events, 117.8 us)
Async XLA Ops:
  12.4 11.9 %copy-start.54 = (bf16[2,128,1024]{2,1,0:T(8,128)(2,1)S(1)}, bf16[2,128,1024]{2,1,0:T(8,128)(2,1)}, u32[]{:S(2)}) copy-start(bf16[2,128,1024]{2,1,0:T(8,128)(2,1)} %param.23) | copy-start | bytes 1572868
  12.4 11.9 %copy-start.45 = (bf16[2,128,2048]{2,1,0:T(8,128)(2,1)S(1)}, bf16[2,128,2048]{2,1,0:T(8,128)(2,1)}, u32[]{:S(2)}) copy-start(bf16[2,128,2048]{2,1,0:T(8,128)(2,1)} %param.22) | copy-start | bytes 3145732
  12.4 67.2 %all-to-all-start = ((bf16[64,8,3200]{2,1,0:T(8,128)(2,1)}), bf16[64,8,3200]{2,1,0:T(8,128)(2,1)}, u32[]{:S(2)}, u32[]{:S(2)}) async-start(bf16[64,8,3200]{2,1,0:T(8,128)(2,1)} %broadcast_in_dim.73), calls=%async_computation | async-start | bytes 6553600 | tf_op jit(solution)/shard_map/all_to_all | solution.py:43
  24.2 53.9 %all-gather.6.cloned.1.call-start = ((), (), s32[]{:S(2)}) async-start(), calls=%async_computation.17 | async-start | bytes 2359296 | tf_op jit(solution)/shard_map/all_gather | solution.py:146
  25.3 72.5 %copy-start.22 = (bf16[128,1024]{1,0:T(8,128)(2,1)S(1)}, bf16[128,1024]{1,0:T(8,128)(2,1)}, u32[]{:S(2)}) copy-start(bf16[128,1024]{1,0:T(8,128)(2,1)} %param.12) | copy-start | bytes 786436
  25.3 71.5 %all-gather.8.cloned.1.call-start = ((), (), s32[]{:S(2)}) async-start(), calls=%async_computation.18 | async-start | bytes 4718592 | tf_op jit(solution)/shard_map/all_gather | solution.py:147
  78.2 138.7 %all-gather.10.cloned.1.call-start = ((), (), s32[]{:S(2)}) async-start(), calls=%async_computation.19 | async-start | bytes 6604800 | tf_op jit(solution)/shard_map/all_gather | solution.py:37
  79.6 18.4 %collective-permute-start = (bf16[64,8,3200]{2,1,0:T(8,128)(2,1)}, bf16[64,8,3200]{2,1,0:T(8,128)(2,1)}, u32[]{:S(2)}, u32[]{:S(2)}) collective-permute-start(bf16[64,8,3200]{2,1,0:T(8,128)(2,1)} %all-to-all-done), channel_id=1, source_target_pairs={{0,1},{1,0},{2,3},{3,2},{4,5},{5,4},{6,7},{7,6},{8,9},{9,8},{10,11... | collective-permute-start | bytes 9830408 | tf_op jit(solution)/shard_map/ppermute | solution.py:45
  104.8 5.5 copy-start.85
  109.5 4.8 copy-start.61
  116.7 47.6 %copy-start.98 = (f32[128]{0:T(128)}, f32[128]{0:T(128)S(1)}, u32[]{:S(2)}) copy-start(f32[128]{0:T(128)S(1)} %add_rsqrt_fusion.2) | copy-start | bytes 1540
  116.9 62.7 %copy-start.18 = (bf16[128,1024]{1,0:T(8,128)(2,1)}, bf16[128,1024]{1,0:T(8,128)(2,1)S(1)}, u32[]{:S(2)}) copy-start(bf16[128,1024]{1,0:T(8,128)(2,1)S(1)} %multiply_convert_fusion.10) | copy-start | bytes 786436
  117.7 46.6 %copy-start.58 = (bf16[512,3072]{1,0:T(8,128)(2,1)S(1)}, bf16[512,3072]{1,0:T(8,128)(2,1)}, u32[]{:S(2)}) copy-start(bf16[512,3072]{1,0:T(8,128)(2,1)} %all-gather.8.cloned.1.call-done) | copy-start | bytes 9437188
  172.4 41.9 %all-to-all-start.2 = ((bf16[32,40,1024]{2,1,0:T(8,128)(2,1)}), bf16[32,40,1024]{2,1,0:T(8,128)(2,1)}, u32[]{:S(2)}, u32[]{:S(2)}) async-start(bf16[32,40,1024]{2,1,0:T(8,128)(2,1)} %bitcast.344), calls=%async_computation.2 | async-start | bytes 5242880 | tf_op jit(solution)/shard_map/all_to_all | solution.py:139
  179.5 109.8 %all-gather.12.cloned.1.call-start = ((), (), s32[]{:S(2)}) async-start(), calls=%async_computation.20 | async-start | bytes 2359296 | tf_op jit(solution)/shard_map/all_gather | solution.py:146
  180.8 36.0 %copy-start.86 = (f32[128]{0:T(128)}, f32[128]{0:T(128)S(1)}, u32[]{:S(2)}) copy-start(f32[128]{0:T(128)S(1)} %get-tuple-element.119) | copy-start | bytes 1540
  180.8 36.0 %copy-start.94 = (f32[128]{0:T(128)}, f32[128]{0:T(128)S(1)}, u32[]{:S(2)}) copy-start(f32[128]{0:T(128)S(1)} %fusion.169) | copy-start | bytes 1540
  218.4 19.6 %copy-start.79 = (f32[1024]{0:T(1024)}, f32[1024]{0:T(1024)S(1)}, u32[]{:S(2)}) copy-start(f32[1024]{0:T(1024)S(1)} %get-tuple-element.63) | copy-start | bytes 12292
  227.2 6.5 copy-start.73
  228.4 5.4 copy-start.65
  228.4 5.4 copy-start.67
  241.2 54.9 %all-to-all-start.3 = ((bf16[32,40,1024]{2,1,0:T(8,128)(2,1)}), bf16[32,40,1024]{2,1,0:T(8,128)(2,1)}, u32[]{:S(2)}, u32[]{:S(2)}) async-start(bf16[32,40,1024]{2,1,0:T(8,128)(2,1)} %bitcast.336), calls=%async_computation.3 | async-start | bytes 5242880 | tf_op jit(solution)/shard_map/all_to_all | solution.py:139
  249.7 57.0 %all-gather.14.cloned.1.call-start = ((), (), s32[]{:S(2)}) async-start(), calls=%async_computation.21 | async-start | bytes 4718592 | tf_op jit(solution)/shard_map/all_gather | solution.py:147
  296.1 44.8 %all-to-all-start.4 = ((bf16[32,40,1024]{2,1,0:T(8,128)(2,1)}), bf16[32,40,1024]{2,1,0:T(8,128)(2,1)}, u32[]{:S(2)}, u32[]{:S(2)}) async-start(bf16[32,40,1024]{2,1,0:T(8,128)(2,1)} %bitcast.337), calls=%async_computation.4 | async-start | bytes 5242880 | tf_op jit(solution)/shard_map/all_to_all | solution.py:139
  310.5 6.1 copy-start.116
  340.9 40.3 %all-to-all-start.5 = ((bf16[32,40,1024]{2,1,0:T(8,128)(2,1)}), bf16[32,40,1024]{2,1,0:T(8,128)(2,1)}, u32[]{:S(2)}, u32[]{:S(2)}) async-start(bf16[32,40,1024]{2,1,0:T(8,128)(2,1)} %bitcast.343), calls=%async_computation.5 | async-start | bytes 5242880 | tf_op jit(solution)/shard_map/all_to_all | solution.py:139
  351.2 5.5 copy-start.60
  381.1 38.3 %all-to-all-start.6 = ((bf16[32,40,1024]{2,1,0:T(8,128)(2,1)}), bf16[32,40,1024]{2,1,0:T(8,128)(2,1)}, u32[]{:S(2)}, u32[]{:S(2)}) async-start(bf16[32,40,1024]{2,1,0:T(8,128)(2,1)} %bitcast.333), calls=%async_computation.6 | async-start | bytes 5242880 | tf_op jit(solution)/shard_map/all_to_all | solution.py:139
  387.5 132.7 %reduce-scatter.12.cloned.1.call-start = ((), (), s32[]{:S(2)}) async-start(), calls=%async_computation.25 | async-start | bytes 4718592 | tf_op jit(solution)/shard_map/reduce_scatter | solution.py:152
  404.0 18.1 %copy-start.80 = (f32[1024]{0:T(1024)S(1)}, f32[1024]{0:T(1024)}, u32[]{:S(2)}) copy-start(f32[1024]{0:T(1024)} %copy-done.79) | copy-start | bytes 12292
  422.1 6.6 copy-start.93
  435.7 5.3 copy-start.28
  443.4 38.7 %all-to-all-start.7 = ((bf16[32,40,1024]{2,1,0:T(8,128)(2,1)}), bf16[32,40,1024]{2,1,0:T(8,128)(2,1)}, u32[]{:S(2)}, u32[]{:S(2)}) async-start(bf16[32,40,1024]{2,1,0:T(8,128)(2,1)} %bitcast.335), calls=%async_computation.7 | async-start | bytes 5242880 | tf_op jit(solution)/shard_map/all_to_all | solution.py:139
  450.0 100.8 %reduce-scatter.6.cloned.1.call-start = ((), (), s32[]{:S(2)}) async-start(), calls=%async_computation.22 | async-start | bytes 4096000 | tf_op jit(solution)/shard_map/reduce_scatter | solution.py:498
  453.4 5.1 copy-start.21
  453.4 5.1 copy-start.78
  453.4 14.5 %collective-permute-start.1 = (bf16[512,2048]{1,0:T(8,128)(2,1)}, bf16[512,2048]{1,0:T(8,128)(2,1)}, u32[]{:S(2)}, u32[]{:S(2)}) collective-permute-start(bf16[512,2048]{1,0:T(8,128)(2,1)} %convolution_convert_fusion.7), channel_id=1, source_target_pairs={{0,1},{1,0},{2,3},{3,2},{4,5},{5,4},{6,7},{7,6},{8,9},{9,8},{10,11... | collective-permute-start | bytes 6291464 | tf_op jit(solution)/shard_map/ppermute | solution.py:188
  455.4 9.9 %collective-permute-start.2 = (bf16[512,1024]{1,0:T(8,128)(2,1)}, bf16[512,1024]{1,0:T(8,128)(2,1)}, u32[]{:S(2)}, u32[]{:S(2)}) collective-permute-start(bf16[512,1024]{1,0:T(8,128)(2,1)} %convolution_convert_fusion.11), channel_id=1, source_target_pairs={{0,1},{1,0},{2,3},{3,2},{4,5},{5,4},{6,7},{7,6},{8,9},{9,8},{10,11... | collective-permute-start | bytes 3145736 | tf_op jit(solution)/shard_map/ppermute | solution.py:188
  463.0 4.9 copy-start.35
  463.1 4.9 copy-start.43
  463.1 4.9 copy-start.48
  463.1 4.9 copy-start.57
  463.1 1.4 collective-permute-start.3
  485.4 85.7 %reduce-scatter.8.cloned.1.call-start = ((), (), s32[]{:S(2)}) async-start(), calls=%async_computation.23 | async-start | bytes 4718592 | tf_op jit(solution)/shard_map/reduce_scatter | solution.py:152
  489.3 5.7 copy-start.1
  507.7 6.9 %copy-start.82 = (f32[1024]{0:T(1024)S(1)}, f32[1024]{0:T(1024)}, u32[]{:S(2)}) copy-start(f32[1024]{0:T(1024)} %copy-done.81) | copy-start | bytes 12292
  507.7 6.9 %copy-start.108 = (f32[128]{0:T(128)S(1)}, f32[128]{0:T(128)}, u32[]{:S(2)}) copy-start(f32[128]{0:T(128)} %copy-done.107) | copy-start | bytes 1540
  507.7 39.5 %all-to-all-start.8 = ((bf16[32,40,1024]{2,1,0:T(8,128)(2,1)}), bf16[32,40,1024]{2,1,0:T(8,128)(2,1)}, u32[]{:S(2)}, u32[]{:S(2)}) async-start(bf16[32,40,1024]{2,1,0:T(8,128)(2,1)} %bitcast.334), calls=%async_computation.8 | async-start | bytes 5242880 | tf_op jit(solution)/shard_map/all_to_all | solution.py:139
  514.2 112.8 %reduce-scatter.14.cloned.1.call-start = ((), (), s32[]{:S(2)}) async-start(), calls=%async_computation.26 | async-start | bytes 2359296 | tf_op jit(solution)/shard_map/reduce_scatter | solution.py:153
  520.2 33.0 %copy-start.99 = (f32[128]{0:T(128)S(1)}, f32[128]{0:T(128)}, u32[]{:S(2)}) copy-start(f32[128]{0:T(128)} %copy-done.98) | copy-start | bytes 1540
  520.2 134.5 %reduce-scatter.10.cloned.1.call-start = ((), (), s32[]{:S(2)}) async-start(), calls=%async_computation.24 | async-start | bytes 2359296 | tf_op jit(solution)/shard_map/reduce_scatter | solution.py:153
  563.8 14.9 %copy-start.55 = (bf16[8,64,128]{2,1,0:T(8,128)(2,1)}, bf16[8,64,128]{2,1,0:T(8,128)(2,1)S(1)}, u32[]{:S(2)}) copy-start(bf16[8,64,128]{2,1,0:T(8,128)(2,1)S(1)} %fusion.59) | copy-start | bytes 393220
  567.0 35.1 %collective-permute-start.4 = (bf16[512,2048]{1,0:T(8,128)(2,1)}, bf16[512,2048]{1,0:T(8,128)(2,1)}, u32[]{:S(2)}, u32[]{:S(2)}) collective-permute-start(bf16[512,2048]{1,0:T(8,128)(2,1)} %convolution_convert_fusion.6), channel_id=1, source_target_pairs={{0,1},{1,0},{2,3},{3,2},{4,5},{5,4},{6,7},{7,6},{8,9},{9,8},{10,11... | collective-permute-start | bytes 6291464 | tf_op jit(solution)/shard_map/ppermute | solution.py:188
  568.2 10.5 %copy-start.109 = (f32[128]{0:T(128)S(1)}, f32[128]{0:T(128)}, u32[]{:S(2)}) copy-start(f32[128]{0:T(128)} %copy-done.107) | copy-start | bytes 1540
  569.6 16.1 %collective-permute-start.6 = (bf16[512,1024]{1,0:T(8,128)(2,1)}, bf16[512,1024]{1,0:T(8,128)(2,1)}, u32[]{:S(2)}, u32[]{:S(2)}) collective-permute-start(bf16[512,1024]{1,0:T(8,128)(2,1)} %convolution_convert_fusion.10), channel_id=1, source_target_pairs={{0,1},{1,0},{2,3},{3,2},{4,5},{5,4},{6,7},{7,6},{8,9},{9,8},{10,11... | collective-permute-start | bytes 3145736 | tf_op jit(solution)/shard_map/ppermute | solution.py:188
  571.2 20.0 %all-to-all-start.10 = ((bf16[16,8,3200]{2,1,0:T(8,128)(2,1)}), bf16[16,8,3200]{2,1,0:T(8,128)(2,1)}, u32[]{:S(2)}, u32[]{:S(2)}) async-start(bf16[16,8,3200]{2,1,0:T(8,128)(2,1)} %bitcast.363), calls=%async_computation.11 | async-start | bytes 1638400 | tf_op jit(solution)/shard_map/all_to_all | solution.py:193
  578.7 5.1 copy-start.44
  578.7 5.1 copy-start.103
  585.5 13.4 %copy-start.27 = (bf16[128,1280]{1,0:T(8,128)(2,1)S(1)}, bf16[128,1280]{1,0:T(8,128)(2,1)}, u32[]{:S(2)}) copy-start(bf16[128,1280]{1,0:T(8,128)(2,1)} %copy-done.26) | copy-start | bytes 983044
  585.6 16.5 %collective-permute-start.5 = (bf16[512,128]{1,0:T(8,128)(2,1)S(1)}, bf16[512,128]{1,0:T(8,128)(2,1)S(1)}, u32[]{:S(2)}, u32[]{:S(2)}) collective-permute-start(bf16[512,128]{1,0:T(8,128)(2,1)S(1)} %slice.539), channel_id=1, source_target_pairs={{0,1},{1,0},{2,3},{3,2},{4,5},{5,4},{6,7},{7,6},{8,9},{9,8},{10,11... | collective-permute-start | bytes 393224 | tf_op jit(solution)/shard_map/ppermute | solution.py:188
  588.4 13.7 %copy-start.30 = (f32[1024,128]{1,0:T(8,128)S(1)}, f32[1024,128]{1,0:T(8,128)}, u32[]{:S(2)}) copy-start(f32[1024,128]{1,0:T(8,128)} %copy-done.29) | copy-start | bytes 1572868
  591.1 24.6 %all-to-all-start.11 = ((bf16[64,8,1024]{2,1,0:T(8,128)(2,1)}), bf16[64,8,1024]{2,1,0:T(8,128)(2,1)}, u32[]{:S(2)}, u32[]{:S(2)}) async-start(bf16[64,8,1024]{2,1,0:T(8,128)(2,1)} %fusion.63), calls=%async_computation.12 | async-start | bytes 2097152 | tf_op jit(solution)/shard_map/all_to_all | solution.py:193
  606.0 15.6 %copy-start.23 = (bf16[128,1024]{1,0:T(8,128)(2,1)S(1)}, bf16[128,1024]{1,0:T(8,128)(2,1)}, u32[]{:S(2)}) copy-start(bf16[128,1024]{1,0:T(8,128)(2,1)} %param.12) | copy-start | bytes 786436
  615.7 43.8 %all-to-all-start.9 = ((bf16[64,8,2176]{2,1,0:T(8,128)(2,1)}), bf16[64,8,2176]{2,1,0:T(8,128)(2,1)S(1)}, u32[]{:S(2)}, u32[]{:S(2)}) async-start(bf16[64,8,2176]{2,1,0:T(8,128)(2,1)} %maximum_bitcast_fusion), calls=%async_computation.10 | async-start | bytes 4456448 | tf_op jit(solution)/shard_map/all_to_all | solution.py:193
  (82 other events, 208.4 us)
Sparse Core Ops, SparseCore 0:
  27.3 50.7 all-gather.5
  79.8 17.0 all-gather.7
  100.4 95.2 all-gather.9
  231.7 57.6 all-gather.11
  290.9 15.8 all-gather.13
  400.2 14.6 reduce-scatter.11
  485.6 65.2 reduce-scatter.5
  553.3 13.2 reduce-scatter.7
  568.9 29.9 reduce-scatter.13
  601.2 53.5 reduce-scatter.9

commit v7 on v6

--- a/solution.py
+++ b/solution.py
@@ -142,15 +142,30 @@
 
 
 def gather_expert(own_in, own_out):
-    both = jnp.concatenate([own_in, own_out], axis=1)
-    both = lax.all_gather(both, "zl", axis=0, tiled=True)
-    return lax.all_gather(both, "c", axis=0, tiled=True)
-
-
-def scatter_expert(grads):
-    both = jnp.concatenate(grads, axis=1).astype(jnp.bfloat16)
-    both = lax.psum_scatter(both, "c", scatter_dimension=0, tiled=True)
-    return lax.psum_scatter(both, "zl", scatter_dimension=0, tiled=True)
+    own = jnp.concatenate([own_in, own_out], axis=1)
+    pair = jnp.concatenate([own, lax.ppermute(own, "zl", SWAP)], axis=0)
+    return jnp.concatenate([pair, lax.ppermute(pair, "c", SWAP)], axis=0)
+
+
+def expert_core_sum(pairs):
+    dims = (((0,), (0,)), ((), ()))
+    half = pairs[0][0].shape[1] // 2
+    kept = [
+        lax.dot_general(left[:, :half], right, dims, preferred_element_type=jnp.float32)
+        for left, right in pairs
+    ]
+    given = [
+        lax.dot_general(left[:, half:], right, dims, preferred_element_type=jnp.float32)
+        for left, right in pairs
+    ]
+    given = jnp.concatenate([g.astype(jnp.bfloat16) for g in given], axis=1)
+    return jnp.concatenate(kept, axis=1) + lax.ppermute(given, "c", SWAP).astype(jnp.float32)
+
+
+def expert_chip_sum(kept):
+    half = kept.shape[0] // 2
+    other = lax.ppermute(kept[half:].astype(jnp.bfloat16), "zl", SWAP)
+    return kept[:half] + other.astype(jnp.float32)
 
 
 def order_table():
@@ -313,16 +328,8 @@
         grad_in_rows
         + jnp.dot(grad_up_pre, expert_in_l[:, MODEL_WIDTH:], preferred_element_type=jnp.float32)
     ).astype(jnp.bfloat16)
-    out_grad = lax.dot_general(
-        units, grad_rows, (((0,), (0,)), ((), ())), preferred_element_type=jnp.float32
-    )
-    gate_w_grad = lax.dot_general(
-        grad_gate_pre, rows_here, (((0,), (0,)), ((), ())), preferred_element_type=jnp.float32
-    )
-    up_w_grad = lax.dot_general(
-        grad_up_pre, rows_here, (((0,), (0,)), ((), ())), preferred_element_type=jnp.float32
-    )
-    return grad_in_rows, (gate_w_grad, up_w_grad, out_grad)
+    pairs = ((grad_gate_pre, rows_here), (grad_up_pre, rows_here), (units, grad_rows))
+    return grad_in_rows, pairs
 
 
 def route_backward(grad_out, weights, chosen, returned, stash):
@@ -454,16 +461,13 @@
     live = live_row.astype(jnp.float32)
     cosine_table, sine_values = rope_tables(position)
     routed, chosen = dispatch_table(routes, live_row)
-    beside = order, live, allowed, cosine_table, sine_values, routed, chosen
+    experts = [gather_expert(expert_in[0], expert_out[0]), None]
+    beside = order, live, allowed, cosine_table, sine_values, routed, chosen, experts[0]
     lead, beside = sent_by_chips(jnp.concatenate(lead + [fill], axis=1), beside)
-    order, live, allowed, cosine_table, sine_values, routed, chosen = beside
+    order, live, allowed, cosine_table, sine_values, routed, chosen, experts[0] = beside
+    lead, own_dense = lax.optimization_barrier((lead, own_dense))
     dense = [cut_weights(lead, DENSE_WIDTHS), None]
-    experts = [gather_expert(expert_in[0], expert_out[0]), None]
-    experts[0], own_dense = lax.optimization_barrier((experts[0], own_dense))
-    gathered = sent_together(own_dense[1], AXES)
-    gathered, expert_in, expert_out = lax.optimization_barrier((gathered, expert_in, expert_out))
-    dense[1] = cut_weights(gathered, DENSE_WIDTHS)
-    experts[1] = gather_expert(expert_in[1], expert_out[1])
+    dense[1] = cut_weights(sent_together(own_dense[1], AXES), DENSE_WIDTHS)
     hidden = hidden_in.astype(jnp.float32)
     grad_hidden = cotangent.astype(jnp.float32)
     saved = []
@@ -474,6 +478,9 @@
         mixed_low = attn_stash[-1]
         hidden = hidden + jnp.dot(mixed_low, dense[layer][1], preferred_element_type=jnp.float32)
         rows, route_stash = route_rows(hidden, dense[layer], routed, chosen)
+        if layer == 0:
+            rows, expert_in, expert_out = lax.optimization_barrier((rows, expert_in, expert_out))
+            experts[1] = gather_expert(expert_in[1], expert_out[1])
         rows_here = trade_rows(rows)
         moved = reorder(attn_stash[2], order), reorder(mixed_low, order)
         grad_rows = None
@@ -485,6 +492,8 @@
         if layer == last:
             results, grad_rows = lax.optimization_barrier((results, grad_rows))
         returned = trade_rows(results)
+        if layer == 0:
+            returned, experts[1] = lax.optimization_barrier((returned, experts[1]))
         hidden = hidden + jnp.dot(route_stash[-1], returned, preferred_element_type=jnp.float32)
         saved.append((attn_stash, moved, route_stash, rows_here, pre, returned, grad_rows))
     output_low = hidden.astype(jnp.bfloat16)
@@ -493,18 +502,24 @@
         attn_stash, moved, route_stash, rows_here, pre, returned, grad_rows = saved[layer]
         if grad_rows is None:
             slots = slot_gradients(grad_hidden, route_stash[-1])
-            grad_rows, sums = lax.optimization_barrier((trade_rows(slots), sums))
+            slots, proj_last = lax.optimization_barrier((slots, proj_last))
+            grad_rows = trade_rows(slots)
+            grad_rows, sums, expert_sums[last] = lax.optimization_barrier(
+                (grad_rows, sums, expert_sums[last])
+            )
             joined = jnp.concatenate(sums, axis=1)
-            joined = lax.psum_scatter(joined, Z_AXES, scatter_dimension=0, tiled=True)
-        grad_in_rows, expert_grads = feed_backward(grad_rows, rows_here, pre, experts[layer])
+        grad_in_rows, pairs = feed_backward(grad_rows, rows_here, pre, experts[layer])
+        grad_in_rows, pairs = lax.optimization_barrier((grad_in_rows, pairs))
         grad_slots = trade_rows(grad_in_rows)
+        expert_kept = expert_core_sum(pairs)
         router_grad, grad_routed = route_backward(
             grad_hidden, dense[layer], chosen, returned, route_stash
         )
-        expert_sums[layer] = scatter_expert(expert_grads)
+        grad_slots, expert_kept = lax.optimization_barrier((grad_slots, expert_kept))
+        expert_sums[layer] = expert_chip_sum(expert_kept)
         if layer != last:
             grad_slots, joined = lax.optimization_barrier((grad_slots, joined))
-            done_last = chip_sum(joined, ("x", "y"))
+            done_last = chip_sum(joined, Z_AXES + ("x", "y"))
         grad_h1, gain_two_grad = rows_backward(
             grad_hidden, dense[layer], chosen, grad_slots, grad_routed, route_stash
         )
@@ -512,13 +527,16 @@
             grad_h1, dense[layer], live, allowed, cosine_table, sine_values, attn_stash, *moved
         )
         small = small_halves(router_grad, gain_one_grad, gain_two_grad, order)
-        sums = [core_sum(qkv_halves), proj_sum, core_sum(small)]
-    proj_done = chip_sum(sums.pop(1), Z_AXES + ("x", "y"))
-    done = chip_sum(jnp.concatenate(sums, axis=1), Z_AXES + ("x", "y"))
-    first = [done[:, :2048], proj_done, done[:, 2048:]]
-    second = [done_last[:, :2048], done_last[:, 2048:3072], done_last[:, 3072:]]
+        if layer == last:
+            proj_last = chip_sum(proj_sum, Z_AXES + ("x", "y"))
+            sums = [core_sum(qkv_halves), core_sum(small)]
+        else:
+            sums = [core_sum(qkv_halves), proj_sum, core_sum(small)]
+            done = chip_sum(jnp.concatenate(sums, axis=1), Z_AXES + ("x", "y"))
+    first = [done[:, :2048], done[:, 2048:3072], done[:, 3072:]]
+    second = [done_last[:, :2048], proj_last, done_last[:, 2048:]]
     qkv, proj, small = [jnp.stack(pair) for pair in zip(first, second)]
-    both = jnp.stack(expert_sums).astype(jnp.float32)
+    both = jnp.stack(expert_sums)
     return (
         output_low,
         grad_hidden,

time: 680 us -> 717 us (1.054)
  blocking collectives: 46.6 us -> 0 us
  waiting for transfers between devices: 276 us -> 303 us
  matrix products: 165 us -> 187 us
  other arithmetic: 40.3 us -> 60.6 us
  starting transfers between devices: 87.6 us -> 103 us
    ppermute x0 -> x8, waiting for transfers between devices: none -> 130 us  [the longest x2 77.9 us: expert_chip_sum(): other = lax.ppermute(kept[half:].astype(jnp.bfloat16), 'zl', SWAP)]
    all_gather x4 -> x0, waiting for transfers between devices: 107 us -> none  [the longest x2 89.8 us: gather_expert(): both = lax.all_gather(both, 'zl', axis=0, tiled=True)]
    all_to_all x1 -> x0, blocking collectives: 46.6 us -> none  [trade_rows(): lax.all_to_all(rows.reshape(E, ROOM, MODEL_WIDTH), EXPERT_AXES, split_axi...]
    reduce_scatter x5 -> x0, waiting for transfers between devices: 31.4 us -> none  [the longest x2 27.7 us: scatter_expert(): return lax.psum_scatter(both, 'zl', scatter_dimension=0, tiled=True)]
    all_to_all x7 -> x8, waiting for transfers between devices: 123 us -> 138 us  [trade_rows(): lax.all_to_all(rows.reshape(E, ROOM, MODEL_WIDTH), EXPERT_AXES, split_axi...]
    dot_general x6 -> x12, matrix products: 17.4 us -> 32.1 us  [the longest x6 16.1 us: expert_core_sum(): lax.dot_general(left[:, half:], right, dims, preferred_element_type=jnp.f...]
    all_to_all x3, waiting for transfers between devices: 12.5 us -> 26.3 us  [chip_sum(): parts = lax.all_to_all(parts, axes, split_axis=0, concat_axis=0, tiled=True)]
    all_to_all x7 -> x8, starting transfers between devices: 52.3 us -> 61.5 us  [trade_rows(): lax.all_to_all(rows.reshape(E, ROOM, MODEL_WIDTH), EXPERT_AXES, split_axi...]
  transfers between devices with their start and end apart: 28 -> 28, of which waited for: 15 -> 17; matrix products, arithmetic and copies ran while one was open for 31% -> 28% of each run, Pallas kernels for 0% -> 0%
where the time goes in v7:
time: 717 us; the launch traced here: 706 us
  waiting for transfers between devices  303 us (42%)
  matrix products  187 us (26%)
  starting transfers between devices  103 us (14%)
  other arithmetic  60.6 us (8%)
  local copies, waits for them, and re-layouts  35.6 us (5%)
  between operations  16.8 us (2%)
    all_to_all x8, waiting for transfers between devices, trade_rows(): lax.all_to_all(rows.reshape(E, ROOM, MODEL_WIDTH), EXPERT_AXES, split_axi...  138 us
    ppermute x2, waiting for transfers between devices, expert_chip_sum(): other = lax.ppermute(kept[half:].astype(jnp.bfloat16), 'zl', SWAP)  77.9 us
    all_to_all x8, starting transfers between devices, trade_rows(): lax.all_to_all(rows.reshape(E, ROOM, MODEL_WIDTH), EXPERT_AXES, split_axi...  61.5 us
    ppermute x2, waiting for transfers between devices, gather_expert(): pair = jnp.concatenate([own, lax.ppermute(own, 'zl', SWAP)], axis=0)  50.4 us
    all_to_all x3, waiting for transfers between devices, chip_sum(): parts = lax.all_to_all(parts, axes, split_axis=0, concat_axis=0, tiled=True)  26.3 us
    all_to_all x3, starting transfers between devices, chip_sum(): parts = lax.all_to_all(parts, axes, split_axis=0, concat_axis=0, tiled=True)  22.3 us
    dot_general x6, matrix products, expert_core_sum(): lax.dot_general(left[:, half:], right, dims, preferred_element_type=jnp.f...  16.1 us
    dot_general x6, matrix products, expert_core_sum(): lax.dot_general(left[:, :half], right, dims, preferred_element_type=jnp.f...  16 us
  transfers between devices with their start and end apart: 28, of which 17 were waited for; matrix products, arithmetic and copies ran while one was open for 28% of the time, Pallas kernels for 0%

profile of v7, /device:TPU:2, one launch (start us, length us, event | category | flops | bytes accessed | tf_op | source)
XLA Modules:
  0.0 705.5 jit_solution(14545142253632461392)
XLA Ops:
  12.3 11.8 %all-to-all-start = ((bf16[64,8,3200]{2,1,0:T(8,128)(2,1)}), bf16[64,8,3200]{2,1,0:T(8,128)(2,1)}, u32[]{:S(2)}, u32[]{:S(2)}) async-start(bf16[64,8,3200]{2,1,0:T(8,128)(2,1)} %broadcast_in_dim.73), calls=%async_computation | async-start | bytes 6553600 | tf_op jit(solution)/shard_map/all_to_all | solution.py:43
  27.1 50.4 %collective-permute-done = bf16[128,3072]{1,0:T(8,128)(2,1)S(1)} collective-permute-done((bf16[128,3072]{1,0:T(8,128)(2,1)S(1)}, bf16[128,3072]{1,0:T(8,128)(2,1)S(1)}, u32[]{:S(2)}, u32[]{:S(2)}) %collective-permute-start) | collective-permute-done | bytes 786464 | tf_op jit(solution)/shard_map/ppermute | solution.py:146
  82.7 4.8 pad_maximum_fusion.1
  87.5 6.1 collective-permute-done.2
  93.6 3.5 select_bitcast_fusion.1
  97.1 3.3 pad_maximum_fusion
  103.0 3.0 fusion.9
  121.1 10.6 %all-to-all-start.1 = ((bf16[32,40,1024]{2,1,0:T(8,128)(2,1)}), bf16[32,40,1024]{2,1,0:T(8,128)(2,1)}, u32[]{:S(2)}, u32[]{:S(2)}) async-start(bf16[32,40,1024]{2,1,0:T(8,128)(2,1)} %bitcast.336), calls=%async_computation.1 | async-start | bytes 5242880 | tf_op jit(solution)/shard_map/all_to_all | solution.py:139
  136.0 31.0 %all-to-all-done.1 = bf16[32,40,1024]{2,1,0:T(8,128)(2,1)} async-done(((bf16[32,40,1024]{2,1,0:T(8,128)(2,1)}), bf16[32,40,1024]{2,1,0:T(8,128)(2,1)}, u32[]{:S(2)}, u32[]{:S(2)}) %all-to-all-start.1) | async-done | bytes 2621472 | tf_op jit(solution)/shard_map/all_to_all | solution.py:139
  167.0 3.8 fusion.83
  170.8 6.1 multiply_convert_fusion.5
  176.9 3.0 convolution_convert_fusion.4
  179.9 7.6 %all-to-all-start.2 = ((bf16[32,40,1024]{2,1,0:T(8,128)(2,1)}), bf16[32,40,1024]{2,1,0:T(8,128)(2,1)}, u32[]{:S(2)}, u32[]{:S(2)}) async-start(bf16[32,40,1024]{2,1,0:T(8,128)(2,1)} %bitcast.340), calls=%async_computation.2 | async-start | bytes 5242880 | tf_op jit(solution)/shard_map/all_to_all | solution.py:139
  192.5 4.7 pad_maximum_fusion.2
  197.2 25.8 %all-to-all-done.2 = bf16[32,40,1024]{2,1,0:T(8,128)(2,1)} async-done(((bf16[32,40,1024]{2,1,0:T(8,128)(2,1)}), bf16[32,40,1024]{2,1,0:T(8,128)(2,1)}, u32[]{:S(2)}, u32[]{:S(2)}) %all-to-all-start.2) | async-done | bytes 2621472 | tf_op jit(solution)/shard_map/all_to_all | solution.py:139
  227.1 2.9 fusion.5
  247.0 8.2 %all-to-all-start.3 = ((bf16[32,40,1024]{2,1,0:T(8,128)(2,1)}), bf16[32,40,1024]{2,1,0:T(8,128)(2,1)}, u32[]{:S(2)}, u32[]{:S(2)}) async-start(bf16[32,40,1024]{2,1,0:T(8,128)(2,1)} %bitcast.337), calls=%async_computation.3 | async-start | bytes 5242880 | tf_op jit(solution)/shard_map/all_to_all | solution.py:139
  258.6 3.3 convolution_convert_fusion.3
  262.0 27.5 %all-to-all-done.3 = bf16[32,40,1024]{2,1,0:T(8,128)(2,1)} async-done(((bf16[32,40,1024]{2,1,0:T(8,128)(2,1)}), bf16[32,40,1024]{2,1,0:T(8,128)(2,1)}, u32[]{:S(2)}, u32[]{:S(2)}) %all-to-all-start.3) | async-done | bytes 2621472 | tf_op jit(solution)/shard_map/all_to_all | solution.py:139
  289.4 6.3 all-to-all-start.4
  299.6 3.8 fusion.73
  303.4 6.1 multiply_convert_fusion.4
  310.5 3.0 convolution_convert_fusion.1
  313.6 16.1 %all-to-all-done.4 = bf16[32,40,1024]{2,1,0:T(8,128)(2,1)} async-done(((bf16[32,40,1024]{2,1,0:T(8,128)(2,1)}), bf16[32,40,1024]{2,1,0:T(8,128)(2,1)}, u32[]{:S(2)}, u32[]{:S(2)}) %all-to-all-start.4) | async-done | bytes 2621472 | tf_op jit(solution)/shard_map/all_to_all | solution.py:139
  329.7 6.4 all-to-all-start.5
  336.1 6.2 multiply_convert_fusion.2
  343.9 3.0 add_convert_fusion.1
  346.9 2.6 convolution_convert_fusion.15
  349.5 2.6 convolution_convert_fusion.16
  352.1 2.6 convolution_convert_fusion.17
  357.2 11.8 %all-to-all-done.5 = bf16[32,40,1024]{2,1,0:T(8,128)(2,1)} async-done(((bf16[32,40,1024]{2,1,0:T(8,128)(2,1)}), bf16[32,40,1024]{2,1,0:T(8,128)(2,1)}, u32[]{:S(2)}, u32[]{:S(2)}) %all-to-all-start.5) | async-done | bytes 2621472 | tf_op jit(solution)/shard_map/all_to_all | solution.py:139
  369.1 7.2 %all-to-all-start.6 = ((bf16[32,40,1024]{2,1,0:T(8,128)(2,1)}), bf16[32,40,1024]{2,1,0:T(8,128)(2,1)}, u32[]{:S(2)}, u32[]{:S(2)}) async-start(bf16[32,40,1024]{2,1,0:T(8,128)(2,1)} %bitcast.332), calls=%async_computation.6 | async-start | bytes 5242880 | tf_op jit(solution)/shard_map/all_to_all | solution.py:139
  378.5 2.7 fusion.101
  381.2 2.7 fusion.103
  384.0 2.6 fusion.105
  386.6 3.7 maximum_add_fusion
  390.3 2.7 fusion.13
  394.7 14.1 %all-to-all-done.6 = bf16[32,40,1024]{2,1,0:T(8,128)(2,1)} async-done(((bf16[32,40,1024]{2,1,0:T(8,128)(2,1)}), bf16[32,40,1024]{2,1,0:T(8,128)(2,1)}, u32[]{:S(2)}, u32[]{:S(2)}) %all-to-all-start.6) | async-done | bytes 2621472 | tf_op jit(solution)/shard_map/all_to_all | solution.py:139
  414.9 3.1 fusion.49
  428.3 3.3 convolution_convert_fusion.7
  432.1 2.7 fusion.64
  434.8 7.6 %all-to-all-start.7 = ((bf16[64,8,1024]{2,1,0:T(8,128)(2,1)}), bf16[64,8,1024]{2,1,0:T(8,128)(2,1)}, u32[]{:S(2)}, u32[]{:S(2)}) async-start(bf16[64,8,1024]{2,1,0:T(8,128)(2,1)} %fusion.64), calls=%async_computation.7 | async-start | bytes 2097152 | tf_op jit(solution)/shard_map/all_to_all | solution.py:208
  442.4 4.2 multiply_reduce_fusion.5
  450.1 9.9 %all-to-all-done.7 = bf16[64,8,1024]{2,1,0:T(8,128)(2,1)} async-done(((bf16[64,8,1024]{2,1,0:T(8,128)(2,1)}), bf16[64,8,1024]{2,1,0:T(8,128)(2,1)}, u32[]{:S(2)}, u32[]{:S(2)}) %all-to-all-start.7) | async-done | bytes 1048608 | tf_op jit(solution)/shard_map/all_to_all | solution.py:208
  462.0 6.0 all-to-all-start.8
  475.3 2.9 convolution_multiply_fusion
  481.4 31.7 %collective-permute-done.9 = bf16[128,3072]{1,0:T(8,128)(2,1)S(1)} collective-permute-done((bf16[128,3072]{1,0:T(8,128)(2,1)S(1)}, bf16[128,3072]{1,0:T(8,128)(2,1)S(1)}, u32[]{:S(2)}, u32[]{:S(2)}) %collective-permute-start.9) | collective-permute-done | bytes 786464 | tf_op jit(solution)/shard_map/ppermute | solution.py:167
  514.6 3.7 add_convert_fusion.3
  518.2 6.2 multiply_convert_fusion
  526.0 3.0 add_convert_fusion
  529.0 9.2 %all-to-all-start.9 = ((bf16[32,40,1024]{2,1,0:T(8,128)(2,1)}), bf16[32,40,1024]{2,1,0:T(8,128)(2,1)}, u32[]{:S(2)}, u32[]{:S(2)}) async-start(bf16[32,40,1024]{2,1,0:T(8,128)(2,1)} %bitcast.333), calls=%async_computation.9 | async-start | bytes 5242880 | tf_op jit(solution)/shard_map/all_to_all | solution.py:139
  538.2 2.9 convolution_convert_fusion.12
  541.2 2.7 convolution_convert_fusion.13
  543.9 2.6 convolution_convert_fusion.14
  548.8 2.6 fusion.92
  551.5 2.6 fusion.94
  554.1 2.8 fusion.96
  560.7 11.9 %all-to-all-done.9 = bf16[32,40,1024]{2,1,0:T(8,128)(2,1)} async-done(((bf16[32,40,1024]{2,1,0:T(8,128)(2,1)}), bf16[32,40,1024]{2,1,0:T(8,128)(2,1)}, u32[]{:S(2)}, u32[]{:S(2)}) %all-to-all-start.9) | async-done | bytes 2621472 | tf_op jit(solution)/shard_map/all_to_all | solution.py:139
  589.8 7.5 %all-to-all-start.11 = ((bf16[64,8,2176]{2,1,0:T(8,128)(2,1)}), bf16[64,8,2176]{2,1,0:T(8,128)(2,1)}, u32[]{:S(2)}, u32[]{:S(2)}) async-start(bf16[64,8,2176]{2,1,0:T(8,128)(2,1)} %bitcast.338), calls=%async_computation.11 | async-start | bytes 4456448 | tf_op jit(solution)/shard_map/all_to_all | solution.py:208
  599.3 4.7 fusion.112
  611.5 16.4 %all-to-all-done.11 = bf16[64,8,2176]{2,1,0:T(8,128)(2,1)} async-done(((bf16[64,8,2176]{2,1,0:T(8,128)(2,1)}), bf16[64,8,2176]{2,1,0:T(8,128)(2,1)}, u32[]{:S(2)}, u32[]{:S(2)}) %all-to-all-start.11) | async-done | bytes 2228256 | tf_op jit(solution)/shard_map/all_to_all | solution.py:208
  627.9 7.3 %all-to-all-start.10 = ((bf16[64,8,3200]{2,1,0:T(8,128)(2,1)}), bf16[64,8,3200]{2,1,0:T(8,128)(2,1)}, u32[]{:S(2)}, u32[]{:S(2)}) async-start(bf16[64,8,3200]{2,1,0:T(8,128)(2,1)} %maximum_bitcast_fusion), calls=%async_computation.10 | async-start | bytes 6553600 | tf_op jit(solution)/shard_map/all_to_all | solution.py:208
  638.3 3.0 fusion.42
  642.3 46.1 %collective-permute-done.14 = bf16[128,3072]{1,0:T(8,128)(2,1)S(1)} collective-permute-done((bf16[128,3072]{1,0:T(8,128)(2,1)S(1)}, bf16[128,3072]{1,0:T(8,128)(2,1)S(1)}, u32[]{:S(2)}, u32[]{:S(2)}) %collective-permute-start.14) | collective-permute-done | bytes 786464 | tf_op jit(solution)/shard_map/ppermute | solution.py:167
  (476 shorter events, 158.6 us)
Async XLA Ops:
  12.3 11.9 %copy-start.61 = (bf16[2,128,1024]{2,1,0:T(8,128)(2,1)S(1)}, bf16[2,128,1024]{2,1,0:T(8,128)(2,1)}, u32[]{:S(2)}) copy-start(bf16[2,128,1024]{2,1,0:T(8,128)(2,1)} %param.23) | copy-start | bytes 1572868
  12.3 11.9 %copy-start.51 = (bf16[2,128,2048]{2,1,0:T(8,128)(2,1)S(1)}, bf16[2,128,2048]{2,1,0:T(8,128)(2,1)}, u32[]{:S(2)}) copy-start(bf16[2,128,2048]{2,1,0:T(8,128)(2,1)} %param.22) | copy-start | bytes 3145732
  12.3 75.1 %all-to-all-start = ((bf16[64,8,3200]{2,1,0:T(8,128)(2,1)}), bf16[64,8,3200]{2,1,0:T(8,128)(2,1)}, u32[]{:S(2)}, u32[]{:S(2)}) async-start(bf16[64,8,3200]{2,1,0:T(8,128)(2,1)} %broadcast_in_dim.73), calls=%async_computation | async-start | bytes 6553600 | tf_op jit(solution)/shard_map/all_to_all | solution.py:43
  24.2 201.3 %all-gather.2.cloned.1.call-start = ((), (), s32[]{:S(2)}) async-start(), calls=%async_computation.12 | async-start | bytes 6604800 | tf_op jit(solution)/shard_map/all_gather | solution.py:37
  24.3 54.6 %copy-start.110 = (s32[128,8]{0,1:T(8,128)S(1)}, s32[128,8]{0,1:T(8,128)}, u32[]{:S(2)}) copy-start(s32[128,8]{0,1:T(8,128)} %param.16) | copy-start | bytes 12292
  24.4 53.1 %collective-permute-start = (bf16[128,3072]{1,0:T(8,128)(2,1)S(1)}, bf16[128,3072]{1,0:T(8,128)(2,1)S(1)}, u32[]{:S(2)}, u32[]{:S(2)}) collective-permute-start(bf16[128,3072]{1,0:T(8,128)(2,1)S(1)} %pad_maximum_fusion.9), channel_id=1, source_target_pairs={{0,2},{2,0},{1,3},{3,1},{4,6},{6,4},{5,7},{7,5},{8,10},{10,8},{9,1... | collective-permute-start | bytes 2359304 | tf_op jit(solution)/shard_map/ppermute | solution.py:146
  78.9 3.8 collective-permute-start.1
  87.4 6.2 collective-permute-start.2
  106.0 5.5 copy-start.93
  121.1 10.6 %copy-start.62 = (bf16[2,128,1024]{2,1,0:T(8,128)(2,1)S(1)}, bf16[2,128,1024]{2,1,0:T(8,128)(2,1)}, u32[]{:S(2)}) copy-start(bf16[2,128,1024]{2,1,0:T(8,128)(2,1)} %param.23) | copy-start | bytes 1572868
  121.1 45.9 %all-to-all-start.1 = ((bf16[32,40,1024]{2,1,0:T(8,128)(2,1)}), bf16[32,40,1024]{2,1,0:T(8,128)(2,1)}, u32[]{:S(2)}, u32[]{:S(2)}) async-start(bf16[32,40,1024]{2,1,0:T(8,128)(2,1)} %bitcast.336), calls=%async_computation.1 | async-start | bytes 5242880 | tf_op jit(solution)/shard_map/all_to_all | solution.py:139
  133.9 53.7 %collective-permute-start.3 = (bf16[128,3072]{1,0:T(8,128)(2,1)}, bf16[128,3072]{1,0:T(8,128)(2,1)}, u32[]{:S(2)}, u32[]{:S(2)}) collective-permute-start(bf16[128,3072]{1,0:T(8,128)(2,1)} %pad_maximum_fusion.10), channel_id=1, source_target_pairs={{0,2},{2,0},{1,3},{3,1},{4,6},{6,4},{5,7},{7,5},{8,10},{10,8},{9,1... | collective-permute-start | bytes 2359304 | tf_op jit(solution)/shard_map/ppermute | solution.py:146
  170.8 6.1 copy-start.132
  179.9 43.1 %all-to-all-start.2 = ((bf16[32,40,1024]{2,1,0:T(8,128)(2,1)}), bf16[32,40,1024]{2,1,0:T(8,128)(2,1)}, u32[]{:S(2)}, u32[]{:S(2)}) async-start(bf16[32,40,1024]{2,1,0:T(8,128)(2,1)} %bitcast.340), calls=%async_computation.2 | async-start | bytes 5242880 | tf_op jit(solution)/shard_map/all_to_all | solution.py:139
  189.0 3.5 collective-permute-start.4
  190.4 6.8 copy-start.94
  190.4 6.7 copy-start.102
  227.1 16.7 %copy-start.86 = (f32[1024]{0:T(1024)}, f32[1024]{0:T(1024)S(1)}, u32[]{:S(2)}) copy-start(f32[1024]{0:T(1024)S(1)} %get-tuple-element.109) | copy-start | bytes 12292
  247.0 42.4 %all-to-all-start.3 = ((bf16[32,40,1024]{2,1,0:T(8,128)(2,1)}), bf16[32,40,1024]{2,1,0:T(8,128)(2,1)}, u32[]{:S(2)}, u32[]{:S(2)}) async-start(bf16[32,40,1024]{2,1,0:T(8,128)(2,1)} %bitcast.337), calls=%async_computation.3 | async-start | bytes 5242880 | tf_op jit(solution)/shard_map/all_to_all | solution.py:139
  289.4 40.2 %all-to-all-start.4 = ((bf16[32,40,1024]{2,1,0:T(8,128)(2,1)}), bf16[32,40,1024]{2,1,0:T(8,128)(2,1)}, u32[]{:S(2)}, u32[]{:S(2)}) async-start(bf16[32,40,1024]{2,1,0:T(8,128)(2,1)} %bitcast.335), calls=%async_computation.4 | async-start | bytes 5242880 | tf_op jit(solution)/shard_map/all_to_all | solution.py:139
  303.4 6.1 copy-start.133
  329.7 39.4 %all-to-all-start.5 = ((bf16[32,40,1024]{2,1,0:T(8,128)(2,1)}), bf16[32,40,1024]{2,1,0:T(8,128)(2,1)}, u32[]{:S(2)}, u32[]{:S(2)}) async-start(bf16[32,40,1024]{2,1,0:T(8,128)(2,1)} %bitcast.339), calls=%async_computation.5 | async-start | bytes 5242880 | tf_op jit(solution)/shard_map/all_to_all | solution.py:139
  336.1 6.2 copy-start.18
  342.3 7.2 %copy-start.40 = (bf16[1280,512]{1,0:T(8,128)(2,1)}, bf16[1280,512]{1,0:T(8,128)(2,1)S(1)}, u32[]{:S(2)}) copy-start(bf16[1280,512]{1,0:T(8,128)(2,1)S(1)} %get-tuple-element.85) | copy-start | bytes 3932164
  342.3 9.8 %copy-start.121 = (bf16[1280,512]{1,0:T(8,128)(2,1)}, bf16[1280,512]{1,0:T(8,128)(2,1)S(1)}, u32[]{:S(2)}) copy-start(bf16[1280,512]{1,0:T(8,128)(2,1)S(1)} %get-tuple-element.83) | copy-start | bytes 3932164
  356.0 30.6 %collective-permute-start.5 = (bf16[256,3072]{1,0:T(8,128)(2,1)}, bf16[256,3072]{1,0:T(8,128)(2,1)}, u32[]{:S(2)}, u32[]{:S(2)}) collective-permute-start(bf16[256,3072]{1,0:T(8,128)(2,1)} %pad_maximum_fusion.6), channel_id=1, source_target_pairs={{0,1},{1,0},{2,3},{3,2},{4,5},{5,4},{6,7},{7,6},{8,9},{9,8},{10,11... | collective-permute-start | bytes 4718600 | tf_op jit(solution)/shard_map/ppermute | solution.py:162
  369.1 39.7 %all-to-all-start.6 = ((bf16[32,40,1024]{2,1,0:T(8,128)(2,1)}), bf16[32,40,1024]{2,1,0:T(8,128)(2,1)}, u32[]{:S(2)}, u32[]{:S(2)}) async-start(bf16[32,40,1024]{2,1,0:T(8,128)(2,1)} %bitcast.332), calls=%async_computation.6 | async-start | bytes 5242880 | tf_op jit(solution)/shard_map/all_to_all | solution.py:139
  413.9 5.9 copy-start.101
  424.3 7.8 %collective-permute-start.6 = (bf16[512,1024]{1,0:T(8,128)(2,1)}, bf16[512,1024]{1,0:T(8,128)(2,1)}, u32[]{:S(2)}, u32[]{:S(2)}) collective-permute-start(bf16[512,1024]{1,0:T(8,128)(2,1)} %convolution_convert_fusion.11), channel_id=1, source_target_pairs={{0,1},{1,0},{2,3},{3,2},{4,5},{5,4},{6,7},{7,6},{8,9},{9,8},{10,11... | collective-permute-start | bytes 3145736 | tf_op jit(solution)/shard_map/ppermute | solution.py:203
  431.6 10.8 %copy-start.92 = (f32[1024]{0:T(1024)S(1)}, f32[1024]{0:T(1024)}, u32[]{:S(2)}) copy-start(f32[1024]{0:T(1024)} %copy-done.90) | copy-start | bytes 12292
  431.6 10.8 %copy-start.120 = (f32[128]{0:T(128)S(1)}, f32[128]{0:T(128)}, u32[]{:S(2)}) copy-start(f32[128]{0:T(128)} %copy-done.118) | copy-start | bytes 1540
  431.6 83.0 %collective-permute-start.7 = (bf16[512,2048]{1,0:T(8,128)(2,1)}, bf16[512,2048]{1,0:T(8,128)(2,1)}, u32[]{:S(2)}, u32[]{:S(2)}) collective-permute-start(bf16[512,2048]{1,0:T(8,128)(2,1)} %convolution_convert_fusion.7), channel_id=1, source_target_pairs={{0,1},{1,0},{2,3},{3,2},{4,5},{5,4},{6,7},{7,6},{8,9},{9,8},{10,11... | collective-permute-start | bytes 6291464 | tf_op jit(solution)/shard_map/ppermute | solution.py:203
  434.8 25.2 %all-to-all-start.7 = ((bf16[64,8,1024]{2,1,0:T(8,128)(2,1)}), bf16[64,8,1024]{2,1,0:T(8,128)(2,1)}, u32[]{:S(2)}, u32[]{:S(2)}) async-start(bf16[64,8,1024]{2,1,0:T(8,128)(2,1)} %fusion.64), calls=%async_computation.7 | async-start | bytes 2097152 | tf_op jit(solution)/shard_map/all_to_all | solution.py:208
  442.4 5.3 copy-start.31
  462.0 6.0 copy-start.85
  462.0 56.2 %all-to-all-start.8 = ((bf16[32,40,1024]{2,1,0:T(8,128)(2,1)}), bf16[32,40,1024]{2,1,0:T(8,128)(2,1)}, u32[]{:S(2)}, u32[]{:S(2)}) async-start(bf16[32,40,1024]{2,1,0:T(8,128)(2,1)} %bitcast.334), calls=%async_computation.8 | async-start | bytes 5242880 | tf_op jit(solution)/shard_map/all_to_all | solution.py:139
  474.9 38.2 %collective-permute-start.9 = (bf16[128,3072]{1,0:T(8,128)(2,1)S(1)}, bf16[128,3072]{1,0:T(8,128)(2,1)S(1)}, u32[]{:S(2)}, u32[]{:S(2)}) collective-permute-start(bf16[128,3072]{1,0:T(8,128)(2,1)S(1)} %slice.640), channel_id=1, source_target_pairs={{0,2},{2,0},{1,3},{3,1},{4,6},{6,4},{5,7},{7,5},{8,10},{10,8},{9,1... | collective-permute-start | bytes 2359304 | tf_op jit(solution)/shard_map/ppermute | solution.py:167
  478.3 34.8 %copy-start.1 = (f32[256,3072]{1,0:T(8,128)S(1)}, f32[256,3072]{1,0:T(8,128)}, u32[]{:S(2)}) copy-start(f32[256,3072]{1,0:T(8,128)} %maximum_add_fusion) | copy-start | bytes 9437188
  479.2 35.3 %copy-start.35 = (bf16[128,16,64]{0,2,1:T(8,128)(2,1)S(1)}, bf16[128,16,64]{0,2,1:T(8,128)(2,1)}, u32[]{:S(2)}) copy-start(bf16[128,16,64]{0,2,1:T(8,128)(2,1)} %pad_maximum_fusion.15) | copy-start | bytes 786436
  479.2 35.3 %copy-start.44 = (bf16[128,8,64]{0,2,1:T(8,128)(2,1)S(1)}, bf16[128,8,64]{0,2,1:T(8,128)(2,1)}, u32[]{:S(2)}) copy-start(bf16[128,8,64]{0,2,1:T(8,128)(2,1)} %pad_maximum_fusion.21) | copy-start | bytes 393220
  479.3 35.3 %copy-start.56 = (bf16[128,1024]{1,0:T(8,128)(2,1)S(1)}, bf16[128,1024]{1,0:T(8,128)(2,1)}, u32[]{:S(2)}) copy-start(bf16[128,1024]{1,0:T(8,128)(2,1)} %convolution_convert_fusion.20) | copy-start | bytes 786436
  479.3 35.3 %copy-start.64 = (bf16[8,64,128]{2,1,0:T(8,128)(2,1)S(1)}, bf16[8,64,128]{2,1,0:T(8,128)(2,1)}, u32[]{:S(2)}) copy-start(bf16[8,64,128]{2,1,0:T(8,128)(2,1)} %fusion.59) | copy-start | bytes 393220
  479.3 1.4 collective-permute-start.8
  518.2 6.2 copy-start.16
  529.0 43.6 %all-to-all-start.9 = ((bf16[32,40,1024]{2,1,0:T(8,128)(2,1)}), bf16[32,40,1024]{2,1,0:T(8,128)(2,1)}, u32[]{:S(2)}, u32[]{:S(2)}) async-start(bf16[32,40,1024]{2,1,0:T(8,128)(2,1)} %bitcast.333), calls=%async_computation.9 | async-start | bytes 5242880 | tf_op jit(solution)/shard_map/all_to_all | solution.py:139
  546.6 11.9 %collective-permute-start.10 = (bf16[256,3072]{1,0:T(8,128)(2,1)S(1)}, bf16[256,3072]{1,0:T(8,128)(2,1)S(1)}, u32[]{:S(2)}, u32[]{:S(2)}) collective-permute-start(bf16[256,3072]{1,0:T(8,128)(2,1)S(1)} %pad_maximum_fusion.7), channel_id=1, source_target_pairs={{0,1},{1,0},{2,3},{3,2},{4,5},{5,4},{6,7},{7,6},{8,9},{9,8},{10,11... | collective-permute-start | bytes 4718600 | tf_op jit(solution)/shard_map/ppermute | solution.py:162
  558.5 14.1 %copy-start.109 = (f32[128]{0:T(128)S(1)}, f32[128]{0:T(128)}, u32[]{:S(2)}) copy-start(f32[128]{0:T(128)} %copy-done.108) | copy-start | bytes 1540
  587.6 19.7 %collective-permute-start.11 = (bf16[512,2048]{1,0:T(8,128)(2,1)}, bf16[512,2048]{1,0:T(8,128)(2,1)}, u32[]{:S(2)}, u32[]{:S(2)}) collective-permute-start(bf16[512,2048]{1,0:T(8,128)(2,1)} %convolution_convert_fusion.6), channel_id=1, source_target_pairs={{0,1},{1,0},{2,3},{3,2},{4,5},{5,4},{6,7},{7,6},{8,9},{9,8},{10,11... | collective-permute-start | bytes 6291464 | tf_op jit(solution)/shard_map/ppermute | solution.py:203
  588.8 8.7 %copy-start.8 = (f32[128,1024]{1,0:T(8,128)S(1)}, f32[128,1024]{1,0:T(8,128)}, u32[]{:S(2)}) copy-start(f32[128,1024]{1,0:T(8,128)} %copy-done.7) | copy-start | bytes 1572868
  589.8 9.4 %copy-start.26 = (bf16[128,1024]{1,0:T(8,128)(2,1)S(1)}, bf16[128,1024]{1,0:T(8,128)(2,1)}, u32[]{:S(2)}) copy-start(bf16[128,1024]{1,0:T(8,128)(2,1)} %param.12) | copy-start | bytes 786436
  589.8 9.4 %copy-start.89 = (f32[1024]{0:T(1024)S(1)}, f32[1024]{0:T(1024)}, u32[]{:S(2)}) copy-start(f32[1024]{0:T(1024)} %copy-done.88) | copy-start | bytes 12292
  589.8 9.4 %copy-start.117 = (f32[128]{0:T(128)S(1)}, f32[128]{0:T(128)}, u32[]{:S(2)}) copy-start(f32[128]{0:T(128)} %copy-done.116) | copy-start | bytes 1540
  589.8 38.0 %all-to-all-start.11 = ((bf16[64,8,2176]{2,1,0:T(8,128)(2,1)}), bf16[64,8,2176]{2,1,0:T(8,128)(2,1)}, u32[]{:S(2)}, u32[]{:S(2)}) async-start(bf16[64,8,2176]{2,1,0:T(8,128)(2,1)} %bitcast.338), calls=%async_computation.11 | async-start | bytes 4456448 | tf_op jit(solution)/shard_map/all_to_all | solution.py:208
  598.9 5.3 copy-start.47
  598.9 5.3 copy-start.112
  598.9 7.9 %collective-permute-start.12 = (bf16[512,1024]{1,0:T(8,128)(2,1)S(1)}, bf16[512,1024]{1,0:T(8,128)(2,1)S(1)}, u32[]{:S(2)}, u32[]{:S(2)}) collective-permute-start(bf16[512,1024]{1,0:T(8,128)(2,1)S(1)} %convolution_convert_fusion.10), channel_id=1, source_target_pairs={{0,1},{1,0},{2,3},{3,2},{4,5},{5,4},{6,7},{7,6},{8,9},{9,8},{10,11... | collective-permute-start | bytes 3145736 | tf_op jit(solution)/shard_map/ppermute | solution.py:203
  605.3 1.5 collective-permute-start.13
  611.5 26.8 %copy-start.30 = (bf16[128,1280]{1,0:T(8,128)(2,1)S(1)}, bf16[128,1280]{1,0:T(8,128)(2,1)}, u32[]{:S(2)}) copy-start(bf16[128,1280]{1,0:T(8,128)(2,1)} %copy-done.29) | copy-start | bytes 983044
  627.9 65.3 %all-to-all-start.10 = ((bf16[64,8,3200]{2,1,0:T(8,128)(2,1)}), bf16[64,8,3200]{2,1,0:T(8,128)(2,1)}, u32[]{:S(2)}, u32[]{:S(2)}) async-start(bf16[64,8,3200]{2,1,0:T(8,128)(2,1)} %maximum_bitcast_fusion), calls=%async_computation.10 | async-start | bytes 6553600 | tf_op jit(solution)/shard_map/all_to_all | solution.py:208
  635.2 6.1 copy-start.60
  636.7 51.7 %copy-start.2 = (f32[256,3072]{1,0:T(8,128)S(1)}, f32[256,3072]{1,0:T(8,128)}, u32[]{:S(2)}) copy-start(f32[256,3072]{1,0:T(8,128)} %maximum_add_fusion.1) | copy-start | bytes 9437188
  636.7 51.7 %collective-permute-start.14 = (bf16[128,3072]{1,0:T(8,128)(2,1)S(1)}, bf16[128,3072]{1,0:T(8,128)(2,1)S(1)}, u32[]{:S(2)}, u32[]{:S(2)}) collective-permute-start(bf16[128,3072]{1,0:T(8,128)(2,1)S(1)} %slice.639), channel_id=1, source_target_pairs={{0,2},{2,0},{1,3},{3,1},{4,6},{6,4},{5,7},{7,5},{8,10},{10,8},{9,1... | collective-permute-start | bytes 2359304 | tf_op jit(solution)/shard_map/ppermute | solution.py:167
  641.3 47.3 %copy-start = (f32[128,3072]{1,0:T(8,128)S(1)}, f32[128,3072]{1,0:T(8,128)}, u32[]{:S(2)}) copy-start(f32[128,3072]{1,0:T(8,128)} %convert_add_fusion) | copy-start | bytes 4718596
  691.2 6.4 copy-start.83
  (98 other events, 246.0 us)
Sparse Core Ops, SparseCore 0:
  101.5 102.9 all-gather.1

commit v8 on v5

--- a/solution.py
+++ b/solution.py
@@ -38,13 +38,14 @@
     return lax.all_gather(both, axis, axis=0, tiled=True)
 
 
-def sent_by_chips(own):
+def sent_by_chips(own, beside):
     core = lax.axis_index("c")
     copies = jnp.broadcast_to(own[None], (64,) + own.shape)
     mine = lax.all_to_all(copies, CHIP_AXES, split_axis=0, concat_axis=0, tiled=True)
+    mine, beside = lax.optimization_barrier((mine, beside))
     other = lax.ppermute(mine, "c", SWAP)
     pair = [jnp.where(core == 0, mine, other), jnp.where(core == 0, other, mine)]
-    return jnp.stack(pair, axis=1).reshape(MODEL_WIDTH, -1)
+    return jnp.stack(pair, axis=1).reshape(MODEL_WIDTH, -1), beside
 
 
 def cut_weights(gathered, widths):
@@ -141,9 +142,17 @@
     ).reshape(ROWS, MODEL_WIDTH)
 
 
-def gather_expert(own_in, own_out):
-    both = jnp.concatenate([own_in, own_out], axis=1)
-    return lax.all_gather(both, GROUP_AXES, axis=0, tiled=True)
+def gather_chip(own):
+    other = lax.ppermute(own, "zl", SWAP)
+    first = lax.axis_index("zl") == 0
+    return jnp.stack([jnp.where(first, own, other), jnp.where(first, other, own)])
+
+
+def gather_core(pair):
+    other = lax.ppermute(pair, "c", SWAP)
+    first = lax.axis_index("c") == 0
+    both = [jnp.where(first, pair, other), jnp.where(first, other, pair)]
+    return jnp.stack(both, axis=1).reshape(-1, pair.shape[2])
 
 
 def scatter_expert(grads):
@@ -448,21 +457,23 @@
     ]
     lead = [part.reshape(8, -1) for part in own_dense[0]]
     fill = jnp.zeros((8, 128 - E - 2), jnp.bfloat16)
-    lead = sent_by_chips(jnp.concatenate(lead + [fill], axis=1))
-    dense = [cut_weights(lead, DENSE_WIDTHS), None]
-    experts = [gather_expert(expert_in[0], expert_out[0]), None]
-    experts[0], own_dense = lax.optimization_barrier((experts[0], own_dense))
-    gathered = sent_together(own_dense[1], AXES)
-    gathered, expert_in, expert_out = lax.optimization_barrier((gathered, expert_in, expert_out))
-    dense[1] = cut_weights(gathered, DENSE_WIDTHS)
-    experts[1] = gather_expert(expert_in[1], expert_out[1])
     position, live_row, allowed = seq_layout(seq_lengths, seq_owner, device)
     live = live_row.astype(jnp.float32)
     cosine_table, sine_values = rope_tables(position)
     routed, chosen = dispatch_table(routes, live_row)
+    own_experts = [
+        jnp.concatenate([expert_in[layer], expert_out[layer]], axis=1) for layer in layers
+    ]
+    beside = order, live, allowed, cosine_table, sine_values, routed, chosen, own_experts
+    lead, beside = sent_by_chips(jnp.concatenate(lead + [fill], axis=1), beside)
+    order, live, allowed, cosine_table, sine_values, routed, chosen, own_experts = beside
+    chip_experts = gather_chip(own_experts[0])
+    lead, own_dense = lax.optimization_barrier((lead, own_dense))
+    dense = [cut_weights(lead, DENSE_WIDTHS), None]
+    dense[1] = cut_weights(sent_together(own_dense[1], AXES), DENSE_WIDTHS)
     hidden = hidden_in.astype(jnp.float32)
     grad_hidden = cotangent.astype(jnp.float32)
-    saved = []
+    saved, experts = [], []
     for layer in layers:
         attn_stash = attend_forward(
             hidden, dense[layer][0], dense[layer][3], live, allowed, cosine_table, sine_values
@@ -470,17 +481,25 @@
         mixed_low = attn_stash[-1]
         hidden = hidden + jnp.dot(mixed_low, dense[layer][1], preferred_element_type=jnp.float32)
         rows, route_stash = route_rows(hidden, dense[layer], routed, chosen)
+        rows, chip_experts = lax.optimization_barrier((rows, chip_experts))
         rows_here = trade_rows(rows)
+        expert = gather_core(chip_experts)
         moved = reorder(attn_stash[2], order), reorder(mixed_low, order)
         grad_rows = None
         if layer == last:
             slots = slot_gradients(grad_hidden, route_stash[-1])
             slots, rows_here = lax.optimization_barrier((slots, rows_here))
             grad_rows = trade_rows(slots)
-        results, pre = feed_forward(rows_here, experts[layer])
+        else:
+            rows_here, expert = lax.optimization_barrier((rows_here, expert))
+        experts.append(expert)
+        results, pre = feed_forward(rows_here, expert)
         if layer == last:
             results, grad_rows = lax.optimization_barrier((results, grad_rows))
         returned = trade_rows(results)
+        if layer != last:
+            returned, own_expert = lax.optimization_barrier((returned, own_experts[layer + 1]))
+            chip_experts = gather_chip(own_expert)
         hidden = hidden + jnp.dot(route_stash[-1], returned, preferred_element_type=jnp.float32)
         saved.append((attn_stash, moved, route_stash, rows_here, pre, returned, grad_rows))
     output_low = hidden.astype(jnp.bfloat16)
@@ -490,7 +509,7 @@
         if grad_rows is None:
             slots = slot_gradients(grad_hidden, route_stash[-1])
             grad_rows, sums = lax.optimization_barrier((trade_rows(slots), sums))
-            joined = jnp.concatenate(sums, axis=1)
+            joined = [jnp.concatenate([sums[0], sums[2]], axis=1), sums[1]]
         grad_in_rows, expert_grads = feed_backward(grad_rows, rows_here, pre, experts[layer])
         grad_slots = trade_rows(grad_in_rows)
         router_grad, grad_routed = route_backward(
@@ -499,7 +518,7 @@
         expert_sums[layer] = scatter_expert(expert_grads)
         if layer != last:
             grad_slots, joined = lax.optimization_barrier((grad_slots, joined))
-            done_last = chip_sum(joined)
+            done_last = chip_sum(joined[0]), chip_sum(joined[1])
         grad_h1, gain_two_grad = rows_backward(
             grad_hidden, dense[layer], chosen, grad_slots, grad_routed, route_stash
         )
@@ -508,9 +527,10 @@
         )
         small = small_halves(router_grad, gain_one_grad, gain_two_grad, order)
         sums = [core_sum(qkv_halves), proj_sum, core_sum(small)]
+    proj_done = chip_sum(sums.pop(1))
     done = chip_sum(jnp.concatenate(sums, axis=1))
-    first = [done[:, :2048], done[:, 2048:3072], done[:, 3072:]]
-    second = [done_last[:, :2048], done_last[:, 2048:3072], done_last[:, 3072:]]
+    first = [done[:, :2048], proj_done, done[:, 2048:]]
+    second = [done_last[0][:, :2048], done_last[1], done_last[0][:, 2048:]]
     qkv, proj, small = [jnp.stack(pair) for pair in zip(first, second)]
     both = jnp.stack(expert_sums).astype(jnp.float32)
     return (

time: 657 us -> 675 us (1.027)
  blocking collectives: 46.9 us -> 0 us
  matrix products: 158 us -> 184 us
  starting transfers between devices: 83 us -> 105 us
  other arithmetic: 40.8 us -> 62.7 us
  waiting for transfers between devices: 270 us -> 261 us
    all_gather x2 -> x0, waiting for transfers between devices: 49.2 us -> none  [gather_expert(): return lax.all_gather(both, GROUP_AXES, axis=0, tiled=True)]
    all_to_all x1 -> x0, blocking collectives: 46.9 us -> none  [trade_rows(): lax.all_to_all(rows.reshape(E, ROOM, MODEL_WIDTH), EXPERT_AXES, split_axi...]
    another operation x14 -> x22, other arithmetic: 5.17 us -> 25.1 us  [the longest x2 3.15 us: sent_by_chips(): return jnp.stack(pair, axis=1).reshape(MODEL_WIDTH, -1)]
    ppermute x0 -> x4, waiting for transfers between devices: none -> 18.9 us  [the longest x2 18.9 us: gather_chip(): other = lax.ppermute(own, 'zl', SWAP)]
    all_to_all x7 -> x8, waiting for transfers between devices: 134 us -> 152 us  [trade_rows(): lax.all_to_all(rows.reshape(E, ROOM, MODEL_WIDTH), EXPERT_AXES, split_axi...]
    all_to_all x2 -> x4, starting transfers between devices: 13.7 us -> 28.7 us  [chip_sum(): lax.all_to_all(parts, Z_AXES + ('x', 'y'), split_axis=0, concat_axis=0, t...]
    all_to_all x7 -> x8, starting transfers between devices: 55.9 us -> 59.2 us  [trade_rows(): lax.all_to_all(rows.reshape(E, ROOM, MODEL_WIDTH), EXPERT_AXES, split_axi...]
    all_to_all x2 -> x4, waiting for transfers between devices: 47.4 us -> 50.3 us  [chip_sum(): lax.all_to_all(parts, Z_AXES + ('x', 'y'), split_axis=0, concat_axis=0, t...]
  transfers between devices with their start and end apart: 22 -> 27, of which waited for: 12 -> 16; matrix products, arithmetic and copies ran while one was open for 28% -> 33% of each run, Pallas kernels for 0% -> 0%
where the time goes in v8:
time: 675 us; the launch traced here: 664 us
  waiting for transfers between devices  261 us (39%)
  matrix products  184 us (27%)
  starting transfers between devices  105 us (16%)
  other arithmetic  62.7 us (9%)
  local copies, waits for them, and re-layouts  35 us (5%)
  between operations  16 us (2%)
    all_to_all x8, waiting for transfers between devices, trade_rows(): lax.all_to_all(rows.reshape(E, ROOM, MODEL_WIDTH), EXPERT_AXES, split_axi...  152 us
    all_to_all x8, starting transfers between devices, trade_rows(): lax.all_to_all(rows.reshape(E, ROOM, MODEL_WIDTH), EXPERT_AXES, split_axi...  59.2 us
    all_to_all x4, waiting for transfers between devices, chip_sum(): lax.all_to_all(parts, Z_AXES + ('x', 'y'), split_axis=0, concat_axis=0, t...  50.3 us
    all_to_all x1, waiting for transfers between devices, sent_by_chips(): lax.all_to_all(copies, CHIP_AXES, split_axis=0, concat_axis=0, tiled=True)  34.5 us
    all_to_all x4, starting transfers between devices, chip_sum(): lax.all_to_all(parts, Z_AXES + ('x', 'y'), split_axis=0, concat_axis=0, t...  28.7 us
    ppermute x2, waiting for transfers between devices, gather_chip(): other = lax.ppermute(own, 'zl', SWAP)  18.9 us
  transfers between devices with their start and end apart: 27, of which 16 were waited for; matrix products, arithmetic and copies ran while one was open for 33% of the time, Pallas kernels for 0%

profile of v8, /device:TPU:2, one launch (start us, length us, event | category | flops | bytes accessed | tf_op | source)
XLA Modules:
  0.0 663.5 jit_solution(18331273047208126826)
XLA Ops:
  13.5 11.8 %all-to-all-start = ((bf16[64,8,3200]{2,1,0:T(8,128)(2,1)}), bf16[64,8,3200]{2,1,0:T(8,128)(2,1)}, u32[]{:S(2)}, u32[]{:S(2)}) async-start(bf16[64,8,3200]{2,1,0:T(8,128)(2,1)} %broadcast_in_dim.73), calls=%async_computation | async-start | bytes 6553600 | tf_op jit(solution)/shard_map/all_to_all | solution.py:44
  31.9 34.5 %all-to-all-done = bf16[64,8,3200]{2,1,0:T(8,128)(2,1)} async-done(((bf16[64,8,3200]{2,1,0:T(8,128)(2,1)}), bf16[64,8,3200]{2,1,0:T(8,128)(2,1)}, u32[]{:S(2)}, u32[]{:S(2)}) %all-to-all-start) | async-done | bytes 3276832 | tf_op jit(solution)/shard_map/all_to_all | solution.py:44
  67.6 5.0 collective-permute-done
  72.6 3.5 select_bitcast_fusion.1
  76.1 3.4 pad_maximum_fusion
  80.4 6.5 collective-permute-done.1
  106.5 8.3 %all-to-all-start.1 = ((bf16[32,40,1024]{2,1,0:T(8,128)(2,1)}), bf16[32,40,1024]{2,1,0:T(8,128)(2,1)}, u32[]{:S(2)}, u32[]{:S(2)}) async-start(bf16[32,40,1024]{2,1,0:T(8,128)(2,1)} %bitcast.354), calls=%async_computation.1 | async-start | bytes 5242880 | tf_op jit(solution)/shard_map/all_to_all | solution.py:140
  118.9 31.5 %all-to-all-done.1 = bf16[32,40,1024]{2,1,0:T(8,128)(2,1)} async-done(((bf16[32,40,1024]{2,1,0:T(8,128)(2,1)}), bf16[32,40,1024]{2,1,0:T(8,128)(2,1)}, u32[]{:S(2)}, u32[]{:S(2)}) %all-to-all-start.1) | async-done | bytes 2621472 | tf_op jit(solution)/shard_map/all_to_all | solution.py:140
  150.4 3.7 fusion.82
  154.1 6.2 multiply_convert_fusion.5
  160.3 3.1 convolution_convert_fusion.4
  163.4 7.5 %all-to-all-start.2 = ((bf16[32,40,1024]{2,1,0:T(8,128)(2,1)}), bf16[32,40,1024]{2,1,0:T(8,128)(2,1)}, u32[]{:S(2)}, u32[]{:S(2)}) async-start(bf16[32,40,1024]{2,1,0:T(8,128)(2,1)} %bitcast.374), calls=%async_computation.2 | async-start | bytes 5242880 | tf_op jit(solution)/shard_map/all_to_all | solution.py:140
  172.2 33.1 %all-to-all-done.2 = bf16[32,40,1024]{2,1,0:T(8,128)(2,1)} async-done(((bf16[32,40,1024]{2,1,0:T(8,128)(2,1)}), bf16[32,40,1024]{2,1,0:T(8,128)(2,1)}, u32[]{:S(2)}, u32[]{:S(2)}) %all-to-all-start.2) | async-done | bytes 2621472 | tf_op jit(solution)/shard_map/all_to_all | solution.py:140
  210.3 12.4 %collective-permute-done.3 = bf16[128,3072]{1,0:T(8,128)(2,1)S(1)} collective-permute-done((bf16[128,3072]{1,0:T(8,128)(2,1)}, bf16[128,3072]{1,0:T(8,128)(2,1)S(1)}, u32[]{:S(2)}, u32[]{:S(2)}) %collective-permute-start.3) | collective-permute-done | bytes 786464 | tf_op jit(solution)/shard_map/ppermute | solution.py:146
  225.6 2.9 fusion.5
  245.6 8.9 %all-to-all-start.3 = ((bf16[32,40,1024]{2,1,0:T(8,128)(2,1)}), bf16[32,40,1024]{2,1,0:T(8,128)(2,1)}, u32[]{:S(2)}, u32[]{:S(2)}) async-start(bf16[32,40,1024]{2,1,0:T(8,128)(2,1)} %bitcast.353), calls=%async_computation.3 | async-start | bytes 5242880 | tf_op jit(solution)/shard_map/all_to_all | solution.py:140
  259.5 3.3 convolution_convert_fusion.3
  262.8 24.1 %all-to-all-done.3 = bf16[32,40,1024]{2,1,0:T(8,128)(2,1)} async-done(((bf16[32,40,1024]{2,1,0:T(8,128)(2,1)}), bf16[32,40,1024]{2,1,0:T(8,128)(2,1)}, u32[]{:S(2)}, u32[]{:S(2)}) %all-to-all-start.3) | async-done | bytes 2621472 | tf_op jit(solution)/shard_map/all_to_all | solution.py:140
  286.8 6.7 %all-to-all-start.4 = ((bf16[32,40,1024]{2,1,0:T(8,128)(2,1)}), bf16[32,40,1024]{2,1,0:T(8,128)(2,1)}, u32[]{:S(2)}, u32[]{:S(2)}) async-start(bf16[32,40,1024]{2,1,0:T(8,128)(2,1)} %bitcast.352), calls=%async_computation.4 | async-start | bytes 5242880 | tf_op jit(solution)/shard_map/all_to_all | solution.py:140
  296.2 4.5 fusion.72
  300.6 6.1 multiply_convert_fusion.4
  307.8 3.0 convolution_convert_fusion.1
  310.8 15.7 %all-to-all-done.4 = bf16[32,40,1024]{2,1,0:T(8,128)(2,1)} async-done(((bf16[32,40,1024]{2,1,0:T(8,128)(2,1)}), bf16[32,40,1024]{2,1,0:T(8,128)(2,1)}, u32[]{:S(2)}, u32[]{:S(2)}) %all-to-all-start.4) | async-done | bytes 2621472 | tf_op jit(solution)/shard_map/all_to_all | solution.py:140
  326.5 7.0 %all-to-all-start.5 = ((bf16[32,40,1024]{2,1,0:T(8,128)(2,1)}), bf16[32,40,1024]{2,1,0:T(8,128)(2,1)}, u32[]{:S(2)}, u32[]{:S(2)}) async-start(bf16[32,40,1024]{2,1,0:T(8,128)(2,1)} %bitcast.373), calls=%async_computation.5 | async-start | bytes 5242880 | tf_op jit(solution)/shard_map/all_to_all | solution.py:140
  338.3 5.0 multiply_convert_fusion.2
  344.8 3.0 add_convert_fusion.1
  347.8 17.8 %all-to-all-done.5 = bf16[32,40,1024]{2,1,0:T(8,128)(2,1)} async-done(((bf16[32,40,1024]{2,1,0:T(8,128)(2,1)}), bf16[32,40,1024]{2,1,0:T(8,128)(2,1)}, u32[]{:S(2)}, u32[]{:S(2)}) %all-to-all-start.5) | async-done | bytes 2621472 | tf_op jit(solution)/shard_map/all_to_all | solution.py:140
  365.6 7.0 %all-to-all-start.6 = ((bf16[32,40,1024]{2,1,0:T(8,128)(2,1)}), bf16[32,40,1024]{2,1,0:T(8,128)(2,1)}, u32[]{:S(2)}, u32[]{:S(2)}) async-start(bf16[32,40,1024]{2,1,0:T(8,128)(2,1)} %bitcast.350), calls=%async_computation.6 | async-start | bytes 5242880 | tf_op jit(solution)/shard_map/all_to_all | solution.py:140
  374.9 4.4 convolution_convert_fusion.12
  379.3 4.4 convolution_convert_fusion.13
  383.7 4.4 convolution_convert_fusion.14
  388.1 2.8 fusion.13
  394.0 10.9 %all-to-all-done.6 = bf16[32,40,1024]{2,1,0:T(8,128)(2,1)} async-done(((bf16[32,40,1024]{2,1,0:T(8,128)(2,1)}), bf16[32,40,1024]{2,1,0:T(8,128)(2,1)}, u32[]{:S(2)}, u32[]{:S(2)}) %all-to-all-start.6) | async-done | bytes 2621472 | tf_op jit(solution)/shard_map/all_to_all | solution.py:140
  409.3 3.1 fusion.48
  422.9 3.9 multiply_reduce_fusion.5
  430.2 6.7 %all-to-all-start.7 = ((bf16[32,40,1024]{2,1,0:T(8,128)(2,1)}), bf16[32,40,1024]{2,1,0:T(8,128)(2,1)}, u32[]{:S(2)}, u32[]{:S(2)}) async-start(bf16[32,40,1024]{2,1,0:T(8,128)(2,1)} %bitcast.351), calls=%async_computation.7 | async-start | bytes 5242880 | tf_op jit(solution)/shard_map/all_to_all | solution.py:140
  437.0 3.3 convolution_convert_fusion.7
  440.3 2.9 pad_maximum_fusion.4
  443.3 2.6 convolution_convert_fusion.11
  454.0 3.3 convolution_multiply_fusion
  459.2 2.6 add_convert_fusion.5
  461.9 3.6 add_convert_fusion.3
  465.6 4.3 all-to-all-done.7
  469.9 6.3 multiply_convert_fusion
  477.7 3.0 add_convert_fusion
  480.7 7.1 %all-to-all-start.8 = ((bf16[32,40,1024]{2,1,0:T(8,128)(2,1)}), bf16[32,40,1024]{2,1,0:T(8,128)(2,1)}, u32[]{:S(2)}, u32[]{:S(2)}) async-start(bf16[32,40,1024]{2,1,0:T(8,128)(2,1)} %bitcast.349), calls=%async_computation.8 | async-start | bytes 5242880 | tf_op jit(solution)/shard_map/all_to_all | solution.py:140
  491.1 3.8 convolution_convert_fusion.15
  494.9 3.4 convolution_convert_fusion.16
  498.3 3.3 convolution_convert_fusion.17
  503.6 3.2 pad_maximum_fusion.5
  506.8 14.7 %all-to-all-done.8 = bf16[32,40,1024]{2,1,0:T(8,128)(2,1)} async-done(((bf16[32,40,1024]{2,1,0:T(8,128)(2,1)}), bf16[32,40,1024]{2,1,0:T(8,128)(2,1)}, u32[]{:S(2)}, u32[]{:S(2)}) %all-to-all-start.8) | async-done | bytes 2621472 | tf_op jit(solution)/shard_map/all_to_all | solution.py:140
  521.5 2.6 multiply_reduce_fusion.2
  533.4 8.5 %all-to-all-start.12 = ((bf16[64,8,1024]{2,1,0:T(8,128)(2,1)}), bf16[64,8,1024]{2,1,0:T(8,128)(2,1)}, u32[]{:S(2)}, u32[]{:S(2)}) async-start(bf16[64,8,1024]{2,1,0:T(8,128)(2,1)} %bitcast.368), calls=%async_computation.12 | async-start | bytes 2097152 | tf_op jit(solution)/shard_map/all_to_all | solution.py:200
  549.8 2.7 fusion.63
  552.4 7.8 %all-to-all-done.12 = bf16[64,8,1024]{2,1,0:T(8,128)(2,1)} async-done(((bf16[64,8,1024]{2,1,0:T(8,128)(2,1)}), bf16[64,8,1024]{2,1,0:T(8,128)(2,1)}, u32[]{:S(2)}, u32[]{:S(2)}) %all-to-all-start.12) | async-done | bytes 1048608 | tf_op jit(solution)/shard_map/all_to_all | solution.py:200
  560.2 6.3 all-to-all-start.11
  568.3 3.0 convolution_convert_fusion.6
  571.4 12.1 %all-to-all-done.11 = bf16[64,8,1024]{2,1,0:T(8,128)(2,1)} async-done(((bf16[64,8,1024]{2,1,0:T(8,128)(2,1)}), bf16[64,8,1024]{2,1,0:T(8,128)(2,1)}, u32[]{:S(2)}, u32[]{:S(2)}) %all-to-all-start.11) | async-done | bytes 1048608 | tf_op jit(solution)/shard_map/all_to_all | solution.py:200
  583.5 6.8 %all-to-all-start.10 = ((bf16[64,8,2176]{2,1,0:T(8,128)(2,1)}), bf16[64,8,2176]{2,1,0:T(8,128)(2,1)}, u32[]{:S(2)}, u32[]{:S(2)}) async-start(bf16[64,8,2176]{2,1,0:T(8,128)(2,1)} %bitcast.355), calls=%async_computation.10 | async-start | bytes 4456448 | tf_op jit(solution)/shard_map/all_to_all | solution.py:200
  591.6 4.8 fusion.93
  597.7 3.1 fusion.41
  604.7 15.0 %all-to-all-done.10 = bf16[64,8,2176]{2,1,0:T(8,128)(2,1)} async-done(((bf16[64,8,2176]{2,1,0:T(8,128)(2,1)}), bf16[64,8,2176]{2,1,0:T(8,128)(2,1)}, u32[]{:S(2)}, u32[]{:S(2)}) %all-to-all-start.10) | async-done | bytes 2228256 | tf_op jit(solution)/shard_map/all_to_all | solution.py:200
  619.8 7.0 %all-to-all-start.9 = ((bf16[64,8,2176]{2,1,0:T(8,128)(2,1)}), bf16[64,8,2176]{2,1,0:T(8,128)(2,1)S(1)}, u32[]{:S(2)}, u32[]{:S(2)}) async-start(bf16[64,8,2176]{2,1,0:T(8,128)(2,1)} %maximum_bitcast_fusion), calls=%async_computation.9 | async-start | bytes 4456448 | tf_op jit(solution)/shard_map/all_to_all | solution.py:200
  639.1 15.4 %all-to-all-done.9 = bf16[64,8,2176]{2,1,0:T(8,128)(2,1)S(1)} async-done(((bf16[64,8,2176]{2,1,0:T(8,128)(2,1)}), bf16[64,8,2176]{2,1,0:T(8,128)(2,1)S(1)}, u32[]{:S(2)}, u32[]{:S(2)}) %all-to-all-start.9) | async-done | bytes 2228256 | tf_op jit(solution)/shard_map/all_to_all | solution.py:200
  (453 shorter events, 158.9 us)
Async XLA Ops:
  13.5 11.9 %copy-start.111 = (s32[512]{0:T(512)S(1)}, s32[512]{0:T(512)}, u32[]{:S(2)}) copy-start(s32[512]{0:T(512)} %param.15) | copy-start | bytes 6148
  13.5 12.6 %copy-start.112 = (s32[512]{0:T(512)S(1)}, s32[512]{0:T(512)}, u32[]{:S(2)}) copy-start(s32[512]{0:T(512)} %param.14) | copy-start | bytes 6148
  13.5 13.1 %copy-start.109 = (s32[128,8]{0,1:T(8,128)S(1)}, s32[128,8]{0,1:T(8,128)}, u32[]{:S(2)}) copy-start(s32[128,8]{0,1:T(8,128)} %param.16) | copy-start | bytes 12292
  13.5 14.9 %copy-start.62 = (bf16[2,128,1024]{2,1,0:T(8,128)(2,1)S(1)}, bf16[2,128,1024]{2,1,0:T(8,128)(2,1)}, u32[]{:S(2)}) copy-start(bf16[2,128,1024]{2,1,0:T(8,128)(2,1)} %param.23) | copy-start | bytes 1572868
  13.5 52.9 %all-to-all-start = ((bf16[64,8,3200]{2,1,0:T(8,128)(2,1)}), bf16[64,8,3200]{2,1,0:T(8,128)(2,1)}, u32[]{:S(2)}, u32[]{:S(2)}) async-start(bf16[64,8,3200]{2,1,0:T(8,128)(2,1)} %broadcast_in_dim.73), calls=%async_computation | async-start | bytes 6553600 | tf_op jit(solution)/shard_map/all_to_all | solution.py:44
  25.3 198.8 %all-gather.2.cloned.1.call-start = ((), (), s32[]{:S(2)}) async-start(), calls=%async_computation.15 | async-start | bytes 6604800 | tf_op jit(solution)/shard_map/all_gather | solution.py:38
  29.3 37.1 %copy-start.25 = (bf16[128,1024]{1,0:T(8,128)(2,1)S(1)}, bf16[128,1024]{1,0:T(8,128)(2,1)}, u32[]{:S(2)}) copy-start(bf16[128,1024]{1,0:T(8,128)(2,1)} %param.12) | copy-start | bytes 786436
  66.4 6.2 collective-permute-start
  66.5 24.8 %copy-start.116 = (f32[128]{0:T(128)}, f32[128]{0:T(128)S(1)}, u32[]{:S(2)}) copy-start(f32[128]{0:T(128)S(1)} %add_rsqrt_fusion.3) | copy-start | bytes 1540
  66.5 20.3 %collective-permute-start.1 = (bf16[128,3072]{1,0:T(8,128)(2,1)}, bf16[128,3072]{1,0:T(8,128)(2,1)}, u32[]{:S(2)}, u32[]{:S(2)}) collective-permute-start(bf16[128,3072]{1,0:T(8,128)(2,1)} %get-tuple-element.52), channel_id=1, source_target_pairs={{0,2},{2,0},{1,3},{3,1},{4,6},{6,4},{5,7},{7,5},{8,10},{10,8},{9,1... | collective-permute-start | bytes 2359304 | tf_op jit(solution)/shard_map/ppermute | solution.py:146
  92.1 5.5 copy-start.93
  96.9 4.8 copy-start.66
  96.9 4.8 copy-start.68
  104.2 66.7 %copy-start.20 = (bf16[128,1024]{1,0:T(8,128)(2,1)}, bf16[128,1024]{1,0:T(8,128)(2,1)S(1)}, u32[]{:S(2)}) copy-start(bf16[128,1024]{1,0:T(8,128)(2,1)S(1)} %multiply_convert_fusion.10) | copy-start | bytes 786436
  106.5 8.4 %collective-permute-start.2 = (bf16[2,128,3072]{2,1,0:T(8,128)(2,1)}, bf16[2,128,3072]{2,1,0:T(8,128)(2,1)}, u32[]{:S(2)}, u32[]{:S(2)}) collective-permute-start(bf16[2,128,3072]{2,1,0:T(8,128)(2,1)} %pad_maximum_fusion.6), channel_id=1, source_target_pairs={{0,1},{1,0},{2,3},{3,2},{4,5},{5,4},{6,7},{7,6},{8,9},{9,8},{10,11... | collective-permute-start | bytes 4718600 | tf_op jit(solution)/shard_map/ppermute | solution.py:152
  106.5 43.8 %all-to-all-start.1 = ((bf16[32,40,1024]{2,1,0:T(8,128)(2,1)}), bf16[32,40,1024]{2,1,0:T(8,128)(2,1)}, u32[]{:S(2)}, u32[]{:S(2)}) async-start(bf16[32,40,1024]{2,1,0:T(8,128)(2,1)} %bitcast.354), calls=%async_computation.1 | async-start | bytes 5242880 | tf_op jit(solution)/shard_map/all_to_all | solution.py:140
  154.1 6.2 copy-start.124
  163.4 41.8 %all-to-all-start.2 = ((bf16[32,40,1024]{2,1,0:T(8,128)(2,1)}), bf16[32,40,1024]{2,1,0:T(8,128)(2,1)}, u32[]{:S(2)}, u32[]{:S(2)}) async-start(bf16[32,40,1024]{2,1,0:T(8,128)(2,1)} %bitcast.374), calls=%async_computation.2 | async-start | bytes 5242880 | tf_op jit(solution)/shard_map/all_to_all | solution.py:140
  172.1 50.7 %copy-start.94 = (f32[128]{0:T(128)}, f32[128]{0:T(128)S(1)}, u32[]{:S(2)}) copy-start(f32[128]{0:T(128)S(1)} %get-tuple-element.147) | copy-start | bytes 1540
  172.2 50.7 %copy-start.102 = (f32[128]{0:T(128)}, f32[128]{0:T(128)S(1)}, u32[]{:S(2)}) copy-start(f32[128]{0:T(128)S(1)} %fusion.170) | copy-start | bytes 1540
  205.2 17.5 %copy-start.30 = (bf16[128,3072]{1,0:T(8,128)(2,1)S(1)}, bf16[128,3072]{1,0:T(8,128)(2,1)}, u32[]{:S(2)}) copy-start(bf16[128,3072]{1,0:T(8,128)(2,1)} %get-tuple-element.64) | copy-start | bytes 2359300
  205.2 17.5 %collective-permute-start.3 = (bf16[128,3072]{1,0:T(8,128)(2,1)}, bf16[128,3072]{1,0:T(8,128)(2,1)S(1)}, u32[]{:S(2)}, u32[]{:S(2)}) collective-permute-start(bf16[128,3072]{1,0:T(8,128)(2,1)} %get-tuple-element.64), channel_id=1, source_target_pairs={{0,2},{2,0},{1,3},{3,1},{4,6},{6,4},{5,7},{7,5},{8,10},{10,8},{9,1... | collective-permute-start | bytes 2359304 | tf_op jit(solution)/shard_map/ppermute | solution.py:146
  210.3 15.3 %copy-start.1 = (f32[128,1024]{1,0:T(8,128)}, f32[128,1024]{1,0:T(8,128)S(1)}, u32[]{:S(2)}) copy-start(f32[128,1024]{1,0:T(8,128)S(1)} %get-tuple-element.152) | copy-start | bytes 1572868
  210.3 15.3 %copy-start.119 = (f32[128]{0:T(128)}, f32[128]{0:T(128)S(1)}, u32[]{:S(2)}) copy-start(f32[128]{0:T(128)S(1)} %add_rsqrt_fusion.1) | copy-start | bytes 1540
  225.6 16.7 %copy-start.85 = (f32[1024]{0:T(1024)}, f32[1024]{0:T(1024)S(1)}, u32[]{:S(2)}) copy-start(f32[1024]{0:T(1024)S(1)} %get-tuple-element.79) | copy-start | bytes 12292
  245.6 41.3 %all-to-all-start.3 = ((bf16[32,40,1024]{2,1,0:T(8,128)(2,1)}), bf16[32,40,1024]{2,1,0:T(8,128)(2,1)}, u32[]{:S(2)}, u32[]{:S(2)}) async-start(bf16[32,40,1024]{2,1,0:T(8,128)(2,1)} %bitcast.353), calls=%async_computation.3 | async-start | bytes 5242880 | tf_op jit(solution)/shard_map/all_to_all | solution.py:140
  254.4 39.1 %collective-permute-start.4 = (bf16[2,128,3072]{2,1,0:T(8,128)(2,1)}, bf16[2,128,3072]{2,1,0:T(8,128)(2,1)}, u32[]{:S(2)}, u32[]{:S(2)}) collective-permute-start(bf16[2,128,3072]{2,1,0:T(8,128)(2,1)} %pad_maximum_fusion.7), channel_id=1, source_target_pairs={{0,1},{1,0},{2,3},{3,2},{4,5},{5,4},{6,7},{7,6},{8,9},{9,8},{10,11... | collective-permute-start | bytes 4718600 | tf_op jit(solution)/shard_map/ppermute | solution.py:152
  286.8 39.7 %all-to-all-start.4 = ((bf16[32,40,1024]{2,1,0:T(8,128)(2,1)}), bf16[32,40,1024]{2,1,0:T(8,128)(2,1)}, u32[]{:S(2)}, u32[]{:S(2)}) async-start(bf16[32,40,1024]{2,1,0:T(8,128)(2,1)} %bitcast.352), calls=%async_computation.4 | async-start | bytes 5242880 | tf_op jit(solution)/shard_map/all_to_all | solution.py:140
  296.2 10.6 %copy-start.14 = (bf16[2,2,128,3072]{3,2,1,0:T(8,128)(2,1)}, bf16[2,2,128,3072]{3,2,1,0:T(8,128)(2,1)S(1)}, u32[]{:S(2)}) copy-start(bf16[2,2,128,3072]{3,2,1,0:T(8,128)(2,1)S(1)} %copy.103) | copy-start | bytes 9437188
  300.6 6.1 copy-start.125
  326.5 39.1 %all-to-all-start.5 = ((bf16[32,40,1024]{2,1,0:T(8,128)(2,1)}), bf16[32,40,1024]{2,1,0:T(8,128)(2,1)}, u32[]{:S(2)}, u32[]{:S(2)}) async-start(bf16[32,40,1024]{2,1,0:T(8,128)(2,1)} %bitcast.373), calls=%async_computation.5 | async-start | bytes 5242880 | tf_op jit(solution)/shard_map/all_to_all | solution.py:140
  365.6 39.3 %all-to-all-start.6 = ((bf16[32,40,1024]{2,1,0:T(8,128)(2,1)}), bf16[32,40,1024]{2,1,0:T(8,128)(2,1)}, u32[]{:S(2)}, u32[]{:S(2)}) async-start(bf16[32,40,1024]{2,1,0:T(8,128)(2,1)} %bitcast.350), calls=%async_computation.6 | async-start | bytes 5242880 | tf_op jit(solution)/shard_map/all_to_all | solution.py:140
  392.0 15.5 %copy-start.86 = (f32[1024]{0:T(1024)S(1)}, f32[1024]{0:T(1024)}, u32[]{:S(2)}) copy-start(f32[1024]{0:T(1024)} %copy-done.85) | copy-start | bytes 12292
  407.6 6.6 copy-start.101
  422.9 5.0 copy-start.34
  430.2 39.6 %all-to-all-start.7 = ((bf16[32,40,1024]{2,1,0:T(8,128)(2,1)}), bf16[32,40,1024]{2,1,0:T(8,128)(2,1)}, u32[]{:S(2)}, u32[]{:S(2)}) async-start(bf16[32,40,1024]{2,1,0:T(8,128)(2,1)} %bitcast.351), calls=%async_computation.7 | async-start | bytes 5242880 | tf_op jit(solution)/shard_map/all_to_all | solution.py:140
  436.9 197.4 %reduce-scatter.5.cloned.1.call-start = ((), (), s32[]{:S(2)}) async-start(), calls=%async_computation.17 | async-start | bytes 3932160 | tf_op jit(solution)/shard_map/reduce_scatter | solution.py:160
  440.3 21.6 %collective-permute-start.5 = (bf16[512,2048]{1,0:T(8,128)(2,1)}, bf16[512,2048]{1,0:T(8,128)(2,1)}, u32[]{:S(2)}, u32[]{:S(2)}) collective-permute-start(bf16[512,2048]{1,0:T(8,128)(2,1)} %convolution_convert_fusion.7), channel_id=1, source_target_pairs={{0,1},{1,0},{2,3},{3,2},{4,5},{5,4},{6,7},{7,6},{8,9},{9,8},{10,11... | collective-permute-start | bytes 6291464 | tf_op jit(solution)/shard_map/ppermute | solution.py:195
  443.2 5.1 copy-start.83
  445.9 13.4 %collective-permute-start.6 = (bf16[512,1024]{1,0:T(8,128)(2,1)}, bf16[512,1024]{1,0:T(8,128)(2,1)}, u32[]{:S(2)}, u32[]{:S(2)}) collective-permute-start(bf16[512,1024]{1,0:T(8,128)(2,1)} %convolution_convert_fusion.11), channel_id=1, source_target_pairs={{0,1},{1,0},{2,3},{3,2},{4,5},{5,4},{6,7},{7,6},{8,9},{9,8},{10,11... | collective-permute-start | bytes 3145736 | tf_op jit(solution)/shard_map/ppermute | solution.py:195
  453.9 5.3 copy-start.8
  453.9 5.3 copy-start.61
  453.9 4.6 collective-permute-start.7
  469.9 6.3 copy-start.13
  480.7 40.8 %all-to-all-start.8 = ((bf16[32,40,1024]{2,1,0:T(8,128)(2,1)}), bf16[32,40,1024]{2,1,0:T(8,128)(2,1)}, u32[]{:S(2)}, u32[]{:S(2)}) async-start(bf16[32,40,1024]{2,1,0:T(8,128)(2,1)} %bitcast.349), calls=%async_computation.8 | async-start | bytes 5242880 | tf_op jit(solution)/shard_map/all_to_all | solution.py:140
  487.8 146.5 %reduce-scatter.3.cloned.1.call-start = ((), (), s32[]{:S(2)}) async-start(), calls=%async_computation.16 | async-start | bytes 3932160 | tf_op jit(solution)/shard_map/reduce_scatter | solution.py:160
  503.5 18.0 %copy-start.108 = (f32[128]{0:T(128)S(1)}, f32[128]{0:T(128)}, u32[]{:S(2)}) copy-start(f32[128]{0:T(128)} %copy-done.107) | copy-start | bytes 1540
  525.1 5.2 copy-start.99
  530.4 19.4 %collective-permute-start.10 = (bf16[512,1024]{1,0:T(8,128)(2,1)}, bf16[512,1024]{1,0:T(8,128)(2,1)}, u32[]{:S(2)}, u32[]{:S(2)}) collective-permute-start(bf16[512,1024]{1,0:T(8,128)(2,1)} %convolution_convert_fusion.10), channel_id=1, source_target_pairs={{0,1},{1,0},{2,3},{3,2},{4,5},{5,4},{6,7},{7,6},{8,9},{9,8},{10,11... | collective-permute-start | bytes 3145736 | tf_op jit(solution)/shard_map/ppermute | solution.py:195
  532.1 9.8 %copy-start.67 = (bf16[128,8,32]{0,2,1:T(8,128)(2,1)S(1)}, bf16[128,8,32]{0,2,1:T(8,128)(2,1)}, u32[]{:S(2)}) copy-start(bf16[128,8,32]{0,2,1:T(8,128)(2,1)} %copy-done.66) | copy-start | bytes 196612
  533.4 26.8 %all-to-all-start.12 = ((bf16[64,8,1024]{2,1,0:T(8,128)(2,1)}), bf16[64,8,1024]{2,1,0:T(8,128)(2,1)}, u32[]{:S(2)}, u32[]{:S(2)}) async-start(bf16[64,8,1024]{2,1,0:T(8,128)(2,1)} %bitcast.368), calls=%async_computation.12 | async-start | bytes 2097152 | tf_op jit(solution)/shard_map/all_to_all | solution.py:200
  549.7 16.8 %copy-start.74 = (bf16[128,8,32]{0,2,1:T(8,128)(2,1)S(1)}, bf16[128,8,32]{0,2,1:T(8,128)(2,1)}, u32[]{:S(2)}) copy-start(bf16[128,8,32]{0,2,1:T(8,128)(2,1)} %get-tuple-element.121) | copy-start | bytes 196612
  549.7 16.8 %copy-start.75 = (bf16[128,8,32]{0,2,1:T(8,128)(2,1)S(1)}, bf16[128,8,32]{0,2,1:T(8,128)(2,1)}, u32[]{:S(2)}) copy-start(bf16[128,8,32]{0,2,1:T(8,128)(2,1)} %get-tuple-element.122) | copy-start | bytes 196612
  560.2 23.3 %all-to-all-start.11 = ((bf16[64,8,1024]{2,1,0:T(8,128)(2,1)}), bf16[64,8,1024]{2,1,0:T(8,128)(2,1)}, u32[]{:S(2)}, u32[]{:S(2)}) async-start(bf16[64,8,1024]{2,1,0:T(8,128)(2,1)} %fusion.63), calls=%async_computation.11 | async-start | bytes 2097152 | tf_op jit(solution)/shard_map/all_to_all | solution.py:200
  571.4 19.0 %copy-start.21 = (bf16[128,1024]{1,0:T(8,128)(2,1)S(1)}, bf16[128,1024]{1,0:T(8,128)(2,1)}, u32[]{:S(2)}) copy-start(bf16[128,1024]{1,0:T(8,128)(2,1)} %copy-done.20) | copy-start | bytes 786436
  571.4 29.4 %collective-permute-start.8 = (bf16[512,2048]{1,0:T(8,128)(2,1)}, bf16[512,2048]{1,0:T(8,128)(2,1)}, u32[]{:S(2)}, u32[]{:S(2)}) collective-permute-start(bf16[512,2048]{1,0:T(8,128)(2,1)} %convolution_convert_fusion.6), channel_id=1, source_target_pairs={{0,1},{1,0},{2,3},{3,2},{4,5},{5,4},{6,7},{7,6},{8,9},{9,8},{10,11... | collective-permute-start | bytes 6291464 | tf_op jit(solution)/shard_map/ppermute | solution.py:195
  583.5 8.1 %copy-start.89 = (f32[1024]{0:T(1024)S(1)}, f32[1024]{0:T(1024)}, u32[]{:S(2)}) copy-start(f32[1024]{0:T(1024)} %copy-done.87) | copy-start | bytes 12292
  583.5 8.1 %copy-start.118 = (f32[128]{0:T(128)S(1)}, f32[128]{0:T(128)}, u32[]{:S(2)}) copy-start(f32[128]{0:T(128)} %copy-done.116) | copy-start | bytes 1540
  583.5 36.3 %all-to-all-start.10 = ((bf16[64,8,2176]{2,1,0:T(8,128)(2,1)}), bf16[64,8,2176]{2,1,0:T(8,128)(2,1)}, u32[]{:S(2)}, u32[]{:S(2)}) async-start(bf16[64,8,2176]{2,1,0:T(8,128)(2,1)} %bitcast.355), calls=%async_computation.10 | async-start | bytes 4456448 | tf_op jit(solution)/shard_map/all_to_all | solution.py:200
  591.6 5.0 copy-start.54
  591.6 5.0 copy-start.110
  597.6 3.2 collective-permute-start.9
  604.7 22.0 %copy-start.27 = (bf16[128,1024]{1,0:T(8,128)(2,1)S(1)}, bf16[128,1024]{1,0:T(8,128)(2,1)}, u32[]{:S(2)}) copy-start(bf16[128,1024]{1,0:T(8,128)(2,1)} %param.12) | copy-start | bytes 786436
  619.8 34.7 %all-to-all-start.9 = ((bf16[64,8,2176]{2,1,0:T(8,128)(2,1)}), bf16[64,8,2176]{2,1,0:T(8,128)(2,1)S(1)}, u32[]{:S(2)}, u32[]{:S(2)}) async-start(bf16[64,8,2176]{2,1,0:T(8,128)(2,1)} %maximum_bitcast_fusion), calls=%async_computation.9 | async-start | bytes 4456448 | tf_op jit(solution)/shard_map/all_to_all | solution.py:200
  (90 other events, 246.9 us)
Sparse Core Ops, SparseCore 0:
  80.5 91.5 all-gather.1
  443.4 80.1 reduce-scatter.4
  526.0 58.3 reduce-scatter.2

commit v9 on v8

--- a/solution.py
+++ b/solution.py
@@ -142,8 +142,7 @@
     ).reshape(ROWS, MODEL_WIDTH)
 
 
-def gather_chip(own):
-    other = lax.ppermute(own, "zl", SWAP)
+def join_chip(own, other):
     first = lax.axis_index("zl") == 0
     return jnp.stack([jnp.where(first, own, other), jnp.where(first, other, own)])
 
@@ -458,16 +457,16 @@
     lead = [part.reshape(8, -1) for part in own_dense[0]]
     fill = jnp.zeros((8, 128 - E - 2), jnp.bfloat16)
     position, live_row, allowed = seq_layout(seq_lengths, seq_owner, device)
-    live = live_row.astype(jnp.float32)
-    cosine_table, sine_values = rope_tables(position)
     routed, chosen = dispatch_table(routes, live_row)
     own_experts = [
         jnp.concatenate([expert_in[layer], expert_out[layer]], axis=1) for layer in layers
     ]
-    beside = order, live, allowed, cosine_table, sine_values, routed, chosen, own_experts
+    beside = order, position, live_row, routed, chosen, own_experts
     lead, beside = sent_by_chips(jnp.concatenate(lead + [fill], axis=1), beside)
-    order, live, allowed, cosine_table, sine_values, routed, chosen, own_experts = beside
-    chip_experts = gather_chip(own_experts[0])
+    order, position, live_row, routed, chosen, own_experts = beside
+    live = live_row.astype(jnp.float32)
+    cosine_table, sine_values = rope_tables(position)
+    other_expert = lax.ppermute(own_experts[0], "zl", SWAP)
     lead, own_dense = lax.optimization_barrier((lead, own_dense))
     dense = [cut_weights(lead, DENSE_WIDTHS), None]
     dense[1] = cut_weights(sent_together(own_dense[1], AXES), DENSE_WIDTHS)
@@ -481,17 +480,15 @@
         mixed_low = attn_stash[-1]
         hidden = hidden + jnp.dot(mixed_low, dense[layer][1], preferred_element_type=jnp.float32)
         rows, route_stash = route_rows(hidden, dense[layer], routed, chosen)
-        rows, chip_experts = lax.optimization_barrier((rows, chip_experts))
+        rows, other_expert = lax.optimization_barrier((rows, other_expert))
         rows_here = trade_rows(rows)
-        expert = gather_core(chip_experts)
+        expert = gather_core(join_chip(own_experts[layer], other_expert))
         moved = reorder(attn_stash[2], order), reorder(mixed_low, order)
         grad_rows = None
         if layer == last:
             slots = slot_gradients(grad_hidden, route_stash[-1])
             slots, rows_here = lax.optimization_barrier((slots, rows_here))
             grad_rows = trade_rows(slots)
-        else:
-            rows_here, expert = lax.optimization_barrier((rows_here, expert))
         experts.append(expert)
         results, pre = feed_forward(rows_here, expert)
         if layer == last:
@@ -499,7 +496,7 @@
         returned = trade_rows(results)
         if layer != last:
             returned, own_expert = lax.optimization_barrier((returned, own_experts[layer + 1]))
-            chip_experts = gather_chip(own_expert)
+            other_expert = lax.ppermute(own_expert, "zl", SWAP)
         hidden = hidden + jnp.dot(route_stash[-1], returned, preferred_element_type=jnp.float32)
         saved.append((attn_stash, moved, route_stash, rows_here, pre, returned, grad_rows))
     output_low = hidden.astype(jnp.bfloat16)
@@ -509,7 +506,7 @@
         if grad_rows is None:
             slots = slot_gradients(grad_hidden, route_stash[-1])
             grad_rows, sums = lax.optimization_barrier((trade_rows(slots), sums))
-            joined = [jnp.concatenate([sums[0], sums[2]], axis=1), sums[1]]
+            joined = jnp.concatenate(sums, axis=1)
         grad_in_rows, expert_grads = feed_backward(grad_rows, rows_here, pre, experts[layer])
         grad_slots = trade_rows(grad_in_rows)
         router_grad, grad_routed = route_backward(
@@ -518,7 +515,7 @@
         expert_sums[layer] = scatter_expert(expert_grads)
         if layer != last:
             grad_slots, joined = lax.optimization_barrier((grad_slots, joined))
-            done_last = chip_sum(joined[0]), chip_sum(joined[1])
+            done_last = chip_sum(joined)
         grad_h1, gain_two_grad = rows_backward(
             grad_hidden, dense[layer], chosen, grad_slots, grad_routed, route_stash
         )
@@ -527,10 +524,8 @@
         )
         small = small_halves(router_grad, gain_one_grad, gain_two_grad, order)
         sums = [core_sum(qkv_halves), proj_sum, core_sum(small)]
-    proj_done = chip_sum(sums.pop(1))
     done = chip_sum(jnp.concatenate(sums, axis=1))
-    first = [done[:, :2048], proj_done, done[:, 2048:]]
-    second = [done_last[0][:, :2048], done_last[1], done_last[0][:, 2048:]]
+    first, second = [(d[:, :2048], d[:, 2048:3072], d[:, 3072:]) for d in (done, done_last)]
     qkv, proj, small = [jnp.stack(pair) for pair in zip(first, second)]
     both = jnp.stack(expert_sums).astype(jnp.float32)
     return (

time: 675 us -> 637 us (0.944)
  starting transfers between devices: 105 us -> 89.9 us
  other arithmetic: 62.7 us -> 53.2 us
  waiting for transfers between devices: 261 us -> 252 us
    reduce_scatter x2, waiting for transfers between devices: 0.04 us -> 34.8 us  [scatter_expert(): return lax.psum_scatter(both, GROUP_AXES, scatter_dimension=0, tiled=True)]
    all_to_all x4 -> x2, waiting for transfers between devices: 50.3 us -> 20.7 us  [chip_sum(): lax.all_to_all(parts, Z_AXES + ('x', 'y'), split_axis=0, concat_axis=0, t...]
    ppermute x2, waiting for transfers between devices: 18.9 us -> 0.01 us  [the longest x1 0.01 us: on_device(): other_expert = lax.ppermute(own_experts[0], 'zl', SWAP)]
    all_to_all x4 -> x2, starting transfers between devices: 28.7 us -> 15.9 us  [chip_sum(): lax.all_to_all(parts, Z_AXES + ('x', 'y'), split_axis=0, concat_axis=0, t...]
  transfers between devices with their start and end apart: 27 -> 25, of which waited for: 16 -> 13; matrix products, arithmetic and copies ran while one was open for 33% -> 35% of each run, Pallas kernels for 0% -> 0%
where the time goes in v9:
time: 637 us; the launch traced here: 625 us
  waiting for transfers between devices  252 us (40%)
  matrix products  179 us (28%)
  starting transfers between devices  89.9 us (14%)
  other arithmetic  53.2 us (8%)
  local copies, waits for them, and re-layouts  33.7 us (5%)
  between operations  16.2 us (3%)
    all_to_all x8, waiting for transfers between devices, trade_rows(): lax.all_to_all(rows.reshape(E, ROOM, MODEL_WIDTH), EXPERT_AXES, split_axi...  153 us
    all_to_all x8, starting transfers between devices, trade_rows(): lax.all_to_all(rows.reshape(E, ROOM, MODEL_WIDTH), EXPERT_AXES, split_axi...  57.1 us
    all_to_all x1, waiting for transfers between devices, sent_by_chips(): lax.all_to_all(copies, CHIP_AXES, split_axis=0, concat_axis=0, tiled=True)  36.5 us
    reduce_scatter x2, waiting for transfers between devices, scatter_expert(): return lax.psum_scatter(both, GROUP_AXES, scatter_dimension=0, tiled=True)  34.8 us
    all_to_all x2, waiting for transfers between devices, chip_sum(): lax.all_to_all(parts, Z_AXES + ('x', 'y'), split_axis=0, concat_axis=0, t...  20.7 us
    all_to_all x2, starting transfers between devices, chip_sum(): lax.all_to_all(parts, Z_AXES + ('x', 'y'), split_axis=0, concat_axis=0, t...  15.9 us
  transfers between devices with their start and end apart: 25, of which 13 were waited for; matrix products, arithmetic and copies ran while one was open for 35% of the time, Pallas kernels for 0%

profile of v9, /device:TPU:2, one launch (start us, length us, event | category | flops | bytes accessed | tf_op | source)
XLA Modules:
  0.0 624.6 jit_solution(4809226028838633005)
XLA Ops:
  12.9 11.8 %all-to-all-start = ((bf16[64,8,3200]{2,1,0:T(8,128)(2,1)}), bf16[64,8,3200]{2,1,0:T(8,128)(2,1)}, u32[]{:S(2)}, u32[]{:S(2)}) async-start(bf16[64,8,3200]{2,1,0:T(8,128)(2,1)} %broadcast_in_dim.73), calls=%async_computation | async-start | bytes 6553600 | tf_op jit(solution)/shard_map/all_to_all | solution.py:44
  29.2 36.5 %all-to-all-done = bf16[64,8,3200]{2,1,0:T(8,128)(2,1)} async-done(((bf16[64,8,3200]{2,1,0:T(8,128)(2,1)}), bf16[64,8,3200]{2,1,0:T(8,128)(2,1)}, u32[]{:S(2)}, u32[]{:S(2)}) %all-to-all-start) | async-done | bytes 3276832 | tf_op jit(solution)/shard_map/all_to_all | solution.py:44
  65.8 6.2 collective-permute-done
  72.0 3.5 select_bitcast_fusion.1
  75.5 3.3 pad_maximum_fusion
  83.3 3.0 fusion.9
  91.8 2.4 fusion.234
  104.2 8.6 %all-to-all-start.1 = ((bf16[32,40,1024]{2,1,0:T(8,128)(2,1)}), bf16[32,40,1024]{2,1,0:T(8,128)(2,1)}, u32[]{:S(2)}, u32[]{:S(2)}) async-start(bf16[32,40,1024]{2,1,0:T(8,128)(2,1)} %bitcast.346), calls=%async_computation.1 | async-start | bytes 5242880 | tf_op jit(solution)/shard_map/all_to_all | solution.py:140
  116.9 32.1 %all-to-all-done.1 = bf16[32,40,1024]{2,1,0:T(8,128)(2,1)} async-done(((bf16[32,40,1024]{2,1,0:T(8,128)(2,1)}), bf16[32,40,1024]{2,1,0:T(8,128)(2,1)}, u32[]{:S(2)}, u32[]{:S(2)}) %all-to-all-start.1) | async-done | bytes 2621472 | tf_op jit(solution)/shard_map/all_to_all | solution.py:140
  149.0 3.7 fusion.81
  152.8 6.1 multiply_convert_fusion.5
  158.9 3.0 convolution_convert_fusion.4
  161.9 8.5 %all-to-all-start.2 = ((bf16[32,40,1024]{2,1,0:T(8,128)(2,1)}), bf16[32,40,1024]{2,1,0:T(8,128)(2,1)}, u32[]{:S(2)}, u32[]{:S(2)}) async-start(bf16[32,40,1024]{2,1,0:T(8,128)(2,1)} %bitcast.366), calls=%async_computation.2 | async-start | bytes 5242880 | tf_op jit(solution)/shard_map/all_to_all | solution.py:140
  172.7 32.0 %all-to-all-done.2 = bf16[32,40,1024]{2,1,0:T(8,128)(2,1)} async-done(((bf16[32,40,1024]{2,1,0:T(8,128)(2,1)}), bf16[32,40,1024]{2,1,0:T(8,128)(2,1)}, u32[]{:S(2)}, u32[]{:S(2)}) %all-to-all-start.2) | async-done | bytes 2621472 | tf_op jit(solution)/shard_map/all_to_all | solution.py:140
  206.2 2.5 multiply_reduce_fusion.9
  210.3 2.9 fusion.5
  220.3 2.4 fusion.236
  230.2 7.2 %all-to-all-start.3 = ((bf16[32,40,1024]{2,1,0:T(8,128)(2,1)}), bf16[32,40,1024]{2,1,0:T(8,128)(2,1)}, u32[]{:S(2)}, u32[]{:S(2)}) async-start(bf16[32,40,1024]{2,1,0:T(8,128)(2,1)} %bitcast.348), calls=%async_computation.3 | async-start | bytes 5242880 | tf_op jit(solution)/shard_map/all_to_all | solution.py:140
  244.6 2.4 convolution_convert_fusion.3
  247.0 22.5 %all-to-all-done.3 = bf16[32,40,1024]{2,1,0:T(8,128)(2,1)} async-done(((bf16[32,40,1024]{2,1,0:T(8,128)(2,1)}), bf16[32,40,1024]{2,1,0:T(8,128)(2,1)}, u32[]{:S(2)}, u32[]{:S(2)}) %all-to-all-start.3) | async-done | bytes 2621472 | tf_op jit(solution)/shard_map/all_to_all | solution.py:140
  269.5 6.8 %all-to-all-start.4 = ((bf16[32,40,1024]{2,1,0:T(8,128)(2,1)}), bf16[32,40,1024]{2,1,0:T(8,128)(2,1)}, u32[]{:S(2)}, u32[]{:S(2)}) async-start(bf16[32,40,1024]{2,1,0:T(8,128)(2,1)} %bitcast.347), calls=%async_computation.4 | async-start | bytes 5242880 | tf_op jit(solution)/shard_map/all_to_all | solution.py:140
  278.9 4.5 fusion.71
  283.4 6.1 multiply_convert_fusion.4
  290.5 3.1 convolution_convert_fusion.1
  293.6 14.6 %all-to-all-done.4 = bf16[32,40,1024]{2,1,0:T(8,128)(2,1)} async-done(((bf16[32,40,1024]{2,1,0:T(8,128)(2,1)}), bf16[32,40,1024]{2,1,0:T(8,128)(2,1)}, u32[]{:S(2)}, u32[]{:S(2)}) %all-to-all-start.4) | async-done | bytes 2621472 | tf_op jit(solution)/shard_map/all_to_all | solution.py:140
  308.2 6.2 all-to-all-start.5
  318.5 5.7 multiply_convert_fusion.2
  325.9 3.0 add_convert_fusion.1
  328.9 18.5 %all-to-all-done.5 = bf16[32,40,1024]{2,1,0:T(8,128)(2,1)} async-done(((bf16[32,40,1024]{2,1,0:T(8,128)(2,1)}), bf16[32,40,1024]{2,1,0:T(8,128)(2,1)}, u32[]{:S(2)}, u32[]{:S(2)}) %all-to-all-start.5) | async-done | bytes 2621472 | tf_op jit(solution)/shard_map/all_to_all | solution.py:140
  347.3 7.1 %all-to-all-start.6 = ((bf16[32,40,1024]{2,1,0:T(8,128)(2,1)}), bf16[32,40,1024]{2,1,0:T(8,128)(2,1)}, u32[]{:S(2)}, u32[]{:S(2)}) async-start(bf16[32,40,1024]{2,1,0:T(8,128)(2,1)} %bitcast.344), calls=%async_computation.6 | async-start | bytes 5242880 | tf_op jit(solution)/shard_map/all_to_all | solution.py:140
  356.7 4.4 convolution_convert_fusion.12
  361.1 4.4 convolution_convert_fusion.13
  365.5 4.4 convolution_convert_fusion.14
  369.9 2.7 fusion.13
  375.8 11.0 %all-to-all-done.6 = bf16[32,40,1024]{2,1,0:T(8,128)(2,1)} async-done(((bf16[32,40,1024]{2,1,0:T(8,128)(2,1)}), bf16[32,40,1024]{2,1,0:T(8,128)(2,1)}, u32[]{:S(2)}, u32[]{:S(2)}) %all-to-all-start.6) | async-done | bytes 2621472 | tf_op jit(solution)/shard_map/all_to_all | solution.py:140
  386.8 2.6 multiply_reduce_fusion.4
  391.1 3.1 fusion.48
  400.6 3.9 multiply_reduce_fusion.5
  405.6 2.4 convolution_convert_fusion
  407.9 6.6 %all-to-all-start.7 = ((bf16[32,40,1024]{2,1,0:T(8,128)(2,1)}), bf16[32,40,1024]{2,1,0:T(8,128)(2,1)}, u32[]{:S(2)}, u32[]{:S(2)}) async-start(bf16[32,40,1024]{2,1,0:T(8,128)(2,1)} %bitcast.345), calls=%async_computation.7 | async-start | bytes 5242880 | tf_op jit(solution)/shard_map/all_to_all | solution.py:140
  414.6 3.3 convolution_convert_fusion.7
  418.0 2.9 pad_maximum_fusion.5
  431.4 3.1 convolution_multiply_fusion
  436.4 2.7 add_convert_fusion.5
  439.1 3.6 add_convert_fusion.3
  442.7 5.8 all-to-all-done.7
  448.5 6.3 %multiply_convert_fusion = (bf16[1280,512]{1,0:T(8,128)(2,1)S(1)}, bf16[1280,512]{1,0:T(8,128)(2,1)S(1)}) fusion(f32[1280,512]{1,0:T(8,128)} %copy-done.134, f32[1280,512]{1,0:T(8,128)} %get-tuple-element.140, bf16[1280,1024]{1,0:T(8,128)(2,1)} %bitcast.89, bf16[512,3072]{1,0:T(8,128)(2,1)} %bitcast.350), kind=kOutput, calls=%fused_computation.35 | convolution fusion | flops 1350696960 | bytes 11534336 | tf_op jit(solution)/shard_map/dot_general | solution.py:308
  456.4 3.1 add_convert_fusion
  459.4 6.1 all-to-all-start.8
  467.2 3.8 convolution_convert_fusion.15
  471.1 3.4 convolution_convert_fusion.16
  474.5 3.3 convolution_convert_fusion.17
  479.6 3.3 pad_maximum_fusion.1
  482.9 16.1 %all-to-all-done.8 = bf16[32,40,1024]{2,1,0:T(8,128)(2,1)} async-done(((bf16[32,40,1024]{2,1,0:T(8,128)(2,1)}), bf16[32,40,1024]{2,1,0:T(8,128)(2,1)}, u32[]{:S(2)}, u32[]{:S(2)}) %all-to-all-start.8) | async-done | bytes 2621472 | tf_op jit(solution)/shard_map/all_to_all | solution.py:140
  499.0 3.1 multiply_reduce_fusion.2
  502.4 2.6 fusion.51
  509.7 8.4 %all-to-all-start.10 = ((bf16[64,8,3200]{2,1,0:T(8,128)(2,1)}), bf16[64,8,3200]{2,1,0:T(8,128)(2,1)}, u32[]{:S(2)}, u32[]{:S(2)}) async-start(bf16[64,8,3200]{2,1,0:T(8,128)(2,1)} %bitcast.342), calls=%async_computation.10 | async-start | bytes 6553600 | tf_op jit(solution)/shard_map/all_to_all | solution.py:199
  520.6 3.0 convolution_convert_fusion.6
  528.2 4.7 fusion.92
  540.3 20.6 %all-to-all-done.10 = bf16[64,8,3200]{2,1,0:T(8,128)(2,1)} async-done(((bf16[64,8,3200]{2,1,0:T(8,128)(2,1)}), bf16[64,8,3200]{2,1,0:T(8,128)(2,1)}, u32[]{:S(2)}, u32[]{:S(2)}) %all-to-all-start.10) | async-done | bytes 3276832 | tf_op jit(solution)/shard_map/all_to_all | solution.py:199
  560.9 7.5 %all-to-all-start.9 = ((bf16[64,8,3200]{2,1,0:T(8,128)(2,1)}), bf16[64,8,3200]{2,1,0:T(8,128)(2,1)S(1)}, u32[]{:S(2)}, u32[]{:S(2)}) async-start(bf16[64,8,3200]{2,1,0:T(8,128)(2,1)} %maximum_bitcast_fusion), calls=%async_computation.9 | async-start | bytes 6553600 | tf_op jit(solution)/shard_map/all_to_all | solution.py:199
  568.4 3.3 fusion.41
  572.7 2.4 convert_reduce_fusion
  575.2 34.8 %reduce-scatter.3.cloned.1.call-done = bf16[128,3072]{1,0:T(8,128)(2,1)} async-done(((bf16[512,3072]{1,0:T(8,128)(2,1)}), bf16[128,3072]{1,0:T(8,128)(2,1)}) %reduce-scatter.3.cloned.1.call-update) | async-done | bytes 786448 | tf_op jit(solution)/shard_map/reduce_scatter | solution.py:159
  (468 shorter events, 129.4 us)
Async XLA Ops:
  12.8 11.9 %copy-start.120 = (s32[512]{0:T(512)S(1)}, s32[512]{0:T(512)}, u32[]{:S(2)}) copy-start(s32[512]{0:T(512)} %param.15) | copy-start | bytes 6148
  12.8 12.5 %copy-start.121 = (s32[512]{0:T(512)S(1)}, s32[512]{0:T(512)}, u32[]{:S(2)}) copy-start(s32[512]{0:T(512)} %param.14) | copy-start | bytes 6148
  12.8 13.1 %copy-start.118 = (s32[128,8]{0,1:T(8,128)S(1)}, s32[128,8]{0,1:T(8,128)}, u32[]{:S(2)}) copy-start(s32[128,8]{0,1:T(8,128)} %param.16) | copy-start | bytes 12292
  12.9 14.1 %copy-start.65 = (bf16[2,128,1024]{2,1,0:T(8,128)(2,1)S(1)}, bf16[2,128,1024]{2,1,0:T(8,128)(2,1)}, u32[]{:S(2)}) copy-start(bf16[2,128,1024]{2,1,0:T(8,128)(2,1)} %param.23) | copy-start | bytes 1572868
  12.9 52.9 %all-to-all-start = ((bf16[64,8,3200]{2,1,0:T(8,128)(2,1)}), bf16[64,8,3200]{2,1,0:T(8,128)(2,1)}, u32[]{:S(2)}, u32[]{:S(2)}) async-start(bf16[64,8,3200]{2,1,0:T(8,128)(2,1)} %broadcast_in_dim.73), calls=%async_computation | async-start | bytes 6553600 | tf_op jit(solution)/shard_map/all_to_all | solution.py:44
  24.7 184.0 %all-gather.2.cloned.1.call-start = ((), (), s32[]{:S(2)}) async-start(), calls=%async_computation.13 | async-start | bytes 6604800 | tf_op jit(solution)/shard_map/all_gather | solution.py:38
  65.8 6.2 collective-permute-start
  75.5 5.6 copy-start.130
  79.9 6.4 %copy-start.124 = (f32[128]{0:T(128)}, f32[128]{0:T(128)S(1)}, u32[]{:S(2)}) copy-start(f32[128]{0:T(128)S(1)} %add_rsqrt_fusion.3) | copy-start | bytes 1540
  80.0 14.2 %copy-start.100 = (pred[128,128]{0,1:T(8,128)(4,1)}, pred[128,128]{0,1:T(8,128)(4,1)S(1)}, u32[]{:S(2)}) copy-start(pred[128,128]{0,1:T(8,128)(4,1)S(1)} %fusion.158) | copy-start | bytes 49156
  80.1 20.6 %collective-permute-start.1 = (bf16[128,3072]{1,0:T(8,128)(2,1)}, bf16[128,3072]{1,0:T(8,128)(2,1)}, u32[]{:S(2)}, u32[]{:S(2)}) collective-permute-start(bf16[128,3072]{1,0:T(8,128)(2,1)} %get-tuple-element.45), channel_id=1, source_target_pairs={{0,2},{2,0},{1,3},{3,1},{4,6},{6,4},{5,7},{7,5},{8,10},{10,8},{9,1... | collective-permute-start | bytes 2359304 | tf_op jit(solution)/shard_map/ppermute | solution.py:469
  91.1 4.8 copy-start.72
  91.1 4.8 copy-start.74
  98.4 72.0 %copy-start.23 = (bf16[128,1024]{1,0:T(8,128)(2,1)}, bf16[128,1024]{1,0:T(8,128)(2,1)S(1)}, u32[]{:S(2)}) copy-start(bf16[128,1024]{1,0:T(8,128)(2,1)S(1)} %multiply_convert_fusion.10) | copy-start | bytes 786436
  104.2 8.6 %collective-permute-start.2 = (bf16[2,128,3072]{2,1,0:T(8,128)(2,1)}, bf16[2,128,3072]{2,1,0:T(8,128)(2,1)}, u32[]{:S(2)}, u32[]{:S(2)}) collective-permute-start(bf16[2,128,3072]{2,1,0:T(8,128)(2,1)} %pad_maximum_fusion.6), channel_id=1, source_target_pairs={{0,1},{1,0},{2,3},{3,2},{4,5},{5,4},{6,7},{7,6},{8,9},{9,8},{10,11... | collective-permute-start | bytes 4718600 | tf_op jit(solution)/shard_map/ppermute | solution.py:151
  104.2 44.8 %all-to-all-start.1 = ((bf16[32,40,1024]{2,1,0:T(8,128)(2,1)}), bf16[32,40,1024]{2,1,0:T(8,128)(2,1)}, u32[]{:S(2)}, u32[]{:S(2)}) async-start(bf16[32,40,1024]{2,1,0:T(8,128)(2,1)} %bitcast.346), calls=%async_computation.1 | async-start | bytes 5242880 | tf_op jit(solution)/shard_map/all_to_all | solution.py:140
  152.8 6.1 copy-start.134
  161.9 42.8 %all-to-all-start.2 = ((bf16[32,40,1024]{2,1,0:T(8,128)(2,1)}), bf16[32,40,1024]{2,1,0:T(8,128)(2,1)}, u32[]{:S(2)}, u32[]{:S(2)}) async-start(bf16[32,40,1024]{2,1,0:T(8,128)(2,1)} %bitcast.366), calls=%async_computation.2 | async-start | bytes 5242880 | tf_op jit(solution)/shard_map/all_to_all | solution.py:140
  171.6 37.0 %copy-start.101 = (f32[128]{0:T(128)}, f32[128]{0:T(128)S(1)}, u32[]{:S(2)}) copy-start(f32[128]{0:T(128)S(1)} %get-tuple-element.137) | copy-start | bytes 1540
  171.6 37.0 %copy-start.111 = (f32[128]{0:T(128)}, f32[128]{0:T(128)S(1)}, u32[]{:S(2)}) copy-start(f32[128]{0:T(128)S(1)} %fusion.169) | copy-start | bytes 1540
  204.7 25.5 %collective-permute-start.3 = (bf16[128,3072]{1,0:T(8,128)(2,1)}, bf16[128,3072]{1,0:T(8,128)(2,1)}, u32[]{:S(2)}, u32[]{:S(2)}) collective-permute-start(bf16[128,3072]{1,0:T(8,128)(2,1)} %get-tuple-element.55), channel_id=1, source_target_pairs={{0,2},{2,0},{1,3},{3,1},{4,6},{6,4},{5,7},{7,5},{8,10},{10,8},{9,1... | collective-permute-start | bytes 2359304 | tf_op jit(solution)/shard_map/ppermute | solution.py:499
  210.3 16.7 %copy-start.93 = (f32[1024]{0:T(1024)}, f32[1024]{0:T(1024)S(1)}, u32[]{:S(2)}) copy-start(f32[1024]{0:T(1024)S(1)} %get-tuple-element.69) | copy-start | bytes 12292
  226.9 162.4 %copy-start = (f32[128,1024]{1,0:T(8,128)}, f32[128,1024]{1,0:T(8,128)S(1)}, u32[]{:S(2)}) copy-start(f32[128,1024]{1,0:T(8,128)S(1)} %get-tuple-element.146) | copy-start | bytes 1572868
  230.2 39.3 %all-to-all-start.3 = ((bf16[32,40,1024]{2,1,0:T(8,128)(2,1)}), bf16[32,40,1024]{2,1,0:T(8,128)(2,1)}, u32[]{:S(2)}, u32[]{:S(2)}) async-start(bf16[32,40,1024]{2,1,0:T(8,128)(2,1)} %bitcast.348), calls=%async_computation.3 | async-start | bytes 5242880 | tf_op jit(solution)/shard_map/all_to_all | solution.py:140
  239.0 5.6 copy-start.37
  241.1 35.3 %collective-permute-start.4 = (bf16[2,128,3072]{2,1,0:T(8,128)(2,1)}, bf16[2,128,3072]{2,1,0:T(8,128)(2,1)}, u32[]{:S(2)}, u32[]{:S(2)}) collective-permute-start(bf16[2,128,3072]{2,1,0:T(8,128)(2,1)} %pad_maximum_fusion.7), channel_id=1, source_target_pairs={{0,1},{1,0},{2,3},{3,2},{4,5},{5,4},{6,7},{7,6},{8,9},{9,8},{10,11... | collective-permute-start | bytes 4718600 | tf_op jit(solution)/shard_map/ppermute | solution.py:151
  269.5 38.7 %all-to-all-start.4 = ((bf16[32,40,1024]{2,1,0:T(8,128)(2,1)}), bf16[32,40,1024]{2,1,0:T(8,128)(2,1)}, u32[]{:S(2)}, u32[]{:S(2)}) async-start(bf16[32,40,1024]{2,1,0:T(8,128)(2,1)} %bitcast.347), calls=%async_computation.4 | async-start | bytes 5242880 | tf_op jit(solution)/shard_map/all_to_all | solution.py:140
  278.9 10.5 %copy-start.17 = (bf16[2,2,128,3072]{3,2,1,0:T(8,128)(2,1)}, bf16[2,2,128,3072]{3,2,1,0:T(8,128)(2,1)S(1)}, u32[]{:S(2)}) copy-start(bf16[2,2,128,3072]{3,2,1,0:T(8,128)(2,1)S(1)} %copy.103) | copy-start | bytes 9437188
  283.4 6.1 copy-start.135
  308.2 39.2 %all-to-all-start.5 = ((bf16[32,40,1024]{2,1,0:T(8,128)(2,1)}), bf16[32,40,1024]{2,1,0:T(8,128)(2,1)}, u32[]{:S(2)}, u32[]{:S(2)}) async-start(bf16[32,40,1024]{2,1,0:T(8,128)(2,1)} %bitcast.365), calls=%async_computation.5 | async-start | bytes 5242880 | tf_op jit(solution)/shard_map/all_to_all | solution.py:140
  347.3 39.4 %all-to-all-start.6 = ((bf16[32,40,1024]{2,1,0:T(8,128)(2,1)}), bf16[32,40,1024]{2,1,0:T(8,128)(2,1)}, u32[]{:S(2)}, u32[]{:S(2)}) async-start(bf16[32,40,1024]{2,1,0:T(8,128)(2,1)} %bitcast.344), calls=%async_computation.6 | async-start | bytes 5242880 | tf_op jit(solution)/shard_map/all_to_all | solution.py:140
  373.8 15.6 %copy-start.94 = (f32[1024]{0:T(1024)S(1)}, f32[1024]{0:T(1024)}, u32[]{:S(2)}) copy-start(f32[1024]{0:T(1024)} %copy-done.93) | copy-start | bytes 12292
  389.4 5.9 copy-start.109
  390.3 5.1 copy-start.78
  390.3 5.1 copy-start.80
  390.3 5.0 copy-start.88
  400.6 4.9 copy-start.36
  407.9 40.6 %all-to-all-start.7 = ((bf16[32,40,1024]{2,1,0:T(8,128)(2,1)}), bf16[32,40,1024]{2,1,0:T(8,128)(2,1)}, u32[]{:S(2)}, u32[]{:S(2)}) async-start(bf16[32,40,1024]{2,1,0:T(8,128)(2,1)} %bitcast.345), calls=%async_computation.7 | async-start | bytes 5242880 | tf_op jit(solution)/shard_map/all_to_all | solution.py:140
  414.5 160.6 %reduce-scatter.5.cloned.1.call-start = ((), (), s32[]{:S(2)}) async-start(), calls=%async_computation.15 | async-start | bytes 3932160 | tf_op jit(solution)/shard_map/reduce_scatter | solution.py:159
  417.9 21.1 %collective-permute-start.5 = (bf16[512,2048]{1,0:T(8,128)(2,1)}, bf16[512,2048]{1,0:T(8,128)(2,1)}, u32[]{:S(2)}, u32[]{:S(2)}) collective-permute-start(bf16[512,2048]{1,0:T(8,128)(2,1)} %convolution_convert_fusion.7), channel_id=1, source_target_pairs={{0,1},{1,0},{2,3},{3,2},{4,5},{5,4},{6,7},{7,6},{8,9},{9,8},{10,11... | collective-permute-start | bytes 6291464 | tf_op jit(solution)/shard_map/ppermute | solution.py:194
  420.9 4.9 copy-start.91
  423.2 13.1 %collective-permute-start.6 = (bf16[512,1024]{1,0:T(8,128)(2,1)}, bf16[512,1024]{1,0:T(8,128)(2,1)}, u32[]{:S(2)}, u32[]{:S(2)}) collective-permute-start(bf16[512,1024]{1,0:T(8,128)(2,1)} %convolution_convert_fusion.11), channel_id=1, source_target_pairs={{0,1},{1,0},{2,3},{3,2},{4,5},{5,4},{6,7},{7,6},{8,9},{9,8},{10,11... | collective-permute-start | bytes 3145736 | tf_op jit(solution)/shard_map/ppermute | solution.py:194
  431.3 5.0 copy-start.62
  431.3 4.3 collective-permute-start.7
  448.5 6.3 %copy-start.16 = (bf16[2,2,128,3072]{3,2,1,0:T(8,128)(2,1)S(1)}, bf16[2,2,128,3072]{3,2,1,0:T(8,128)(2,1)}, u32[]{:S(2)}) copy-start(bf16[2,2,128,3072]{3,2,1,0:T(8,128)(2,1)} %pad_maximum_fusion.2) | copy-start | bytes 9437188
  459.4 6.6 %copy-start.92 = (f32[128,32]{0,1:T(8,128)S(1)}, f32[128,32]{0,1:T(8,128)}, u32[]{:S(2)}) copy-start(f32[128,32]{0,1:T(8,128)} %get-tuple-element.158) | copy-start | bytes 49156
  459.4 39.5 %all-to-all-start.8 = ((bf16[32,40,1024]{2,1,0:T(8,128)(2,1)}), bf16[32,40,1024]{2,1,0:T(8,128)(2,1)}, u32[]{:S(2)}, u32[]{:S(2)}) async-start(bf16[32,40,1024]{2,1,0:T(8,128)(2,1)} %bitcast.343), calls=%async_computation.8 | async-start | bytes 5242880 | tf_op jit(solution)/shard_map/all_to_all | solution.py:140
  465.5 144.4 %reduce-scatter.3.cloned.1.call-start = ((), (), s32[]{:S(2)}) async-start(), calls=%async_computation.14 | async-start | bytes 3932160 | tf_op jit(solution)/shard_map/reduce_scatter | solution.py:159
  479.6 19.4 %copy-start.117 = (f32[128]{0:T(128)S(1)}, f32[128]{0:T(128)}, u32[]{:S(2)}) copy-start(f32[128]{0:T(128)} %copy-done.116) | copy-start | bytes 1540
  502.4 33.2 %copy-start.4 = (f32[128,1024]{1,0:T(8,128)}, f32[128,1024]{1,0:T(8,128)S(1)}, u32[]{:S(2)}) copy-start(f32[128,1024]{1,0:T(8,128)S(1)} %multiply_add_fusion) | copy-start | bytes 1572868
  509.6 8.5 %copy-start.66 = (bf16[128,16,32]{0,2,1:T(8,128)(2,1)S(1)}, bf16[128,16,32]{0,2,1:T(8,128)(2,1)}, u32[]{:S(2)}) copy-start(bf16[128,16,32]{0,2,1:T(8,128)(2,1)} %get-tuple-element.101) | copy-start | bytes 393220
  509.6 8.5 %copy-start.67 = (bf16[128,16,32]{0,2,1:T(8,128)(2,1)S(1)}, bf16[128,16,32]{0,2,1:T(8,128)(2,1)}, u32[]{:S(2)}) copy-start(bf16[128,16,32]{0,2,1:T(8,128)(2,1)} %get-tuple-element.102) | copy-start | bytes 393220
  509.6 8.5 %copy-start.82 = (bf16[128,8,32]{0,2,1:T(8,128)(2,1)S(1)}, bf16[128,8,32]{0,2,1:T(8,128)(2,1)}, u32[]{:S(2)}) copy-start(bf16[128,8,32]{0,2,1:T(8,128)(2,1)} %get-tuple-element.111) | copy-start | bytes 196612
  509.6 8.5 %copy-start.83 = (bf16[128,8,32]{0,2,1:T(8,128)(2,1)S(1)}, bf16[128,8,32]{0,2,1:T(8,128)(2,1)}, u32[]{:S(2)}) copy-start(bf16[128,8,32]{0,2,1:T(8,128)(2,1)} %get-tuple-element.112) | copy-start | bytes 196612
  509.6 8.5 %copy-start.76 = (bf16[128,8,32]{0,2,1:T(8,128)(2,1)S(1)}, bf16[128,8,32]{0,2,1:T(8,128)(2,1)}, u32[]{:S(2)}) copy-start(bf16[128,8,32]{0,2,1:T(8,128)(2,1)} %copy-done.74) | copy-start | bytes 196612
  509.6 8.5 %copy-start.107 = (f32[8,2,128]{2,1,0:T(2,128)S(1)}, f32[8,2,128]{2,1,0:T(2,128)}, u32[]{:S(2)}) copy-start(f32[8,2,128]{2,1,0:T(2,128)} %copy-done.105) | copy-start | bytes 24580
  509.7 51.3 %all-to-all-start.10 = ((bf16[64,8,3200]{2,1,0:T(8,128)(2,1)}), bf16[64,8,3200]{2,1,0:T(8,128)(2,1)}, u32[]{:S(2)}, u32[]{:S(2)}) async-start(bf16[64,8,3200]{2,1,0:T(8,128)(2,1)} %bitcast.342), calls=%async_computation.10 | async-start | bytes 6553600 | tf_op jit(solution)/shard_map/all_to_all | solution.py:199
  520.6 5.3 copy-start.110
  523.6 12.4 %collective-permute-start.8 = (bf16[512,2048]{1,0:T(8,128)(2,1)}, bf16[512,2048]{1,0:T(8,128)(2,1)}, u32[]{:S(2)}, u32[]{:S(2)}) collective-permute-start(bf16[512,2048]{1,0:T(8,128)(2,1)} %convolution_convert_fusion.6), channel_id=1, source_target_pairs={{0,1},{1,0},{2,3},{3,2},{4,5},{5,4},{6,7},{7,6},{8,9},{9,8},{10,11... | collective-permute-start | bytes 6291464 | tf_op jit(solution)/shard_map/ppermute | solution.py:194
  527.5 5.6 copy-start.56
  527.5 5.6 copy-start.119
  527.5 8.1 %collective-permute-start.9 = (bf16[512,1024]{1,0:T(8,128)(2,1)S(1)}, bf16[512,1024]{1,0:T(8,128)(2,1)S(1)}, u32[]{:S(2)}, u32[]{:S(2)}) collective-permute-start(bf16[512,1024]{1,0:T(8,128)(2,1)S(1)} %convolution_convert_fusion.10), channel_id=1, source_target_pairs={{0,1},{1,0},{2,3},{3,2},{4,5},{5,4},{6,7},{7,6},{8,9},{9,8},{10,11... | collective-permute-start | bytes 3145736 | tf_op jit(solution)/shard_map/ppermute | solution.py:194
  534.1 1.4 collective-permute-start.10
  560.9 53.8 %all-to-all-start.9 = ((bf16[64,8,3200]{2,1,0:T(8,128)(2,1)}), bf16[64,8,3200]{2,1,0:T(8,128)(2,1)S(1)}, u32[]{:S(2)}, u32[]{:S(2)}) async-start(bf16[64,8,3200]{2,1,0:T(8,128)(2,1)} %maximum_bitcast_fusion), calls=%async_computation.9 | async-start | bytes 6553600 | tf_op jit(solution)/shard_map/all_to_all | solution.py:199
  (97 other events, 260.8 us)
Sparse Core Ops, SparseCore 0:
  79.9 89.2 all-gather.1
  421.0 79.0 reduce-scatter.4
  502.5 107.3 reduce-scatter.2

commit v10 on v9

--- a/solution.py
+++ b/solution.py
@@ -3,6 +3,8 @@
 import jax
 import jax.numpy as jnp
 from jax import lax
+from jax.experimental import pallas as pl
+from jax.experimental.pallas import tpu as pltpu
 from jax.sharding import Mesh, PartitionSpec as P
 
 MODEL_WIDTH = 1024
@@ -23,6 +25,7 @@
 
 ROOM = 40
 ROWS = E * ROOM
+ROW_BLOCK = 256
 AXES = ("x", "y", "zh", "zl", "c")
 EXPERT_AXES = ("x", "y", "zh")
 CHIP_AXES = ("x", "y", "zh", "zl")
@@ -280,54 +283,104 @@
     ).astype(jnp.bfloat16)
 
 
+ACROSS = (((1,), (1,)), ((), ()))
+
+
+def forward_kernel(rows_ref, expert_ref, results_ref, gate_ref, up_ref):
+    rows = rows_ref[...]
+    gate_pre = lax.dot_general(
+        rows, expert_ref[:, :MODEL_WIDTH], ACROSS, preferred_element_type=jnp.float32
+    )
+    up_pre = lax.dot_general(
+        rows,
+        expert_ref[:, MODEL_WIDTH : 2 * MODEL_WIDTH],
+        ACROSS,
+        preferred_element_type=jnp.float32,
+    )
+    gate_ref[...] = gate_pre
+    up_ref[...] = up_pre
+    units = (gate_pre / (1.0 + jnp.exp(-gate_pre)) * up_pre).astype(jnp.bfloat16)
+    results_ref[...] = jnp.dot(
+        units, expert_ref[:, 2 * MODEL_WIDTH :], preferred_element_type=jnp.float32
+    ).astype(jnp.bfloat16)
+
+
+def backward_kernel(
+    grad_ref, gate_ref, up_ref, expert_ref, rows_ref, grad_gate_ref, grad_up_ref, units_ref
+):
+    gate_pre, up_pre = gate_ref[...], up_ref[...]
+    sigmoid_pre = 1.0 / (1.0 + jnp.exp(-gate_pre))
+    activated = gate_pre * sigmoid_pre
+    units_ref[...] = (activated * up_pre).astype(jnp.bfloat16)
+    grad_units = lax.dot_general(
+        grad_ref[...],
+        expert_ref[:, 2 * MODEL_WIDTH :],
+        ACROSS,
+        preferred_element_type=jnp.float32,
+    )
+    grad_gate = (
+        grad_units * up_pre * (sigmoid_pre * (1.0 + gate_pre * (1.0 - sigmoid_pre)))
+    ).astype(jnp.bfloat16)
+    grad_up = (grad_units * activated).astype(jnp.bfloat16)
+    grad_gate_ref[...] = grad_gate
+    grad_up_ref[...] = grad_up
+    grad_rows = jnp.dot(
+        grad_gate, expert_ref[:, :MODEL_WIDTH], preferred_element_type=jnp.float32
+    ) + jnp.dot(
+        grad_up,
+        expert_ref[:, MODEL_WIDTH : 2 * MODEL_WIDTH],
+        preferred_element_type=jnp.float32,
+    )
+    rows_ref[...] = grad_rows.astype(jnp.bfloat16)
+
+
+def row_blocks(kernel, ins, expert_at, outs):
+    def blocked(width):
+        return pl.BlockSpec((ROW_BLOCK, width), lambda i: (i, 0))
+
+    specs = [
+        pl.BlockSpec(a.shape, lambda i: (0, 0)) if at == expert_at else blocked(a.shape[1])
+        for at, a in enumerate(ins)
+    ]
+    flops = 2 * ROWS * 3 * MODEL_WIDTH * ins[expert_at].shape[0]
+    moved = sum(a.size * a.dtype.itemsize for a in ins)
+    return pl.pallas_call(
+        kernel,
+        grid=(ROWS // ROW_BLOCK,),
+        in_specs=specs,
+        out_specs=[blocked(width) for width, _ in outs],
+        out_shape=[jax.ShapeDtypeStruct((ROWS, width), kind) for width, kind in outs],
+        compiler_params=pltpu.CompilerParams(vmem_limit_bytes=40 * 1024 * 1024),
+        cost_estimate=pl.CostEstimate(flops=flops, bytes_accessed=2 * moved, transcendentals=0),
+    )(*ins)
+
+
 def feed_forward(rows_here, expert):
-    expert_in_l, expert_out_l = expert[:, : 2 * MODEL_WIDTH], expert[:, 2 * MODEL_WIDTH :]
-    gate_pre = lax.dot_general(
-        rows_here,
-        expert_in_l[:, :MODEL_WIDTH],
-        (((1,), (1,)), ((), ())),
-        preferred_element_type=jnp.float32,
-    )
-    up_pre = lax.dot_general(
-        rows_here,
-        expert_in_l[:, MODEL_WIDTH:],
-        (((1,), (1,)), ((), ())),
-        preferred_element_type=jnp.float32,
-    )
-    units = (jax.nn.silu(gate_pre) * up_pre).astype(jnp.bfloat16)
-    results = jnp.dot(units, expert_out_l, preferred_element_type=jnp.float32).astype(jnp.bfloat16)
+    hidden_units = expert.shape[0]
+    outs = (
+        (MODEL_WIDTH, jnp.bfloat16),
+        (hidden_units, jnp.float32),
+        (hidden_units, jnp.float32),
+    )
+    results, gate_pre, up_pre = row_blocks(forward_kernel, (rows_here, expert), 1, outs)
     return results, (gate_pre, up_pre)
 
 
 def feed_backward(grad_rows, rows_here, pre, expert):
-    expert_in_l, expert_out_l = expert[:, : 2 * MODEL_WIDTH], expert[:, 2 * MODEL_WIDTH :]
-    gate_pre, up_pre = pre
-    sigmoid_pre = jax.nn.sigmoid(gate_pre)
-    activated = gate_pre * sigmoid_pre
-    units = (activated * up_pre).astype(jnp.bfloat16)
-    grad_units = lax.dot_general(
-        grad_rows, expert_out_l, (((1,), (1,)), ((), ())), preferred_element_type=jnp.float32
-    )
-    grad_gate_pre = (
-        grad_units * up_pre * (sigmoid_pre * (1.0 + gate_pre * (1.0 - sigmoid_pre)))
-    ).astype(jnp.bfloat16)
-    grad_up_pre = (grad_units * activated).astype(jnp.bfloat16)
-    grad_in_rows = jnp.dot(
-        grad_gate_pre, expert_in_l[:, :MODEL_WIDTH], preferred_element_type=jnp.float32
-    )
-    grad_in_rows = (
-        grad_in_rows
-        + jnp.dot(grad_up_pre, expert_in_l[:, MODEL_WIDTH:], preferred_element_type=jnp.float32)
-    ).astype(jnp.bfloat16)
-    out_grad = lax.dot_general(
-        units, grad_rows, (((0,), (0,)), ((), ())), preferred_element_type=jnp.float32
-    )
-    gate_w_grad = lax.dot_general(
-        grad_gate_pre, rows_here, (((0,), (0,)), ((), ())), preferred_element_type=jnp.float32
-    )
-    up_w_grad = lax.dot_general(
-        grad_up_pre, rows_here, (((0,), (0,)), ((), ())), preferred_element_type=jnp.float32
-    )
+    hidden_units = expert.shape[0]
+    outs = ((MODEL_WIDTH, jnp.bfloat16),) + ((hidden_units, jnp.bfloat16),) * 3
+    grad_in_rows, grad_gate_pre, grad_up_pre, units = row_blocks(
+        backward_kernel, (grad_rows, *pre, expert), 3, outs
+    )
+    pair = (((0,), (0,)), ((), ()))
+    gate_w_grad, up_w_grad, out_grad = [
+        lax.dot_general(left, right, pair, preferred_element_type=jnp.float32)
+        for left, right in (
+            (grad_gate_pre, rows_here),
+            (grad_up_pre, rows_here),
+            (units, grad_rows),
+        )
+    ]
     return grad_in_rows, (gate_w_grad, up_w_grad, out_grad)
 
 
@@ -461,9 +514,9 @@
     own_experts = [
         jnp.concatenate([expert_in[layer], expert_out[layer]], axis=1) for layer in layers
     ]
-    beside = order, position, live_row, routed, chosen, own_experts
+    beside = order, routed, chosen, own_experts
     lead, beside = sent_by_chips(jnp.concatenate(lead + [fill], axis=1), beside)
-    order, position, live_row, routed, chosen, own_experts = beside
+    order, routed, chosen, own_experts = beside
     live = live_row.astype(jnp.float32)
     cosine_table, sine_values = rope_tables(position)
     other_expert = lax.ppermute(own_experts[0], "zl", SWAP)

time: 637 us -> 634 us (level)
  matrix products: 179 us -> 123 us
  Pallas kernels: 0 us -> 29 us
  local copies, waits for them, and re-layouts: 33.7 us -> 59.2 us
  waiting for transfers between devices: 252 us -> 260 us
    dot_general x18 -> x6, matrix products: 71.3 us -> 17.4 us  [feed_backward(): lax.dot_general(left, right, pair, preferred_element_type=jnp.float32)]
    reduce_scatter x2, waiting for transfers between devices: 34.8 us -> 0.04 us  [scatter_expert(): return lax.psum_scatter(both, GROUP_AXES, scatter_dimension=0, tiled=True)]
    all_to_all x2, waiting for transfers between devices: 20.7 us -> 51.3 us  [chip_sum(): lax.all_to_all(parts, Z_AXES + ('x', 'y'), split_axis=0, concat_axis=0, t...]
    pallas_call x0 -> x4, Pallas kernels: none -> 29 us  [row_blocks(): pl.pallas_call(kernel, grid=(ROWS // ROW_BLOCK,), in_specs=specs, out_spe...]
    unnamed x272 -> x298, local copies, waits for them, and re-layouts: 9.47 us -> 35.8 us
    all_to_all x8, waiting for transfers between devices: 153 us -> 159 us  [trade_rows(): lax.all_to_all(rows.reshape(E, ROOM, MODEL_WIDTH), EXPERT_AXES, split_axi...]
  transfers between devices with their start and end apart: 25 -> 25, of which waited for: 13 -> 14; matrix products, arithmetic and copies ran while one was open for 35% -> 28% of each run, Pallas kernels for 0% -> 5%
where the time goes in v10:
time: 634 us; the launch traced here: 623 us
  waiting for transfers between devices  260 us (41%)
  matrix products  123 us (19%)
  starting transfers between devices  88.8 us (14%)
  local copies, waits for them, and re-layouts  59.2 us (9%)
  other arithmetic  47.5 us (7%)
  Pallas kernels  29 us (5%)
  between operations  16.3 us (3%)
    all_to_all x8, waiting for transfers between devices, trade_rows(): lax.all_to_all(rows.reshape(E, ROOM, MODEL_WIDTH), EXPERT_AXES, split_axi...  159 us
    all_to_all x8, starting transfers between devices, trade_rows(): lax.all_to_all(rows.reshape(E, ROOM, MODEL_WIDTH), EXPERT_AXES, split_axi...  58.6 us
    all_to_all x2, waiting for transfers between devices, chip_sum(): lax.all_to_all(parts, Z_AXES + ('x', 'y'), split_axis=0, concat_axis=0, t...  51.3 us
    unnamed x298, local copies, waits for them, and re-layouts  35.8 us
    all_to_all x1, waiting for transfers between devices, sent_by_chips(): lax.all_to_all(copies, CHIP_AXES, split_axis=0, concat_axis=0, tiled=True)  35.1 us
    pallas_call x4, Pallas kernels, row_blocks(): pl.pallas_call(kernel, grid=(ROWS // ROW_BLOCK,), in_specs=specs, out_spe...  29 us
    dot_general x6, matrix products, feed_backward(): lax.dot_general(left, right, pair, preferred_element_type=jnp.float32)  17.4 us
    all_to_all x2, starting transfers between devices, chip_sum(): lax.all_to_all(parts, Z_AXES + ('x', 'y'), split_axis=0, concat_axis=0, t...  14.9 us
  transfers between devices with their start and end apart: 25, of which 14 were waited for; matrix products, arithmetic and copies ran while one was open for 28% of the time, Pallas kernels for 5%

profile of v10, /device:TPU:2, one launch (start us, length us, event | category | flops | bytes accessed | tf_op | source)
XLA Modules:
  0.0 623.4 jit_solution(106861306681695213)
XLA Ops:
  12.8 11.8 %all-to-all-start = ((bf16[64,8,3200]{2,1,0:T(8,128)(2,1)}), bf16[64,8,3200]{2,1,0:T(8,128)(2,1)}, u32[]{:S(2)}, u32[]{:S(2)}) async-start(bf16[64,8,3200]{2,1,0:T(8,128)(2,1)} %broadcast_in_dim.73), calls=%async_computation | async-start | bytes 6553600 | tf_op jit(solution)/shard_map/all_to_all | solution.py:47
  30.6 35.1 %all-to-all-done = bf16[64,8,3200]{2,1,0:T(8,128)(2,1)} async-done(((bf16[64,8,3200]{2,1,0:T(8,128)(2,1)}), bf16[64,8,3200]{2,1,0:T(8,128)(2,1)}, u32[]{:S(2)}, u32[]{:S(2)}) %all-to-all-start) | async-done | bytes 3276832 | tf_op jit(solution)/shard_map/all_to_all | solution.py:47
  65.7 6.2 collective-permute-done
  71.9 3.5 select_bitcast_fusion.1
  75.5 3.3 pad_maximum_fusion
  82.8 3.0 fusion.9
  89.4 2.3 multiply_reduce_fusion.10
  91.9 2.3 convolution_convert_fusion.3
  94.2 6.3 %collective-permute-done.1 = bf16[128,3072]{1,0:T(8,128)(2,1)} collective-permute-done((bf16[128,3072]{1,0:T(8,128)(2,1)S(1)}, bf16[128,3072]{1,0:T(8,128)(2,1)}, u32[]{:S(2)}, u32[]{:S(2)}) %collective-permute-start.1) | collective-permute-done | bytes 786464 | tf_op jit(solution)/shard_map/ppermute | solution.py:522
  103.9 8.0 %all-to-all-start.1 = ((bf16[32,40,1024]{2,1,0:T(8,128)(2,1)}), bf16[32,40,1024]{2,1,0:T(8,128)(2,1)S(1)}, u32[]{:S(2)}, u32[]{:S(2)}) async-start(bf16[32,40,1024]{2,1,0:T(8,128)(2,1)} %bitcast.340), calls=%async_computation.1 | async-start | bytes 5242880 | tf_op jit(solution)/shard_map/all_to_all | solution.py:143
  116.2 32.7 %all-to-all-done.1 = bf16[32,40,1024]{2,1,0:T(8,128)(2,1)S(1)} async-done(((bf16[32,40,1024]{2,1,0:T(8,128)(2,1)}), bf16[32,40,1024]{2,1,0:T(8,128)(2,1)S(1)}, u32[]{:S(2)}, u32[]{:S(2)}) %all-to-all-start.1) | async-done | bytes 2621472 | tf_op jit(solution)/shard_map/all_to_all | solution.py:143
  150.7 5.5 shard_map.187
  160.7 9.7 %all-to-all-start.2 = ((bf16[32,40,1024]{2,1,0:T(8,128)(2,1)}), bf16[32,40,1024]{2,1,0:T(8,128)(2,1)}, u32[]{:S(2)}, u32[]{:S(2)}) async-start(bf16[32,40,1024]{2,1,0:T(8,128)(2,1)} %bitcast.331), calls=%async_computation.2 | async-start | bytes 5242880 | tf_op jit(solution)/shard_map/all_to_all | solution.py:143
  172.7 32.2 %all-to-all-done.2 = bf16[32,40,1024]{2,1,0:T(8,128)(2,1)} async-done(((bf16[32,40,1024]{2,1,0:T(8,128)(2,1)}), bf16[32,40,1024]{2,1,0:T(8,128)(2,1)}, u32[]{:S(2)}, u32[]{:S(2)}) %all-to-all-start.2) | async-done | bytes 2621472 | tf_op jit(solution)/shard_map/all_to_all | solution.py:143
  205.1 3.2 multiply_reduce_fusion.9
  209.8 3.1 fusion.5
  220.0 2.4 fusion.215
  224.3 2.3 multiply_reduce_fusion.8
  227.5 2.3 convolution_convert_fusion.1
  229.8 7.4 %all-to-all-start.3 = ((bf16[32,40,1024]{2,1,0:T(8,128)(2,1)}), bf16[32,40,1024]{2,1,0:T(8,128)(2,1)}, u32[]{:S(2)}, u32[]{:S(2)}) async-start(bf16[32,40,1024]{2,1,0:T(8,128)(2,1)} %bitcast.342), calls=%async_computation.3 | async-start | bytes 5242880 | tf_op jit(solution)/shard_map/all_to_all | solution.py:143
  243.9 2.4 convolution_convert_fusion.2
  246.3 23.7 %all-to-all-done.3 = bf16[32,40,1024]{2,1,0:T(8,128)(2,1)} async-done(((bf16[32,40,1024]{2,1,0:T(8,128)(2,1)}), bf16[32,40,1024]{2,1,0:T(8,128)(2,1)}, u32[]{:S(2)}, u32[]{:S(2)}) %all-to-all-start.3) | async-done | bytes 2621472 | tf_op jit(solution)/shard_map/all_to_all | solution.py:143
  270.0 7.2 %all-to-all-start.4 = ((bf16[32,40,1024]{2,1,0:T(8,128)(2,1)}), bf16[32,40,1024]{2,1,0:T(8,128)(2,1)}, u32[]{:S(2)}, u32[]{:S(2)}) async-start(bf16[32,40,1024]{2,1,0:T(8,128)(2,1)} %bitcast.341), calls=%async_computation.4 | async-start | bytes 5242880 | tf_op jit(solution)/shard_map/all_to_all | solution.py:143
  279.8 6.6 %shard_map.188 = (bf16[1280,1024]{1,0:T(8,128)(2,1)S(1)}, f32[1280,512]{1,0:T(8,128)S(1)}, f32[1280,512]{1,0:T(8,128)S(1)}) custom-call(bf16[1280,1024]{1,0:T(8,128)(2,1)} %bitcast.58.rows_ref, bf16[512,3072]{1,0:T(8,128)(2,1)S(1)} %bitcast.326), custom_call_target="tpu_custom_call" | custom-call | flops 4026531840 | bytes 11534336 | tf_op jit(solution)/shard_map/pallas_call | solution.py:347
  292.4 16.9 %all-to-all-done.4 = bf16[32,40,1024]{2,1,0:T(8,128)(2,1)} async-done(((bf16[32,40,1024]{2,1,0:T(8,128)(2,1)}), bf16[32,40,1024]{2,1,0:T(8,128)(2,1)}, u32[]{:S(2)}, u32[]{:S(2)}) %all-to-all-start.4) | async-done | bytes 2621472 | tf_op jit(solution)/shard_map/all_to_all | solution.py:143
  309.4 6.4 %all-to-all-start.5 = ((bf16[32,40,1024]{2,1,0:T(8,128)(2,1)}), bf16[32,40,1024]{2,1,0:T(8,128)(2,1)}, u32[]{:S(2)}, u32[]{:S(2)}) async-start(bf16[32,40,1024]{2,1,0:T(8,128)(2,1)} %bitcast.330), calls=%async_computation.5 | async-start | bytes 5242880 | tf_op jit(solution)/shard_map/all_to_all | solution.py:143
  316.4 3.0 convolution_convert_fusion.17
  319.5 3.0 convolution_convert_fusion.19
  322.4 8.5 %shard_map.189 = (bf16[1280,1024]{1,0:T(8,128)(2,1)S(1)}, bf16[1280,512]{1,0:T(8,128)(2,1)S(1)}, bf16[1280,512]{1,0:T(8,128)(2,1)S(1)}, bf16[1280,512]{1,0:T(8,128)(2,1)S(1)}) custom-call(bf16[1280,1024]{1,0:T(8,128)(2,1)} %bitcast.65.grad_ref, f32[1280,512]{1,0:T(8,128)S(1)} %copy-done.21, f32[1280,512]{1,0:T(8,128)S(1)} %copy-done.23, ...), custom_call_target="tpu_custom_call" | custom-call | flops 4026531840 | bytes 22020096 | tf_op jit(solution)/shard_map/pallas_call | solution.py:347
  335.6 12.5 %all-to-all-done.5 = bf16[32,40,1024]{2,1,0:T(8,128)(2,1)} async-done(((bf16[32,40,1024]{2,1,0:T(8,128)(2,1)}), bf16[32,40,1024]{2,1,0:T(8,128)(2,1)}, u32[]{:S(2)}, u32[]{:S(2)}) %all-to-all-start.5) | async-done | bytes 2621472 | tf_op jit(solution)/shard_map/all_to_all | solution.py:143
  348.1 6.6 %all-to-all-start.6 = ((bf16[32,40,1024]{2,1,0:T(8,128)(2,1)}), bf16[32,40,1024]{2,1,0:T(8,128)(2,1)}, u32[]{:S(2)}, u32[]{:S(2)}) async-start(bf16[32,40,1024]{2,1,0:T(8,128)(2,1)} %bitcast.328), calls=%async_computation.6 | async-start | bytes 5242880 | tf_op jit(solution)/shard_map/all_to_all | solution.py:143
  354.8 3.8 convolution_convert_fusion.10
  358.6 3.4 convolution_convert_fusion.11
  362.0 3.3 convolution_convert_fusion.12
  367.1 2.7 fusion.11
  373.0 15.3 %all-to-all-done.6 = bf16[32,40,1024]{2,1,0:T(8,128)(2,1)} async-done(((bf16[32,40,1024]{2,1,0:T(8,128)(2,1)}), bf16[32,40,1024]{2,1,0:T(8,128)(2,1)}, u32[]{:S(2)}, u32[]{:S(2)}) %all-to-all-start.6) | async-done | bytes 2621472 | tf_op jit(solution)/shard_map/all_to_all | solution.py:143
  388.3 2.6 multiply_reduce_fusion.4
  392.6 3.2 fusion.46
  397.0 2.2 fusion.56
  402.3 4.0 multiply_reduce_fusion.5
  407.3 2.4 convolution_convert_fusion
  409.8 6.4 %all-to-all-start.7 = ((bf16[32,40,1024]{2,1,0:T(8,128)(2,1)}), bf16[32,40,1024]{2,1,0:T(8,128)(2,1)}, u32[]{:S(2)}, u32[]{:S(2)}) async-start(bf16[32,40,1024]{2,1,0:T(8,128)(2,1)} %bitcast.339), calls=%async_computation.7 | async-start | bytes 5242880 | tf_op jit(solution)/shard_map/all_to_all | solution.py:143
  416.2 3.3 convolution_convert_fusion.5
  427.3 2.7 fusion.76
  430.2 2.7 convolution_multiply_fusion
  434.8 2.7 add_convert_fusion.3
  437.5 3.7 add_convert_fusion.1
  441.2 7.2 %all-to-all-done.7 = bf16[32,40,1024]{2,1,0:T(8,128)(2,1)} async-done(((bf16[32,40,1024]{2,1,0:T(8,128)(2,1)}), bf16[32,40,1024]{2,1,0:T(8,128)(2,1)}, u32[]{:S(2)}, u32[]{:S(2)}) %all-to-all-start.7) | async-done | bytes 2621472 | tf_op jit(solution)/shard_map/all_to_all | solution.py:143
  451.9 8.5 %shard_map.190 = (bf16[1280,1024]{1,0:T(8,128)(2,1)S(1)}, bf16[1280,512]{1,0:T(8,128)(2,1)S(1)}, bf16[1280,512]{1,0:T(8,128)(2,1)S(1)}, bf16[1280,512]{1,0:T(8,128)(2,1)S(1)}) custom-call(bf16[1280,1024]{1,0:T(8,128)(2,1)} %bitcast.88.grad_ref, f32[1280,512]{1,0:T(8,128)S(1)} %copy-done.17, f32[1280,512]{1,0:T(8,128)S(1)} %copy-done.19, ...), custom_call_target="tpu_custom_call" | custom-call | flops 4026531840 | bytes 22020096 | tf_op jit(solution)/shard_map/pallas_call | solution.py:347
  465.2 6.9 %all-to-all-start.8 = ((bf16[32,40,1024]{2,1,0:T(8,128)(2,1)}), bf16[32,40,1024]{2,1,0:T(8,128)(2,1)}, u32[]{:S(2)}, u32[]{:S(2)}) async-start(bf16[32,40,1024]{2,1,0:T(8,128)(2,1)} %bitcast.329), calls=%async_computation.8 | async-start | bytes 5242880 | tf_op jit(solution)/shard_map/all_to_all | solution.py:143
  473.6 3.8 convolution_convert_fusion.13
  483.9 3.1 pad_maximum_fusion.1
  487.0 18.8 %all-to-all-done.8 = bf16[32,40,1024]{2,1,0:T(8,128)(2,1)} async-done(((bf16[32,40,1024]{2,1,0:T(8,128)(2,1)}), bf16[32,40,1024]{2,1,0:T(8,128)(2,1)}, u32[]{:S(2)}, u32[]{:S(2)}) %all-to-all-start.8) | async-done | bytes 2621472 | tf_op jit(solution)/shard_map/all_to_all | solution.py:143
  505.8 3.0 multiply_reduce_fusion.2
  509.1 2.7 fusion.49
  513.8 8.4 %all-to-all-start.10 = ((bf16[64,8,3200]{2,1,0:T(8,128)(2,1)}), bf16[64,8,3200]{2,1,0:T(8,128)(2,1)}, u32[]{:S(2)}, u32[]{:S(2)}) async-start(bf16[64,8,3200]{2,1,0:T(8,128)(2,1)} %bitcast.109), calls=%async_computation.10 | async-start | bytes 6553600 | tf_op jit(solution)/shard_map/all_to_all | solution.py:202
  524.4 3.2 convolution_convert_fusion.4
  532.2 4.5 fusion.70
  540.0 2.3 add_convert_fusion
  544.1 20.0 %all-to-all-done.10 = bf16[64,8,3200]{2,1,0:T(8,128)(2,1)} async-done(((bf16[64,8,3200]{2,1,0:T(8,128)(2,1)}), bf16[64,8,3200]{2,1,0:T(8,128)(2,1)}, u32[]{:S(2)}, u32[]{:S(2)}) %all-to-all-start.10) | async-done | bytes 3276832 | tf_op jit(solution)/shard_map/all_to_all | solution.py:202
  564.1 6.5 %all-to-all-start.9 = ((bf16[64,8,3200]{2,1,0:T(8,128)(2,1)}), bf16[64,8,3200]{2,1,0:T(8,128)(2,1)S(1)}, u32[]{:S(2)}, u32[]{:S(2)}) async-start(bf16[64,8,3200]{2,1,0:T(8,128)(2,1)} %maximum_bitcast_fusion), calls=%async_computation.9 | async-start | bytes 6553600 | tf_op jit(solution)/shard_map/all_to_all | solution.py:202
  570.7 3.2 fusion.39
  575.0 2.4 convert_reduce_fusion
  582.2 31.3 %all-to-all-done.9 = bf16[64,8,3200]{2,1,0:T(8,128)(2,1)S(1)} async-done(((bf16[64,8,3200]{2,1,0:T(8,128)(2,1)}), bf16[64,8,3200]{2,1,0:T(8,128)(2,1)S(1)}, u32[]{:S(2)}, u32[]{:S(2)}) %all-to-all-start.9) | async-done | bytes 3276832 | tf_op jit(solution)/shard_map/all_to_all | solution.py:202
  (485 shorter events, 127.5 us)
Async XLA Ops:
  12.8 11.9 %copy-start.134 = (s32[512]{0:T(512)S(1)}, s32[512]{0:T(512)}, u32[]{:S(2)}) copy-start(s32[512]{0:T(512)} %param.15) | copy-start | bytes 6148
  12.8 12.5 %copy-start.135 = (s32[512]{0:T(512)S(1)}, s32[512]{0:T(512)}, u32[]{:S(2)}) copy-start(s32[512]{0:T(512)} %param.14) | copy-start | bytes 6148
  12.8 13.4 %copy-start.132 = (s32[128,8]{0,1:T(8,128)S(1)}, s32[128,8]{0,1:T(8,128)}, u32[]{:S(2)}) copy-start(s32[128,8]{0,1:T(8,128)} %param.16) | copy-start | bytes 12292
  12.8 14.4 %copy-start.76 = (bf16[2,128,1024]{2,1,0:T(8,128)(2,1)S(1)}, bf16[2,128,1024]{2,1,0:T(8,128)(2,1)}, u32[]{:S(2)}) copy-start(bf16[2,128,1024]{2,1,0:T(8,128)(2,1)} %param.23) | copy-start | bytes 1572868
  12.8 52.9 %all-to-all-start = ((bf16[64,8,3200]{2,1,0:T(8,128)(2,1)}), bf16[64,8,3200]{2,1,0:T(8,128)(2,1)}, u32[]{:S(2)}, u32[]{:S(2)}) async-start(bf16[64,8,3200]{2,1,0:T(8,128)(2,1)} %broadcast_in_dim.73), calls=%async_computation | async-start | bytes 6553600 | tf_op jit(solution)/shard_map/all_to_all | solution.py:47
  24.7 4.9 copy-start.66
  24.7 183.7 %all-gather.2.cloned.1.call-start = ((), (), s32[]{:S(2)}) async-start(), calls=%async_computation.13 | async-start | bytes 6604800 | tf_op jit(solution)/shard_map/all_gather | solution.py:41
  65.7 6.2 collective-permute-start
  80.0 5.8 copy-start.138
  80.1 8.5 %copy-start.113 = (pred[128,128]{0,1:T(8,128)(4,1)}, pred[128,128]{0,1:T(8,128)(4,1)S(1)}, u32[]{:S(2)}) copy-start(pred[128,128]{0,1:T(8,128)(4,1)S(1)} %fusion.136) | copy-start | bytes 49156
  80.3 20.2 %collective-permute-start.1 = (bf16[128,3072]{1,0:T(8,128)(2,1)S(1)}, bf16[128,3072]{1,0:T(8,128)(2,1)}, u32[]{:S(2)}, u32[]{:S(2)}) collective-permute-start(bf16[128,3072]{1,0:T(8,128)(2,1)S(1)} %get-tuple-element.55), channel_id=1, source_target_pairs={{0,2},{2,0},{1,3},{3,1},{4,6},{6,4},{5,7},{7,5},{8,10},{10,8},{9,1... | collective-permute-start | bytes 2359304 | tf_op jit(solution)/shard_map/ppermute | solution.py:522
  91.7 113.4 %copy-start.27 = (f32[128,1024]{1,0:T(8,128)}, f32[128,1024]{1,0:T(8,128)S(1)}, u32[]{:S(2)}) copy-start(f32[128,1024]{1,0:T(8,128)S(1)} %get-tuple-element.157) | copy-start | bytes 1572868
  91.7 10.0 %copy-start.130 = (f32[128]{0:T(128)}, f32[128]{0:T(128)S(1)}, u32[]{:S(2)}) copy-start(f32[128]{0:T(128)S(1)} %add_rsqrt_fusion.2) | copy-start | bytes 1540
  103.9 8.0 %collective-permute-start.2 = (bf16[2,128,3072]{2,1,0:T(8,128)(2,1)}, bf16[2,128,3072]{2,1,0:T(8,128)(2,1)}, u32[]{:S(2)}, u32[]{:S(2)}) collective-permute-start(bf16[2,128,3072]{2,1,0:T(8,128)(2,1)} %pad_maximum_fusion.6), channel_id=1, source_target_pairs={{0,1},{1,0},{2,3},{3,2},{4,5},{5,4},{6,7},{7,6},{8,9},{9,8},{10,11... | collective-permute-start | bytes 4718600 | tf_op jit(solution)/shard_map/ppermute | solution.py:154
  103.9 44.9 %all-to-all-start.1 = ((bf16[32,40,1024]{2,1,0:T(8,128)(2,1)}), bf16[32,40,1024]{2,1,0:T(8,128)(2,1)S(1)}, u32[]{:S(2)}, u32[]{:S(2)}) async-start(bf16[32,40,1024]{2,1,0:T(8,128)(2,1)} %bitcast.340), calls=%async_computation.1 | async-start | bytes 5242880 | tf_op jit(solution)/shard_map/all_to_all | solution.py:143
  160.7 44.2 %all-to-all-start.2 = ((bf16[32,40,1024]{2,1,0:T(8,128)(2,1)}), bf16[32,40,1024]{2,1,0:T(8,128)(2,1)}, u32[]{:S(2)}, u32[]{:S(2)}) async-start(bf16[32,40,1024]{2,1,0:T(8,128)(2,1)} %bitcast.331), calls=%async_computation.2 | async-start | bytes 5242880 | tf_op jit(solution)/shard_map/all_to_all | solution.py:143
  171.7 36.6 %copy-start.114 = (f32[128]{0:T(128)}, f32[128]{0:T(128)S(1)}, u32[]{:S(2)}) copy-start(f32[128]{0:T(128)S(1)} %get-tuple-element.158) | copy-start | bytes 1540
  171.7 36.6 %copy-start.124 = (f32[128]{0:T(128)}, f32[128]{0:T(128)S(1)}, u32[]{:S(2)}) copy-start(f32[128]{0:T(128)S(1)} %fusion.147) | copy-start | bytes 1540
  204.9 25.0 %collective-permute-start.3 = (bf16[128,3072]{1,0:T(8,128)(2,1)}, bf16[128,3072]{1,0:T(8,128)(2,1)}, u32[]{:S(2)}, u32[]{:S(2)}) collective-permute-start(bf16[128,3072]{1,0:T(8,128)(2,1)} %get-tuple-element.66), channel_id=1, source_target_pairs={{0,2},{2,0},{1,3},{3,1},{4,6},{6,4},{5,7},{7,5},{8,10},{10,8},{9,1... | collective-permute-start | bytes 2359304 | tf_op jit(solution)/shard_map/ppermute | solution.py:552
  209.8 16.9 %copy-start.106 = (f32[1024]{0:T(1024)}, f32[1024]{0:T(1024)S(1)}, u32[]{:S(2)}) copy-start(f32[1024]{0:T(1024)S(1)} %get-tuple-element.93) | copy-start | bytes 12292
  226.6 164.3 %copy-start.26 = (f32[128,1024]{1,0:T(8,128)}, f32[128,1024]{1,0:T(8,128)S(1)}, u32[]{:S(2)}) copy-start(f32[128,1024]{1,0:T(8,128)S(1)} %get-tuple-element.165) | copy-start | bytes 1572868
  229.8 40.1 %all-to-all-start.3 = ((bf16[32,40,1024]{2,1,0:T(8,128)(2,1)}), bf16[32,40,1024]{2,1,0:T(8,128)(2,1)}, u32[]{:S(2)}, u32[]{:S(2)}) async-start(bf16[32,40,1024]{2,1,0:T(8,128)(2,1)} %bitcast.342), calls=%async_computation.3 | async-start | bytes 5242880 | tf_op jit(solution)/shard_map/all_to_all | solution.py:143
  238.8 5.1 copy-start.53
  241.0 36.2 %collective-permute-start.4 = (bf16[2,128,3072]{2,1,0:T(8,128)(2,1)}, bf16[2,128,3072]{2,1,0:T(8,128)(2,1)}, u32[]{:S(2)}, u32[]{:S(2)}) collective-permute-start(bf16[2,128,3072]{2,1,0:T(8,128)(2,1)} %pad_maximum_fusion.7), channel_id=1, source_target_pairs={{0,1},{1,0},{2,3},{3,2},{4,5},{5,4},{6,7},{7,6},{8,9},{9,8},{10,11... | collective-permute-start | bytes 4718600 | tf_op jit(solution)/shard_map/ppermute | solution.py:154
  270.0 39.4 %all-to-all-start.4 = ((bf16[32,40,1024]{2,1,0:T(8,128)(2,1)}), bf16[32,40,1024]{2,1,0:T(8,128)(2,1)}, u32[]{:S(2)}, u32[]{:S(2)}) async-start(bf16[32,40,1024]{2,1,0:T(8,128)(2,1)} %bitcast.341), calls=%async_computation.4 | async-start | bytes 5242880 | tf_op jit(solution)/shard_map/all_to_all | solution.py:143
  309.4 38.8 %all-to-all-start.5 = ((bf16[32,40,1024]{2,1,0:T(8,128)(2,1)}), bf16[32,40,1024]{2,1,0:T(8,128)(2,1)}, u32[]{:S(2)}, u32[]{:S(2)}) async-start(bf16[32,40,1024]{2,1,0:T(8,128)(2,1)} %bitcast.330), calls=%async_computation.5 | async-start | bytes 5242880 | tf_op jit(solution)/shard_map/all_to_all | solution.py:143
  316.4 6.0 copy-start.21
  316.4 6.0 copy-start.23
  348.1 40.2 %all-to-all-start.6 = ((bf16[32,40,1024]{2,1,0:T(8,128)(2,1)}), bf16[32,40,1024]{2,1,0:T(8,128)(2,1)}, u32[]{:S(2)}, u32[]{:S(2)}) async-start(bf16[32,40,1024]{2,1,0:T(8,128)(2,1)} %bitcast.328), calls=%async_computation.6 | async-start | bytes 5242880 | tf_op jit(solution)/shard_map/all_to_all | solution.py:143
  354.7 222.7 %reduce-scatter.5.cloned.1.call-start = ((), (), s32[]{:S(2)}) async-start(), calls=%async_computation.15 | async-start | bytes 3932160 | tf_op jit(solution)/shard_map/reduce_scatter | solution.py:162
  371.0 19.9 %copy-start.107 = (f32[1024]{0:T(1024)S(1)}, f32[1024]{0:T(1024)}, u32[]{:S(2)}) copy-start(f32[1024]{0:T(1024)} %copy-done.106) | copy-start | bytes 12292
  390.9 6.0 copy-start.122
  391.8 5.1 copy-start.87
  391.8 5.1 copy-start.89
  391.8 5.1 copy-start.99
  402.3 5.0 copy-start.52
  409.8 38.7 %all-to-all-start.7 = ((bf16[32,40,1024]{2,1,0:T(8,128)(2,1)}), bf16[32,40,1024]{2,1,0:T(8,128)(2,1)}, u32[]{:S(2)}, u32[]{:S(2)}) async-start(bf16[32,40,1024]{2,1,0:T(8,128)(2,1)} %bitcast.339), calls=%async_computation.7 | async-start | bytes 5242880 | tf_op jit(solution)/shard_map/all_to_all | solution.py:143
  419.5 5.3 copy-start.46
  419.5 5.3 copy-start.104
  419.5 17.9 %collective-permute-start.5 = (bf16[512,2048]{1,0:T(8,128)(2,1)}, bf16[512,2048]{1,0:T(8,128)(2,1)}, u32[]{:S(2)}, u32[]{:S(2)}) collective-permute-start(bf16[512,2048]{1,0:T(8,128)(2,1)} %convolution_convert_fusion.5), channel_id=1, source_target_pairs={{0,1},{1,0},{2,3},{3,2},{4,5},{5,4},{6,7},{7,6},{8,9},{9,8},{10,11... | collective-permute-start | bytes 6291464 | tf_op jit(solution)/shard_map/ppermute | solution.py:197
  422.6 12.2 %collective-permute-start.6 = (bf16[512,1024]{1,0:T(8,128)(2,1)}, bf16[512,1024]{1,0:T(8,128)(2,1)}, u32[]{:S(2)}, u32[]{:S(2)}) collective-permute-start(bf16[512,1024]{1,0:T(8,128)(2,1)} %convolution_convert_fusion.9), channel_id=1, source_target_pairs={{0,1},{1,0},{2,3},{3,2},{4,5},{5,4},{6,7},{7,6},{8,9},{9,8},{10,11... | collective-permute-start | bytes 3145736 | tf_op jit(solution)/shard_map/ppermute | solution.py:197
  430.1 4.0 collective-permute-start.7
  465.2 7.1 %copy-start.105 = (f32[128,32]{0,1:T(8,128)S(1)}, f32[128,32]{0,1:T(8,128)}, u32[]{:S(2)}) copy-start(f32[128,32]{0,1:T(8,128)} %get-tuple-element.175) | copy-start | bytes 49156
  465.2 40.6 %all-to-all-start.8 = ((bf16[32,40,1024]{2,1,0:T(8,128)(2,1)}), bf16[32,40,1024]{2,1,0:T(8,128)(2,1)}, u32[]{:S(2)}, u32[]{:S(2)}) async-start(bf16[32,40,1024]{2,1,0:T(8,128)(2,1)} %bitcast.329), calls=%async_computation.8 | async-start | bytes 5242880 | tf_op jit(solution)/shard_map/all_to_all | solution.py:143
  472.1 105.3 %reduce-scatter.3.cloned.1.call-start = ((), (), s32[]{:S(2)}) async-start(), calls=%async_computation.14 | async-start | bytes 3932160 | tf_op jit(solution)/shard_map/reduce_scatter | solution.py:162
  483.9 21.9 %copy-start.28 = (f32[128,1024]{1,0:T(8,128)S(1)}, f32[128,1024]{1,0:T(8,128)}, u32[]{:S(2)}) copy-start(f32[128,1024]{1,0:T(8,128)} %copy-done.27) | copy-start | bytes 1572868
  483.9 21.9 %copy-start.131 = (f32[128]{0:T(128)S(1)}, f32[128]{0:T(128)}, u32[]{:S(2)}) copy-start(f32[128]{0:T(128)} %copy-done.130) | copy-start | bytes 1540
  487.0 21.8 %copy-start.37 = (f32[128,1024]{1,0:T(8,128)S(1)}, f32[128,1024]{1,0:T(8,128)}, u32[]{:S(2)}) copy-start(f32[128,1024]{1,0:T(8,128)} %copy-done.35) | copy-start | bytes 1572868
  509.0 30.4 %copy-start.31 = (f32[128,1024]{1,0:T(8,128)}, f32[128,1024]{1,0:T(8,128)S(1)}, u32[]{:S(2)}) copy-start(f32[128,1024]{1,0:T(8,128)S(1)} %multiply_add_fusion) | copy-start | bytes 1572868
  513.8 8.5 %copy-start.82 = (bf16[128,8,32]{0,2,1:T(8,128)(2,1)S(1)}, bf16[128,8,32]{0,2,1:T(8,128)(2,1)}, u32[]{:S(2)}) copy-start(bf16[128,8,32]{0,2,1:T(8,128)(2,1)} %copy-done.80) | copy-start | bytes 196612
  513.8 8.5 %copy-start.85 = (bf16[128,8,32]{0,2,1:T(8,128)(2,1)S(1)}, bf16[128,8,32]{0,2,1:T(8,128)(2,1)}, u32[]{:S(2)}) copy-start(bf16[128,8,32]{0,2,1:T(8,128)(2,1)} %copy-done.83) | copy-start | bytes 196612
  513.8 8.5 %copy-start.91 = (bf16[128,1024]{0,1:T(8,128)(2,1)S(1)}, bf16[128,1024]{0,1:T(8,128)(2,1)}, u32[]{:S(2)}) copy-start(bf16[128,1024]{0,1:T(8,128)(2,1)} %copy-done.90) | copy-start | bytes 786436
  513.8 8.5 %copy-start.94 = (bf16[128,16,32]{0,2,1:T(8,128)(2,1)S(1)}, bf16[128,16,32]{0,2,1:T(8,128)(2,1)}, u32[]{:S(2)}) copy-start(bf16[128,16,32]{0,2,1:T(8,128)(2,1)} %copy-done.92) | copy-start | bytes 393220
  513.8 8.5 %copy-start.97 = (bf16[128,16,32]{0,2,1:T(8,128)(2,1)S(1)}, bf16[128,16,32]{0,2,1:T(8,128)(2,1)}, u32[]{:S(2)}) copy-start(bf16[128,16,32]{0,2,1:T(8,128)(2,1)} %copy-done.95) | copy-start | bytes 393220
  513.8 8.5 %copy-start.120 = (f32[8,2,128]{2,1,0:T(2,128)S(1)}, f32[8,2,128]{2,1,0:T(2,128)}, u32[]{:S(2)}) copy-start(f32[8,2,128]{2,1,0:T(2,128)} %copy-done.118) | copy-start | bytes 24580
  513.8 50.3 %all-to-all-start.10 = ((bf16[64,8,3200]{2,1,0:T(8,128)(2,1)}), bf16[64,8,3200]{2,1,0:T(8,128)(2,1)}, u32[]{:S(2)}, u32[]{:S(2)}) async-start(bf16[64,8,3200]{2,1,0:T(8,128)(2,1)} %bitcast.109), calls=%async_computation.10 | async-start | bytes 6553600 | tf_op jit(solution)/shard_map/all_to_all | solution.py:202
  522.2 10.0 %copy-start.59 = (bf16[128,16,64]{0,2,1:T(8,128)(2,1)}, bf16[128,16,64]{0,2,1:T(8,128)(2,1)S(1)}, u32[]{:S(2)}) copy-start(bf16[128,16,64]{0,2,1:T(8,128)(2,1)S(1)} %pad_maximum_fusion.15) | copy-start | bytes 786436
  524.4 5.4 copy-start.123
  527.6 12.3 %collective-permute-start.8 = (bf16[512,2048]{1,0:T(8,128)(2,1)}, bf16[512,2048]{1,0:T(8,128)(2,1)}, u32[]{:S(2)}, u32[]{:S(2)}) collective-permute-start(bf16[512,2048]{1,0:T(8,128)(2,1)} %convolution_convert_fusion.4), channel_id=1, source_target_pairs={{0,1},{1,0},{2,3},{3,2},{4,5},{5,4},{6,7},{7,6},{8,9},{9,8},{10,11... | collective-permute-start | bytes 6291464 | tf_op jit(solution)/shard_map/ppermute | solution.py:197
  531.4 5.5 copy-start.65
  531.4 5.5 copy-start.133
  531.4 8.0 %collective-permute-start.9 = (bf16[512,1024]{1,0:T(8,128)(2,1)S(1)}, bf16[512,1024]{1,0:T(8,128)(2,1)S(1)}, u32[]{:S(2)}, u32[]{:S(2)}) collective-permute-start(bf16[512,1024]{1,0:T(8,128)(2,1)S(1)} %convolution_convert_fusion.8), channel_id=1, source_target_pairs={{0,1},{1,0},{2,3},{3,2},{4,5},{5,4},{6,7},{7,6},{8,9},{9,8},{10,11... | collective-permute-start | bytes 3145736 | tf_op jit(solution)/shard_map/ppermute | solution.py:197
  538.0 1.4 collective-permute-start.10
  564.1 49.4 %all-to-all-start.9 = ((bf16[64,8,3200]{2,1,0:T(8,128)(2,1)}), bf16[64,8,3200]{2,1,0:T(8,128)(2,1)S(1)}, u32[]{:S(2)}, u32[]{:S(2)}) async-start(bf16[64,8,3200]{2,1,0:T(8,128)(2,1)} %maximum_bitcast_fusion), calls=%async_computation.9 | async-start | bytes 6553600 | tf_op jit(solution)/shard_map/all_to_all | solution.py:202
  (110 other events, 263.4 us)
Sparse Core Ops, SparseCore 0:
  79.9 89.5 all-gather.1
  367.2 47.1 reduce-scatter.4
  482.5 84.0 reduce-scatter.2

commit v11 on v10

--- a/solution.py
+++ b/solution.py
@@ -350,7 +350,7 @@
         in_specs=specs,
         out_specs=[blocked(width) for width, _ in outs],
         out_shape=[jax.ShapeDtypeStruct((ROWS, width), kind) for width, kind in outs],
-        compiler_params=pltpu.CompilerParams(vmem_limit_bytes=40 * 1024 * 1024),
+        compiler_params=pltpu.CompilerParams(vmem_limit_bytes=56 * 1024 * 1024),
         cost_estimate=pl.CostEstimate(flops=flops, bytes_accessed=2 * moved, transcendentals=0),
     )(*ins)
 

time: 634 us -> 625 us (0.986)
  local copies, waits for them, and re-layouts: 59.2 us -> 36.9 us
  Pallas kernels: 29 us -> 38.4 us
    unnamed x298 -> x250, local copies, waits for them, and re-layouts: 35.8 us -> 9.37 us
    pallas_call x4, Pallas kernels: 29 us -> 38.4 us  [row_blocks(): pl.pallas_call(kernel, grid=(ROWS // ROW_BLOCK,), in_specs=specs, out_spe...]
  transfers between devices with their start and end apart: 25 -> 25, of which waited for: 14 -> 14; matrix products, arithmetic and copies ran while one was open for 28% -> 30% of each run, Pallas kernels for 5% -> 6%
where the time goes in v11:
time: 625 us; the launch traced here: 614 us
  waiting for transfers between devices  259 us (41%)
  matrix products  125 us (20%)
  starting transfers between devices  88.8 us (14%)
  other arithmetic  49.9 us (8%)
  Pallas kernels  38.4 us (6%)
  local copies, waits for them, and re-layouts  36.9 us (6%)
  between operations  16.2 us (3%)
    all_to_all x8, waiting for transfers between devices, trade_rows(): lax.all_to_all(rows.reshape(E, ROOM, MODEL_WIDTH), EXPERT_AXES, split_axi...  165 us
    all_to_all x8, starting transfers between devices, trade_rows(): lax.all_to_all(rows.reshape(E, ROOM, MODEL_WIDTH), EXPERT_AXES, split_axi...  58.1 us
    all_to_all x2, waiting for transfers between devices, chip_sum(): lax.all_to_all(parts, Z_AXES + ('x', 'y'), split_axis=0, concat_axis=0, t...  49.9 us
    pallas_call x4, Pallas kernels, row_blocks(): pl.pallas_call(kernel, grid=(ROWS // ROW_BLOCK,), in_specs=specs, out_spe...  38.4 us
    all_to_all x1, waiting for transfers between devices, sent_by_chips(): lax.all_to_all(copies, CHIP_AXES, split_axis=0, concat_axis=0, tiled=True)  36.2 us
    dot_general x6, matrix products, feed_backward(): lax.dot_general(left, right, pair, preferred_element_type=jnp.float32)  21 us
    all_to_all x2, starting transfers between devices, chip_sum(): lax.all_to_all(parts, Z_AXES + ('x', 'y'), split_axis=0, concat_axis=0, t...  13.6 us
  transfers between devices with their start and end apart: 25, of which 14 were waited for; matrix products, arithmetic and copies ran while one was open for 30% of the time, Pallas kernels for 6%

profile of v11, /device:TPU:2, one launch (start us, length us, event | category | flops | bytes accessed | tf_op | source)
XLA Modules:
  0.0 614.4 jit_solution(18042134318505012605)
XLA Ops:
  12.9 11.8 %all-to-all-start = ((bf16[64,8,3200]{2,1,0:T(8,128)(2,1)}), bf16[64,8,3200]{2,1,0:T(8,128)(2,1)}, u32[]{:S(2)}, u32[]{:S(2)}) async-start(bf16[64,8,3200]{2,1,0:T(8,128)(2,1)} %broadcast_in_dim.73), calls=%async_computation | async-start | bytes 6553600 | tf_op jit(solution)/shard_map/all_to_all | solution.py:47
  29.6 36.2 %all-to-all-done = bf16[64,8,3200]{2,1,0:T(8,128)(2,1)} async-done(((bf16[64,8,3200]{2,1,0:T(8,128)(2,1)}), bf16[64,8,3200]{2,1,0:T(8,128)(2,1)}, u32[]{:S(2)}, u32[]{:S(2)}) %all-to-all-start) | async-done | bytes 3276832 | tf_op jit(solution)/shard_map/all_to_all | solution.py:47
  65.8 6.2 %collective-permute-done = bf16[64,8,3200]{2,1,0:T(8,128)(2,1)} collective-permute-done((bf16[64,8,3200]{2,1,0:T(8,128)(2,1)}, bf16[64,8,3200]{2,1,0:T(8,128)(2,1)}, u32[]{:S(2)}, u32[]{:S(2)}) %collective-permute-start) | collective-permute-done | bytes 3276832 | tf_op jit(solution)/shard_map/ppermute | solution.py:49
  72.0 3.5 select_bitcast_fusion.1
  75.5 3.4 pad_maximum_fusion
  82.9 3.0 fusion.9
  91.4 2.4 fusion.213
  95.5 2.2 multiply_reduce_fusion.10
  97.9 2.3 convolution_convert_fusion.3
  104.3 8.1 %all-to-all-start.1 = ((bf16[32,40,1024]{2,1,0:T(8,128)(2,1)}), bf16[32,40,1024]{2,1,0:T(8,128)(2,1)}, u32[]{:S(2)}, u32[]{:S(2)}) async-start(bf16[32,40,1024]{2,1,0:T(8,128)(2,1)} %bitcast.330), calls=%async_computation.1 | async-start | bytes 5242880 | tf_op jit(solution)/shard_map/all_to_all | solution.py:143
  116.6 32.7 %all-to-all-done.1 = bf16[32,40,1024]{2,1,0:T(8,128)(2,1)} async-done(((bf16[32,40,1024]{2,1,0:T(8,128)(2,1)}), bf16[32,40,1024]{2,1,0:T(8,128)(2,1)}, u32[]{:S(2)}, u32[]{:S(2)}) %all-to-all-start.1) | async-done | bytes 2621472 | tf_op jit(solution)/shard_map/all_to_all | solution.py:143
  149.2 8.7 %shard_map.187 = (bf16[1280,1024]{1,0:T(8,128)(2,1)}, f32[1280,512]{1,0:T(8,128)}, f32[1280,512]{1,0:T(8,128)}) custom-call(bf16[1280,1024]{1,0:T(8,128)(2,1)} %bitcast.35.rows_ref, bf16[512,3072]{1,0:T(8,128)(2,1)} %bitcast.333), custom_call_target="tpu_custom_call" | custom-call | flops 4026531840 | bytes 11534336 | tf_op jit(solution)/shard_map/pallas_call | solution.py:347
  158.0 8.0 %all-to-all-start.2 = ((bf16[32,40,1024]{2,1,0:T(8,128)(2,1)}), bf16[32,40,1024]{2,1,0:T(8,128)(2,1)}, u32[]{:S(2)}, u32[]{:S(2)}) async-start(bf16[32,40,1024]{2,1,0:T(8,128)(2,1)} %bitcast.344), calls=%async_computation.2 | async-start | bytes 5242880 | tf_op jit(solution)/shard_map/all_to_all | solution.py:143
  168.3 32.0 %all-to-all-done.2 = bf16[32,40,1024]{2,1,0:T(8,128)(2,1)} async-done(((bf16[32,40,1024]{2,1,0:T(8,128)(2,1)}), bf16[32,40,1024]{2,1,0:T(8,128)(2,1)}, u32[]{:S(2)}, u32[]{:S(2)}) %all-to-all-start.2) | async-done | bytes 2621472 | tf_op jit(solution)/shard_map/all_to_all | solution.py:143
  202.3 2.5 multiply_reduce_fusion.9
  206.4 2.9 fusion.5
  216.4 2.4 fusion.215
  220.7 2.3 multiply_reduce_fusion.8
  223.9 2.4 convolution_convert_fusion.1
  226.3 7.1 %all-to-all-start.3 = ((bf16[32,40,1024]{2,1,0:T(8,128)(2,1)}), bf16[32,40,1024]{2,1,0:T(8,128)(2,1)}, u32[]{:S(2)}, u32[]{:S(2)}) async-start(bf16[32,40,1024]{2,1,0:T(8,128)(2,1)} %bitcast.332), calls=%async_computation.3 | async-start | bytes 5242880 | tf_op jit(solution)/shard_map/all_to_all | solution.py:143
  240.2 2.3 convolution_convert_fusion.2
  242.5 24.0 %all-to-all-done.3 = bf16[32,40,1024]{2,1,0:T(8,128)(2,1)} async-done(((bf16[32,40,1024]{2,1,0:T(8,128)(2,1)}), bf16[32,40,1024]{2,1,0:T(8,128)(2,1)}, u32[]{:S(2)}, u32[]{:S(2)}) %all-to-all-start.3) | async-done | bytes 2621472 | tf_op jit(solution)/shard_map/all_to_all | solution.py:143
  266.5 6.5 %all-to-all-start.4 = ((bf16[32,40,1024]{2,1,0:T(8,128)(2,1)}), bf16[32,40,1024]{2,1,0:T(8,128)(2,1)}, u32[]{:S(2)}, u32[]{:S(2)}) async-start(bf16[32,40,1024]{2,1,0:T(8,128)(2,1)} %bitcast.331), calls=%async_computation.4 | async-start | bytes 5242880 | tf_op jit(solution)/shard_map/all_to_all | solution.py:143
  277.3 8.6 %shard_map.188 = (bf16[1280,1024]{1,0:T(8,128)(2,1)}, f32[1280,512]{1,0:T(8,128)}, f32[1280,512]{1,0:T(8,128)}) custom-call(bf16[1280,1024]{1,0:T(8,128)(2,1)} %bitcast.58.rows_ref, bf16[512,3072]{1,0:T(8,128)(2,1)} %bitcast.335), custom_call_target="tpu_custom_call" | custom-call | flops 4026531840 | bytes 11534336 | tf_op jit(solution)/shard_map/pallas_call | solution.py:347
  285.9 19.9 %all-to-all-done.4 = bf16[32,40,1024]{2,1,0:T(8,128)(2,1)} async-done(((bf16[32,40,1024]{2,1,0:T(8,128)(2,1)}), bf16[32,40,1024]{2,1,0:T(8,128)(2,1)}, u32[]{:S(2)}, u32[]{:S(2)}) %all-to-all-start.4) | async-done | bytes 2621472 | tf_op jit(solution)/shard_map/all_to_all | solution.py:143
  305.8 7.2 %all-to-all-start.5 = ((bf16[32,40,1024]{2,1,0:T(8,128)(2,1)}), bf16[32,40,1024]{2,1,0:T(8,128)(2,1)}, u32[]{:S(2)}, u32[]{:S(2)}) async-start(bf16[32,40,1024]{2,1,0:T(8,128)(2,1)} %bitcast.343), calls=%async_computation.5 | async-start | bytes 5242880 | tf_op jit(solution)/shard_map/all_to_all | solution.py:143
  313.5 2.1 convolution_convert_fusion.17
  316.9 10.5 %shard_map.189 = (bf16[1280,1024]{1,0:T(8,128)(2,1)}, bf16[1280,512]{1,0:T(8,128)(2,1)}, bf16[1280,512]{1,0:T(8,128)(2,1)}, bf16[1280,512]{1,0:T(8,128)(2,1)}) custom-call(bf16[1280,1024]{1,0:T(8,128)(2,1)} %bitcast.65.grad_ref, f32[1280,512]{1,0:T(8,128)} %get-tuple-element.74.gate_ref, f32[1280,512]{1,0:T(8,128)} %get-tuple-element.75.up_ref, ...), custom_call_target="tpu_custom_call" | custom-call | flops 4026531840 | bytes 22020096 | tf_op jit(solution)/shard_map/pallas_call | solution.py:347
  327.4 18.5 %all-to-all-done.5 = bf16[32,40,1024]{2,1,0:T(8,128)(2,1)} async-done(((bf16[32,40,1024]{2,1,0:T(8,128)(2,1)}), bf16[32,40,1024]{2,1,0:T(8,128)(2,1)}, u32[]{:S(2)}, u32[]{:S(2)}) %all-to-all-start.5) | async-done | bytes 2621472 | tf_op jit(solution)/shard_map/all_to_all | solution.py:143
  345.9 6.8 %all-to-all-start.6 = ((bf16[32,40,1024]{2,1,0:T(8,128)(2,1)}), bf16[32,40,1024]{2,1,0:T(8,128)(2,1)}, u32[]{:S(2)}, u32[]{:S(2)}) async-start(bf16[32,40,1024]{2,1,0:T(8,128)(2,1)} %bitcast.341), calls=%async_computation.6 | async-start | bytes 5242880 | tf_op jit(solution)/shard_map/all_to_all | solution.py:143
  352.7 3.8 convolution_convert_fusion.10
  356.5 3.4 convolution_convert_fusion.11
  360.0 3.3 convolution_convert_fusion.12
  365.1 2.7 fusion.11
  371.0 14.5 %all-to-all-done.6 = bf16[32,40,1024]{2,1,0:T(8,128)(2,1)} async-done(((bf16[32,40,1024]{2,1,0:T(8,128)(2,1)}), bf16[32,40,1024]{2,1,0:T(8,128)(2,1)}, u32[]{:S(2)}, u32[]{:S(2)}) %all-to-all-start.6) | async-done | bytes 2621472 | tf_op jit(solution)/shard_map/all_to_all | solution.py:143
  385.5 2.7 multiply_reduce_fusion.4
  389.8 3.2 fusion.46
  394.2 2.2 fusion.56
  399.5 4.0 multiply_reduce_fusion.5
  404.5 2.4 convolution_convert_fusion
  406.8 7.2 %all-to-all-start.7 = ((bf16[32,40,1024]{2,1,0:T(8,128)(2,1)}), bf16[32,40,1024]{2,1,0:T(8,128)(2,1)}, u32[]{:S(2)}, u32[]{:S(2)}) async-start(bf16[32,40,1024]{2,1,0:T(8,128)(2,1)} %bitcast.329), calls=%async_computation.7 | async-start | bytes 5242880 | tf_op jit(solution)/shard_map/all_to_all | solution.py:143
  414.0 3.2 convolution_convert_fusion.5
  427.3 2.7 convolution_multiply_fusion
  431.9 2.7 add_convert_fusion.3
  434.6 3.7 add_convert_fusion.1
  438.3 8.5 %all-to-all-done.7 = bf16[32,40,1024]{2,1,0:T(8,128)(2,1)} async-done(((bf16[32,40,1024]{2,1,0:T(8,128)(2,1)}), bf16[32,40,1024]{2,1,0:T(8,128)(2,1)}, u32[]{:S(2)}, u32[]{:S(2)}) %all-to-all-start.7) | async-done | bytes 2621472 | tf_op jit(solution)/shard_map/all_to_all | solution.py:143
  446.8 10.5 %shard_map.190 = (bf16[1280,1024]{1,0:T(8,128)(2,1)}, bf16[1280,512]{1,0:T(8,128)(2,1)}, bf16[1280,512]{1,0:T(8,128)(2,1)}, bf16[1280,512]{1,0:T(8,128)(2,1)}) custom-call(bf16[1280,1024]{1,0:T(8,128)(2,1)} %bitcast.88.grad_ref, f32[1280,512]{1,0:T(8,128)} %get-tuple-element.79.gate_ref, f32[1280,512]{1,0:T(8,128)} %get-tuple-element.80.up_ref, ...), custom_call_target="tpu_custom_call" | custom-call | flops 4026531840 | bytes 22020096 | tf_op jit(solution)/shard_map/pallas_call | solution.py:347
  457.3 7.2 %all-to-all-start.8 = ((bf16[32,40,1024]{2,1,0:T(8,128)(2,1)}), bf16[32,40,1024]{2,1,0:T(8,128)(2,1)}, u32[]{:S(2)}, u32[]{:S(2)}) async-start(bf16[32,40,1024]{2,1,0:T(8,128)(2,1)} %bitcast.342), calls=%async_computation.8 | async-start | bytes 5242880 | tf_op jit(solution)/shard_map/all_to_all | solution.py:143
  465.9 3.8 convolution_convert_fusion.13
  469.7 3.4 convolution_convert_fusion.14
  473.2 3.3 convolution_convert_fusion.15
  478.2 3.3 pad_maximum_fusion.1
  481.6 15.0 %all-to-all-done.8 = bf16[32,40,1024]{2,1,0:T(8,128)(2,1)} async-done(((bf16[32,40,1024]{2,1,0:T(8,128)(2,1)}), bf16[32,40,1024]{2,1,0:T(8,128)(2,1)}, u32[]{:S(2)}, u32[]{:S(2)}) %all-to-all-start.8) | async-done | bytes 2621472 | tf_op jit(solution)/shard_map/all_to_all | solution.py:143
  496.6 3.1 multiply_reduce_fusion.2
  499.9 2.7 fusion.49
  507.3 7.4 %all-to-all-start.10 = ((bf16[64,8,3200]{2,1,0:T(8,128)(2,1)}), bf16[64,8,3200]{2,1,0:T(8,128)(2,1)}, u32[]{:S(2)}, u32[]{:S(2)}) async-start(bf16[64,8,3200]{2,1,0:T(8,128)(2,1)} %bitcast.328), calls=%async_computation.10 | async-start | bytes 6553600 | tf_op jit(solution)/shard_map/all_to_all | solution.py:202
  517.3 3.0 convolution_convert_fusion.4
  524.9 4.7 fusion.70
  532.7 2.3 add_convert_fusion
  536.9 19.4 %all-to-all-done.10 = bf16[64,8,3200]{2,1,0:T(8,128)(2,1)} async-done(((bf16[64,8,3200]{2,1,0:T(8,128)(2,1)}), bf16[64,8,3200]{2,1,0:T(8,128)(2,1)}, u32[]{:S(2)}, u32[]{:S(2)}) %all-to-all-start.10) | async-done | bytes 3276832 | tf_op jit(solution)/shard_map/all_to_all | solution.py:202
  556.3 6.2 %all-to-all-start.9 = ((bf16[64,8,3200]{2,1,0:T(8,128)(2,1)}), bf16[64,8,3200]{2,1,0:T(8,128)(2,1)S(1)}, u32[]{:S(2)}, u32[]{:S(2)}) async-start(bf16[64,8,3200]{2,1,0:T(8,128)(2,1)} %maximum_bitcast_fusion), calls=%async_computation.9 | async-start | bytes 6553600 | tf_op jit(solution)/shard_map/all_to_all | solution.py:202
  562.5 3.2 fusion.39
  566.8 2.4 convert_reduce_fusion
  574.0 30.5 %all-to-all-done.9 = bf16[64,8,3200]{2,1,0:T(8,128)(2,1)S(1)} async-done(((bf16[64,8,3200]{2,1,0:T(8,128)(2,1)}), bf16[64,8,3200]{2,1,0:T(8,128)(2,1)S(1)}, u32[]{:S(2)}, u32[]{:S(2)}) %all-to-all-start.9) | async-done | bytes 3276832 | tf_op jit(solution)/shard_map/all_to_all | solution.py:202
  (437 shorter events, 110.1 us)
Async XLA Ops:
  12.9 11.9 %copy-start.110 = (s32[512]{0:T(512)S(1)}, s32[512]{0:T(512)}, u32[]{:S(2)}) copy-start(s32[512]{0:T(512)} %param.15) | copy-start | bytes 6148
  12.9 12.5 %copy-start.111 = (s32[512]{0:T(512)S(1)}, s32[512]{0:T(512)}, u32[]{:S(2)}) copy-start(s32[512]{0:T(512)} %param.14) | copy-start | bytes 6148
  12.9 13.4 %copy-start.108 = (s32[128,8]{0,1:T(8,128)S(1)}, s32[128,8]{0,1:T(8,128)}, u32[]{:S(2)}) copy-start(s32[128,8]{0,1:T(8,128)} %param.16) | copy-start | bytes 12292
  12.9 14.4 %copy-start.54 = (bf16[2,128,1024]{2,1,0:T(8,128)(2,1)S(1)}, bf16[2,128,1024]{2,1,0:T(8,128)(2,1)}, u32[]{:S(2)}) copy-start(bf16[2,128,1024]{2,1,0:T(8,128)(2,1)} %param.23) | copy-start | bytes 1572868
  12.9 52.9 %all-to-all-start = ((bf16[64,8,3200]{2,1,0:T(8,128)(2,1)}), bf16[64,8,3200]{2,1,0:T(8,128)(2,1)}, u32[]{:S(2)}, u32[]{:S(2)}) async-start(bf16[64,8,3200]{2,1,0:T(8,128)(2,1)} %broadcast_in_dim.73), calls=%async_computation | async-start | bytes 6553600 | tf_op jit(solution)/shard_map/all_to_all | solution.py:47
  24.7 180.1 %all-gather.2.cloned.1.call-start = ((), (), s32[]{:S(2)}) async-start(), calls=%async_computation.13 | async-start | bytes 6604800 | tf_op jit(solution)/shard_map/all_gather | solution.py:41
  65.8 6.2 %collective-permute-start = (bf16[64,8,3200]{2,1,0:T(8,128)(2,1)}, bf16[64,8,3200]{2,1,0:T(8,128)(2,1)}, u32[]{:S(2)}, u32[]{:S(2)}) collective-permute-start(bf16[64,8,3200]{2,1,0:T(8,128)(2,1)} %all-to-all-done), channel_id=1, source_target_pairs={{0,1},{1,0},{2,3},{3,2},{4,5},{5,4},{6,7},{7,6},{8,9},{9,8},{10,11... | collective-permute-start | bytes 9830408 | tf_op jit(solution)/shard_map/ppermute | solution.py:49
  80.1 5.8 copy-start.114
  80.2 13.6 %copy-start.89 = (pred[128,128]{0,1:T(8,128)(4,1)}, pred[128,128]{0,1:T(8,128)(4,1)S(1)}, u32[]{:S(2)}) copy-start(pred[128,128]{0,1:T(8,128)(4,1)S(1)} %fusion.136) | copy-start | bytes 49156
  80.4 20.4 %collective-permute-start.1 = (bf16[128,3072]{1,0:T(8,128)(2,1)}, bf16[128,3072]{1,0:T(8,128)(2,1)}, u32[]{:S(2)}, u32[]{:S(2)}) collective-permute-start(bf16[128,3072]{1,0:T(8,128)(2,1)} %get-tuple-element.55), channel_id=1, source_target_pairs={{0,2},{2,0},{1,3},{3,1},{4,6},{6,4},{5,7},{7,5},{8,10},{10,8},{9,1... | collective-permute-start | bytes 2359304 | tf_op jit(solution)/shard_map/ppermute | solution.py:522
  90.6 4.8 copy-start.61
  90.6 4.8 copy-start.63
  97.9 68.1 %copy-start.15 = (bf16[128,1024]{1,0:T(8,128)(2,1)}, bf16[128,1024]{1,0:T(8,128)(2,1)S(1)}, u32[]{:S(2)}) copy-start(bf16[128,1024]{1,0:T(8,128)(2,1)S(1)} %multiply_convert_fusion.4) | copy-start | bytes 786436
  104.3 8.1 %collective-permute-start.2 = (bf16[2,128,3072]{2,1,0:T(8,128)(2,1)}, bf16[2,128,3072]{2,1,0:T(8,128)(2,1)}, u32[]{:S(2)}, u32[]{:S(2)}) collective-permute-start(bf16[2,128,3072]{2,1,0:T(8,128)(2,1)} %pad_maximum_fusion.6), channel_id=1, source_target_pairs={{0,1},{1,0},{2,3},{3,2},{4,5},{5,4},{6,7},{7,6},{8,9},{9,8},{10,11... | collective-permute-start | bytes 4718600 | tf_op jit(solution)/shard_map/ppermute | solution.py:154
  104.3 44.9 %all-to-all-start.1 = ((bf16[32,40,1024]{2,1,0:T(8,128)(2,1)}), bf16[32,40,1024]{2,1,0:T(8,128)(2,1)}, u32[]{:S(2)}, u32[]{:S(2)}) async-start(bf16[32,40,1024]{2,1,0:T(8,128)(2,1)} %bitcast.330), calls=%async_computation.1 | async-start | bytes 5242880 | tf_op jit(solution)/shard_map/all_to_all | solution.py:143
  158.0 42.3 %all-to-all-start.2 = ((bf16[32,40,1024]{2,1,0:T(8,128)(2,1)}), bf16[32,40,1024]{2,1,0:T(8,128)(2,1)}, u32[]{:S(2)}, u32[]{:S(2)}) async-start(bf16[32,40,1024]{2,1,0:T(8,128)(2,1)} %bitcast.344), calls=%async_computation.2 | async-start | bytes 5242880 | tf_op jit(solution)/shard_map/all_to_all | solution.py:143
  167.2 37.5 %copy-start.90 = (f32[128]{0:T(128)}, f32[128]{0:T(128)S(1)}, u32[]{:S(2)}) copy-start(f32[128]{0:T(128)S(1)} %get-tuple-element.158) | copy-start | bytes 1540
  167.3 37.5 %copy-start.100 = (f32[128]{0:T(128)}, f32[128]{0:T(128)S(1)}, u32[]{:S(2)}) copy-start(f32[128]{0:T(128)S(1)} %fusion.147) | copy-start | bytes 1540
  200.3 26.0 %collective-permute-start.3 = (bf16[128,3072]{1,0:T(8,128)(2,1)}, bf16[128,3072]{1,0:T(8,128)(2,1)}, u32[]{:S(2)}, u32[]{:S(2)}) collective-permute-start(bf16[128,3072]{1,0:T(8,128)(2,1)} %get-tuple-element.66), channel_id=1, source_target_pairs={{0,2},{2,0},{1,3},{3,1},{4,6},{6,4},{5,7},{7,5},{8,10},{10,8},{9,1... | collective-permute-start | bytes 2359304 | tf_op jit(solution)/shard_map/ppermute | solution.py:552
  204.7 4.6 copy-start.1
  206.4 16.7 %copy-start.82 = (f32[1024]{0:T(1024)}, f32[1024]{0:T(1024)S(1)}, u32[]{:S(2)}) copy-start(f32[1024]{0:T(1024)S(1)} %get-tuple-element.93) | copy-start | bytes 12292
  223.0 165.2 %copy-start = (f32[128,1024]{1,0:T(8,128)}, f32[128,1024]{1,0:T(8,128)S(1)}, u32[]{:S(2)}) copy-start(f32[128,1024]{1,0:T(8,128)S(1)} %get-tuple-element.165) | copy-start | bytes 1572868
  226.3 40.2 %all-to-all-start.3 = ((bf16[32,40,1024]{2,1,0:T(8,128)(2,1)}), bf16[32,40,1024]{2,1,0:T(8,128)(2,1)}, u32[]{:S(2)}, u32[]{:S(2)}) async-start(bf16[32,40,1024]{2,1,0:T(8,128)(2,1)} %bitcast.332), calls=%async_computation.3 | async-start | bytes 5242880 | tf_op jit(solution)/shard_map/all_to_all | solution.py:143
  235.0 5.2 copy-start.28
  237.2 35.9 %collective-permute-start.4 = (bf16[2,128,3072]{2,1,0:T(8,128)(2,1)}, bf16[2,128,3072]{2,1,0:T(8,128)(2,1)}, u32[]{:S(2)}, u32[]{:S(2)}) collective-permute-start(bf16[2,128,3072]{2,1,0:T(8,128)(2,1)} %pad_maximum_fusion.7), channel_id=1, source_target_pairs={{0,1},{1,0},{2,3},{3,2},{4,5},{5,4},{6,7},{7,6},{8,9},{9,8},{10,11... | collective-permute-start | bytes 4718600 | tf_op jit(solution)/shard_map/ppermute | solution.py:154
  266.5 39.3 %all-to-all-start.4 = ((bf16[32,40,1024]{2,1,0:T(8,128)(2,1)}), bf16[32,40,1024]{2,1,0:T(8,128)(2,1)}, u32[]{:S(2)}, u32[]{:S(2)}) async-start(bf16[32,40,1024]{2,1,0:T(8,128)(2,1)} %bitcast.331), calls=%async_computation.4 | async-start | bytes 5242880 | tf_op jit(solution)/shard_map/all_to_all | solution.py:143
  305.8 40.1 %all-to-all-start.5 = ((bf16[32,40,1024]{2,1,0:T(8,128)(2,1)}), bf16[32,40,1024]{2,1,0:T(8,128)(2,1)}, u32[]{:S(2)}, u32[]{:S(2)}) async-start(bf16[32,40,1024]{2,1,0:T(8,128)(2,1)} %bitcast.343), calls=%async_computation.5 | async-start | bytes 5242880 | tf_op jit(solution)/shard_map/all_to_all | solution.py:143
  345.9 39.6 %all-to-all-start.6 = ((bf16[32,40,1024]{2,1,0:T(8,128)(2,1)}), bf16[32,40,1024]{2,1,0:T(8,128)(2,1)}, u32[]{:S(2)}, u32[]{:S(2)}) async-start(bf16[32,40,1024]{2,1,0:T(8,128)(2,1)} %bitcast.341), calls=%async_computation.6 | async-start | bytes 5242880 | tf_op jit(solution)/shard_map/all_to_all | solution.py:143
  352.7 216.6 %reduce-scatter.5.cloned.1.call-start = ((), (), s32[]{:S(2)}) async-start(), calls=%async_computation.15 | async-start | bytes 3932160 | tf_op jit(solution)/shard_map/reduce_scatter | solution.py:162
  369.0 19.1 %copy-start.83 = (f32[1024]{0:T(1024)S(1)}, f32[1024]{0:T(1024)}, u32[]{:S(2)}) copy-start(f32[1024]{0:T(1024)} %copy-done.82) | copy-start | bytes 12292
  388.2 6.0 copy-start.98
  389.0 5.1 copy-start.67
  389.1 5.1 copy-start.69
  389.1 5.1 copy-start.77
  399.5 5.0 copy-start.27
  406.8 39.9 %all-to-all-start.7 = ((bf16[32,40,1024]{2,1,0:T(8,128)(2,1)}), bf16[32,40,1024]{2,1,0:T(8,128)(2,1)}, u32[]{:S(2)}, u32[]{:S(2)}) async-start(bf16[32,40,1024]{2,1,0:T(8,128)(2,1)} %bitcast.329), calls=%async_computation.7 | async-start | bytes 5242880 | tf_op jit(solution)/shard_map/all_to_all | solution.py:143
  417.3 5.3 copy-start.19
  417.3 5.3 copy-start.80
  417.3 17.3 %collective-permute-start.5 = (bf16[512,2048]{1,0:T(8,128)(2,1)}, bf16[512,2048]{1,0:T(8,128)(2,1)}, u32[]{:S(2)}, u32[]{:S(2)}) collective-permute-start(bf16[512,2048]{1,0:T(8,128)(2,1)} %convolution_convert_fusion.5), channel_id=1, source_target_pairs={{0,1},{1,0},{2,3},{3,2},{4,5},{5,4},{6,7},{7,6},{8,9},{9,8},{10,11... | collective-permute-start | bytes 6291464 | tf_op jit(solution)/shard_map/ppermute | solution.py:197
  420.3 11.6 %collective-permute-start.6 = (bf16[512,1024]{1,0:T(8,128)(2,1)}, bf16[512,1024]{1,0:T(8,128)(2,1)}, u32[]{:S(2)}, u32[]{:S(2)}) collective-permute-start(bf16[512,1024]{1,0:T(8,128)(2,1)} %convolution_convert_fusion.9), channel_id=1, source_target_pairs={{0,1},{1,0},{2,3},{3,2},{4,5},{5,4},{6,7},{7,6},{8,9},{9,8},{10,11... | collective-permute-start | bytes 3145736 | tf_op jit(solution)/shard_map/ppermute | solution.py:197
  427.2 4.7 copy-start.51
  427.2 4.0 collective-permute-start.7
  457.3 7.4 %copy-start.81 = (f32[128,32]{0,1:T(8,128)S(1)}, f32[128,32]{0,1:T(8,128)}, u32[]{:S(2)}) copy-start(f32[128,32]{0,1:T(8,128)} %get-tuple-element.175) | copy-start | bytes 49156
  457.3 39.3 %all-to-all-start.8 = ((bf16[32,40,1024]{2,1,0:T(8,128)(2,1)}), bf16[32,40,1024]{2,1,0:T(8,128)(2,1)}, u32[]{:S(2)}, u32[]{:S(2)}) async-start(bf16[32,40,1024]{2,1,0:T(8,128)(2,1)} %bitcast.342), calls=%async_computation.8 | async-start | bytes 5242880 | tf_op jit(solution)/shard_map/all_to_all | solution.py:143
  464.5 104.8 %reduce-scatter.3.cloned.1.call-start = ((), (), s32[]{:S(2)}) async-start(), calls=%async_computation.14 | async-start | bytes 3932160 | tf_op jit(solution)/shard_map/reduce_scatter | solution.py:162
  478.2 18.4 %copy-start.107 = (f32[128]{0:T(128)S(1)}, f32[128]{0:T(128)}, u32[]{:S(2)}) copy-start(f32[128]{0:T(128)} %copy-done.106) | copy-start | bytes 1540
  499.9 32.3 %copy-start.4 = (f32[128,1024]{1,0:T(8,128)}, f32[128,1024]{1,0:T(8,128)S(1)}, u32[]{:S(2)}) copy-start(f32[128,1024]{1,0:T(8,128)S(1)} %multiply_add_fusion) | copy-start | bytes 1572868
  507.2 7.5 %copy-start.55 = (bf16[128,16,32]{0,2,1:T(8,128)(2,1)S(1)}, bf16[128,16,32]{0,2,1:T(8,128)(2,1)}, u32[]{:S(2)}) copy-start(bf16[128,16,32]{0,2,1:T(8,128)(2,1)} %get-tuple-element.121) | copy-start | bytes 393220
  507.2 7.5 %copy-start.56 = (bf16[128,16,32]{0,2,1:T(8,128)(2,1)S(1)}, bf16[128,16,32]{0,2,1:T(8,128)(2,1)}, u32[]{:S(2)}) copy-start(bf16[128,16,32]{0,2,1:T(8,128)(2,1)} %get-tuple-element.122) | copy-start | bytes 393220
  507.2 7.5 %copy-start.71 = (bf16[128,8,32]{0,2,1:T(8,128)(2,1)S(1)}, bf16[128,8,32]{0,2,1:T(8,128)(2,1)}, u32[]{:S(2)}) copy-start(bf16[128,8,32]{0,2,1:T(8,128)(2,1)} %get-tuple-element.131) | copy-start | bytes 196612
  507.2 7.5 %copy-start.72 = (bf16[128,8,32]{0,2,1:T(8,128)(2,1)S(1)}, bf16[128,8,32]{0,2,1:T(8,128)(2,1)}, u32[]{:S(2)}) copy-start(bf16[128,8,32]{0,2,1:T(8,128)(2,1)} %get-tuple-element.132) | copy-start | bytes 196612
  507.2 7.6 %copy-start.65 = (bf16[128,8,32]{0,2,1:T(8,128)(2,1)S(1)}, bf16[128,8,32]{0,2,1:T(8,128)(2,1)}, u32[]{:S(2)}) copy-start(bf16[128,8,32]{0,2,1:T(8,128)(2,1)} %copy-done.63) | copy-start | bytes 196612
  507.2 7.6 %copy-start.96 = (f32[8,2,128]{2,1,0:T(2,128)S(1)}, f32[8,2,128]{2,1,0:T(2,128)}, u32[]{:S(2)}) copy-start(f32[8,2,128]{2,1,0:T(2,128)} %copy-done.94) | copy-start | bytes 24580
  507.3 49.0 %all-to-all-start.10 = ((bf16[64,8,3200]{2,1,0:T(8,128)(2,1)}), bf16[64,8,3200]{2,1,0:T(8,128)(2,1)}, u32[]{:S(2)}, u32[]{:S(2)}) async-start(bf16[64,8,3200]{2,1,0:T(8,128)(2,1)} %bitcast.328), calls=%async_computation.10 | async-start | bytes 6553600 | tf_op jit(solution)/shard_map/all_to_all | solution.py:202
  517.3 5.2 copy-start.99
  520.3 4.6 copy-start.21
  520.3 4.6 copy-start.85
  520.3 4.6 copy-start.115
  520.3 12.4 %collective-permute-start.8 = (bf16[512,2048]{1,0:T(8,128)(2,1)}, bf16[512,2048]{1,0:T(8,128)(2,1)}, u32[]{:S(2)}, u32[]{:S(2)}) collective-permute-start(bf16[512,2048]{1,0:T(8,128)(2,1)} %convolution_convert_fusion.4), channel_id=1, source_target_pairs={{0,1},{1,0},{2,3},{3,2},{4,5},{5,4},{6,7},{7,6},{8,9},{9,8},{10,11... | collective-permute-start | bytes 6291464 | tf_op jit(solution)/shard_map/ppermute | solution.py:197
  524.0 5.7 copy-start.44
  524.1 5.7 copy-start.109
  524.1 8.1 %collective-permute-start.9 = (bf16[512,1024]{1,0:T(8,128)(2,1)S(1)}, bf16[512,1024]{1,0:T(8,128)(2,1)S(1)}, u32[]{:S(2)}, u32[]{:S(2)}) collective-permute-start(bf16[512,1024]{1,0:T(8,128)(2,1)S(1)} %convolution_convert_fusion.8), channel_id=1, source_target_pairs={{0,1},{1,0},{2,3},{3,2},{4,5},{5,4},{6,7},{7,6},{8,9},{9,8},{10,11... | collective-permute-start | bytes 3145736 | tf_op jit(solution)/shard_map/ppermute | solution.py:197
  530.7 1.4 collective-permute-start.10
  556.3 48.3 %all-to-all-start.9 = ((bf16[64,8,3200]{2,1,0:T(8,128)(2,1)}), bf16[64,8,3200]{2,1,0:T(8,128)(2,1)S(1)}, u32[]{:S(2)}, u32[]{:S(2)}) async-start(bf16[64,8,3200]{2,1,0:T(8,128)(2,1)} %maximum_bitcast_fusion), calls=%async_computation.9 | async-start | bytes 6553600 | tf_op jit(solution)/shard_map/all_to_all | solution.py:202
  (86 other events, 221.4 us)
Sparse Core Ops, SparseCore 0:
  79.9 91.9 all-gather.1
  365.2 44.2 reduce-scatter.4
  478.4 77.0 reduce-scatter.2
